TPU v7x, 32 devices: a whole 2x2x4 slice. The times are simulated.
32 devices in a mesh: expert: 16 (over z, y, x), ffn: 2 (over core).
Axes of the slice: x: 2, y: 2, z: 4, core: 2. Of those that a mesh axis runs over, the one named last changes fastest.
Arguments:
- tokens: bfloat16 [2048, 4096], P('expert'), may hold values from -6 to 6
- cotangent: bfloat16 [2048, 4096], P('expert'), may hold values from -6 to 6
- expert_ids: int32 [2048, 1], P('expert'), may hold values from 0 to 1; in each aligned block of 128 rows (0 to 127, 128 to 255, ...) at most 80 rows name the same one
- in_weight: bfloat16 [16, 512, 5120], P('expert', None, 'ffn'), may hold values from -0.09375 to 0.09375
- out_weight: bfloat16 [16, 5120, 512], P('expert', 'ffn'), may hold values from -0.078125 to 0.078125
- width_states: float32 [2, 2, 4096], replicated, may hold values from 76.8 to 768
- hidden_states: float32 [2, 2, 5120], P(None, None, 'ffn'), may hold values from 76.8 to 768
Outputs:
- update_in: bfloat16 [16, 512, 5120], P('expert', None, 'ffn')
- update_out: bfloat16 [16, 5120, 512], P('expert', 'ffn')
Inputs may be any that keep to these rules, and one draw needn't show every extreme that they name: `expert_ids`: within each block of 128 consecutive rows at most 80 name the same expert; in some block some expert is named by exactly 80 rows; every expert is named somewhere.
All inputs are finite; a program needn't handle non-finite values.
Results may differ from a plain program's by a relative error of at most 0.0049.
Values may be sent and summed in bfloat16 or wider, within the bound.
No kernel may reach another device: no remote copies, remote signals or barrier semaphores. Data moves between devices by JAX's collectives and lax.ppermute only.
A program may use at most 128 MiB of HBM per device.

v0:
```python
import functools
import math

import jax
import jax.numpy as jnp
from jax import lax
from jax.experimental import pallas as pl
from jax.experimental.pallas import tpu as pltpu
from jax.sharding import PartitionSpec as P

D = 4096
FF = 5120
GROUP = 8


DECAY_RATE = 0.9
EPS_ONE = 1e-30
ROOT_COEF = math.sqrt(2.0 / math.pi)
CUBIC_COEF = 0.044715

MASKS = (1, 2, 4)

VMEM_BYTES = 48 * 1024 * 1024


def swap(value, mask, axis="expert"):
    pairs = [(source, source ^ mask) for source in range(lax.axis_size(axis))]
    return lax.ppermute(value, axis, pairs)


def gelu_pair(inputs):
    inner = ROOT_COEF * (inputs + CUBIC_COEF * inputs * inputs * inputs)
    tangent = jnp.tanh(inner)
    act_value = 0.5 * inputs * (1.0 + tangent)
    act_slope = 0.5 * (1.0 + tangent) + 0.5 * inputs * (1.0 - tangent * tangent) * ROOT_COEF * (
        1.0 + 3.0 * CUBIC_COEF * inputs * inputs
    )
    return (act_value, act_slope)


def ffn_total(values):
    mask = 1
    while mask < lax.axis_size("ffn"):
        values = values + swap(values, mask, "ffn")
        mask *= 2
    return values


def set_bounds(hidden):
    unit = next(unit for unit in (256, 128, 2) if hidden % unit == 0 and hidden // unit >= 3)
    units = hidden // unit
    bounds, low = [], 0
    for k in range(3):
        high = low + (units // 3 + (k < units % 3)) * unit
        bounds.append((low, high))
        low = high
    return bounds


def dot(left, right, left_dim, right_dim):
    return lax.dot_general(
        left, right, (((left_dim,), (right_dim,)), ((), ())), preferred_element_type=jnp.float32
    )


def call(kernel, out_shape, *operands):
    return pl.pallas_call(
        kernel,
        out_shape=out_shape,
        in_specs=[pl.BlockSpec(memory_space=pltpu.VMEM)] * len(operands),
        out_specs=jax.tree.map(lambda _: pl.BlockSpec(memory_space=pltpu.VMEM), out_shape),
        compiler_params=pltpu.CompilerParams(vmem_limit_bytes=VMEM_BYTES),
    )(*operands)


def place_in_group():
    return lax.rem(lax.axis_index("expert"), GROUP)


def bit(place, k):
    return lax.rem(lax.div(place, 1 << k), 2)


def flipped(place, mask):
    for k in range(3):
        if mask >> k & 1:
            place = place + (1 - 2 * bit(place, k)) * (1 << k)
    return place


def weight_part(weight_ref, k, low, half, by_row):
    side = bit(place_in_group(), k)
    if by_row:
        return weight_ref[pl.ds(pl.multiple_of(low + side * half, math.gcd(low, half)), half), :]
    if half % 128 == 0:
        return weight_ref[:, pl.ds(pl.multiple_of(low + side * half, 128), half)]
    return jnp.where(side == 1, weight_ref[:, low + half : low + 2 * half], weight_ref[:, low : low + half])


def partial_sum(rows, own_weight, got_weight, by_row):
    width = rows.shape[1] // 2
    contract = 1 if by_row else 0
    return dot(rows[:, :width], own_weight, 1, contract) + dot(rows[:, width:], got_weight, 1, contract)


def sent_kernel(k, low, half, by_row, *refs):
    own, own_other, pair, pair_other, weight, got_weight, rows_out, sent_out = refs
    count, width = own.shape[1], own.shape[2]
    first, second = 1 << (k + 1) % 3, 1 << (k + 2) % 3
    for i in range(2):
        for j in range(2):
            for l in range(2):
                chunk = flipped(place_in_group(), i * first + j * second + l * (1 << k))
                at = (j * 2 + l) * 2 * count
                rows_out[i, at : at + count, :width] = own[chunk]
                rows_out[i, at : at + count, width:] = pair[chunk]
                rows_out[i, at + count : at + 2 * count, :width] = own_other[chunk]
                rows_out[i, at + count : at + 2 * count, width:] = pair_other[chunk]
    own_weight = weight_part(weight, k, low, half, by_row)
    sent_out[...] = partial_sum(rows_out[1], own_weight, got_weight[...], by_row).astype(sent_out.dtype)


def kept_kernel(k, low, half, by_row, rows, weight, got_weight, received, kept_out, sent_out):
    own_weight = weight_part(weight, k, low, half, by_row)
    total = partial_sum(rows[0], own_weight, got_weight[...], by_row) + received[...].astype(jnp.float32)
    middle = total.shape[0] // 2
    kept_out[...] = total[:middle]
    sent_out[...] = total[middle:].astype(sent_out.dtype)


def gradient_kernel(hidden_first, rows, near, far, grad_out, sent_out, by_width_out, by_hidden_out):
    width = rows.shape[2] // 2
    if hidden_first:
        grad = dot(near[...], rows[0], 0, 0) + dot(far[...], rows[1], 0, 0)
        sent_out[...] = grad[:, width:].astype(sent_out.dtype)
    else:
        grad = dot(rows[0], near[...], 0, 0) + dot(rows[1], far[...], 0, 0)
        sent_out[...] = grad[width:].astype(sent_out.dtype)
    grad_out[...] = grad
    square = grad * grad + EPS_ONE
    down = jnp.sum(square, axis=0, keepdims=True)
    across = dot(jnp.ones((8, square.shape[1]), jnp.float32), square, 1, 1)
    down = jnp.broadcast_to(down, (8, square.shape[1]))
    by_width_out[...] = down if hidden_first else across
    by_hidden_out[...] = across if hidden_first else down


IN_WIDTH, OUT_WIDTH, IN_HIDDEN, OUT_HIDDEN, TOTALS, STAT_ROWS = 0, 8, 16, 22, 28, 32


def collect_kernel(hidden_prev, *refs):
    stats_out = refs[-1]
    place = place_in_group()
    stats_out[...] = jnp.zeros_like(stats_out)
    lanes = stats_out.shape[1]
    for which in range(2):
        by_width, by_hidden = refs[which * 6 : which * 6 + 3], refs[which * 6 + 3 : which * 6 + 6]
        width_row, hidden_row = (IN_WIDTH, OUT_WIDTH)[which], (IN_HIDDEN, OUT_HIDDEN)[which]
        width = by_width[0].shape[1] // 2
        own = sum(ref[0:1, :width] for ref in by_width)
        stats_out[pl.ds(width_row + place, 1), :width] = own
        total = 0.0
        for k in range(3):
            stats_out[pl.ds(width_row + flipped(place, 1 << k), 1), :width] = by_width[k][0:1, width:]
            half = by_hidden[k].shape[1]
            row = by_hidden[k][0:1, :]
            stats_out[pl.ds(hidden_row + 2 * k + bit(place, k), 1), :half] = row
            total = total + jnp.sum(row, axis=1, keepdims=True)
        stats_out[TOTALS + which : TOTALS + which + 1, :] = jnp.broadcast_to(total, (1, lanes))
    previous = jnp.sum(hidden_prev[...], axis=1, keepdims=True)
    stats_out[TOTALS + 2 : TOTALS + 3, :] = jnp.broadcast_to(previous, (1, lanes))


def stat_row(stats_ref, index):
    return stats_ref[pl.ds(index, 1), :]


def upright(row):
    return jnp.transpose(jnp.broadcast_to(row, (8, row.shape[1])))[:, 0:1]


def norm_kernel(prev, group_sums, whole_sums, *refs):
    grads_in, grads_out, factors_out, norms_out = refs[:3], refs[3:6], refs[6], refs[7]
    place = place_in_group()
    width = grads_in[0].shape[0] // 2
    row = lax.broadcasted_iota(jnp.int32, prev.shape, 0)
    by_width = row < IN_HIDDEN
    mean = jnp.where(by_width, whole_sums[...] / FF, group_sums[...] / D)
    factors_out[...] = DECAY_RATE * prev[...] + (1.0 - DECAY_RATE) * mean
    norm_in, norm_out = 0.0, 0.0
    for k in range(3):
        half = grads_in[k].shape[1]
        partner = flipped(place, 1 << k)
        own_row = stat_row(factors_out, IN_WIDTH + place)[:, :width]
        pair_row = stat_row(factors_out, IN_WIDTH + partner)[:, :width]
        hidden_row = stat_row(factors_out, IN_HIDDEN + 2 * k + bit(place, k))[:, :half]
        down = jnp.sum(grads_in[k][:width] * grads_in[k][:width] * upright(1.0 / own_row), axis=0, keepdims=True)
        down = down + jnp.sum(
            grads_in[k][width:] * grads_in[k][width:] * upright(1.0 / pair_row), axis=0, keepdims=True
        )
        norm_in = norm_in + jnp.sum(down / hidden_row, axis=1, keepdims=True)
        own_row = stat_row(factors_out, OUT_WIDTH + place)[:, :width]
        pair_row = stat_row(factors_out, OUT_WIDTH + partner)[:, :width]
        hidden_row = stat_row(factors_out, OUT_HIDDEN + 2 * k + bit(place, k))[:, :half]
        down = jnp.sum(grads_out[k][...] * grads_out[k][...] * upright(1.0 / hidden_row), axis=0, keepdims=True)
        norm_out = norm_out + jnp.sum(down[:, :width] / own_row, axis=1, keepdims=True)
        norm_out = norm_out + jnp.sum(down[:, width:] / pair_row, axis=1, keepdims=True)
    row = lax.broadcasted_iota(jnp.int32, norms_out.shape, 0)
    norms_out[...] = jnp.where(row == 0, norm_in, norm_out)


def final_kernel(bounds, prev, factors, whole_sums, norms, *refs):
    grads_in, grads_out, got_in, got_out = refs[:3], refs[3:6], refs[6:9], refs[9:12]
    update_in, update_out = refs[12:]
    place = place_in_group()
    width = update_in.shape[0]
    count = float(D) * float(FF)
    mean_in = DECAY_RATE * jnp.mean(prev[IN_WIDTH : IN_WIDTH + 8, :width], keepdims=True)
    mean_in = mean_in + (1.0 - DECAY_RATE) * whole_sums[TOTALS : TOTALS + 1, 0:1] / count
    mean_out = DECAY_RATE * whole_sums[TOTALS + 2 : TOTALS + 3, 0:1] / (FF * GROUP)
    mean_out = mean_out + (1.0 - DECAY_RATE) * whole_sums[TOTALS + 1 : TOTALS + 2, 0:1] / count
    factor_in = jnp.sqrt(mean_in) / jnp.maximum(1.0, jnp.sqrt(mean_in * norms[0:1, 0:1] / count))
    factor_out = jnp.sqrt(mean_out) / jnp.maximum(1.0, jnp.sqrt(mean_out * norms[1:2, 0:1] / count))
    width_in = upright(lax.rsqrt(stat_row(factors, IN_WIDTH + place)[:, :width]) * factor_in)
    width_out = lax.rsqrt(stat_row(factors, OUT_WIDTH + place)[:, :width]) * factor_out
    for k in range(3):
        low, half = bounds[k][0], (bounds[k][1] - bounds[k][0]) // 2
        own_bit = bit(place, k)
        if half % 128:
            width_scaled = (grads_in[k][:width] * width_in, got_in[k][...].astype(jnp.float32) * width_in)
            for side in range(2):
                hidden_in = lax.rsqrt(factors[IN_HIDDEN + 2 * k + side : IN_HIDDEN + 2 * k + side + 1, :half])
                value = jnp.where(own_bit == side, *width_scaled) * hidden_in
                update_in[:, low + side * half : low + side * half + half] = value.astype(update_in.dtype)
        for own in (True, False):
            side = own_bit if own else 1 - own_bit
            start = pl.multiple_of(low + side * half, math.gcd(low, half))
            hidden_out = upright(lax.rsqrt(stat_row(factors, OUT_HIDDEN + 2 * k + side)[:, :half]))
            if half % 128 == 0:
                hidden_in = lax.rsqrt(stat_row(factors, IN_HIDDEN + 2 * k + side)[:, :half])
                value = grads_in[k][:width] if own else got_in[k][...].astype(jnp.float32)
                update_in[:, pl.ds(start, half)] = (value * width_in * hidden_in).astype(update_in.dtype)
            value = grads_out[k][:, :width] if own else got_out[k][...].astype(jnp.float32)
            update_out[pl.ds(start, half), :] = (value * hidden_out * width_out).astype(update_out.dtype)


def shards(tokens, cotangent, expert_ids, in_weight, out_weight, width_states, hidden_states):
    bf16, f32 = jnp.bfloat16, jnp.float32
    shape = jax.ShapeDtypeStruct
    experts = width_states.shape[1]
    tok_rows, width = tokens.shape
    capacity = 5 * tok_rows // (4 * experts)
    part_cap = capacity // 2
    places = lax.axis_size("expert")
    block_width = width // GROUP
    position = lax.axis_index("expert")
    expert = position // GROUP
    part = lax.axis_index("ffn") % 2
    bits = [position >> k & 1 for k in range(3)]
    bounds = set_bounds(in_weight.shape[2])
    halves = [(high - low) // 2 for low, high in bounds]
    sets = range(3)
    firsts = [MASKS[(k + 1) % 3] for k in sets]
    seconds = [MASKS[(k + 2) % 3] for k in sets]
    local_in = in_weight[0]
    local_out = out_weight[0]

    def pair_side(values, k, dim):
        return lax.dynamic_slice_in_dim(values, bounds[k][0] + (1 - bits[k]) * halves[k], halves[k], dim)

    in_got = [swap(pair_side(local_in, k, 1), MASKS[k]) for k in sets]
    out_got = [swap(pair_side(local_out, k, 0), MASKS[k]) for k in sets]

    route_ids = expert_ids[:, 0]
    onehot = (route_ids[:, None] == jnp.arange(experts, dtype=jnp.int32)[None, :]).astype(jnp.int32)
    before = jnp.cumsum(onehot, axis=0) - onehot
    slot_index = jnp.sum(before * onehot, axis=1) - part * part_cap
    valid = (slot_index >= 0) & (slot_index < part_cap)
    target = jnp.where(valid, route_ids * part_cap + slot_index, -1)
    select = (jnp.arange(experts * part_cap, dtype=jnp.int32)[:, None] == target[None, :]).astype(bf16)

    def route(values):
        routed = dot(select, values, 1, 0).astype(bf16)
        routed = routed.reshape(experts, part_cap, GROUP, block_width).transpose(0, 2, 1, 3)
        return routed.reshape(places, part_cap, block_width)

    routed = jnp.concatenate([route(tokens), route(cotangent)], axis=2)
    got = lax.all_to_all(routed, "expert", split_axis=0, concat_axis=0, tiled=True)
    got = got.reshape(places // GROUP, GROUP, part_cap, 2 * block_width).transpose(1, 0, 2, 3)
    got = got.reshape(GROUP, -1, 2 * block_width)

    def exchanged(own):
        pairs = [swap(own, MASKS[k]) for k in sets]
        return (own, swap(own, 1, "ffn")), [(pair, swap(pair, 1, "ffn")) for pair in pairs]

    got_tokens, got_cotangent = got[:, :, :block_width], got[:, :, block_width:]
    own_tokens, pair_tokens = exchanged(got_tokens)
    own_cotangent, pair_cotangent = exchanged(got_cotangent)

    def scatter_sum(own, pairs, weight, got_weights, by_row):
        results, rows, kept = [], [], []
        received = []
        for k in sets:
            count = own[0].shape[1] * 2 * 4
            args = (k, bounds[k][0], halves[k], by_row)
            row, sent = call(
                functools.partial(sent_kernel, *args),
                (shape((2, count, 2 * block_width), bf16), shape((count, halves[k]), bf16)),
                *own, *pairs[k], weight, got_weights[k],
            )
            rows.append(row)
            received.append(swap(sent, firsts[k]))
        for k in sets:
            count = rows[k].shape[1] // 2
            args = (k, bounds[k][0], halves[k], by_row)
            keep, sent = call(
                functools.partial(kept_kernel, *args),
                (shape((count, halves[k]), f32), shape((count, halves[k]), bf16)),
                rows[k], weight, got_weights[k], received[k],
            )
            kept.append((keep, swap(sent, seconds[k])))
        return rows, [keep + got.astype(f32) for keep, got in kept]

    def gather(owns):
        near = [jnp.concatenate([owns[k], swap(owns[k], seconds[k])]) for k in sets]
        return [(near[k], swap(near[k], firsts[k])) for k in sets]

    token_rows, pre = scatter_sum(own_tokens, pair_tokens, local_in, in_got, False)
    cotangent_rows, back = scatter_sum(own_cotangent, pair_cotangent, local_out, out_got, True)
    acts = [gelu_pair(value) for value in pre]
    hidden = gather([act[0].astype(bf16) for act in acts])
    pre_grad = gather([(value * act[1]).astype(bf16) for value, act in zip(back, acts)])

    def gradient(rows, values, hidden_first):
        half, wide = values[0].shape[1], 2 * block_width
        grad_shape = (half, wide) if hidden_first else (wide, half)
        sent_shape = (half, block_width) if hidden_first else (block_width, half)
        return call(
            functools.partial(gradient_kernel, hidden_first),
            (shape(grad_shape, f32), shape(sent_shape, bf16), shape((8, wide), f32), shape((8, half), f32)),
            rows, *values,
        )

    out_results = [gradient(cotangent_rows[k], hidden[k], True) for k in sets]
    out_sent = [result[1] for result in out_results]
    pre_grad, out_sent = lax.optimization_barrier((pre_grad, out_sent))
    got_out = [swap(out_sent[k], MASKS[k]) for k in sets]
    in_results = [gradient(token_rows[k], pre_grad[k], False) for k in sets]
    got_in = [swap(in_results[k][1], MASKS[k]) for k in sets]

    lanes = max(block_width, *halves)
    width_pick = lax.dynamic_index_in_dim(width_states, expert, 1, keepdims=False)
    hidden_pick = lax.dynamic_index_in_dim(hidden_states, expert, 1, keepdims=False)

    def padded(values):
        return jnp.pad(values, ((0, 0), (0, lanes - values.shape[1])), constant_values=1.0)

    prev = [padded(width_pick.reshape(2 * GROUP, block_width))]
    for which in range(2):
        for k in sets:
            low, high = bounds[k]
            prev.append(padded(hidden_pick[which, low:high].reshape(2, halves[k])))
    prev.append(jnp.ones((STAT_ROWS - TOTALS, lanes), f32))
    prev = jnp.concatenate(prev)

    def cube_total(values):
        values = values + swap(values, 1) + swap(values, 2) + swap(values, 3)
        return values + swap(values, 4)

    def whole_tiles(values):
        return values if values.shape[1] > 128 else jnp.pad(values, ((0, 0), (0, lanes - values.shape[1])))

    sums = []
    for results in (in_results, out_results):
        sums += [result[2] for result in results] + [whole_tiles(result[3]) for result in results]
    stats = call(collect_kernel, shape((STAT_ROWS, lanes), f32), hidden_pick[1:2], *sums)
    group_sums = cube_total(stats)
    whole_sums = ffn_total(group_sums)
    grads = [result[0] for result in in_results] + [result[0] for result in out_results]
    factors, norms = call(
        norm_kernel,
        (shape((STAT_ROWS, lanes), f32), shape((8, 128), f32)),
        prev, group_sums, whole_sums, *grads,
    )
    norms = ffn_total(cube_total(norms))
    update_in, update_out = call(
        functools.partial(final_kernel, bounds),
        (shape(local_in.shape, bf16), shape(local_out.shape, bf16)),
        prev, factors, whole_sums, norms, *grads, *got_in, *got_out,
    )
    return (update_in[None], update_out[None])


def solution(mesh):
    return jax.shard_map(
        shards,
        mesh=mesh,
        in_specs=(
            P("expert", None),
            P("expert", None),
            P("expert", None),
            P("expert", None, "ffn"),
            P("expert", "ffn", None),
            P(),
            P(None, None, "ffn"),
        ),
        out_specs=(P("expert", None, "ffn"), P("expert", "ffn", None)),
        check_vma=False,
    )
```

profile of v0, /device:TPU:1, one launch (start us, length us, event | category | flops | bytes accessed | tf_op | source)
XLA Modules:
  0.0 291.6 jit_solution(8161462970762326307)
XLA Ops:
  6.4 7.6 %all-to-all-start = ((bf16[16,40,1024]{2,1,0:T(8,128)(2,1)}), bf16[16,40,1024]{2,1,0:T(8,128)(2,1)}, u32[]{:S(2)}, u32[]{:S(2)}) async-start(bf16[16,40,1024]{2,1,0:T(8,128)(2,1)} %pad_maximum_fusion), calls=%async_computation | async-start | bytes 2621440 | tf_op jit(solution)/shard_map/all_to_all | solution.py:288
  18.3 2.1 dynamic-slice_bitcast_fusion.2
  22.1 1.9 dynamic-slice_bitcast_fusion.1
  24.0 17.1 %all-to-all-done = bf16[16,40,1024]{2,1,0:T(8,128)(2,1)} async-done(((bf16[16,40,1024]{2,1,0:T(8,128)(2,1)}), bf16[16,40,1024]{2,1,0:T(8,128)(2,1)}, u32[]{:S(2)}, u32[]{:S(2)}) %all-to-all-start) | async-done | bytes 1310752 | tf_op jit(solution)/shard_map/all_to_all | solution.py:288
  41.1 1.5 copy.11
  42.6 2.6 collective-permute-done.28.refs_5_.got_weight
  46.5 7.1 %collective-permute-done.33.refs_5_.got_weight = bf16[512,384]{1,0:T(8,128)(2,1)S(1)} collective-permute-done((bf16[512,384]{1,0:T(8,128)(2,1)}, bf16[512,384]{1,0:T(8,128)(2,1)S(1)}, u32[]{:S(2)}, u32[]{:S(2)}) %collective-permute-start.33) | collective-permute-done | bytes 393248 | tf_op jit(solution)/shard_map/ppermute | solution.py:28
  56.9 1.8 collective-permute-start.14
  58.8 12.6 %collective-permute-done.26.refs_2_ = bf16[8,80,512]{2,1,0:T(8,128)(2,1)S(1)} collective-permute-done((bf16[8,80,512]{2,1,0:T(8,128)(2,1)S(1)}, bf16[8,80,512]{2,1,0:T(8,128)(2,1)S(1)}, u32[]{:S(2)}, u32[]{:S(2)}) %collective-permute-start.26) | collective-permute-done | bytes 655392 | tf_op jit(solution)/shard_map/ppermute | solution.py:28
  72.9 12.7 %collective-permute-done.31.refs_2_ = bf16[8,80,512]{2,1,0:T(8,128)(2,1)S(1)} collective-permute-done((bf16[8,80,512]{2,1,0:T(8,128)(2,1)S(1)}, bf16[8,80,512]{2,1,0:T(8,128)(2,1)S(1)}, u32[]{:S(2)}, u32[]{:S(2)}) %collective-permute-start.31) | collective-permute-done | bytes 655392 | tf_op jit(solution)/shard_map/ppermute | solution.py:28
  86.4 2.0 collective-permute-start.15
  88.4 2.0 collective-permute-start.6
  90.5 10.0 %collective-permute-done.1.refs_2_ = bf16[8,80,512]{2,1,0:T(8,128)(2,1)} collective-permute-done((bf16[8,80,512]{2,1,0:T(8,128)(2,1)S(1)}, bf16[8,80,512]{2,1,0:T(8,128)(2,1)}, u32[]{:S(2)}, u32[]{:S(2)}) %collective-permute-start.1) | collective-permute-done | bytes 655392 | tf_op jit(solution)/shard_map/ppermute | solution.py:28
  100.5 2.2 collective-permute-start.2
  102.7 3.5 %shard_map.94 = (bf16[2,640,1024]{2,1,0:T(8,128)(2,1)S(1)}, bf16[640,384]{1,0:T(8,128)(2,1)}) custom-call(bf16[8,80,512]{2,1,0:T(8,128)(2,1)S(1)} %get-tuple-element.134.refs_0_, bf16[8,80,512]{2,1,0:T(8,128)(2,1)S(1)} %collective-permute-done.4.refs_1_, bf16[8,80,512]{2,1,0:T(8,128)(2,1)S(1)} %collective-permute-done.26.refs_2_, ...), custom_call_target="tpu_custom_call" | custom-call | tf_op jit(solution)/shard_map/pallas_call | solution.py:67
  108.5 3.5 %shard_map.96 = (bf16[2,640,1024]{2,1,0:T(8,128)(2,1)S(1)}, bf16[640,384]{1,0:T(8,128)(2,1)}) custom-call(bf16[8,80,512]{2,1,0:T(8,128)(2,1)S(1)} %get-tuple-element.135.refs_0_, bf16[8,80,512]{2,1,0:T(8,128)(2,1)S(1)} %collective-permute-done.refs_1_, bf16[8,80,512]{2,1,0:T(8,128)(2,1)S(1)} %collective-permute-done.31.refs_2_, ...), custom_call_target="tpu_custom_call" | custom-call | tf_op jit(solution)/shard_map/pallas_call | solution.py:67
  114.5 3.4 %shard_map.90 = (bf16[2,640,1024]{2,1,0:T(8,128)(2,1)S(1)}, bf16[640,384]{1,0:T(8,128)(2,1)}) custom-call(bf16[8,80,512]{2,1,0:T(8,128)(2,1)S(1)} %get-tuple-element.134.refs_0_, bf16[8,80,512]{2,1,0:T(8,128)(2,1)S(1)} %collective-permute-done.4.refs_1_, bf16[8,80,512]{2,1,0:T(8,128)(2,1)S(1)} %copy-done.34, bf16[8,80,512]{2,1,0:T(8,128)(2,1)S(1)} %copy-done.38, ...), custom_call_target="tpu_custom_call" | custom-call | tf_op jit(solution)/shard_map/pallas_call | solution.py:67
  120.1 4.4 %shard_map.87 = (bf16[2,640,1024]{2,1,0:T(8,128)(2,1)}, bf16[640,512]{1,0:T(8,128)(2,1)}) custom-call(bf16[8,80,512]{2,1,0:T(8,128)(2,1)S(1)} %get-tuple-element.134.refs_0_, bf16[8,80,512]{2,1,0:T(8,128)(2,1)S(1)} %collective-permute-done.4.refs_1_, bf16[8,80,512]{2,1,0:T(8,128)(2,1)} %collective-permute-done.5.refs_2_, bf16[8,80,512]{2,1,0:T(8,128)(2,1)S(1)} %copy-done.36, ...), custom_call_target="tpu_custom_call" | custom-call | tf_op jit(solution)/shard_map/pallas_call | solution.py:67
  124.5 1.8 collective-permute-start.8
  126.2 4.6 %shard_map.86 = (bf16[2,640,1024]{2,1,0:T(8,128)(2,1)}, bf16[640,512]{1,0:T(8,128)(2,1)}) custom-call(bf16[8,80,512]{2,1,0:T(8,128)(2,1)S(1)} %get-tuple-element.135.refs_0_, bf16[8,80,512]{2,1,0:T(8,128)(2,1)S(1)} %collective-permute-done.refs_1_, bf16[8,80,512]{2,1,0:T(8,128)(2,1)} %collective-permute-done.1.refs_2_, ...), custom_call_target="tpu_custom_call" | custom-call | tf_op jit(solution)/shard_map/pallas_call | solution.py:67
  132.0 2.8 shard_map.92
  137.5 2.7 shard_map.95
  142.5 3.4 %shard_map.97 = (f32[320,384]{1,0:T(8,128)S(1)}, bf16[320,384]{1,0:T(8,128)(2,1)}) custom-call(bf16[2,640,1024]{2,1,0:T(8,128)(2,1)S(1)} %get-tuple-element.83.rows, bf16[512,2560]{1,0:T(8,128)(2,1)} %bitcast.50, bf16[512,384]{1,0:T(8,128)(2,1)S(1)} %copy-done.30, bf16[640,384]{1,0:T(8,128)(2,1)} %collective-permute-done.34.received), custom_call_target="tpu_custom_call" | custom-call | tf_op jit(solution)/shard_map/pallas_call | solution.py:67
  146.7 3.6 %shard_map.91 = (f32[320,384]{1,0:T(8,128)S(1)}, bf16[320,384]{1,0:T(8,128)(2,1)}) custom-call(bf16[2,640,1024]{2,1,0:T(8,128)(2,1)S(1)} %get-tuple-element.71.rows, bf16[2560,512]{1,0:T(8,128)(2,1)} %bitcast.45, bf16[384,512]{1,0:T(8,128)(2,1)S(1)} %copy-done.27, bf16[640,384]{1,0:T(8,128)(2,1)} %collective-permute-done.17.received), custom_call_target="tpu_custom_call" | custom-call | tf_op jit(solution)/shard_map/pallas_call | solution.py:67
  151.8 2.7 shard_map.93
  156.1 2.9 shard_map.88
  159.3 2.7 shard_map.89
  163.3 1.6 collective-permute-done.35
  167.8 1.5 multiply_convert_fusion.2
  170.1 2.3 collective-permute-done.11
  180.5 5.1 %collective-permute-done.12 = bf16[320,512]{1,0:T(8,128)(2,1)S(1)} collective-permute-done((bf16[320,512]{1,0:T(8,128)(2,1)S(1)}, bf16[320,512]{1,0:T(8,128)(2,1)S(1)}, u32[]{:S(2)}, u32[]{:S(2)}) %collective-permute-start.12) | collective-permute-done | bytes 327712 | tf_op jit(solution)/shard_map/ppermute | solution.py:28
  191.2 1.7 copy-done.4
  195.0 1.6 shard_map.100
  198.5 2.8 shard_map.99
  202.4 4.2 %shard_map.98 = (f32[512,1024]{1,0:T(8,128)S(1)}, bf16[512,512]{1,0:T(8,128)(2,1)S(1)}, f32[8,1024]{1,0:T(8,128)S(1)}, f32[8,512]{1,0:T(8,128)S(1)}) custom-call(bf16[2,640,1024]{2,1,0:T(8,128)(2,1)} %get-tuple-element.64.rows, bf16[640,512]{1,0:T(8,128)(2,1)} %pad_maximum_fusion.2.near, bf16[640,512]{1,0:T(8,128)(2,1)} %collective-permute-done.39.far), custom_call_target="tpu_custom_call" | custom-call | tf_op jit(solution)/shard_map/pallas_call | solution.py:67
  208.9 3.9 %shard_map.103 = (f32[1024,384]{1,0:T(8,128)S(1)}, bf16[512,384]{1,0:T(8,128)(2,1)}, f32[8,1024]{1,0:T(8,128)S(1)}, f32[8,384]{1,0:T(8,128)S(1)}) custom-call(bf16[2,640,1024]{2,1,0:T(8,128)(2,1)S(1)} %get-tuple-element.83.rows, bf16[640,384]{1,0:T(8,128)(2,1)} %pad_maximum_fusion.4.near, bf16[640,384]{1,0:T(8,128)(2,1)} %collective-permute-done.37.far), custom_call_target="tpu_custom_call" | custom-call | tf_op jit(solution)/shard_map/pallas_call | solution.py:67
  214.0 3.1 %shard_map.102 = (f32[1024,384]{1,0:T(8,128)S(1)}, bf16[512,384]{1,0:T(8,128)(2,1)S(1)}, f32[8,1024]{1,0:T(8,128)S(1)}, f32[8,384]{1,0:T(8,128)S(1)}) custom-call(bf16[2,640,1024]{2,1,0:T(8,128)(2,1)S(1)} %copy-done.10, bf16[640,384]{1,0:T(8,128)(2,1)} %pad_maximum_fusion.3.near, bf16[640,384]{1,0:T(8,128)(2,1)} %collective-permute-done.25.far), custom_call_target="tpu_custom_call" | custom-call | tf_op jit(solution)/shard_map/pallas_call | solution.py:67
  218.3 4.1 %shard_map.101 = (f32[1024,512]{1,0:T(8,128)S(1)}, bf16[512,512]{1,0:T(8,128)(2,1)S(1)}, f32[8,1024]{1,0:T(8,128)S(1)}, f32[8,512]{1,0:T(8,128)S(1)}) custom-call(bf16[2,640,1024]{2,1,0:T(8,128)(2,1)} %get-tuple-element.63.rows, bf16[640,512]{1,0:T(8,128)(2,1)S(1)} %pad_maximum_fusion.1.near, bf16[640,512]{1,0:T(8,128)(2,1)} %collective-permute-done.13.far), custom_call_target="tpu_custom_call" | custom-call | tf_op jit(solution)/shard_map/pallas_call | solution.py:67
  227.7 2.3 collective-permute-done.46
  230.8 3.3 %collective-permute-done.47 = f32[32,512]{1,0:T(8,128)S(1)} collective-permute-done((f32[32,512]{1,0:T(8,128)S(1)}, f32[32,512]{1,0:T(8,128)S(1)}, u32[]{:S(2)}, u32[]{:S(2)}) %collective-permute-start.47) | collective-permute-done | bytes 65568 | tf_op jit(solution)/shard_map/ppermute | solution.py:28
  234.1 11.8 %collective-permute-start.48 = (f32[32,512]{1,0:T(8,128)S(1)}, f32[32,512]{1,0:T(8,128)S(1)}, u32[]{:S(2)}, u32[]{:S(2)}) collective-permute-start(f32[32,512]{1,0:T(8,128)S(1)} %add.166.group_sums), channel_id=1, source_target_pairs={{0,1},{1,0},{2,3},{3,2},{4,5},{5,4},{6,7},{7,6},{8,9},{9,8},{10,11... | collective-permute-start | bytes 196616 | tf_op jit(solution)/shard_map/ppermute | solution.py:28
  249.7 5.0 %shard_map.105 = (f32[32,512]{1,0:T(8,128)S(1)}, f32[8,128]{1,0:T(8,128)S(1)}) custom-call(f32[32,512]{1,0:T(8,128)S(1)} %concatenate.24.prev, f32[32,512]{1,0:T(8,128)S(1)} %add.166.group_sums, f32[32,512]{1,0:T(8,128)S(1)} %add.167.whole_sums, f32[1024,512]{1,0:T(8,128)} %copy-done.12, f32[1024,384]{1,0:T(8,128)S(1)} %copy-done.19, ...), custom_call_target="tpu_custom_call" | custom-call | tf_op jit(solution)/shard_map/pallas_call | solution.py:67
  260.0 1.5 collective-permute-start.52
  262.8 2.9 collective-permute-start.53
  267.1 1.5 collective-permute-start.59
  268.6 7.7 %collective-permute-done.55.refs_7_ = bf16[512,384]{1,0:T(8,128)(2,1)S(1)} collective-permute-done((bf16[512,384]{1,0:T(8,128)(2,1)S(1)}, bf16[512,384]{1,0:T(8,128)(2,1)S(1)}, u32[]{:S(2)}, u32[]{:S(2)}) %collective-permute-start.55) | collective-permute-done | bytes 393248 | tf_op jit(solution)/shard_map/ppermute | solution.py:28
  276.3 8.4 %collective-permute-done.58.refs_10_ = bf16[384,512]{1,0:T(8,128)(2,1)S(1)} collective-permute-done((bf16[384,512]{1,0:T(8,128)(2,1)S(1)}, bf16[384,512]{1,0:T(8,128)(2,1)S(1)}, u32[]{:S(2)}, u32[]{:S(2)}) %collective-permute-start.58) | collective-permute-done | bytes 393248 | tf_op jit(solution)/shard_map/ppermute | solution.py:28
  284.8 6.9 %shard_map.106 = (bf16[512,2560]{1,0:T(8,128)(2,1)}, bf16[2560,512]{1,0:T(8,128)(2,1)}) custom-call(f32[32,512]{1,0:T(8,128)S(1)} %concatenate.24.prev, f32[32,512]{1,0:T(8,128)S(1)} %get-tuple-element.114.factors, f32[32,512]{1,0:T(8,128)S(1)} %add.167.whole_sums, f32[8,128]{1,0:T(8,128)S(1)} %add.172.norms, f32[1024,512]{1,0:T(8,128)} %copy-done.12, ...), custom_call_target="tpu_custom_call" | custom-call | tf_op jit(solution)/shard_map/pallas_call | solution.py:67
  (270 shorter events, 82.2 us)
Async XLA Ops:
  6.4 34.7 %all-to-all-start = ((bf16[16,40,1024]{2,1,0:T(8,128)(2,1)}), bf16[16,40,1024]{2,1,0:T(8,128)(2,1)}, u32[]{:S(2)}, u32[]{:S(2)}) async-start(bf16[16,40,1024]{2,1,0:T(8,128)(2,1)} %pad_maximum_fusion), calls=%async_computation | async-start | bytes 2621440 | tf_op jit(solution)/shard_map/all_to_all | solution.py:288
  15.0 30.2 %collective-permute-start.28 = (bf16[384,512]{1,0:T(8,128)(2,1)}, bf16[384,512]{1,0:T(8,128)(2,1)S(1)}, u32[]{:S(2)}, u32[]{:S(2)}) collective-permute-start(bf16[384,512]{1,0:T(8,128)(2,1)} %get-tuple-element.132), channel_id=1, source_target_pairs={{0,8},{2,10},{4,12},{6,14},{8,0},{10,2},{12,4},{14,6},{16,24},{18,... | collective-permute-start | bytes 1179656 | tf_op jit(solution)/shard_map/ppermute | solution.py:28
  17.1 38.5 %collective-permute-start.7 = (bf16[512,512]{1,0:T(8,128)(2,1)}, bf16[512,512]{1,0:T(8,128)(2,1)S(1)}, u32[]{:S(2)}, u32[]{:S(2)}) collective-permute-start(bf16[512,512]{1,0:T(8,128)(2,1)} %dynamic-slice_bitcast_fusion), channel_id=1, source_target_pairs={{0,2},{2,0},{4,6},{6,4},{8,10},{10,8},{12,14},{14,12},{16,18},{18,... | collective-permute-start | bytes 1572872 | tf_op jit(solution)/shard_map/ppermute | solution.py:28
  20.4 33.2 %collective-permute-start.33 = (bf16[512,384]{1,0:T(8,128)(2,1)}, bf16[512,384]{1,0:T(8,128)(2,1)S(1)}, u32[]{:S(2)}, u32[]{:S(2)}) collective-permute-start(bf16[512,384]{1,0:T(8,128)(2,1)} %get-tuple-element.130), channel_id=1, source_target_pairs={{0,8},{2,10},{4,12},{6,14},{8,0},{10,2},{12,4},{14,6},{16,24},{18,... | collective-permute-start | bytes 1179656 | tf_op jit(solution)/shard_map/ppermute | solution.py:28
  20.6 34.4 %collective-permute-start.16 = (bf16[384,512]{1,0:T(8,128)(2,1)}, bf16[384,512]{1,0:T(8,128)(2,1)S(1)}, u32[]{:S(2)}, u32[]{:S(2)}) collective-permute-start(bf16[384,512]{1,0:T(8,128)(2,1)} %get-tuple-element.133), channel_id=1, source_target_pairs={{0,4},{2,6},{4,0},{6,2},{8,12},{10,14},{12,8},{14,10},{16,20},{18,... | collective-permute-start | bytes 1179656 | tf_op jit(solution)/shard_map/ppermute | solution.py:28
  21.8 33.4 %collective-permute-start.21 = (bf16[512,384]{1,0:T(8,128)(2,1)}, bf16[512,384]{1,0:T(8,128)(2,1)S(1)}, u32[]{:S(2)}, u32[]{:S(2)}) collective-permute-start(bf16[512,384]{1,0:T(8,128)(2,1)} %get-tuple-element.131), channel_id=1, source_target_pairs={{0,4},{2,6},{4,0},{6,2},{8,12},{10,14},{12,8},{14,10},{16,20},{18,... | collective-permute-start | bytes 1179656 | tf_op jit(solution)/shard_map/ppermute | solution.py:28
  45.2 11.7 %collective-permute-start.3 = (bf16[512,512]{1,0:T(8,128)(2,1)S(1)}, bf16[512,512]{1,0:T(8,128)(2,1)S(1)}, u32[]{:S(2)}, u32[]{:S(2)}) collective-permute-start(bf16[512,512]{1,0:T(8,128)(2,1)S(1)} %copy-done.59), channel_id=1, source_target_pairs={{0,2},{2,0},{4,6},{6,4},{8,10},{10,8},{12,14},{14,12},{16,18},{18,... | collective-permute-start | bytes 1572872 | tf_op jit(solution)/shard_map/ppermute | solution.py:28
  55.1 16.3 %collective-permute-start.26 = (bf16[8,80,512]{2,1,0:T(8,128)(2,1)S(1)}, bf16[8,80,512]{2,1,0:T(8,128)(2,1)S(1)}, u32[]{:S(2)}, u32[]{:S(2)}) collective-permute-start(bf16[8,80,512]{2,1,0:T(8,128)(2,1)S(1)} %get-tuple-element.134.refs_0_), channel_id=1, source_target_pairs={{0,8},{2,10},{4,12},{6,14},{8,0},{10,2},{12,4},{14,6},{16,24},{18,... | collective-permute-start | bytes 1966088 | tf_op jit(solution)/shard_map/ppermute | solution.py:28
  55.2 17.3 %collective-permute-start = (bf16[8,80,512]{2,1,0:T(8,128)(2,1)S(1)}, bf16[8,80,512]{2,1,0:T(8,128)(2,1)S(1)}, u32[]{:S(2)}, u32[]{:S(2)}) collective-permute-start(bf16[8,80,512]{2,1,0:T(8,128)(2,1)S(1)} %get-tuple-element.135.refs_0_), channel_id=1, source_target_pairs={{0,1},{1,0},{2,3},{3,2},{4,5},{5,4},{6,7},{7,6},{8,9},{9,8},{10,11... | collective-permute-start | bytes 1966088 | tf_op jit(solution)/shard_map/ppermute | solution.py:28
  55.6 30.0 %collective-permute-start.31 = (bf16[8,80,512]{2,1,0:T(8,128)(2,1)S(1)}, bf16[8,80,512]{2,1,0:T(8,128)(2,1)S(1)}, u32[]{:S(2)}, u32[]{:S(2)}) collective-permute-start(bf16[8,80,512]{2,1,0:T(8,128)(2,1)S(1)} %get-tuple-element.135.refs_0_), channel_id=1, source_target_pairs={{0,8},{2,10},{4,12},{6,14},{8,0},{10,2},{12,4},{14,6},{16,24},{18,... | collective-permute-start | bytes 1966088 | tf_op jit(solution)/shard_map/ppermute | solution.py:28
  56.9 29.4 %collective-permute-start.14 = (bf16[8,80,512]{2,1,0:T(8,128)(2,1)S(1)}, bf16[8,80,512]{2,1,0:T(8,128)(2,1)S(1)}, u32[]{:S(2)}, u32[]{:S(2)}) collective-permute-start(bf16[8,80,512]{2,1,0:T(8,128)(2,1)S(1)} %get-tuple-element.134.refs_0_), channel_id=1, source_target_pairs={{0,4},{2,6},{4,0},{6,2},{8,12},{10,14},{12,8},{14,10},{16,20},{18,... | collective-permute-start | bytes 1966088 | tf_op jit(solution)/shard_map/ppermute | solution.py:28
  58.7 27.7 %collective-permute-start.19 = (bf16[8,80,512]{2,1,0:T(8,128)(2,1)S(1)}, bf16[8,80,512]{2,1,0:T(8,128)(2,1)S(1)}, u32[]{:S(2)}, u32[]{:S(2)}) collective-permute-start(bf16[8,80,512]{2,1,0:T(8,128)(2,1)S(1)} %get-tuple-element.135.refs_0_), channel_id=1, source_target_pairs={{0,4},{2,6},{4,0},{6,2},{8,12},{10,14},{12,8},{14,10},{16,20},{18,... | collective-permute-start | bytes 1966088 | tf_op jit(solution)/shard_map/ppermute | solution.py:28
  71.4 17.0 %collective-permute-start.5 = (bf16[8,80,512]{2,1,0:T(8,128)(2,1)S(1)}, bf16[8,80,512]{2,1,0:T(8,128)(2,1)}, u32[]{:S(2)}, u32[]{:S(2)}) collective-permute-start(bf16[8,80,512]{2,1,0:T(8,128)(2,1)S(1)} %get-tuple-element.134.refs_0_), channel_id=1, source_target_pairs={{0,2},{2,0},{4,6},{6,4},{8,10},{10,8},{12,14},{14,12},{16,18},{18,... | collective-permute-start | bytes 1966088 | tf_op jit(solution)/shard_map/ppermute | solution.py:28
  72.6 27.9 %collective-permute-start.1 = (bf16[8,80,512]{2,1,0:T(8,128)(2,1)S(1)}, bf16[8,80,512]{2,1,0:T(8,128)(2,1)}, u32[]{:S(2)}, u32[]{:S(2)}) collective-permute-start(bf16[8,80,512]{2,1,0:T(8,128)(2,1)S(1)} %get-tuple-element.135.refs_0_), channel_id=1, source_target_pairs={{0,2},{2,0},{4,6},{6,4},{8,10},{10,8},{12,14},{14,12},{16,18},{18,... | collective-permute-start | bytes 1966088 | tf_op jit(solution)/shard_map/ppermute | solution.py:28
  85.5 17.2 %collective-permute-start.27 = (bf16[8,80,512]{2,1,0:T(8,128)(2,1)S(1)}, bf16[8,80,512]{2,1,0:T(8,128)(2,1)S(1)}, u32[]{:S(2)}, u32[]{:S(2)}) collective-permute-start(bf16[8,80,512]{2,1,0:T(8,128)(2,1)S(1)} %collective-permute-done.26.refs_2_), channel_id=1, source_target_pairs={{0,1},{1,0},{2,3},{3,2},{4,5},{5,4},{6,7},{7,6},{8,9},{9,8},{10,11... | collective-permute-start | bytes 1966088 | tf_op jit(solution)/shard_map/ppermute | solution.py:28
  86.3 19.9 %collective-permute-start.32 = (bf16[8,80,512]{2,1,0:T(8,128)(2,1)S(1)}, bf16[8,80,512]{2,1,0:T(8,128)(2,1)S(1)}, u32[]{:S(2)}, u32[]{:S(2)}) collective-permute-start(bf16[8,80,512]{2,1,0:T(8,128)(2,1)S(1)} %collective-permute-done.31.refs_2_), channel_id=1, source_target_pairs={{0,1},{1,0},{2,3},{3,2},{4,5},{5,4},{6,7},{7,6},{8,9},{9,8},{10,11... | collective-permute-start | bytes 1966088 | tf_op jit(solution)/shard_map/ppermute | solution.py:28
  86.4 25.6 %collective-permute-start.15 = (bf16[8,80,512]{2,1,0:T(8,128)(2,1)S(1)}, bf16[8,80,512]{2,1,0:T(8,128)(2,1)S(1)}, u32[]{:S(2)}, u32[]{:S(2)}) collective-permute-start(bf16[8,80,512]{2,1,0:T(8,128)(2,1)S(1)} %collective-permute-done.14.refs_2_), channel_id=1, source_target_pairs={{0,1},{1,0},{2,3},{3,2},{4,5},{5,4},{6,7},{7,6},{8,9},{9,8},{10,11... | collective-permute-start | bytes 1966088 | tf_op jit(solution)/shard_map/ppermute | solution.py:28
  88.4 29.5 %collective-permute-start.6 = (bf16[8,80,512]{2,1,0:T(8,128)(2,1)}, bf16[8,80,512]{2,1,0:T(8,128)(2,1)S(1)}, u32[]{:S(2)}, u32[]{:S(2)}) collective-permute-start(bf16[8,80,512]{2,1,0:T(8,128)(2,1)} %collective-permute-done.5.refs_2_), channel_id=1, source_target_pairs={{0,1},{1,0},{2,3},{3,2},{4,5},{5,4},{6,7},{7,6},{8,9},{9,8},{10,11... | collective-permute-start | bytes 1966088 | tf_op jit(solution)/shard_map/ppermute | solution.py:28
  100.5 24.0 %collective-permute-start.2 = (bf16[8,80,512]{2,1,0:T(8,128)(2,1)}, bf16[8,80,512]{2,1,0:T(8,128)(2,1)}, u32[]{:S(2)}, u32[]{:S(2)}) collective-permute-start(bf16[8,80,512]{2,1,0:T(8,128)(2,1)} %collective-permute-done.1.refs_2_), channel_id=1, source_target_pairs={{0,1},{1,0},{2,3},{3,2},{4,5},{5,4},{6,7},{7,6},{8,9},{9,8},{10,11... | collective-permute-start | bytes 1966088 | tf_op jit(solution)/shard_map/ppermute | solution.py:28
  102.7 28.1 %collective-permute-start.20 = (bf16[8,80,512]{2,1,0:T(8,128)(2,1)S(1)}, bf16[8,80,512]{2,1,0:T(8,128)(2,1)}, u32[]{:S(2)}, u32[]{:S(2)}) collective-permute-start(bf16[8,80,512]{2,1,0:T(8,128)(2,1)S(1)} %collective-permute-done.19.refs_2_), channel_id=1, source_target_pairs={{0,1},{1,0},{2,3},{3,2},{4,5},{5,4},{6,7},{7,6},{8,9},{9,8},{10,11... | collective-permute-start | bytes 1966088 | tf_op jit(solution)/shard_map/ppermute | solution.py:28
  106.2 30.1 %collective-permute-start.29 = (bf16[640,384]{1,0:T(8,128)(2,1)}, bf16[640,384]{1,0:T(8,128)(2,1)}, u32[]{:S(2)}, u32[]{:S(2)}) collective-permute-start(bf16[640,384]{1,0:T(8,128)(2,1)} %get-tuple-element.80), channel_id=1, source_target_pairs={{0,2},{2,0},{4,6},{6,4},{8,10},{10,8},{12,14},{14,12},{16,18},{18,... | collective-permute-start | bytes 1474568 | tf_op jit(solution)/shard_map/ppermute | solution.py:28
  112.8 28.2 %collective-permute-start.34 = (bf16[640,384]{1,0:T(8,128)(2,1)}, bf16[640,384]{1,0:T(8,128)(2,1)}, u32[]{:S(2)}, u32[]{:S(2)}) collective-permute-start(bf16[640,384]{1,0:T(8,128)(2,1)} %get-tuple-element.84), channel_id=1, source_target_pairs={{0,2},{2,0},{4,6},{6,4},{8,10},{10,8},{12,14},{14,12},{16,18},{18,... | collective-permute-start | bytes 1474568 | tf_op jit(solution)/shard_map/ppermute | solution.py:28
  118.8 27.8 %collective-permute-start.17 = (bf16[640,384]{1,0:T(8,128)(2,1)}, bf16[640,384]{1,0:T(8,128)(2,1)}, u32[]{:S(2)}, u32[]{:S(2)}) collective-permute-start(bf16[640,384]{1,0:T(8,128)(2,1)} %get-tuple-element.72), channel_id=1, source_target_pairs={{0,8},{2,10},{4,12},{6,14},{8,0},{10,2},{12,4},{14,6},{16,24},{18,... | collective-permute-start | bytes 1474568 | tf_op jit(solution)/shard_map/ppermute | solution.py:28
  124.5 30.9 %collective-permute-start.8 = (bf16[640,512]{1,0:T(8,128)(2,1)}, bf16[640,512]{1,0:T(8,128)(2,1)}, u32[]{:S(2)}, u32[]{:S(2)}) collective-permute-start(bf16[640,512]{1,0:T(8,128)(2,1)} %get-tuple-element.65), channel_id=1, source_target_pairs={{0,4},{2,6},{4,0},{6,2},{8,12},{10,14},{12,8},{14,10},{16,20},{18,... | collective-permute-start | bytes 1966088 | tf_op jit(solution)/shard_map/ppermute | solution.py:28
  130.8 28.2 %collective-permute-start.10 = (bf16[640,512]{1,0:T(8,128)(2,1)}, bf16[640,512]{1,0:T(8,128)(2,1)S(1)}, u32[]{:S(2)}, u32[]{:S(2)}) collective-permute-start(bf16[640,512]{1,0:T(8,128)(2,1)} %get-tuple-element.68), channel_id=1, source_target_pairs={{0,4},{2,6},{4,0},{6,2},{8,12},{10,14},{12,8},{14,10},{16,20},{18,... | collective-permute-start | bytes 1966088 | tf_op jit(solution)/shard_map/ppermute | solution.py:28
  136.3 14.8 %collective-permute-start.22 = (bf16[640,384]{1,0:T(8,128)(2,1)S(1)}, bf16[640,384]{1,0:T(8,128)(2,1)S(1)}, u32[]{:S(2)}, u32[]{:S(2)}) collective-permute-start(bf16[640,384]{1,0:T(8,128)(2,1)S(1)} %get-tuple-element.76), channel_id=1, source_target_pairs={{0,8},{2,10},{4,12},{6,14},{8,0},{10,2},{12,4},{14,6},{16,24},{18,... | collective-permute-start | bytes 1474568 | tf_op jit(solution)/shard_map/ppermute | solution.py:28
  141.0 21.0 %collective-permute-start.30 = (bf16[320,384]{1,0:T(8,128)(2,1)S(1)}, bf16[320,384]{1,0:T(8,128)(2,1)}, u32[]{:S(2)}, u32[]{:S(2)}) collective-permute-start(bf16[320,384]{1,0:T(8,128)(2,1)S(1)} %get-tuple-element.82), channel_id=1, source_target_pairs={{0,4},{2,6},{4,0},{6,2},{8,12},{10,14},{12,8},{14,10},{16,20},{18,... | collective-permute-start | bytes 737288 | tf_op jit(solution)/shard_map/ppermute | solution.py:28
  146.6 18.3 %collective-permute-start.35 = (bf16[320,384]{1,0:T(8,128)(2,1)}, bf16[320,384]{1,0:T(8,128)(2,1)}, u32[]{:S(2)}, u32[]{:S(2)}) collective-permute-start(bf16[320,384]{1,0:T(8,128)(2,1)} %get-tuple-element.86), channel_id=1, source_target_pairs={{0,4},{2,6},{4,0},{6,2},{8,12},{10,14},{12,8},{14,10},{16,20},{18,... | collective-permute-start | bytes 737288 | tf_op jit(solution)/shard_map/ppermute | solution.py:28
  151.1 16.8 %collective-permute-start.18 = (bf16[320,384]{1,0:T(8,128)(2,1)}, bf16[320,384]{1,0:T(8,128)(2,1)}, u32[]{:S(2)}, u32[]{:S(2)}) collective-permute-start(bf16[320,384]{1,0:T(8,128)(2,1)} %get-tuple-element.74), channel_id=1, source_target_pairs={{0,2},{2,0},{4,6},{6,4},{8,10},{10,8},{12,14},{14,12},{16,18},{18,... | collective-permute-start | bytes 737288 | tf_op jit(solution)/shard_map/ppermute | solution.py:28
  155.4 12.4 %collective-permute-start.23 = (bf16[320,384]{1,0:T(8,128)(2,1)S(1)}, bf16[320,384]{1,0:T(8,128)(2,1)S(1)}, u32[]{:S(2)}, u32[]{:S(2)}) collective-permute-start(bf16[320,384]{1,0:T(8,128)(2,1)S(1)} %get-tuple-element.78), channel_id=1, source_target_pairs={{0,2},{2,0},{4,6},{6,4},{8,10},{10,8},{12,14},{14,12},{16,18},{18,... | collective-permute-start | bytes 737288 | tf_op jit(solution)/shard_map/ppermute | solution.py:28
  159.0 11.1 %collective-permute-start.9 = (bf16[320,512]{1,0:T(8,128)(2,1)S(1)}, bf16[320,512]{1,0:T(8,128)(2,1)S(1)}, u32[]{:S(2)}, u32[]{:S(2)}) collective-permute-start(bf16[320,512]{1,0:T(8,128)(2,1)S(1)} %get-tuple-element.67), channel_id=1, source_target_pairs={{0,8},{2,10},{4,12},{6,14},{8,0},{10,2},{12,4},{14,6},{16,24},{18,... | collective-permute-start | bytes 983048 | tf_op jit(solution)/shard_map/ppermute | solution.py:28
  162.0 10.3 %collective-permute-start.11 = (bf16[320,512]{1,0:T(8,128)(2,1)S(1)}, bf16[320,512]{1,0:T(8,128)(2,1)S(1)}, u32[]{:S(2)}, u32[]{:S(2)}) collective-permute-start(bf16[320,512]{1,0:T(8,128)(2,1)S(1)} %get-tuple-element.70), channel_id=1, source_target_pairs={{0,8},{2,10},{4,12},{6,14},{8,0},{10,2},{12,4},{14,6},{16,24},{18,... | collective-permute-start | bytes 983048 | tf_op jit(solution)/shard_map/ppermute | solution.py:28
  173.6 13.1 %collective-permute-start.36 = (bf16[320,384]{1,0:T(8,128)(2,1)S(1)}, bf16[320,384]{1,0:T(8,128)(2,1)S(1)}, u32[]{:S(2)}, u32[]{:S(2)}) collective-permute-start(bf16[320,384]{1,0:T(8,128)(2,1)S(1)} %get-tuple-element.139), channel_id=1, source_target_pairs={{0,4},{2,6},{4,0},{6,2},{8,12},{10,14},{12,8},{14,10},{16,20},{18,... | collective-permute-start | bytes 737288 | tf_op jit(solution)/shard_map/ppermute | solution.py:28
  175.0 12.9 %collective-permute-start.24 = (bf16[320,384]{1,0:T(8,128)(2,1)S(1)}, bf16[320,384]{1,0:T(8,128)(2,1)S(1)}, u32[]{:S(2)}, u32[]{:S(2)}) collective-permute-start(bf16[320,384]{1,0:T(8,128)(2,1)S(1)} %get-tuple-element.141), channel_id=1, source_target_pairs={{0,2},{2,0},{4,6},{6,4},{8,10},{10,8},{12,14},{14,12},{16,18},{18,... | collective-permute-start | bytes 737288 | tf_op jit(solution)/shard_map/ppermute | solution.py:28
  175.9 9.7 %collective-permute-start.12 = (bf16[320,512]{1,0:T(8,128)(2,1)S(1)}, bf16[320,512]{1,0:T(8,128)(2,1)S(1)}, u32[]{:S(2)}, u32[]{:S(2)}) collective-permute-start(bf16[320,512]{1,0:T(8,128)(2,1)S(1)} %get-tuple-element.137), channel_id=1, source_target_pairs={{0,8},{2,10},{4,12},{6,14},{8,0},{10,2},{12,4},{14,6},{16,24},{18,... | collective-permute-start | bytes 983048 | tf_op jit(solution)/shard_map/ppermute | solution.py:28
  176.3 13.1 %collective-permute-start.43 = (bf16[640,384]{1,0:T(8,128)(2,1)S(1)}, bf16[640,384]{1,0:T(8,128)(2,1)S(1)}, u32[]{:S(2)}, u32[]{:S(2)}) collective-permute-start(bf16[640,384]{1,0:T(8,128)(2,1)S(1)} %pad_maximum_fusion.6.near), channel_id=1, source_target_pairs={{0,2},{2,0},{4,6},{6,4},{8,10},{10,8},{12,14},{14,12},{16,18},{18,... | collective-permute-start | bytes 1474568 | tf_op jit(solution)/shard_map/ppermute | solution.py:28
  179.1 19.4 %collective-permute-start.41 = (bf16[640,384]{1,0:T(8,128)(2,1)}, bf16[640,384]{1,0:T(8,128)(2,1)}, u32[]{:S(2)}, u32[]{:S(2)}) collective-permute-start(bf16[640,384]{1,0:T(8,128)(2,1)} %pad_maximum_fusion.5.near), channel_id=1, source_target_pairs={{0,8},{2,10},{4,12},{6,14},{8,0},{10,2},{12,4},{14,6},{16,24},{18,... | collective-permute-start | bytes 1474568 | tf_op jit(solution)/shard_map/ppermute | solution.py:28
  185.5 16.9 %collective-permute-start.39 = (bf16[640,512]{1,0:T(8,128)(2,1)}, bf16[640,512]{1,0:T(8,128)(2,1)}, u32[]{:S(2)}, u32[]{:S(2)}) collective-permute-start(bf16[640,512]{1,0:T(8,128)(2,1)} %pad_maximum_fusion.2.near), channel_id=1, source_target_pairs={{0,4},{2,6},{4,0},{6,2},{8,12},{10,14},{12,8},{14,10},{16,20},{18,... | collective-permute-start | bytes 1966088 | tf_op jit(solution)/shard_map/ppermute | solution.py:28
  186.8 22.1 %collective-permute-start.13 = (bf16[640,512]{1,0:T(8,128)(2,1)S(1)}, bf16[640,512]{1,0:T(8,128)(2,1)}, u32[]{:S(2)}, u32[]{:S(2)}) collective-permute-start(bf16[640,512]{1,0:T(8,128)(2,1)S(1)} %pad_maximum_fusion.1.near), channel_id=1, source_target_pairs={{0,4},{2,6},{4,0},{6,2},{8,12},{10,14},{12,8},{14,10},{16,20},{18,... | collective-permute-start | bytes 1966088 | tf_op jit(solution)/shard_map/ppermute | solution.py:28
  188.0 21.0 %collective-permute-start.37 = (bf16[640,384]{1,0:T(8,128)(2,1)}, bf16[640,384]{1,0:T(8,128)(2,1)}, u32[]{:S(2)}, u32[]{:S(2)}) collective-permute-start(bf16[640,384]{1,0:T(8,128)(2,1)} %pad_maximum_fusion.4.near), channel_id=1, source_target_pairs={{0,2},{2,0},{4,6},{6,4},{8,10},{10,8},{12,14},{14,12},{16,18},{18,... | collective-permute-start | bytes 1474568 | tf_op jit(solution)/shard_map/ppermute | solution.py:28
  190.2 18.7 %collective-permute-start.25 = (bf16[640,384]{1,0:T(8,128)(2,1)}, bf16[640,384]{1,0:T(8,128)(2,1)}, u32[]{:S(2)}, u32[]{:S(2)}) collective-permute-start(bf16[640,384]{1,0:T(8,128)(2,1)} %pad_maximum_fusion.3.near), channel_id=1, source_target_pairs={{0,8},{2,10},{4,12},{6,14},{8,0},{10,2},{12,4},{14,6},{16,24},{18,... | collective-permute-start | bytes 1474568 | tf_op jit(solution)/shard_map/ppermute | solution.py:28
  226.5 40.6 %collective-permute-start.56 = (bf16[512,384]{1,0:T(8,128)(2,1)}, bf16[512,384]{1,0:T(8,128)(2,1)S(1)}, u32[]{:S(2)}, u32[]{:S(2)}) collective-permute-start(bf16[512,384]{1,0:T(8,128)(2,1)} %get-tuple-element.118), channel_id=1, source_target_pairs={{0,8},{2,10},{4,12},{6,14},{8,0},{10,2},{12,4},{14,6},{16,24},{18,... | collective-permute-start | bytes 1179656 | tf_op jit(solution)/shard_map/ppermute | solution.py:28
  234.1 12.7 %collective-permute-start.48 = (f32[32,512]{1,0:T(8,128)S(1)}, f32[32,512]{1,0:T(8,128)S(1)}, u32[]{:S(2)}, u32[]{:S(2)}) collective-permute-start(f32[32,512]{1,0:T(8,128)S(1)} %add.166.group_sums), channel_id=1, source_target_pairs={{0,1},{1,0},{2,3},{3,2},{4,5},{5,4},{6,7},{7,6},{8,9},{9,8},{10,11... | collective-permute-start | bytes 196616 | tf_op jit(solution)/shard_map/ppermute | solution.py:28
  257.3 27.5 %collective-permute-start.54 = (bf16[512,512]{1,0:T(8,128)(2,1)S(1)}, bf16[512,512]{1,0:T(8,128)(2,1)S(1)}, u32[]{:S(2)}, u32[]{:S(2)}) collective-permute-start(bf16[512,512]{1,0:T(8,128)(2,1)S(1)} %get-tuple-element.116), channel_id=1, source_target_pairs={{0,2},{2,0},{4,6},{6,4},{8,10},{10,8},{12,14},{14,12},{16,18},{18,... | collective-permute-start | bytes 1572872 | tf_op jit(solution)/shard_map/ppermute | solution.py:28
  258.0 26.8 %collective-permute-start.57 = (bf16[512,512]{1,0:T(8,128)(2,1)S(1)}, bf16[512,512]{1,0:T(8,128)(2,1)S(1)}, u32[]{:S(2)}, u32[]{:S(2)}) collective-permute-start(bf16[512,512]{1,0:T(8,128)(2,1)S(1)} %copy-done.50), channel_id=1, source_target_pairs={{0,2},{2,0},{4,6},{6,4},{8,10},{10,8},{12,14},{14,12},{16,18},{18,... | collective-permute-start | bytes 1572872 | tf_op jit(solution)/shard_map/ppermute | solution.py:28
  265.6 10.7 %collective-permute-start.55 = (bf16[512,384]{1,0:T(8,128)(2,1)S(1)}, bf16[512,384]{1,0:T(8,128)(2,1)S(1)}, u32[]{:S(2)}, u32[]{:S(2)}) collective-permute-start(bf16[512,384]{1,0:T(8,128)(2,1)S(1)} %copy-done.56), channel_id=1, source_target_pairs={{0,4},{2,6},{4,0},{6,2},{8,12},{10,14},{12,8},{14,10},{16,20},{18,... | collective-permute-start | bytes 1179656 | tf_op jit(solution)/shard_map/ppermute | solution.py:28
  266.5 18.3 %collective-permute-start.58 = (bf16[384,512]{1,0:T(8,128)(2,1)S(1)}, bf16[384,512]{1,0:T(8,128)(2,1)S(1)}, u32[]{:S(2)}, u32[]{:S(2)}) collective-permute-start(bf16[384,512]{1,0:T(8,128)(2,1)S(1)} %copy-done.54), channel_id=1, source_target_pairs={{0,4},{2,6},{4,0},{6,2},{8,12},{10,14},{12,8},{14,10},{16,20},{18,... | collective-permute-start | bytes 1179656 | tf_op jit(solution)/shard_map/ppermute | solution.py:28
  267.1 17.6 %collective-permute-start.59 = (bf16[384,512]{1,0:T(8,128)(2,1)S(1)}, bf16[384,512]{1,0:T(8,128)(2,1)S(1)}, u32[]{:S(2)}, u32[]{:S(2)}) collective-permute-start(bf16[384,512]{1,0:T(8,128)(2,1)S(1)} %copy-done.52), channel_id=1, source_target_pairs={{0,8},{2,10},{4,12},{6,14},{8,0},{10,2},{12,4},{14,6},{16,24},{18,... | collective-permute-start | bytes 1179656 | tf_op jit(solution)/shard_map/ppermute | solution.py:28
  (75 other events, 648.4 us)
where the time goes:
time: 293 us; the launch traced here: 292 us
  waiting for transfers between devices  98.3 us (34%)
  starting transfers between devices  72.5 us (25%)
  Pallas kernels  71.7 us (24%)
  local copies, waits for them, and re-layouts  36.3 us (12%)
  other arithmetic  10.8 us (4%)
    ppermute x60, waiting for transfers between devices, swap(): return lax.ppermute(value, axis, pairs)  81.2 us
    pallas_call x21, Pallas kernels, call(): pl.pallas_call(kernel, out_shape=out_shape, in_specs=[pl.BlockSpec(memory...  71.7 us
    ppermute x60, starting transfers between devices, swap(): return lax.ppermute(value, axis, pairs)  65 us
    unnamed x127, local copies, waits for them, and re-layouts  28.2 us
    all_to_all x1, waiting for transfers between devices, shards(): lax.all_to_all(routed, 'expert', split_axis=0, concat_axis=0, tiled=True)  17.1 us
    all_to_all x1, starting transfers between devices, shards(): lax.all_to_all(routed, 'expert', split_axis=0, concat_axis=0, tiled=True)  7.58 us
  transfers between devices with their start and end apart: 61, of which 19 were waited for; matrix products, arithmetic and copies ran while one was open for 5% of the time, Pallas kernels for 18%

commit v1 on v0

--- a/solution.py
+++ b/solution.py
@@ -20,7 +20,7 @@
 
 MASKS = (1, 2, 4)
 
-VMEM_BYTES = 48 * 1024 * 1024
+MIB = 1024 * 1024
 
 
 def swap(value, mask, axis="expert"):
@@ -63,13 +63,13 @@
     )
 
 
-def call(kernel, out_shape, *operands):
+def call(kernel, mib, out_shape, *operands):
     return pl.pallas_call(
         kernel,
         out_shape=out_shape,
         in_specs=[pl.BlockSpec(memory_space=pltpu.VMEM)] * len(operands),
         out_specs=jax.tree.map(lambda _: pl.BlockSpec(memory_space=pltpu.VMEM), out_shape),
-        compiler_params=pltpu.CompilerParams(vmem_limit_bytes=VMEM_BYTES),
+        compiler_params=pltpu.CompilerParams(vmem_limit_bytes=mib * MIB),
     )(*operands)
 
 
@@ -103,46 +103,75 @@
     return dot(rows[:, :width], own_weight, 1, contract) + dot(rows[:, width:], got_weight, 1, contract)
 
 
-def sent_kernel(k, low, half, by_row, *refs):
-    own, own_other, pair, pair_other, weight, got_weight, rows_out, sent_out = refs
+def sums_kernel(bounds, by_row, *refs):
+    own, own_other, pairs, weight, got_weights = refs[0], refs[1], refs[2:8], refs[8], refs[9:12]
+    rows_out, sent_out, kept_out = refs[12:15], refs[15:18], refs[18:21]
     count, width = own.shape[1], own.shape[2]
-    first, second = 1 << (k + 1) % 3, 1 << (k + 2) % 3
-    for i in range(2):
-        for j in range(2):
-            for l in range(2):
-                chunk = flipped(place_in_group(), i * first + j * second + l * (1 << k))
-                at = (j * 2 + l) * 2 * count
-                rows_out[i, at : at + count, :width] = own[chunk]
-                rows_out[i, at : at + count, width:] = pair[chunk]
-                rows_out[i, at + count : at + 2 * count, :width] = own_other[chunk]
-                rows_out[i, at + count : at + 2 * count, width:] = pair_other[chunk]
-    own_weight = weight_part(weight, k, low, half, by_row)
-    sent_out[...] = partial_sum(rows_out[1], own_weight, got_weight[...], by_row).astype(sent_out.dtype)
-
-
-def kept_kernel(k, low, half, by_row, rows, weight, got_weight, received, kept_out, sent_out):
-    own_weight = weight_part(weight, k, low, half, by_row)
-    total = partial_sum(rows[0], own_weight, got_weight[...], by_row) + received[...].astype(jnp.float32)
-    middle = total.shape[0] // 2
-    kept_out[...] = total[:middle]
-    sent_out[...] = total[middle:].astype(sent_out.dtype)
-
-
-def gradient_kernel(hidden_first, rows, near, far, grad_out, sent_out, by_width_out, by_hidden_out):
-    width = rows.shape[2] // 2
-    if hidden_first:
-        grad = dot(near[...], rows[0], 0, 0) + dot(far[...], rows[1], 0, 0)
-        sent_out[...] = grad[:, width:].astype(sent_out.dtype)
-    else:
-        grad = dot(rows[0], near[...], 0, 0) + dot(rows[1], far[...], 0, 0)
-        sent_out[...] = grad[width:].astype(sent_out.dtype)
-    grad_out[...] = grad
-    square = grad * grad + EPS_ONE
-    down = jnp.sum(square, axis=0, keepdims=True)
-    across = dot(jnp.ones((8, square.shape[1]), jnp.float32), square, 1, 1)
-    down = jnp.broadcast_to(down, (8, square.shape[1]))
-    by_width_out[...] = down if hidden_first else across
-    by_hidden_out[...] = across if hidden_first else down
+    for k in range(3):
+        pair, pair_other = pairs[2 * k : 2 * k + 2]
+        first, second = 1 << (k + 1) % 3, 1 << (k + 2) % 3
+        for i in range(2):
+            for j in range(2):
+                for l in range(2):
+                    chunk = flipped(place_in_group(), i * first + j * second + l * (1 << k))
+                    at = (j * 2 + l) * 2 * count
+                    rows_out[k][i, at : at + count, :width] = own[chunk]
+                    rows_out[k][i, at : at + count, width:] = pair[chunk]
+                    rows_out[k][i, at + count : at + 2 * count, :width] = own_other[chunk]
+                    rows_out[k][i, at + count : at + 2 * count, width:] = pair_other[chunk]
+        own_weight = weight_part(weight, k, bounds[k][0], (bounds[k][1] - bounds[k][0]) // 2, by_row)
+        got_weight = got_weights[k][...]
+        sent_out[k][...] = partial_sum(rows_out[k][1], own_weight, got_weight, by_row).astype(jnp.bfloat16)
+        kept_out[k][...] = partial_sum(rows_out[k][0], own_weight, got_weight, by_row)
+
+
+def add_kernel(*refs):
+    kept, received, total_out, sent_out = refs[:3], refs[3:6], refs[6:9], refs[9:12]
+    for k in range(3):
+        middle = kept[k].shape[0] // 2
+        total_out[k][...] = kept[k][:middle] + received[k][:middle].astype(jnp.float32)
+        total = kept[k][middle:] + received[k][middle:].astype(jnp.float32)
+        sent_out[k][...] = total.astype(jnp.bfloat16)
+
+
+def hidden_kernel(*refs):
+    kept, received, hidden_out, slope_out = refs[:3], refs[3:6], refs[6:9], refs[9:12]
+    for k in range(3):
+        act_value, act_slope = gelu_pair(kept[k][...] + received[k][...].astype(jnp.float32))
+        hidden_out[k][...] = act_value.astype(jnp.bfloat16)
+        slope_out[k][...] = act_slope
+
+
+def pre_grad_kernel(*refs):
+    kept, received, slope, pre_grad_out = refs[:3], refs[3:6], refs[6:9], refs[9:12]
+    for k in range(3):
+        value = (kept[k][...] + received[k][...].astype(jnp.float32)) * slope[k][...]
+        pre_grad_out[k][...] = value.astype(jnp.bfloat16)
+
+
+def gradient_kernel(hidden_first, *refs):
+    all_rows, values, outs = refs[:3], refs[3:15], refs[15:]
+    width = all_rows[0].shape[2] // 2
+    for k in range(3):
+        rows = all_rows[k]
+        pieces = values[4 * k : 4 * k + 4]
+        own_out, sent_out, by_width_out, by_hidden_out = outs[4 * k : 4 * k + 4]
+        near = jnp.concatenate([pieces[0][...], pieces[1][...]])
+        far = jnp.concatenate([pieces[2][...], pieces[3][...]])
+        if hidden_first:
+            grad = dot(near, rows[0], 0, 0) + dot(far, rows[1], 0, 0)
+            own_out[...] = grad[:, :width]
+            sent_out[...] = grad[:, width:].astype(sent_out.dtype)
+        else:
+            grad = dot(rows[0], near, 0, 0) + dot(rows[1], far, 0, 0)
+            own_out[...] = grad[:width]
+            sent_out[...] = grad[width:].astype(sent_out.dtype)
+        square = grad * grad + EPS_ONE
+        down = jnp.sum(square, axis=0, keepdims=True)
+        across = dot(jnp.ones((8, square.shape[1]), jnp.float32), square, 1, 1)
+        down = jnp.broadcast_to(down, (8, square.shape[1]))
+        by_width_out[...] = down if hidden_first else across
+        by_hidden_out[...] = across if hidden_first else down
 
 
 IN_WIDTH, OUT_WIDTH, IN_HIDDEN, OUT_HIDDEN, TOTALS, STAT_ROWS = 0, 8, 16, 22, 28, 32
@@ -180,37 +209,39 @@
 
 
 def norm_kernel(prev, group_sums, whole_sums, *refs):
-    grads_in, grads_out, factors_out, norms_out = refs[:3], refs[3:6], refs[6], refs[7]
+    own_in, sent_in, own_out, sent_out = refs[:3], refs[3:6], refs[6:9], refs[9:12]
+    factors_out, norms_out = refs[12], refs[13]
     place = place_in_group()
-    width = grads_in[0].shape[0] // 2
+    width = own_in[0].shape[0]
     row = lax.broadcasted_iota(jnp.int32, prev.shape, 0)
     by_width = row < IN_HIDDEN
     mean = jnp.where(by_width, whole_sums[...] / FF, group_sums[...] / D)
     factors_out[...] = DECAY_RATE * prev[...] + (1.0 - DECAY_RATE) * mean
     norm_in, norm_out = 0.0, 0.0
     for k in range(3):
-        half = grads_in[k].shape[1]
+        half = own_in[k].shape[1]
         partner = flipped(place, 1 << k)
         own_row = stat_row(factors_out, IN_WIDTH + place)[:, :width]
         pair_row = stat_row(factors_out, IN_WIDTH + partner)[:, :width]
         hidden_row = stat_row(factors_out, IN_HIDDEN + 2 * k + bit(place, k))[:, :half]
-        down = jnp.sum(grads_in[k][:width] * grads_in[k][:width] * upright(1.0 / own_row), axis=0, keepdims=True)
-        down = down + jnp.sum(
-            grads_in[k][width:] * grads_in[k][width:] * upright(1.0 / pair_row), axis=0, keepdims=True
-        )
+        sent = sent_in[k][...].astype(jnp.float32)
+        down = jnp.sum(own_in[k][...] * own_in[k][...] * upright(1.0 / own_row), axis=0, keepdims=True)
+        down = down + jnp.sum(sent * sent * upright(1.0 / pair_row), axis=0, keepdims=True)
         norm_in = norm_in + jnp.sum(down / hidden_row, axis=1, keepdims=True)
         own_row = stat_row(factors_out, OUT_WIDTH + place)[:, :width]
         pair_row = stat_row(factors_out, OUT_WIDTH + partner)[:, :width]
         hidden_row = stat_row(factors_out, OUT_HIDDEN + 2 * k + bit(place, k))[:, :half]
-        down = jnp.sum(grads_out[k][...] * grads_out[k][...] * upright(1.0 / hidden_row), axis=0, keepdims=True)
-        norm_out = norm_out + jnp.sum(down[:, :width] / own_row, axis=1, keepdims=True)
-        norm_out = norm_out + jnp.sum(down[:, width:] / pair_row, axis=1, keepdims=True)
+        inverse = upright(1.0 / hidden_row)
+        sent = sent_out[k][...].astype(jnp.float32)
+        down = jnp.sum(own_out[k][...] * own_out[k][...] * inverse, axis=0, keepdims=True) / own_row
+        down = down + jnp.sum(sent * sent * inverse, axis=0, keepdims=True) / pair_row
+        norm_out = norm_out + jnp.sum(down, axis=1, keepdims=True)
     row = lax.broadcasted_iota(jnp.int32, norms_out.shape, 0)
     norms_out[...] = jnp.where(row == 0, norm_in, norm_out)
 
 
 def final_kernel(bounds, prev, factors, whole_sums, norms, *refs):
-    grads_in, grads_out, got_in, got_out = refs[:3], refs[3:6], refs[6:9], refs[9:12]
+    own_in, own_out, got_in, got_out = refs[:3], refs[3:6], refs[6:9], refs[9:12]
     update_in, update_out = refs[12:]
     place = place_in_group()
     width = update_in.shape[0]
@@ -227,7 +258,7 @@
         low, half = bounds[k][0], (bounds[k][1] - bounds[k][0]) // 2
         own_bit = bit(place, k)
         if half % 128:
-            width_scaled = (grads_in[k][:width] * width_in, got_in[k][...].astype(jnp.float32) * width_in)
+            width_scaled = (own_in[k][...] * width_in, got_in[k][...].astype(jnp.float32) * width_in)
             for side in range(2):
                 hidden_in = lax.rsqrt(factors[IN_HIDDEN + 2 * k + side : IN_HIDDEN + 2 * k + side + 1, :half])
                 value = jnp.where(own_bit == side, *width_scaled) * hidden_in
@@ -238,9 +269,9 @@
             hidden_out = upright(lax.rsqrt(stat_row(factors, OUT_HIDDEN + 2 * k + side)[:, :half]))
             if half % 128 == 0:
                 hidden_in = lax.rsqrt(stat_row(factors, IN_HIDDEN + 2 * k + side)[:, :half])
-                value = grads_in[k][:width] if own else got_in[k][...].astype(jnp.float32)
+                value = own_in[k][...] if own else got_in[k][...].astype(jnp.float32)
                 update_in[:, pl.ds(start, half)] = (value * width_in * hidden_in).astype(update_in.dtype)
-            value = grads_out[k][:, :width] if own else got_out[k][...].astype(jnp.float32)
+            value = own_out[k][...] if own else got_out[k][...].astype(jnp.float32)
             update_out[pl.ds(start, half), :] = (value * hidden_out * width_out).astype(update_out.dtype)
 
 
@@ -285,6 +316,7 @@
         return routed.reshape(places, part_cap, block_width)
 
     routed = jnp.concatenate([route(tokens), route(cotangent)], axis=2)
+    routed, in_got, out_got = lax.optimization_barrier((routed, in_got, out_got))
     got = lax.all_to_all(routed, "expert", split_axis=0, concat_axis=0, tiled=True)
     got = got.reshape(places // GROUP, GROUP, part_cap, 2 * block_width).transpose(1, 0, 2, 3)
     got = got.reshape(GROUP, -1, 2 * block_width)
@@ -297,56 +329,51 @@
     own_tokens, pair_tokens = exchanged(got_tokens)
     own_cotangent, pair_cotangent = exchanged(got_cotangent)
 
+    def shapes(rows, dtype):
+        return [shape((rows, half), dtype) for half in halves]
+
+    count = got.shape[1] * 8
+    wide = 2 * block_width
+
     def scatter_sum(own, pairs, weight, got_weights, by_row):
-        results, rows, kept = [], [], []
-        received = []
+        outs = call(
+            functools.partial(sums_kernel, bounds, by_row), 40,
+            [shape((2, count, wide), bf16)] * 3 + shapes(count, bf16) + shapes(count, f32),
+            *own, *pairs[0], *pairs[1], *pairs[2], weight, *got_weights,
+        )
+        rows, sent, kept = outs[:3], outs[3:6], outs[6:]
+        received = [swap(sent[k], firsts[k]) for k in sets]
+        outs = call(add_kernel, 16, shapes(count // 2, f32) + shapes(count // 2, bf16), *kept, *received)
+        kept, sent = outs[:3], outs[3:]
+        return rows, kept, [swap(sent[k], seconds[k]) for k in sets]
+
+    def gather(owns):
+        pieces = []
         for k in sets:
-            count = own[0].shape[1] * 2 * 4
-            args = (k, bounds[k][0], halves[k], by_row)
-            row, sent = call(
-                functools.partial(sent_kernel, *args),
-                (shape((2, count, 2 * block_width), bf16), shape((count, halves[k]), bf16)),
-                *own, *pairs[k], weight, got_weights[k],
-            )
-            rows.append(row)
-            received.append(swap(sent, firsts[k]))
-        for k in sets:
-            count = rows[k].shape[1] // 2
-            args = (k, bounds[k][0], halves[k], by_row)
-            keep, sent = call(
-                functools.partial(kept_kernel, *args),
-                (shape((count, halves[k]), f32), shape((count, halves[k]), bf16)),
-                rows[k], weight, got_weights[k], received[k],
-            )
-            kept.append((keep, swap(sent, seconds[k])))
-        return rows, [keep + got.astype(f32) for keep, got in kept]
-
-    def gather(owns):
-        near = [jnp.concatenate([owns[k], swap(owns[k], seconds[k])]) for k in sets]
-        return [(near[k], swap(near[k], firsts[k])) for k in sets]
-
-    token_rows, pre = scatter_sum(own_tokens, pair_tokens, local_in, in_got, False)
-    cotangent_rows, back = scatter_sum(own_cotangent, pair_cotangent, local_out, out_got, True)
-    acts = [gelu_pair(value) for value in pre]
-    hidden = gather([act[0].astype(bf16) for act in acts])
-    pre_grad = gather([(value * act[1]).astype(bf16) for value, act in zip(back, acts)])
+            near = swap(owns[k], seconds[k])
+            pieces += [owns[k], near, swap(owns[k], firsts[k]), swap(near, firsts[k])]
+        return pieces
+
+    token_rows, *pre = scatter_sum(own_tokens, pair_tokens, local_in, in_got, False)
+    cotangent_rows, *back = scatter_sum(own_cotangent, pair_cotangent, local_out, out_got, True)
+    outs = call(hidden_kernel, 16, shapes(count // 2, bf16) + shapes(count // 2, f32), *pre[0], *pre[1])
+    hidden, slope = gather(outs[:3]), outs[3:]
+    outs = call(pre_grad_kernel, 16, shapes(count // 2, bf16), *back[0], *back[1], *slope)
+    pre_grad = gather(outs)
 
     def gradient(rows, values, hidden_first):
-        half, wide = values[0].shape[1], 2 * block_width
-        grad_shape = (half, wide) if hidden_first else (wide, half)
-        sent_shape = (half, block_width) if hidden_first else (block_width, half)
-        return call(
-            functools.partial(gradient_kernel, hidden_first),
-            (shape(grad_shape, f32), shape(sent_shape, bf16), shape((8, wide), f32), shape((8, half), f32)),
-            rows, *values,
-        )
-
-    out_results = [gradient(cotangent_rows[k], hidden[k], True) for k in sets]
-    out_sent = [result[1] for result in out_results]
-    pre_grad, out_sent = lax.optimization_barrier((pre_grad, out_sent))
+        out_shapes = []
+        for half in halves:
+            part = (half, block_width) if hidden_first else (block_width, half)
+            out_shapes += [shape(part, f32), shape(part, bf16), shape((8, wide), f32), shape((8, half), f32)]
+        outs = call(functools.partial(gradient_kernel, hidden_first), 40, out_shapes, *rows, *values)
+        return outs[0::4], outs[1::4], outs[2::4], outs[3::4]
+
+    out_own, out_sent, *out_sums = gradient(cotangent_rows, hidden, True)
     got_out = [swap(out_sent[k], MASKS[k]) for k in sets]
-    in_results = [gradient(token_rows[k], pre_grad[k], False) for k in sets]
-    got_in = [swap(in_results[k][1], MASKS[k]) for k in sets]
+    pre_grad, got_out = lax.optimization_barrier((pre_grad, got_out))
+    in_own, in_sent, *in_sums = gradient(token_rows, pre_grad, False)
+    got_in = [swap(in_sent[k], MASKS[k]) for k in sets]
 
     lanes = max(block_width, *halves)
     width_pick = lax.dynamic_index_in_dim(width_states, expert, 1, keepdims=False)
@@ -371,22 +398,22 @@
         return values if values.shape[1] > 128 else jnp.pad(values, ((0, 0), (0, lanes - values.shape[1])))
 
     sums = []
-    for results in (in_results, out_results):
-        sums += [result[2] for result in results] + [whole_tiles(result[3]) for result in results]
-    stats = call(collect_kernel, shape((STAT_ROWS, lanes), f32), hidden_pick[1:2], *sums)
+    for by_width, by_hidden in (in_sums, out_sums):
+        sums += [*by_width, *map(whole_tiles, by_hidden)]
+    stats = call(collect_kernel, 4, shape((STAT_ROWS, lanes), f32), hidden_pick[1:2], *sums)
     group_sums = cube_total(stats)
     whole_sums = ffn_total(group_sums)
-    grads = [result[0] for result in in_results] + [result[0] for result in out_results]
+    whole_sums, got_in = lax.optimization_barrier((whole_sums, got_in))
     factors, norms = call(
-        norm_kernel,
+        norm_kernel, 20,
         (shape((STAT_ROWS, lanes), f32), shape((8, 128), f32)),
-        prev, group_sums, whole_sums, *grads,
+        prev, group_sums, whole_sums, *in_own, *in_sent, *out_own, *out_sent,
     )
     norms = ffn_total(cube_total(norms))
     update_in, update_out = call(
-        functools.partial(final_kernel, bounds),
+        functools.partial(final_kernel, bounds), 24,
         (shape(local_in.shape, bf16), shape(local_out.shape, bf16)),
-        prev, factors, whole_sums, norms, *grads, *got_in, *got_out,
+        prev, factors, whole_sums, norms, *in_own, *out_own, *got_in, *got_out,
     )
     return (update_in[None], update_out[None])
 

time: 293 us -> 275 us (0.939)
  blocking collectives: 0 us -> 35.9 us
  Pallas kernels: 71.7 us -> 44.2 us
  waiting for transfers between devices: 98.3 us -> 84.3 us
  other arithmetic: 10.8 us -> 0.65 us
    all_to_all x0 -> x1, blocking collectives: none -> 35.9 us  [shards(): lax.all_to_all(routed, 'expert', split_axis=0, concat_axis=0, tiled=True)]
    pallas_call x21 -> x11, Pallas kernels: 71.7 us -> 44.2 us  [call(): pl.pallas_call(kernel, out_shape=out_shape, in_specs=[pl.BlockSpec(memory...]
    all_to_all x1 -> x0, waiting for transfers between devices: 17.1 us -> none  [shards(): lax.all_to_all(routed, 'expert', split_axis=0, concat_axis=0, tiled=True)]
    all_to_all x1 -> x0, starting transfers between devices: 7.58 us -> none  [shards(): lax.all_to_all(routed, 'expert', split_axis=0, concat_axis=0, tiled=True)]
    ppermute x60 -> x66, starting transfers between devices: 65 us -> 71.7 us  [swap(): return lax.ppermute(value, axis, pairs)]
    convert_element_type x3 -> x0, other arithmetic: 3.58 us -> none  [shards(): hidden = gather([act[0].astype(bf16) for act in acts])]
    concatenate x6 -> x0, other arithmetic: 3.49 us -> none  [gather(): near = [jnp.concatenate([owns[k], swap(owns[k], seconds[k])]) for k in sets]]
    unnamed x127 -> x107, local copies, waits for them, and re-layouts: 28.2 us -> 25 us
  transfers between devices with their start and end apart: 61 -> 66, of which waited for: 19 -> 28; matrix products, arithmetic and copies ran while one was open for 5% -> 3% of each run, Pallas kernels for 18% -> 10%
where the time goes in v1:
time: 275 us; the launch traced here: 273 us
  waiting for transfers between devices  84.3 us (31%)
  starting transfers between devices  71.7 us (26%)
  Pallas kernels  44.2 us (16%)
  blocking collectives  35.9 us (13%)
  local copies, waits for them, and re-layouts  34.7 us (13%)
    ppermute x66, waiting for transfers between devices, swap(): return lax.ppermute(value, axis, pairs)  84.3 us
    ppermute x66, starting transfers between devices, swap(): return lax.ppermute(value, axis, pairs)  71.7 us
    pallas_call x11, Pallas kernels, call(): pl.pallas_call(kernel, out_shape=out_shape, in_specs=[pl.BlockSpec(memory...  44.2 us
    all_to_all x1, blocking collectives, shards(): lax.all_to_all(routed, 'expert', split_axis=0, concat_axis=0, tiled=True)  35.9 us
    unnamed x107, local copies, waits for them, and re-layouts  25 us
    dynamic_slice x4, local copies, waits for them, and re-layouts, pair_side(): lax.dynamic_slice_in_dim(values, bounds[k][0] + (1 - bits[k]) * halves[k]...  7.94 us
  transfers between devices with their start and end apart: 66, of which 28 were waited for; matrix products, arithmetic and copies ran while one was open for 3% of the time, Pallas kernels for 10%

profile of v1, /device:TPU:1, one launch (start us, length us, event | category | flops | bytes accessed | tf_op | source)
XLA Modules:
  0.0 273.4 jit_solution(7162208980737337305)
XLA Ops:
  0.7 2.2 dynamic-slice_bitcast_fusion.4
  2.8 2.1 collective-permute-start.1
  4.9 1.3 collective-permute-start.2
  6.2 2.0 dynamic-slice_bitcast_fusion.2
  8.5 1.9 dynamic-slice_bitcast_fusion.1
  11.6 1.9 dynamic-slice_bitcast_fusion
  16.4 5.9 %collective-permute-done.4.refs_10_ = bf16[384,512]{1,0:T(8,128)(2,1)S(1)} collective-permute-done((bf16[384,512]{1,0:T(8,128)(2,1)}, bf16[384,512]{1,0:T(8,128)(2,1)S(1)}, u32[]{:S(2)}, u32[]{:S(2)}) %collective-permute-start.4) | collective-permute-done | bytes 393248 | tf_op jit(solution)/shard_map/ppermute | solution.py:28
  22.4 1.3 collective-permute-done.5.refs_11_
  23.7 10.0 %collective-permute-done.3.refs_9_ = bf16[512,512]{1,0:T(8,128)(2,1)S(1)} collective-permute-done((bf16[512,512]{1,0:T(8,128)(2,1)}, bf16[512,512]{1,0:T(8,128)(2,1)S(1)}, u32[]{:S(2)}, u32[]{:S(2)}) %collective-permute-start.3) | collective-permute-done | bytes 524320 | tf_op jit(solution)/shard_map/ppermute | solution.py:28
  33.7 35.9 %all_to_all.5 = bf16[16,40,1024]{2,1,0:T(8,128)(2,1)S(1)} all-to-all(bf16[16,40,1024]{2,1,0:T(8,128)(2,1)S(1)} %pad_maximum_fusion), channel_id=1, replica_groups=mesh['expert'=16,'ffn'=2] {'expert'}, dimensions={0} | all-to-all | bytes 2621440 | tf_op jit(solution)/shard_map/all_to_all | solution.py:320
  72.1 3.1 %collective-permute-start.6 = (bf16[8,80,512]{2,1,0:T(8,128)(2,1)S(1)}, bf16[8,80,512]{2,1,0:T(8,128)(2,1)S(1)}, u32[]{:S(2)}, u32[]{:S(2)}) collective-permute-start(bf16[8,80,512]{2,1,0:T(8,128)(2,1)S(1)} %get-tuple-element.199.refs_0_), channel_id=1, source_target_pairs={{0,1},{1,0},{2,3},{3,2},{4,5},{5,4},{6,7},{7,6},{8,9},{9,8},{10,11... | collective-permute-start | bytes 1966088 | tf_op jit(solution)/shard_map/ppermute | solution.py:28
  76.3 6.9 %collective-permute-done.9.refs_4_ = bf16[8,80,512]{2,1,0:T(8,128)(2,1)S(1)} collective-permute-done((bf16[8,80,512]{2,1,0:T(8,128)(2,1)S(1)}, bf16[8,80,512]{2,1,0:T(8,128)(2,1)S(1)}, u32[]{:S(2)}, u32[]{:S(2)}) %collective-permute-start.9) | collective-permute-done | bytes 655392 | tf_op jit(solution)/shard_map/ppermute | solution.py:28
  83.2 1.3 collective-permute-start.16
  84.5 1.3 collective-permute-start.18
  85.8 6.4 %collective-permute-start.10 = (bf16[8,80,512]{2,1,0:T(8,128)(2,1)S(1)}, bf16[8,80,512]{2,1,0:T(8,128)(2,1)S(1)}, u32[]{:S(2)}, u32[]{:S(2)}) collective-permute-start(bf16[8,80,512]{2,1,0:T(8,128)(2,1)S(1)} %collective-permute-done.9.refs_4_), channel_id=1, source_target_pairs={{0,1},{1,0},{2,3},{3,2},{4,5},{5,4},{6,7},{7,6},{8,9},{9,8},{10,11... | collective-permute-start | bytes 1966088 | tf_op jit(solution)/shard_map/ppermute | solution.py:28
  92.3 7.1 %collective-permute-done.14.refs_2_ = bf16[8,80,512]{2,1,0:T(8,128)(2,1)S(1)} collective-permute-done((bf16[8,80,512]{2,1,0:T(8,128)(2,1)S(1)}, bf16[8,80,512]{2,1,0:T(8,128)(2,1)S(1)}, u32[]{:S(2)}, u32[]{:S(2)}) %collective-permute-start.14) | collective-permute-done | bytes 655392 | tf_op jit(solution)/shard_map/ppermute | solution.py:28
  99.3 3.7 %collective-permute-start.8 = (bf16[8,80,512]{2,1,0:T(8,128)(2,1)S(1)}, bf16[8,80,512]{2,1,0:T(8,128)(2,1)S(1)}, u32[]{:S(2)}, u32[]{:S(2)}) collective-permute-start(bf16[8,80,512]{2,1,0:T(8,128)(2,1)S(1)} %collective-permute-done.7.refs_2_), channel_id=1, source_target_pairs={{0,1},{1,0},{2,3},{3,2},{4,5},{5,4},{6,7},{7,6},{8,9},{9,8},{10,11... | collective-permute-start | bytes 1966088 | tf_op jit(solution)/shard_map/ppermute | solution.py:28
  104.7 8.1 %shard_map.86 = (bf16[2,640,1024]{2,1,0:T(8,128)(2,1)S(1)}, bf16[2,640,1024]{2,1,0:T(8,128)(2,1)}, bf16[2,640,1024]{2,1,0:T(8,128)(2,1)}, bf16[640,512]{1,0:T(8,...) custom-call(bf16[8,80,512]{2,1,0:T(8,128)(2,1)S(1)} %get-tuple-eleme, ...), custom_call_target="tpu_custom_call" | custom-call | tf_op jit(solution)/shard_map/pallas_call | solution.py:67
  112.9 1.5 copy-done.13
  115.7 8.1 %shard_map.87 = (bf16[2,640,1024]{2,1,0:T(8,128)(2,1)S(1)}, bf16[2,640,1024]{2,1,0:T(8,128)(2,1)}, bf16[2,640,1024]{2,1,0:T(8,128)(2,1)}, bf16[640,512]{1,0:T(8,...) custom-call(bf16[8,80,512]{2,1,0:T(8,128)(2,1)S(1)} %get-tuple-eleme, ...), custom_call_target="tpu_custom_call" | custom-call | tf_op jit(solution)/shard_map/pallas_call | solution.py:67
  127.2 3.2 %collective-permute-done.26.refs_3_ = bf16[640,512]{1,0:T(8,128)(2,1)S(1)} collective-permute-done((bf16[640,512]{1,0:T(8,128)(2,1)S(1)}, bf16[640,512]{1,0:T(8,128)(2,1)S(1)}, u32[]{:S(2)}, u32[]{:S(2)}) %collective-permute-start.26) | collective-permute-done | bytes 655392 | tf_op jit(solution)/shard_map/ppermute | solution.py:28
  132.1 4.2 %collective-permute-done.21.refs_4_ = bf16[640,384]{1,0:T(8,128)(2,1)S(1)} collective-permute-done((bf16[640,384]{1,0:T(8,128)(2,1)S(1)}, bf16[640,384]{1,0:T(8,128)(2,1)S(1)}, u32[]{:S(2)}, u32[]{:S(2)}) %collective-permute-start.21) | collective-permute-done | bytes 491552 | tf_op jit(solution)/shard_map/ppermute | solution.py:28
  138.2 6.3 %collective-permute-done.20.refs_3_ = bf16[640,512]{1,0:T(8,128)(2,1)S(1)} collective-permute-done((bf16[640,512]{1,0:T(8,128)(2,1)S(1)}, bf16[640,512]{1,0:T(8,128)(2,1)S(1)}, u32[]{:S(2)}, u32[]{:S(2)}) %collective-permute-start.20) | collective-permute-done | bytes 655392 | tf_op jit(solution)/shard_map/ppermute | solution.py:28
  146.9 2.8 %collective-permute-done.31.refs_5_ = bf16[320,384]{1,0:T(8,128)(2,1)S(1)} collective-permute-done((bf16[320,384]{1,0:T(8,128)(2,1)S(1)}, bf16[320,384]{1,0:T(8,128)(2,1)S(1)}, u32[]{:S(2)}, u32[]{:S(2)}) %collective-permute-start.31) | collective-permute-done | bytes 245792 | tf_op jit(solution)/shard_map/ppermute | solution.py:28
  153.2 1.3 collective-permute-done.25.refs_5_
  154.5 1.5 collective-permute-start.41
  156.9 1.5 collective-permute-start.35
  158.4 1.4 collective-permute-done.47.refs_12_
  164.1 3.4 %collective-permute-done.35.refs_8_ = bf16[320,384]{1,0:T(8,128)(2,1)} collective-permute-done((bf16[320,384]{1,0:T(8,128)(2,1)S(1)}, bf16[320,384]{1,0:T(8,128)(2,1)}, u32[]{:S(2)}, u32[]{:S(2)}) %collective-permute-start.35) | collective-permute-done | bytes 245792 | tf_op jit(solution)/shard_map/ppermute | solution.py:28
  167.9 4.2 %collective-permute-done.38.refs_12_ = bf16[320,384]{1,0:T(8,128)(2,1)S(1)} collective-permute-done((bf16[320,384]{1,0:T(8,128)(2,1)S(1)}, bf16[320,384]{1,0:T(8,128)(2,1)S(1)}, u32[]{:S(2)}, u32[]{:S(2)}) %collective-permute-start.38) | collective-permute-done | bytes 245792 | tf_op jit(solution)/shard_map/ppermute | solution.py:28
  173.7 5.4 %collective-permute-done.43.refs_6_ = bf16[320,512]{1,0:T(8,128)(2,1)S(1)} collective-permute-done((bf16[320,512]{1,0:T(8,128)(2,1)S(1)}, bf16[320,512]{1,0:T(8,128)(2,1)S(1)}, u32[]{:S(2)}, u32[]{:S(2)}) %collective-permute-start.43) | collective-permute-done | bytes 327712 | tf_op jit(solution)/shard_map/ppermute | solution.py:28
  179.8 7.6 %shard_map.92 = (f32[512,512]{1,0:T(8,128)S(1)}, bf16[512,512]{1,0:T(8,128)(2,1)S(1)}, f32[8,1024]{1,0:T(8,128)S(1)}, f32[8,512]{1,0:T(8,128)S(1)}, f32[384,512]...) custom-call(bf16[2,640,1024]{2,1,0:T(8,128)(2,1)S(1)} %get-tuple-ele, ...), custom_call_target="tpu_custom_call" | custom-call | tf_op jit(solution)/shard_map/pallas_call | solution.py:67
  194.5 1.5 collective-permute-start.40
  196.1 1.3 collective-permute-start.34
  198.1 5.6 %collective-permute-done.40.refs_14_ = bf16[320,384]{1,0:T(8,128)(2,1)S(1)} collective-permute-done((bf16[320,384]{1,0:T(8,128)(2,1)}, bf16[320,384]{1,0:T(8,128)(2,1)S(1)}, u32[]{:S(2)}, u32[]{:S(2)}) %collective-permute-start.40) | collective-permute-done | bytes 245792 | tf_op jit(solution)/shard_map/ppermute | solution.py:28
  206.0 1.7 copy-done.14
  207.8 1.7 copy-done.15
  213.3 8.5 %shard_map.93 = (f32[512,512]{1,0:T(8,128)S(1)}, bf16[512,512]{1,0:T(8,128)(2,1)}, f32[8,1024]{1,0:T(8,128)S(1)}, f32[8,512]{1,0:T(8,128)S(1)}, f32[512,384]{1,0...) custom-call(bf16[2,640,1024]{2,1,0:T(8,128)(2,1)S(1)} %copy-done.14,, ...), custom_call_target="tpu_custom_call" | custom-call | tf_op jit(solution)/shard_map/pallas_call | solution.py:67
  223.7 1.4 collective-permute-start.53
  226.4 1.4 collective-permute-start.58
  231.1 5.3 %collective-permute-done.56 = f32[32,512]{1,0:T(8,128)S(1)} collective-permute-done((f32[32,512]{1,0:T(8,128)S(1)}, f32[32,512]{1,0:T(8,128)S(1)}, u32[]{:S(2)}, u32[]{:S(2)}) %collective-permute-start.56) | collective-permute-done | bytes 65568 | tf_op jit(solution)/shard_map/ppermute | solution.py:28
  236.5 10.9 %collective-permute-start.57 = (f32[32,512]{1,0:T(8,128)S(1)}, f32[32,512]{1,0:T(8,128)S(1)}, u32[]{:S(2)}, u32[]{:S(2)}) collective-permute-start(f32[32,512]{1,0:T(8,128)S(1)} %add.91.group_sums), channel_id=1, source_target_pairs={{0,1},{1,0},{2,3},{3,2},{4,5},{5,4},{6,7},{7,6},{8,9},{9,8},{10,11... | collective-permute-start | bytes 196616 | tf_op jit(solution)/shard_map/ppermute | solution.py:28
  252.8 3.7 %shard_map.95 = (f32[32,512]{1,0:T(8,128)S(1)}, f32[8,128]{1,0:T(8,128)S(1)}) custom-call(f32[32,512]{1,0:T(8,128)S(1)} %concatenate.6.prev, f32[32,512]{1,0:T(8,128)S(1)} %add.91.group_sums, f32[32,512]{1,0:T(8,128)S(1)} %add.92.whole_sums, f32[512,512]{1,0:T(8,128)S(1)} %get-tuple-element.172.refs_0_, f32[512,384]{1,0:T(8,128)S(1)} %copy-done.8, ...), custom_call_target="tpu_custom_call" | custom-call | tf_op jit(solution)/shard_map/pallas_call | solution.py:67
  257.2 1.9 collective-permute-start.63
  259.1 1.4 collective-permute-done.63
  261.2 1.8 collective-permute-done.64
  263.0 3.0 %collective-permute-start.65 = (f32[8,128]{1,0:T(8,128)S(1)}, f32[8,128]{1,0:T(8,128)S(1)}, u32[]{:S(2)}, u32[]{:S(2)}) collective-permute-start(f32[8,128]{1,0:T(8,128)S(1)} %add.96), channel_id=1, source_target_pairs={{0,1},{1,0},{2,3},{3,2},{4,5},{5,4},{6,7},{7,6},{8,9},{9,8},{10,11... | collective-permute-start | bytes 12296 | tf_op jit(solution)/shard_map/ppermute | solution.py:28
  268.1 5.3 %shard_map.96 = (bf16[512,2560]{1,0:T(8,128)(2,1)}, bf16[2560,512]{1,0:T(8,128)(2,1)}) custom-call(f32[32,512]{1,0:T(8,128)S(1)} %concatenate.6.prev, f32[32,512]{1,0:T(8,128)S(1)} %get-tuple-element.178.factors, f32[32,512]{1,0:T(8,128)S(1)} %add.92.whole_sums, f32[8,128]{1,0:T(8,128)S(1)} %add.97.norms, f32[512,512]{1,0:T(8,128)S(1)} %get-tuple-element.172.refs_0_, ...), custom_call_target="tpu_custom_call" | custom-call | tf_op jit(solution)/shard_map/pallas_call | solution.py:67
  (242 shorter events, 60.8 us)
Async XLA Ops:
  2.8 12.1 %collective-permute-start.1 = (bf16[512,384]{1,0:T(8,128)(2,1)}, bf16[512,384]{1,0:T(8,128)(2,1)S(1)}, u32[]{:S(2)}, u32[]{:S(2)}) collective-permute-start(bf16[512,384]{1,0:T(8,128)(2,1)} %get-tuple-element.197), channel_id=1, source_target_pairs={{0,4},{2,6},{4,0},{6,2},{8,12},{10,14},{12,8},{14,10},{16,20},{18,... | collective-permute-start | bytes 1179656 | tf_op jit(solution)/shard_map/ppermute | solution.py:28
  4.9 11.5 %collective-permute-start.2 = (bf16[512,384]{1,0:T(8,128)(2,1)}, bf16[512,384]{1,0:T(8,128)(2,1)S(1)}, u32[]{:S(2)}, u32[]{:S(2)}) collective-permute-start(bf16[512,384]{1,0:T(8,128)(2,1)} %get-tuple-element.196), channel_id=1, source_target_pairs={{0,8},{2,10},{4,12},{6,14},{8,0},{10,2},{12,4},{14,6},{16,24},{18,... | collective-permute-start | bytes 1179656 | tf_op jit(solution)/shard_map/ppermute | solution.py:28
  8.2 14.1 %collective-permute-start.4 = (bf16[384,512]{1,0:T(8,128)(2,1)}, bf16[384,512]{1,0:T(8,128)(2,1)S(1)}, u32[]{:S(2)}, u32[]{:S(2)}) collective-permute-start(bf16[384,512]{1,0:T(8,128)(2,1)} %get-tuple-element.195), channel_id=1, source_target_pairs={{0,4},{2,6},{4,0},{6,2},{8,12},{10,14},{12,8},{14,10},{16,20},{18,... | collective-permute-start | bytes 1179656 | tf_op jit(solution)/shard_map/ppermute | solution.py:28
  10.3 13.3 %collective-permute-start = (bf16[512,512]{1,0:T(8,128)(2,1)}, bf16[512,512]{1,0:T(8,128)(2,1)S(1)}, u32[]{:S(2)}, u32[]{:S(2)}) collective-permute-start(bf16[512,512]{1,0:T(8,128)(2,1)} %dynamic-slice_bitcast_fusion.1), channel_id=1, source_target_pairs={{0,2},{2,0},{4,6},{6,4},{8,10},{10,8},{12,14},{14,12},{16,18},{18,... | collective-permute-start | bytes 1572872 | tf_op jit(solution)/shard_map/ppermute | solution.py:28
  13.4 20.3 %collective-permute-start.3 = (bf16[512,512]{1,0:T(8,128)(2,1)}, bf16[512,512]{1,0:T(8,128)(2,1)S(1)}, u32[]{:S(2)}, u32[]{:S(2)}) collective-permute-start(bf16[512,512]{1,0:T(8,128)(2,1)} %dynamic-slice_bitcast_fusion), channel_id=1, source_target_pairs={{0,2},{2,0},{4,6},{6,4},{8,10},{10,8},{12,14},{14,12},{16,18},{18,... | collective-permute-start | bytes 1572872 | tf_op jit(solution)/shard_map/ppermute | solution.py:28
  15.1 8.5 %collective-permute-start.5 = (bf16[384,512]{1,0:T(8,128)(2,1)S(1)}, bf16[384,512]{1,0:T(8,128)(2,1)S(1)}, u32[]{:S(2)}, u32[]{:S(2)}) collective-permute-start(bf16[384,512]{1,0:T(8,128)(2,1)S(1)} %copy-done.48), channel_id=1, source_target_pairs={{0,8},{2,10},{4,12},{6,14},{8,0},{10,2},{12,4},{14,6},{16,24},{18,... | collective-permute-start | bytes 1179656 | tf_op jit(solution)/shard_map/ppermute | solution.py:28
  69.9 13.3 %collective-permute-start.9 = (bf16[8,80,512]{2,1,0:T(8,128)(2,1)S(1)}, bf16[8,80,512]{2,1,0:T(8,128)(2,1)S(1)}, u32[]{:S(2)}, u32[]{:S(2)}) collective-permute-start(bf16[8,80,512]{2,1,0:T(8,128)(2,1)S(1)} %get-tuple-element.199.refs_0_), channel_id=1, source_target_pairs={{0,4},{2,6},{4,0},{6,2},{8,12},{10,14},{12,8},{14,10},{16,20},{18,... | collective-permute-start | bytes 1966088 | tf_op jit(solution)/shard_map/ppermute | solution.py:28
  70.8 13.7 %collective-permute-start.11 = (bf16[8,80,512]{2,1,0:T(8,128)(2,1)S(1)}, bf16[8,80,512]{2,1,0:T(8,128)(2,1)S(1)}, u32[]{:S(2)}, u32[]{:S(2)}) collective-permute-start(bf16[8,80,512]{2,1,0:T(8,128)(2,1)S(1)} %get-tuple-element.199.refs_0_), channel_id=1, source_target_pairs={{0,8},{2,10},{4,12},{6,14},{8,0},{10,2},{12,4},{14,6},{16,24},{18,... | collective-permute-start | bytes 1966088 | tf_op jit(solution)/shard_map/ppermute | solution.py:28
  71.8 14.0 %collective-permute-start.7 = (bf16[8,80,512]{2,1,0:T(8,128)(2,1)S(1)}, bf16[8,80,512]{2,1,0:T(8,128)(2,1)S(1)}, u32[]{:S(2)}, u32[]{:S(2)}) collective-permute-start(bf16[8,80,512]{2,1,0:T(8,128)(2,1)S(1)} %get-tuple-element.199.refs_0_), channel_id=1, source_target_pairs={{0,2},{2,0},{4,6},{6,4},{8,10},{10,8},{12,14},{14,12},{16,18},{18,... | collective-permute-start | bytes 1966088 | tf_op jit(solution)/shard_map/ppermute | solution.py:28
  72.1 20.2 %collective-permute-start.6 = (bf16[8,80,512]{2,1,0:T(8,128)(2,1)S(1)}, bf16[8,80,512]{2,1,0:T(8,128)(2,1)S(1)}, u32[]{:S(2)}, u32[]{:S(2)}) collective-permute-start(bf16[8,80,512]{2,1,0:T(8,128)(2,1)S(1)} %get-tuple-element.199.refs_0_), channel_id=1, source_target_pairs={{0,1},{1,0},{2,3},{3,2},{4,5},{5,4},{6,7},{7,6},{8,9},{9,8},{10,11... | collective-permute-start | bytes 1966088 | tf_op jit(solution)/shard_map/ppermute | solution.py:28
  75.2 24.2 %collective-permute-start.14 = (bf16[8,80,512]{2,1,0:T(8,128)(2,1)S(1)}, bf16[8,80,512]{2,1,0:T(8,128)(2,1)S(1)}, u32[]{:S(2)}, u32[]{:S(2)}) collective-permute-start(bf16[8,80,512]{2,1,0:T(8,128)(2,1)S(1)} %get-tuple-element.198.refs_0_), channel_id=1, source_target_pairs={{0,2},{2,0},{4,6},{6,4},{8,10},{10,8},{12,14},{14,12},{16,18},{18,... | collective-permute-start | bytes 1966088 | tf_op jit(solution)/shard_map/ppermute | solution.py:28
  83.2 19.8 %collective-permute-start.16 = (bf16[8,80,512]{2,1,0:T(8,128)(2,1)S(1)}, bf16[8,80,512]{2,1,0:T(8,128)(2,1)S(1)}, u32[]{:S(2)}, u32[]{:S(2)}) collective-permute-start(bf16[8,80,512]{2,1,0:T(8,128)(2,1)S(1)} %get-tuple-element.198.refs_0_), channel_id=1, source_target_pairs={{0,4},{2,6},{4,0},{6,2},{8,12},{10,14},{12,8},{14,10},{16,20},{18,... | collective-permute-start | bytes 1966088 | tf_op jit(solution)/shard_map/ppermute | solution.py:28
  84.5 18.5 %collective-permute-start.18 = (bf16[8,80,512]{2,1,0:T(8,128)(2,1)S(1)}, bf16[8,80,512]{2,1,0:T(8,128)(2,1)S(1)}, u32[]{:S(2)}, u32[]{:S(2)}) collective-permute-start(bf16[8,80,512]{2,1,0:T(8,128)(2,1)S(1)} %get-tuple-element.198.refs_0_), channel_id=1, source_target_pairs={{0,8},{2,10},{4,12},{6,14},{8,0},{10,2},{12,4},{14,6},{16,24},{18,... | collective-permute-start | bytes 1966088 | tf_op jit(solution)/shard_map/ppermute | solution.py:28
  85.8 17.7 %collective-permute-start.10 = (bf16[8,80,512]{2,1,0:T(8,128)(2,1)S(1)}, bf16[8,80,512]{2,1,0:T(8,128)(2,1)S(1)}, u32[]{:S(2)}, u32[]{:S(2)}) collective-permute-start(bf16[8,80,512]{2,1,0:T(8,128)(2,1)S(1)} %collective-permute-done.9.refs_4_), channel_id=1, source_target_pairs={{0,1},{1,0},{2,3},{3,2},{4,5},{5,4},{6,7},{7,6},{8,9},{9,8},{10,11... | collective-permute-start | bytes 1966088 | tf_op jit(solution)/shard_map/ppermute | solution.py:28
  92.3 11.3 %collective-permute-start.12 = (bf16[8,80,512]{2,1,0:T(8,128)(2,1)S(1)}, bf16[8,80,512]{2,1,0:T(8,128)(2,1)S(1)}, u32[]{:S(2)}, u32[]{:S(2)}) collective-permute-start(bf16[8,80,512]{2,1,0:T(8,128)(2,1)S(1)} %collective-permute-done.11.refs_6_), channel_id=1, source_target_pairs={{0,1},{1,0},{2,3},{3,2},{4,5},{5,4},{6,7},{7,6},{8,9},{9,8},{10,11... | collective-permute-start | bytes 1966088 | tf_op jit(solution)/shard_map/ppermute | solution.py:28
  103.0 11.8 %collective-permute-start.13 = (bf16[8,80,512]{2,1,0:T(8,128)(2,1)S(1)}, bf16[8,80,512]{2,1,0:T(8,128)(2,1)S(1)}, u32[]{:S(2)}, u32[]{:S(2)}) collective-permute-start(bf16[8,80,512]{2,1,0:T(8,128)(2,1)S(1)} %get-tuple-element.198.refs_0_), channel_id=1, source_target_pairs={{0,1},{1,0},{2,3},{3,2},{4,5},{5,4},{6,7},{7,6},{8,9},{9,8},{10,11... | collective-permute-start | bytes 1966088 | tf_op jit(solution)/shard_map/ppermute | solution.py:28
  103.0 12.4 %collective-permute-start.15 = (bf16[8,80,512]{2,1,0:T(8,128)(2,1)S(1)}, bf16[8,80,512]{2,1,0:T(8,128)(2,1)S(1)}, u32[]{:S(2)}, u32[]{:S(2)}) collective-permute-start(bf16[8,80,512]{2,1,0:T(8,128)(2,1)S(1)} %collective-permute-done.14.refs_2_), channel_id=1, source_target_pairs={{0,1},{1,0},{2,3},{3,2},{4,5},{5,4},{6,7},{7,6},{8,9},{9,8},{10,11... | collective-permute-start | bytes 1966088 | tf_op jit(solution)/shard_map/ppermute | solution.py:28
  103.5 12.2 %collective-permute-start.17 = (bf16[8,80,512]{2,1,0:T(8,128)(2,1)S(1)}, bf16[8,80,512]{2,1,0:T(8,128)(2,1)S(1)}, u32[]{:S(2)}, u32[]{:S(2)}) collective-permute-start(bf16[8,80,512]{2,1,0:T(8,128)(2,1)S(1)} %collective-permute-done.16.refs_4_), channel_id=1, source_target_pairs={{0,1},{1,0},{2,3},{3,2},{4,5},{5,4},{6,7},{7,6},{8,9},{9,8},{10,11... | collective-permute-start | bytes 1966088 | tf_op jit(solution)/shard_map/ppermute | solution.py:28
  103.6 12.1 %collective-permute-start.19 = (bf16[8,80,512]{2,1,0:T(8,128)(2,1)S(1)}, bf16[8,80,512]{2,1,0:T(8,128)(2,1)S(1)}, u32[]{:S(2)}, u32[]{:S(2)}) collective-permute-start(bf16[8,80,512]{2,1,0:T(8,128)(2,1)S(1)} %collective-permute-done.18.refs_6_), channel_id=1, source_target_pairs={{0,1},{1,0},{2,3},{3,2},{4,5},{5,4},{6,7},{7,6},{8,9},{9,8},{10,11... | collective-permute-start | bytes 1966088 | tf_op jit(solution)/shard_map/ppermute | solution.py:28
  114.4 12.4 %collective-permute-start.27 = (bf16[640,384]{1,0:T(8,128)(2,1)S(1)}, bf16[640,384]{1,0:T(8,128)(2,1)S(1)}, u32[]{:S(2)}, u32[]{:S(2)}) collective-permute-start(bf16[640,384]{1,0:T(8,128)(2,1)S(1)} %get-tuple-element.121), channel_id=1, source_target_pairs={{0,8},{2,10},{4,12},{6,14},{8,0},{10,2},{12,4},{14,6},{16,24},{18,... | collective-permute-start | bytes 1474568 | tf_op jit(solution)/shard_map/ppermute | solution.py:28
  114.8 15.6 %collective-permute-start.26 = (bf16[640,512]{1,0:T(8,128)(2,1)S(1)}, bf16[640,512]{1,0:T(8,128)(2,1)S(1)}, u32[]{:S(2)}, u32[]{:S(2)}) collective-permute-start(bf16[640,512]{1,0:T(8,128)(2,1)S(1)} %get-tuple-element.120), channel_id=1, source_target_pairs={{0,4},{2,6},{4,0},{6,2},{8,12},{10,14},{12,8},{14,10},{16,20},{18,... | collective-permute-start | bytes 1966088 | tf_op jit(solution)/shard_map/ppermute | solution.py:28
  115.4 11.8 %collective-permute-start.28 = (bf16[640,384]{1,0:T(8,128)(2,1)S(1)}, bf16[640,384]{1,0:T(8,128)(2,1)S(1)}, u32[]{:S(2)}, u32[]{:S(2)}) collective-permute-start(bf16[640,384]{1,0:T(8,128)(2,1)S(1)} %get-tuple-element.122), channel_id=1, source_target_pairs={{0,2},{2,0},{4,6},{6,4},{8,10},{10,8},{12,14},{14,12},{16,18},{18,... | collective-permute-start | bytes 1474568 | tf_op jit(solution)/shard_map/ppermute | solution.py:28
  123.9 20.6 %collective-permute-start.20 = (bf16[640,512]{1,0:T(8,128)(2,1)S(1)}, bf16[640,512]{1,0:T(8,128)(2,1)S(1)}, u32[]{:S(2)}, u32[]{:S(2)}) collective-permute-start(bf16[640,512]{1,0:T(8,128)(2,1)S(1)} %get-tuple-element.108), channel_id=1, source_target_pairs={{0,4},{2,6},{4,0},{6,2},{8,12},{10,14},{12,8},{14,10},{16,20},{18,... | collective-permute-start | bytes 1966088 | tf_op jit(solution)/shard_map/ppermute | solution.py:28
  124.8 11.5 %collective-permute-start.21 = (bf16[640,384]{1,0:T(8,128)(2,1)S(1)}, bf16[640,384]{1,0:T(8,128)(2,1)S(1)}, u32[]{:S(2)}, u32[]{:S(2)}) collective-permute-start(bf16[640,384]{1,0:T(8,128)(2,1)S(1)} %get-tuple-element.109), channel_id=1, source_target_pairs={{0,8},{2,10},{4,12},{6,14},{8,0},{10,2},{12,4},{14,6},{16,24},{18,... | collective-permute-start | bytes 1474568 | tf_op jit(solution)/shard_map/ppermute | solution.py:28
  126.8 11.4 %collective-permute-start.22 = (bf16[640,384]{1,0:T(8,128)(2,1)S(1)}, bf16[640,384]{1,0:T(8,128)(2,1)S(1)}, u32[]{:S(2)}, u32[]{:S(2)}) collective-permute-start(bf16[640,384]{1,0:T(8,128)(2,1)S(1)} %get-tuple-element.110), channel_id=1, source_target_pairs={{0,2},{2,0},{4,6},{6,4},{8,10},{10,8},{12,14},{14,12},{16,18},{18,... | collective-permute-start | bytes 1474568 | tf_op jit(solution)/shard_map/ppermute | solution.py:28
  130.7 15.4 %collective-permute-start.30 = (bf16[320,384]{1,0:T(8,128)(2,1)S(1)}, bf16[320,384]{1,0:T(8,128)(2,1)S(1)}, u32[]{:S(2)}, u32[]{:S(2)}) collective-permute-start(bf16[320,384]{1,0:T(8,128)(2,1)S(1)} %get-tuple-element.127), channel_id=1, source_target_pairs={{0,2},{2,0},{4,6},{6,4},{8,10},{10,8},{12,14},{14,12},{16,18},{18,... | collective-permute-start | bytes 737288 | tf_op jit(solution)/shard_map/ppermute | solution.py:28
  131.1 18.7 %collective-permute-start.29 = (bf16[320,512]{1,0:T(8,128)(2,1)S(1)}, bf16[320,512]{1,0:T(8,128)(2,1)S(1)}, u32[]{:S(2)}, u32[]{:S(2)}) collective-permute-start(bf16[320,512]{1,0:T(8,128)(2,1)S(1)} %get-tuple-element.126), channel_id=1, source_target_pairs={{0,8},{2,10},{4,12},{6,14},{8,0},{10,2},{12,4},{14,6},{16,24},{18,... | collective-permute-start | bytes 983048 | tf_op jit(solution)/shard_map/ppermute | solution.py:28
  136.2 13.5 %collective-permute-start.31 = (bf16[320,384]{1,0:T(8,128)(2,1)S(1)}, bf16[320,384]{1,0:T(8,128)(2,1)S(1)}, u32[]{:S(2)}, u32[]{:S(2)}) collective-permute-start(bf16[320,384]{1,0:T(8,128)(2,1)S(1)} %get-tuple-element.128), channel_id=1, source_target_pairs={{0,4},{2,6},{4,0},{6,2},{8,12},{10,14},{12,8},{14,10},{16,20},{18,... | collective-permute-start | bytes 737288 | tf_op jit(solution)/shard_map/ppermute | solution.py:28
  145.1 10.9 %collective-permute-start.23 = (bf16[320,512]{1,0:T(8,128)(2,1)S(1)}, bf16[320,512]{1,0:T(8,128)(2,1)S(1)}, u32[]{:S(2)}, u32[]{:S(2)}) collective-permute-start(bf16[320,512]{1,0:T(8,128)(2,1)S(1)} %get-tuple-element.114), channel_id=1, source_target_pairs={{0,8},{2,10},{4,12},{6,14},{8,0},{10,2},{12,4},{14,6},{16,24},{18,... | collective-permute-start | bytes 983048 | tf_op jit(solution)/shard_map/ppermute | solution.py:28
  154.5 9.3 %collective-permute-start.41 = (bf16[320,512]{1,0:T(8,128)(2,1)S(1)}, bf16[320,512]{1,0:T(8,128)(2,1)S(1)}, u32[]{:S(2)}, u32[]{:S(2)}) collective-permute-start(bf16[320,512]{1,0:T(8,128)(2,1)S(1)} %get-tuple-element.138.refs_3_), channel_id=1, source_target_pairs={{0,8},{2,10},{4,12},{6,14},{8,0},{10,2},{12,4},{14,6},{16,24},{18,... | collective-permute-start | bytes 983048 | tf_op jit(solution)/shard_map/ppermute | solution.py:28
  156.9 10.5 %collective-permute-start.35 = (bf16[320,384]{1,0:T(8,128)(2,1)S(1)}, bf16[320,384]{1,0:T(8,128)(2,1)}, u32[]{:S(2)}, u32[]{:S(2)}) collective-permute-start(bf16[320,384]{1,0:T(8,128)(2,1)S(1)} %get-tuple-element.148.refs_7_), channel_id=1, source_target_pairs={{0,2},{2,0},{4,6},{6,4},{8,10},{10,8},{12,14},{14,12},{16,18},{18,... | collective-permute-start | bytes 737288 | tf_op jit(solution)/shard_map/ppermute | solution.py:28
  159.8 13.0 %collective-permute-start.42 = (bf16[320,512]{1,0:T(8,128)(2,1)S(1)}, bf16[320,512]{1,0:T(8,128)(2,1)S(1)}, u32[]{:S(2)}, u32[]{:S(2)}) collective-permute-start(bf16[320,512]{1,0:T(8,128)(2,1)S(1)} %get-tuple-element.138.refs_3_), channel_id=1, source_target_pairs={{0,4},{2,6},{4,0},{6,2},{8,12},{10,14},{12,8},{14,10},{16,20},{18,... | collective-permute-start | bytes 983048 | tf_op jit(solution)/shard_map/ppermute | solution.py:28
  160.1 12.0 %collective-permute-start.38 = (bf16[320,384]{1,0:T(8,128)(2,1)S(1)}, bf16[320,384]{1,0:T(8,128)(2,1)S(1)}, u32[]{:S(2)}, u32[]{:S(2)}) collective-permute-start(bf16[320,384]{1,0:T(8,128)(2,1)S(1)} %get-tuple-element.152.refs_11_), channel_id=1, source_target_pairs={{0,4},{2,6},{4,0},{6,2},{8,12},{10,14},{12,8},{14,10},{16,20},{18,... | collective-permute-start | bytes 737288 | tf_op jit(solution)/shard_map/ppermute | solution.py:28
  162.2 11.4 %collective-permute-start.46 = (bf16[320,384]{1,0:T(8,128)(2,1)S(1)}, bf16[320,384]{1,0:T(8,128)(2,1)S(1)}, u32[]{:S(2)}, u32[]{:S(2)}) collective-permute-start(bf16[320,384]{1,0:T(8,128)(2,1)S(1)} %collective-permute-done.44.refs_8_), channel_id=1, source_target_pairs={{0,8},{2,10},{4,12},{6,14},{8,0},{10,2},{12,4},{14,6},{16,24},{18,... | collective-permute-start | bytes 737288 | tf_op jit(solution)/shard_map/ppermute | solution.py:28
  163.8 15.3 %collective-permute-start.43 = (bf16[320,512]{1,0:T(8,128)(2,1)S(1)}, bf16[320,512]{1,0:T(8,128)(2,1)S(1)}, u32[]{:S(2)}, u32[]{:S(2)}) collective-permute-start(bf16[320,512]{1,0:T(8,128)(2,1)S(1)} %collective-permute-done.41.refs_4_), channel_id=1, source_target_pairs={{0,4},{2,6},{4,0},{6,2},{8,12},{10,14},{12,8},{14,10},{16,20},{18,... | collective-permute-start | bytes 983048 | tf_op jit(solution)/shard_map/ppermute | solution.py:28
  172.1 19.3 %collective-permute-start.36 = (bf16[320,384]{1,0:T(8,128)(2,1)S(1)}, bf16[320,384]{1,0:T(8,128)(2,1)S(1)}, u32[]{:S(2)}, u32[]{:S(2)}) collective-permute-start(bf16[320,384]{1,0:T(8,128)(2,1)S(1)} %get-tuple-element.148.refs_7_), channel_id=1, source_target_pairs={{0,8},{2,10},{4,12},{6,14},{8,0},{10,2},{12,4},{14,6},{16,24},{18,... | collective-permute-start | bytes 737288 | tf_op jit(solution)/shard_map/ppermute | solution.py:28
  172.8 21.7 %collective-permute-start.32 = (bf16[320,512]{1,0:T(8,128)(2,1)}, bf16[320,512]{1,0:T(8,128)(2,1)}, u32[]{:S(2)}, u32[]{:S(2)}) collective-permute-start(bf16[320,512]{1,0:T(8,128)(2,1)} %get-tuple-element.144.refs_3_), channel_id=1, source_target_pairs={{0,8},{2,10},{4,12},{6,14},{8,0},{10,2},{12,4},{14,6},{16,24},{18,... | collective-permute-start | bytes 983048 | tf_op jit(solution)/shard_map/ppermute | solution.py:28
  173.6 21.0 %collective-permute-start.33 = (bf16[320,512]{1,0:T(8,128)(2,1)}, bf16[320,512]{1,0:T(8,128)(2,1)}, u32[]{:S(2)}, u32[]{:S(2)}) collective-permute-start(bf16[320,512]{1,0:T(8,128)(2,1)} %get-tuple-element.144.refs_3_), channel_id=1, source_target_pairs={{0,4},{2,6},{4,0},{6,2},{8,12},{10,14},{12,8},{14,10},{16,20},{18,... | collective-permute-start | bytes 983048 | tf_op jit(solution)/shard_map/ppermute | solution.py:28
  173.7 19.3 %collective-permute-start.39 = (bf16[320,384]{1,0:T(8,128)(2,1)S(1)}, bf16[320,384]{1,0:T(8,128)(2,1)S(1)}, u32[]{:S(2)}, u32[]{:S(2)}) collective-permute-start(bf16[320,384]{1,0:T(8,128)(2,1)S(1)} %get-tuple-element.152.refs_11_), channel_id=1, source_target_pairs={{0,2},{2,0},{4,6},{6,4},{8,10},{10,8},{12,14},{14,12},{16,18},{18,... | collective-permute-start | bytes 737288 | tf_op jit(solution)/shard_map/ppermute | solution.py:28
  179.1 16.9 %collective-permute-start.37 = (bf16[320,384]{1,0:T(8,128)(2,1)}, bf16[320,384]{1,0:T(8,128)(2,1)}, u32[]{:S(2)}, u32[]{:S(2)}) collective-permute-start(bf16[320,384]{1,0:T(8,128)(2,1)} %collective-permute-done.35.refs_8_), channel_id=1, source_target_pairs={{0,8},{2,10},{4,12},{6,14},{8,0},{10,2},{12,4},{14,6},{16,24},{18,... | collective-permute-start | bytes 737288 | tf_op jit(solution)/shard_map/ppermute | solution.py:28
  192.2 13.1 %collective-permute-start.50 = (bf16[512,512]{1,0:T(8,128)(2,1)S(1)}, bf16[512,512]{1,0:T(8,128)(2,1)S(1)}, u32[]{:S(2)}, u32[]{:S(2)}) collective-permute-start(bf16[512,512]{1,0:T(8,128)(2,1)S(1)} %get-tuple-element.141.refs_9_), channel_id=1, source_target_pairs={{0,2},{2,0},{4,6},{6,4},{8,10},{10,8},{12,14},{14,12},{16,18},{18,... | collective-permute-start | bytes 1572872 | tf_op jit(solution)/shard_map/ppermute | solution.py:28
  193.7 10.7 %collective-permute-start.51 = (bf16[384,512]{1,0:T(8,128)(2,1)}, bf16[384,512]{1,0:T(8,128)(2,1)S(1)}, u32[]{:S(2)}, u32[]{:S(2)}) collective-permute-start(bf16[384,512]{1,0:T(8,128)(2,1)} %get-tuple-element.142.refs_10_), channel_id=1, source_target_pairs={{0,4},{2,6},{4,0},{6,2},{8,12},{10,14},{12,8},{14,10},{16,20},{18,... | collective-permute-start | bytes 1179656 | tf_op jit(solution)/shard_map/ppermute | solution.py:28
  194.5 10.7 %collective-permute-start.52 = (bf16[384,512]{1,0:T(8,128)(2,1)}, bf16[384,512]{1,0:T(8,128)(2,1)}, u32[]{:S(2)}, u32[]{:S(2)}) collective-permute-start(bf16[384,512]{1,0:T(8,128)(2,1)} %get-tuple-element.143.refs_11_), channel_id=1, source_target_pairs={{0,8},{2,10},{4,12},{6,14},{8,0},{10,2},{12,4},{14,6},{16,24},{18,... | collective-permute-start | bytes 1179656 | tf_op jit(solution)/shard_map/ppermute | solution.py:28
  194.5 9.2 %collective-permute-start.40 = (bf16[320,384]{1,0:T(8,128)(2,1)}, bf16[320,384]{1,0:T(8,128)(2,1)S(1)}, u32[]{:S(2)}, u32[]{:S(2)}) collective-permute-start(bf16[320,384]{1,0:T(8,128)(2,1)} %copy-done.31), channel_id=1, source_target_pairs={{0,2},{2,0},{4,6},{6,4},{8,10},{10,8},{12,14},{14,12},{16,18},{18,... | collective-permute-start | bytes 737288 | tf_op jit(solution)/shard_map/ppermute | solution.py:28
  226.4 21.8 %collective-permute-start.58 = (bf16[512,512]{1,0:T(8,128)(2,1)}, bf16[512,512]{1,0:T(8,128)(2,1)}, u32[]{:S(2)}, u32[]{:S(2)}) collective-permute-start(bf16[512,512]{1,0:T(8,128)(2,1)} %get-tuple-element.168.refs_3_), channel_id=1, source_target_pairs={{0,2},{2,0},{4,6},{6,4},{8,10},{10,8},{12,14},{14,12},{16,18},{18,... | collective-permute-start | bytes 1572872 | tf_op jit(solution)/shard_map/ppermute | solution.py:28
  228.0 20.2 %collective-permute-start.59 = (bf16[512,384]{1,0:T(8,128)(2,1)}, bf16[512,384]{1,0:T(8,128)(2,1)}, u32[]{:S(2)}, u32[]{:S(2)}) collective-permute-start(bf16[512,384]{1,0:T(8,128)(2,1)} %get-tuple-element.169.refs_4_), channel_id=1, source_target_pairs={{0,4},{2,6},{4,0},{6,2},{8,12},{10,14},{12,8},{14,10},{16,20},{18,... | collective-permute-start | bytes 1179656 | tf_op jit(solution)/shard_map/ppermute | solution.py:28
  228.9 19.4 %collective-permute-start.60 = (bf16[512,384]{1,0:T(8,128)(2,1)}, bf16[512,384]{1,0:T(8,128)(2,1)}, u32[]{:S(2)}, u32[]{:S(2)}) collective-permute-start(bf16[512,384]{1,0:T(8,128)(2,1)} %get-tuple-element.170.refs_5_), channel_id=1, source_target_pairs={{0,8},{2,10},{4,12},{6,14},{8,0},{10,2},{12,4},{14,6},{16,24},{18,... | collective-permute-start | bytes 1179656 | tf_op jit(solution)/shard_map/ppermute | solution.py:28
  236.5 11.8 %collective-permute-start.57 = (f32[32,512]{1,0:T(8,128)S(1)}, f32[32,512]{1,0:T(8,128)S(1)}, u32[]{:S(2)}, u32[]{:S(2)}) collective-permute-start(f32[32,512]{1,0:T(8,128)S(1)} %add.91.group_sums), channel_id=1, source_target_pairs={{0,1},{1,0},{2,3},{3,2},{4,5},{5,4},{6,7},{7,6},{8,9},{9,8},{10,11... | collective-permute-start | bytes 196616 | tf_op jit(solution)/shard_map/ppermute | solution.py:28
  (70 other events, 617.3 us)

commit v2 on v1

--- a/solution.py
+++ b/solution.py
@@ -63,12 +63,14 @@
     )
 
 
-def call(kernel, mib, out_shape, *operands):
+def call(kernel, mib, out_shape, *operands, scratch=(), whole=False):
+    space = pl.ANY if whole else pltpu.VMEM
     return pl.pallas_call(
         kernel,
         out_shape=out_shape,
-        in_specs=[pl.BlockSpec(memory_space=pltpu.VMEM)] * len(operands),
+        in_specs=[pl.BlockSpec(memory_space=space)] * len(operands),
         out_specs=jax.tree.map(lambda _: pl.BlockSpec(memory_space=pltpu.VMEM), out_shape),
+        scratch_shapes=list(scratch),
         compiler_params=pltpu.CompilerParams(vmem_limit_bytes=mib * MIB),
     )(*operands)
 
@@ -86,15 +88,6 @@
         if mask >> k & 1:
             place = place + (1 - 2 * bit(place, k)) * (1 << k)
     return place
-
-
-def weight_part(weight_ref, k, low, half, by_row):
-    side = bit(place_in_group(), k)
-    if by_row:
-        return weight_ref[pl.ds(pl.multiple_of(low + side * half, math.gcd(low, half)), half), :]
-    if half % 128 == 0:
-        return weight_ref[:, pl.ds(pl.multiple_of(low + side * half, 128), half)]
-    return jnp.where(side == 1, weight_ref[:, low + half : low + 2 * half], weight_ref[:, low : low + half])
 
 
 def partial_sum(rows, own_weight, got_weight, by_row):
@@ -103,26 +96,41 @@
     return dot(rows[:, :width], own_weight, 1, contract) + dot(rows[:, width:], got_weight, 1, contract)
 
 
-def sums_kernel(bounds, by_row, *refs):
-    own, own_other, pairs, weight, got_weights = refs[0], refs[1], refs[2:8], refs[8], refs[9:12]
-    rows_out, sent_out, kept_out = refs[12:15], refs[15:18], refs[18:21]
+def cut_kernel(bounds, weight_in, weight_out, *refs):
+    cuts, sems = refs[:12], refs[12]
+    copies = []
+    for k in range(3):
+        low, half = bounds[k][0], (bounds[k][1] - bounds[k][0]) // 2
+        side = bit(place_in_group(), k)
+        for taken in range(2):
+            at = (1 - side) if taken else side
+            part = pl.ds(pl.multiple_of(low + at * half, 128), half)
+            n = 6 * taken + k
+            copies.append(pltpu.make_async_copy(weight_in.at[:, part], cuts[n], sems.at[n]))
+            copies.append(pltpu.make_async_copy(weight_out.at[part, :], cuts[n + 3], sems.at[n + 3]))
+    for copy in copies:
+        copy.start()
+    for copy in copies:
+        copy.wait()
+
+
+def sums_kernel(side, by_row, *refs):
+    own, own_other, pairs, own_weights, got_weights = refs[0], refs[1], refs[2:8], refs[8:11], refs[11:14]
+    rows_out, sums_out = refs[14:17], refs[17:20]
     count, width = own.shape[1], own.shape[2]
     for k in range(3):
         pair, pair_other = pairs[2 * k : 2 * k + 2]
         first, second = 1 << (k + 1) % 3, 1 << (k + 2) % 3
-        for i in range(2):
-            for j in range(2):
-                for l in range(2):
-                    chunk = flipped(place_in_group(), i * first + j * second + l * (1 << k))
-                    at = (j * 2 + l) * 2 * count
-                    rows_out[k][i, at : at + count, :width] = own[chunk]
-                    rows_out[k][i, at : at + count, width:] = pair[chunk]
-                    rows_out[k][i, at + count : at + 2 * count, :width] = own_other[chunk]
-                    rows_out[k][i, at + count : at + 2 * count, width:] = pair_other[chunk]
-        own_weight = weight_part(weight, k, bounds[k][0], (bounds[k][1] - bounds[k][0]) // 2, by_row)
-        got_weight = got_weights[k][...]
-        sent_out[k][...] = partial_sum(rows_out[k][1], own_weight, got_weight, by_row).astype(jnp.bfloat16)
-        kept_out[k][...] = partial_sum(rows_out[k][0], own_weight, got_weight, by_row)
+        for j in range(2):
+            for l in range(2):
+                chunk = flipped(place_in_group(), side * first + j * second + l * (1 << k))
+                at = (j * 2 + l) * 2 * count
+                rows_out[k][at : at + count, :width] = own[chunk]
+                rows_out[k][at : at + count, width:] = pair[chunk]
+                rows_out[k][at + count : at + 2 * count, :width] = own_other[chunk]
+                rows_out[k][at + count : at + 2 * count, width:] = pair_other[chunk]
+        sums = partial_sum(rows_out[k][...], own_weights[k][...], got_weights[k][...], by_row)
+        sums_out[k][...] = sums.astype(sums_out[k].dtype)
 
 
 def add_kernel(*refs):
@@ -149,51 +157,57 @@
         pre_grad_out[k][...] = value.astype(jnp.bfloat16)
 
 
-def gradient_kernel(hidden_first, *refs):
-    all_rows, values, outs = refs[:3], refs[3:15], refs[15:]
-    width = all_rows[0].shape[2] // 2
-    for k in range(3):
-        rows = all_rows[k]
+def gradients(hidden_first, near_rows, far_rows, values, own_out, sent_out, sums_out):
+    width = near_rows[0].shape[1] // 2
+    for k in range(3):
         pieces = values[4 * k : 4 * k + 4]
-        own_out, sent_out, by_width_out, by_hidden_out = outs[4 * k : 4 * k + 4]
         near = jnp.concatenate([pieces[0][...], pieces[1][...]])
         far = jnp.concatenate([pieces[2][...], pieces[3][...]])
         if hidden_first:
-            grad = dot(near, rows[0], 0, 0) + dot(far, rows[1], 0, 0)
-            own_out[...] = grad[:, :width]
-            sent_out[...] = grad[:, width:].astype(sent_out.dtype)
+            grad = dot(near, near_rows[k][...], 0, 0) + dot(far, far_rows[k][...], 0, 0)
+            own_out[k][...] = grad[:, :width]
+            sent_out[k][...] = grad[:, width:].astype(jnp.bfloat16)
         else:
-            grad = dot(rows[0], near, 0, 0) + dot(rows[1], far, 0, 0)
-            own_out[...] = grad[:width]
-            sent_out[...] = grad[width:].astype(sent_out.dtype)
+            grad = dot(near_rows[k][...], near, 0, 0) + dot(far_rows[k][...], far, 0, 0)
+            own_out[k][...] = grad[:width]
+            sent_out[k][...] = grad[width:].astype(jnp.bfloat16)
         square = grad * grad + EPS_ONE
         down = jnp.sum(square, axis=0, keepdims=True)
         across = dot(jnp.ones((8, square.shape[1]), jnp.float32), square, 1, 1)
         down = jnp.broadcast_to(down, (8, square.shape[1]))
-        by_width_out[...] = down if hidden_first else across
-        by_hidden_out[...] = across if hidden_first else down
+        by_width, by_hidden = (down, across) if hidden_first else (across, down)
+        sums_out[k] = by_width
+        sums_out[3 + k] = jnp.zeros(sums_out.shape[1:], jnp.float32)
+        sums_out[3 + k, :, : by_hidden.shape[1]] = by_hidden
+
+
+def grad_out_kernel(*refs):
+    gradients(True, refs[:3], refs[3:6], refs[6:18], refs[18:21], refs[21:24], refs[24])
+
+
+def grad_in_kernel(*refs):
+    other_sums, hidden_prev, stats_out, sums = refs[18], refs[19], refs[26], refs[27]
+    gradients(False, refs[:3], refs[3:6], refs[6:18], refs[20:23], refs[23:26], sums)
+    collect(hidden_prev, (sums, other_sums), stats_out)
 
 
 IN_WIDTH, OUT_WIDTH, IN_HIDDEN, OUT_HIDDEN, TOTALS, STAT_ROWS = 0, 8, 16, 22, 28, 32
 
 
-def collect_kernel(hidden_prev, *refs):
-    stats_out = refs[-1]
+def collect(hidden_prev, all_sums, stats_out):
     place = place_in_group()
     stats_out[...] = jnp.zeros_like(stats_out)
     lanes = stats_out.shape[1]
     for which in range(2):
-        by_width, by_hidden = refs[which * 6 : which * 6 + 3], refs[which * 6 + 3 : which * 6 + 6]
+        sums = all_sums[which]
         width_row, hidden_row = (IN_WIDTH, OUT_WIDTH)[which], (IN_HIDDEN, OUT_HIDDEN)[which]
-        width = by_width[0].shape[1] // 2
-        own = sum(ref[0:1, :width] for ref in by_width)
-        stats_out[pl.ds(width_row + place, 1), :width] = own
+        width = sums.shape[2] // 2
+        stats_out[pl.ds(width_row + place, 1), :] = sum(sums[k, 0:1, :width] for k in range(3))
         total = 0.0
         for k in range(3):
-            stats_out[pl.ds(width_row + flipped(place, 1 << k), 1), :width] = by_width[k][0:1, width:]
-            half = by_hidden[k].shape[1]
-            row = by_hidden[k][0:1, :]
-            stats_out[pl.ds(hidden_row + 2 * k + bit(place, k), 1), :half] = row
+            stats_out[pl.ds(width_row + flipped(place, 1 << k), 1), :] = sums[k, 0:1, width:]
+            row = sums[3 + k, 0:1, :lanes]
+            stats_out[pl.ds(hidden_row + 2 * k + bit(place, k), 1), :] = row
             total = total + jnp.sum(row, axis=1, keepdims=True)
         stats_out[TOTALS + which : TOTALS + which + 1, :] = jnp.broadcast_to(total, (1, lanes))
     previous = jnp.sum(hidden_prev[...], axis=1, keepdims=True)
@@ -296,11 +310,22 @@
     local_in = in_weight[0]
     local_out = out_weight[0]
 
-    def pair_side(values, k, dim):
-        return lax.dynamic_slice_in_dim(values, bounds[k][0] + (1 - bits[k]) * halves[k], halves[k], dim)
-
-    in_got = [swap(pair_side(local_in, k, 1), MASKS[k]) for k in sets]
-    out_got = [swap(pair_side(local_out, k, 0), MASKS[k]) for k in sets]
+    if all(half % 128 == 0 for half in halves):
+        cut_shapes = [shape((block_width, half), bf16) for half in halves]
+        cut_shapes += [shape((half, block_width), bf16) for half in halves]
+        cuts = call(
+            functools.partial(cut_kernel, bounds), 48, cut_shapes * 2, local_in, local_out,
+            scratch=[pltpu.SemaphoreType.DMA((12,))], whole=True,
+        )
+    else:
+        cuts = []
+        for taken in range(2):
+            at = [bounds[k][0] + (1 - bits[k] if taken else bits[k]) * halves[k] for k in sets]
+            cuts += [lax.dynamic_slice_in_dim(local_in, at[k], halves[k], 1) for k in sets]
+            cuts += [lax.dynamic_slice_in_dim(local_out, at[k], halves[k], 0) for k in sets]
+    in_own_weights, out_own_weights = cuts[:3], cuts[3:6]
+    in_got = [swap(cuts[6 + k], MASKS[k]) for k in sets]
+    out_got = [swap(cuts[9 + k], MASKS[k]) for k in sets]
 
     route_ids = expert_ids[:, 0]
     onehot = (route_ids[:, None] == jnp.arange(experts, dtype=jnp.int32)[None, :]).astype(jnp.int32)
@@ -316,8 +341,8 @@
         return routed.reshape(places, part_cap, block_width)
 
     routed = jnp.concatenate([route(tokens), route(cotangent)], axis=2)
-    routed, in_got, out_got = lax.optimization_barrier((routed, in_got, out_got))
     got = lax.all_to_all(routed, "expert", split_axis=0, concat_axis=0, tiled=True)
+    got, in_got, out_got = lax.optimization_barrier((got, in_got, out_got))
     got = got.reshape(places // GROUP, GROUP, part_cap, 2 * block_width).transpose(1, 0, 2, 3)
     got = got.reshape(GROUP, -1, 2 * block_width)
 
@@ -335,17 +360,15 @@
     count = got.shape[1] * 8
     wide = 2 * block_width
 
-    def scatter_sum(own, pairs, weight, got_weights, by_row):
-        outs = call(
-            functools.partial(sums_kernel, bounds, by_row), 40,
-            [shape((2, count, wide), bf16)] * 3 + shapes(count, bf16) + shapes(count, f32),
-            *own, *pairs[0], *pairs[1], *pairs[2], weight, *got_weights,
-        )
-        rows, sent, kept = outs[:3], outs[3:6], outs[6:]
-        received = [swap(sent[k], firsts[k]) for k in sets]
-        outs = call(add_kernel, 16, shapes(count // 2, f32) + shapes(count // 2, bf16), *kept, *received)
-        kept, sent = outs[:3], outs[3:]
-        return rows, kept, [swap(sent[k], seconds[k]) for k in sets]
+    def scatter_sum(own, pairs, own_weights, got_weights, by_row):
+        operands = (*own, *pairs[0], *pairs[1], *pairs[2], *own_weights, *got_weights)
+        row_shapes = [shape((count, wide), bf16)] * 3
+        outs = call(functools.partial(sums_kernel, 1, by_row), 24, row_shapes + shapes(count, bf16), *operands)
+        far_rows, received = outs[:3], [swap(outs[3 + k], firsts[k]) for k in sets]
+        outs = call(functools.partial(sums_kernel, 0, by_row), 24, row_shapes + shapes(count, f32), *operands)
+        near_rows, kept = outs[:3], outs[3:]
+        outs = call(add_kernel, 12, shapes(count // 2, f32) + shapes(count // 2, bf16), *kept, *received)
+        return near_rows + far_rows, outs[:3], [swap(outs[3 + k], seconds[k]) for k in sets]
 
     def gather(owns):
         pieces = []
@@ -354,30 +377,40 @@
             pieces += [owns[k], near, swap(owns[k], firsts[k]), swap(near, firsts[k])]
         return pieces
 
-    token_rows, *pre = scatter_sum(own_tokens, pair_tokens, local_in, in_got, False)
-    cotangent_rows, *back = scatter_sum(own_cotangent, pair_cotangent, local_out, out_got, True)
-    outs = call(hidden_kernel, 16, shapes(count // 2, bf16) + shapes(count // 2, f32), *pre[0], *pre[1])
+    token_rows, *pre = scatter_sum(own_tokens, pair_tokens, in_own_weights, in_got, False)
+    cotangent_rows, *back = scatter_sum(own_cotangent, pair_cotangent, out_own_weights, out_got, True)
+    outs = call(hidden_kernel, 12, shapes(count // 2, bf16) + shapes(count // 2, f32), *pre[0], *pre[1])
     hidden, slope = gather(outs[:3]), outs[3:]
-    outs = call(pre_grad_kernel, 16, shapes(count // 2, bf16), *back[0], *back[1], *slope)
+    outs = call(pre_grad_kernel, 12, shapes(count // 2, bf16), *back[0], *back[1], *slope)
     pre_grad = gather(outs)
 
-    def gradient(rows, values, hidden_first):
-        out_shapes = []
-        for half in halves:
-            part = (half, block_width) if hidden_first else (block_width, half)
-            out_shapes += [shape(part, f32), shape(part, bf16), shape((8, wide), f32), shape((8, half), f32)]
-        outs = call(functools.partial(gradient_kernel, hidden_first), 40, out_shapes, *rows, *values)
-        return outs[0::4], outs[1::4], outs[2::4], outs[3::4]
-
-    out_own, out_sent, *out_sums = gradient(cotangent_rows, hidden, True)
+    hidden, near = lax.optimization_barrier((hidden, pre_grad[1::4]))
+    pre_grad[1::4] = near
+    lanes = max(block_width, *halves)
+    hidden_pick = lax.dynamic_index_in_dim(hidden_states, expert, 1, keepdims=False)
+    sums_shape = (6, 8, wide)
+    outs = call(
+        grad_out_kernel, 24,
+        [shape((half, block_width), f32) for half in halves]
+        + [shape((half, block_width), bf16) for half in halves]
+        + [shape(sums_shape, f32)],
+        *cotangent_rows, *hidden,
+    )
+    out_own, out_sent, out_sums = outs[:3], outs[3:6], outs[6]
     got_out = [swap(out_sent[k], MASKS[k]) for k in sets]
     pre_grad, got_out = lax.optimization_barrier((pre_grad, got_out))
-    in_own, in_sent, *in_sums = gradient(token_rows, pre_grad, False)
+    outs = call(
+        grad_in_kernel, 24,
+        [shape((block_width, half), f32) for half in halves]
+        + [shape((block_width, half), bf16) for half in halves]
+        + [shape((STAT_ROWS, lanes), f32)],
+        *token_rows, *pre_grad, out_sums, hidden_pick[1:2],
+        scratch=[pltpu.VMEM(sums_shape, f32)],
+    )
+    in_own, in_sent, stats = outs[:3], outs[3:6], outs[6]
     got_in = [swap(in_sent[k], MASKS[k]) for k in sets]
 
-    lanes = max(block_width, *halves)
     width_pick = lax.dynamic_index_in_dim(width_states, expert, 1, keepdims=False)
-    hidden_pick = lax.dynamic_index_in_dim(hidden_states, expert, 1, keepdims=False)
 
     def padded(values):
         return jnp.pad(values, ((0, 0), (0, lanes - values.shape[1])), constant_values=1.0)
@@ -394,24 +427,17 @@
         values = values + swap(values, 1) + swap(values, 2) + swap(values, 3)
         return values + swap(values, 4)
 
-    def whole_tiles(values):
-        return values if values.shape[1] > 128 else jnp.pad(values, ((0, 0), (0, lanes - values.shape[1])))
-
-    sums = []
-    for by_width, by_hidden in (in_sums, out_sums):
-        sums += [*by_width, *map(whole_tiles, by_hidden)]
-    stats = call(collect_kernel, 4, shape((STAT_ROWS, lanes), f32), hidden_pick[1:2], *sums)
     group_sums = cube_total(stats)
     whole_sums = ffn_total(group_sums)
     whole_sums, got_in = lax.optimization_barrier((whole_sums, got_in))
     factors, norms = call(
-        norm_kernel, 20,
+        norm_kernel, 12,
         (shape((STAT_ROWS, lanes), f32), shape((8, 128), f32)),
         prev, group_sums, whole_sums, *in_own, *in_sent, *out_own, *out_sent,
     )
     norms = ffn_total(cube_total(norms))
     update_in, update_out = call(
-        functools.partial(final_kernel, bounds), 24,
+        functools.partial(final_kernel, bounds), 18,
         (shape(local_in.shape, bf16), shape(local_out.shape, bf16)),
         prev, factors, whole_sums, norms, *in_own, *out_own, *got_in, *got_out,
     )

time: 275 us -> 265 us (0.964)
  blocking collectives: 35.9 us -> 0 us
  waiting for transfers between devices: 84.3 us -> 109 us
  Pallas kernels: 44.2 us -> 37.1 us
  starting transfers between devices: 71.7 us -> 76 us
  other arithmetic: 0.65 us -> 3.76 us
    all_to_all x1 -> x0, blocking collectives: 35.9 us -> none  [shards(): lax.all_to_all(routed, 'expert', split_axis=0, concat_axis=0, tiled=True)]
    ppermute x66, waiting for transfers between devices: 84.3 us -> 109 us  [swap(): return lax.ppermute(value, axis, pairs)]
    dynamic_slice x4 -> x0, local copies, waits for them, and re-layouts: 7.94 us -> none  [pair_side(): lax.dynamic_slice_in_dim(values, bounds[k][0] + (1 - bits[k]) * halves[k]...]
    unnamed x107 -> x111, local copies, waits for them, and re-layouts: 25 us -> 32.9 us
    all_to_all x0 -> x1, starting transfers between devices: none -> 7.47 us  [shards(): lax.all_to_all(routed, 'expert', split_axis=0, concat_axis=0, tiled=True)]
    pallas_call x11 -> x13, Pallas kernels: 44.2 us -> 37.1 us  [call(): pl.pallas_call(kernel, out_shape=out_shape, in_specs=[pl.BlockSpec(memory...]
    ppermute x66, starting transfers between devices: 71.7 us -> 68.6 us  [swap(): return lax.ppermute(value, axis, pairs)]
  transfers between devices with their start and end apart: 66 -> 67, of which waited for: 28 -> 29; matrix products, arithmetic and copies ran while one was open for 3% -> 0% of each run, Pallas kernels for 10% -> 7%
where the time goes in v2:
time: 265 us; the launch traced here: 263 us
  waiting for transfers between devices  109 us (41%)
  starting transfers between devices  76 us (29%)
  Pallas kernels  37.1 us (14%)
  local copies, waits for them, and re-layouts  35.9 us (14%)
  other arithmetic  3.76 us (1%)
    ppermute x66, waiting for transfers between devices, swap(): return lax.ppermute(value, axis, pairs)  109 us
    ppermute x66, starting transfers between devices, swap(): return lax.ppermute(value, axis, pairs)  68.6 us
    pallas_call x13, Pallas kernels, call(): pl.pallas_call(kernel, out_shape=out_shape, in_specs=[pl.BlockSpec(memory...  37.1 us
    unnamed x111, local copies, waits for them, and re-layouts  32.9 us
    all_to_all x1, starting transfers between devices, shards(): lax.all_to_all(routed, 'expert', split_axis=0, concat_axis=0, tiled=True)  7.47 us
  transfers between devices with their start and end apart: 67, of which 29 were waited for; matrix products, arithmetic and copies ran while one was open for 0% of the time, Pallas kernels for 7%

profile of v2, /device:TPU:1, one launch (start us, length us, event | category | flops | bytes accessed | tf_op | source)
XLA Modules:
  0.0 263.3 jit_solution(3939282285481615606)
XLA Ops:
  6.7 7.5 %all-to-all-start = ((bf16[16,40,1024]{2,1,0:T(8,128)(2,1)}), bf16[16,40,1024]{2,1,0:T(8,128)(2,1)}, u32[]{:S(2)}, u32[]{:S(2)}) async-start(bf16[16,40,1024]{2,1,0:T(8,128)(2,1)} %pad_maximum_fusion), calls=%async_computation | async-start | bytes 2621440 | tf_op jit(solution)/shard_map/all_to_all | solution.py:344
  14.2 2.6 shard_map.86
  22.5 12.6 %collective-permute-done.1.refs_12_ = bf16[512,384]{1,0:T(8,128)(2,1)S(1)} collective-permute-done((bf16[512,384]{1,0:T(8,128)(2,1)S(1)}, bf16[512,384]{1,0:T(8,128)(2,1)S(1)}, u32[]{:S(2)}, u32[]{:S(2)}) %collective-permute-start.1) | collective-permute-done | bytes 393248 | tf_op jit(solution)/shard_map/ppermute | solution.py:28
  35.9 9.5 %collective-permute-done.2.refs_13_ = bf16[512,384]{1,0:T(8,128)(2,1)S(1)} collective-permute-done((bf16[512,384]{1,0:T(8,128)(2,1)S(1)}, bf16[512,384]{1,0:T(8,128)(2,1)S(1)}, u32[]{:S(2)}, u32[]{:S(2)}) %collective-permute-start.2) | collective-permute-done | bytes 393248 | tf_op jit(solution)/shard_map/ppermute | solution.py:28
  47.1 6.7 %collective-permute-done.5.refs_13_ = bf16[384,512]{1,0:T(8,128)(2,1)S(1)} collective-permute-done((bf16[384,512]{1,0:T(8,128)(2,1)S(1)}, bf16[384,512]{1,0:T(8,128)(2,1)S(1)}, u32[]{:S(2)}, u32[]{:S(2)}) %collective-permute-start.5) | collective-permute-done | bytes 393248 | tf_op jit(solution)/shard_map/ppermute | solution.py:28
  54.6 1.4 copy.11
  56.2 1.8 collective-permute-start.9
  59.0 2.2 collective-permute-start.6
  61.6 9.9 %collective-permute-done.9.refs_4_ = bf16[8,80,512]{2,1,0:T(8,128)(2,1)S(1)} collective-permute-done((bf16[8,80,512]{2,1,0:T(8,128)(2,1)S(1)}, bf16[8,80,512]{2,1,0:T(8,128)(2,1)S(1)}, u32[]{:S(2)}, u32[]{:S(2)}) %collective-permute-start.9) | collective-permute-done | bytes 655392 | tf_op jit(solution)/shard_map/ppermute | solution.py:28
  72.7 4.8 %collective-permute-start.10 = (bf16[8,80,512]{2,1,0:T(8,128)(2,1)S(1)}, bf16[8,80,512]{2,1,0:T(8,128)(2,1)S(1)}, u32[]{:S(2)}, u32[]{:S(2)}) collective-permute-start(bf16[8,80,512]{2,1,0:T(8,128)(2,1)S(1)} %collective-permute-done.9.refs_4_), channel_id=1, source_target_pairs={{0,1},{1,0},{2,3},{3,2},{4,5},{5,4},{6,7},{7,6},{8,9},{9,8},{10,11... | collective-permute-start | bytes 1966088 | tf_op jit(solution)/shard_map/ppermute | solution.py:28
  77.5 8.9 %collective-permute-done.14.refs_2_ = bf16[8,80,512]{2,1,0:T(8,128)(2,1)S(1)} collective-permute-done((bf16[8,80,512]{2,1,0:T(8,128)(2,1)S(1)}, bf16[8,80,512]{2,1,0:T(8,128)(2,1)S(1)}, u32[]{:S(2)}, u32[]{:S(2)}) %collective-permute-start.14) | collective-permute-done | bytes 655392 | tf_op jit(solution)/shard_map/ppermute | solution.py:28
  86.4 2.8 %collective-permute-start.8 = (bf16[8,80,512]{2,1,0:T(8,128)(2,1)S(1)}, bf16[8,80,512]{2,1,0:T(8,128)(2,1)S(1)}, u32[]{:S(2)}, u32[]{:S(2)}) collective-permute-start(bf16[8,80,512]{2,1,0:T(8,128)(2,1)S(1)} %collective-permute-done.7.refs_2_), channel_id=1, source_target_pairs={{0,1},{1,0},{2,3},{3,2},{4,5},{5,4},{6,7},{7,6},{8,9},{9,8},{10,11... | collective-permute-start | bytes 1966088 | tf_op jit(solution)/shard_map/ppermute | solution.py:28
  90.9 2.2 shard_map.88
  95.3 1.5 collective-permute-start.27
  97.9 2.2 shard_map.90
  100.2 1.5 collective-permute-start.20
  101.7 6.0 %collective-permute-done.27.refs_4_ = bf16[640,384]{1,0:T(8,128)(2,1)S(1)} collective-permute-done((bf16[640,384]{1,0:T(8,128)(2,1)S(1)}, bf16[640,384]{1,0:T(8,128)(2,1)S(1)}, u32[]{:S(2)}, u32[]{:S(2)}) %collective-permute-start.27) | collective-permute-done | bytes 491552 | tf_op jit(solution)/shard_map/ppermute | solution.py:28
  108.8 2.2 shard_map.87
  111.0 1.3 collective-permute-done.26.refs_3_
  113.8 2.2 shard_map.89
  118.4 8.0 %collective-permute-done.20.refs_3_ = bf16[640,512]{1,0:T(8,128)(2,1)S(1)} collective-permute-done((bf16[640,512]{1,0:T(8,128)(2,1)S(1)}, bf16[640,512]{1,0:T(8,128)(2,1)S(1)}, u32[]{:S(2)}, u32[]{:S(2)}) %collective-permute-start.20) | collective-permute-done | bytes 655392 | tf_op jit(solution)/shard_map/ppermute | solution.py:28
  128.0 1.4 collective-permute-start.25
  129.4 3.2 %collective-permute-done.31.refs_5_ = bf16[320,384]{1,0:T(8,128)(2,1)S(1)} collective-permute-done((bf16[320,384]{1,0:T(8,128)(2,1)S(1)}, bf16[320,384]{1,0:T(8,128)(2,1)S(1)}, u32[]{:S(2)}, u32[]{:S(2)}) %collective-permute-start.31) | collective-permute-done | bytes 245792 | tf_op jit(solution)/shard_map/ppermute | solution.py:28
  133.8 4.0 %collective-permute-done.25.refs_5_ = bf16[320,384]{1,0:T(8,128)(2,1)S(1)} collective-permute-done((bf16[320,384]{1,0:T(8,128)(2,1)S(1)}, bf16[320,384]{1,0:T(8,128)(2,1)S(1)}, u32[]{:S(2)}, u32[]{:S(2)}) %collective-permute-start.25) | collective-permute-done | bytes 245792 | tf_op jit(solution)/shard_map/ppermute | solution.py:28
  140.2 1.5 collective-permute-start.38
  146.2 2.7 %collective-permute-done.35.refs_11_ = bf16[320,384]{1,0:T(8,128)(2,1)S(1)} collective-permute-done((bf16[320,384]{1,0:T(8,128)(2,1)S(1)}, bf16[320,384]{1,0:T(8,128)(2,1)S(1)}, u32[]{:S(2)}, u32[]{:S(2)}) %collective-permute-start.35) | collective-permute-done | bytes 245792 | tf_op jit(solution)/shard_map/ppermute | solution.py:28
  150.2 2.2 collective-permute-done.36.refs_12_
  155.1 4.3 %collective-permute-done.41.refs_7_ = bf16[320,512]{1,0:T(8,128)(2,1)S(1)} collective-permute-done((bf16[320,512]{1,0:T(8,128)(2,1)}, bf16[320,512]{1,0:T(8,128)(2,1)S(1)}, u32[]{:S(2)}, u32[]{:S(2)}) %collective-permute-start.41) | collective-permute-done | bytes 327712 | tf_op jit(solution)/shard_map/ppermute | solution.py:28
  160.7 4.0 %collective-permute-done.37.refs_13_ = bf16[320,384]{1,0:T(8,128)(2,1)S(1)} collective-permute-done((bf16[320,384]{1,0:T(8,128)(2,1)S(1)}, bf16[320,384]{1,0:T(8,128)(2,1)S(1)}, u32[]{:S(2)}, u32[]{:S(2)}) %collective-permute-start.37) | collective-permute-done | bytes 245792 | tf_op jit(solution)/shard_map/ppermute | solution.py:28
  166.9 5.5 %shard_map.95 = (f32[512,512]{1,0:T(8,128)S(1)}, f32[384,512]{1,0:T(8,128)S(1)}, f32[384,512]{1,0:T(8,128)S(1)}, bf16[512,512]{1,0:T(8,128)(2,1)S(1)}, bf16[384,...) custom-call(bf16[640,1024]{1,0:T(8,128)(2,1)S(1)} %get-tuple-element.179.refs_0_, ...), custom_call_target="tpu_custom_call" | custom-call | tf_op jit(solution)/shard_map/pallas_call | solution.py:68
  178.1 1.4 collective-permute-start.45
  180.3 8.0 %collective-permute-done.49.refs_17_ = bf16[320,384]{1,0:T(8,128)(2,1)S(1)} collective-permute-done((bf16[320,384]{1,0:T(8,128)(2,1)}, bf16[320,384]{1,0:T(8,128)(2,1)S(1)}, u32[]{:S(2)}, u32[]{:S(2)}) %collective-permute-start.49) | collective-permute-done | bytes 245792 | tf_op jit(solution)/shard_map/ppermute | solution.py:28
  189.9 1.3 copy-done.24
  191.2 1.3 copy-done.26
  192.6 1.3 copy-done.28
  193.9 1.3 copy-done.30
  195.2 1.3 copy-done.32
  196.5 1.3 copy-done.34
  202.6 8.1 %shard_map.96 = (f32[512,512]{1,0:T(8,128)S(1)}, f32[512,384]{1,0:T(8,128)S(1)}, f32[512,384]{1,0:T(8,128)S(1)}, bf16[512,512]{1,0:T(8,128)(2,1)}, bf16[512,384]...) custom-call(bf16[640,1024]{1,0:T(8,128)(2,1)S(1)} %copy-done.30, bf16[640,1024]{1,0:T(8,128)(2,1)S(1)} %copy-done.32, ...), custom_call_target="tpu_custom_call" | custom-call | tf_op jit(solution)/shard_map/pallas_call | solution.py:68
  212.8 2.2 collective-permute-start.55
  217.5 5.7 %collective-permute-done.56 = f32[32,512]{1,0:T(8,128)S(1)} collective-permute-done((f32[32,512]{1,0:T(8,128)S(1)}, f32[32,512]{1,0:T(8,128)S(1)}, u32[]{:S(2)}, u32[]{:S(2)}) %collective-permute-start.56) | collective-permute-done | bytes 65568 | tf_op jit(solution)/shard_map/ppermute | solution.py:28
  223.2 12.5 %collective-permute-start.57 = (f32[32,512]{1,0:T(8,128)S(1)}, f32[32,512]{1,0:T(8,128)S(1)}, u32[]{:S(2)}, u32[]{:S(2)}) collective-permute-start(f32[32,512]{1,0:T(8,128)S(1)} %add.62.group_sums), channel_id=1, source_target_pairs={{0,1},{1,0},{2,3},{3,2},{4,5},{5,4},{6,7},{7,6},{8,9},{9,8},{10,11... | collective-permute-start | bytes 196616 | tf_op jit(solution)/shard_map/ppermute | solution.py:28
  241.1 4.0 %shard_map.97 = (f32[32,512]{1,0:T(8,128)S(1)}, f32[8,128]{1,0:T(8,128)S(1)}) custom-call(f32[32,512]{1,0:T(8,128)S(1)} %concatenate.6.prev, f32[32,512]{1,0:T(8,128)S(1)} %add.62.group_sums, f32[32,512]{1,0:T(8,128)S(1)} %add.63.whole_sums, f32[512,512]{1,0:T(8,128)S(1)} %get-tuple-element.218.refs_0_, f32[512,384]{1,0:T(8,128)S(1)} %copy-done.8, ...), custom_call_target="tpu_custom_call" | custom-call | tf_op jit(solution)/shard_map/pallas_call | solution.py:68
  245.5 1.4 collective-permute-start.62
  247.9 2.3 collective-permute-done.63
  250.4 2.3 collective-permute-done.64
  252.7 3.2 %collective-permute-start.65 = (f32[8,128]{1,0:T(8,128)S(1)}, f32[8,128]{1,0:T(8,128)S(1)}, u32[]{:S(2)}, u32[]{:S(2)}) collective-permute-start(f32[8,128]{1,0:T(8,128)S(1)} %add.67), channel_id=1, source_target_pairs={{0,1},{1,0},{2,3},{3,2},{4,5},{5,4},{6,7},{7,6},{8,9},{9,8},{10,11... | collective-permute-start | bytes 12296 | tf_op jit(solution)/shard_map/ppermute | solution.py:28
  257.9 5.4 %shard_map.98 = (bf16[512,2560]{1,0:T(8,128)(2,1)}, bf16[2560,512]{1,0:T(8,128)(2,1)}) custom-call(f32[32,512]{1,0:T(8,128)S(1)} %concatenate.6.prev, f32[32,512]{1,0:T(8,128)S(1)} %get-tuple-element.224.factors, f32[32,512]{1,0:T(8,128)S(1)} %add.63.whole_sums, f32[8,128]{1,0:T(8,128)S(1)} %add.68.norms, f32[512,512]{1,0:T(8,128)S(1)} %get-tuple-element.218.refs_0_, ...), custom_call_target="tpu_custom_call" | custom-call | tf_op jit(solution)/shard_map/pallas_call | solution.py:68
  (245 shorter events, 71.1 us)
Async XLA Ops:
  6.7 47.9 %all-to-all-start = ((bf16[16,40,1024]{2,1,0:T(8,128)(2,1)}), bf16[16,40,1024]{2,1,0:T(8,128)(2,1)}, u32[]{:S(2)}, u32[]{:S(2)}) async-start(bf16[16,40,1024]{2,1,0:T(8,128)(2,1)} %pad_maximum_fusion), calls=%async_computation | async-start | bytes 2621440 | tf_op jit(solution)/shard_map/all_to_all | solution.py:344
  18.3 16.9 %collective-permute-start.1 = (bf16[512,384]{1,0:T(8,128)(2,1)S(1)}, bf16[512,384]{1,0:T(8,128)(2,1)S(1)}, u32[]{:S(2)}, u32[]{:S(2)}) collective-permute-start(bf16[512,384]{1,0:T(8,128)(2,1)S(1)} %get-tuple-element.119), channel_id=1, source_target_pairs={{0,4},{2,6},{4,0},{6,2},{8,12},{10,14},{12,8},{14,10},{16,20},{18,... | collective-permute-start | bytes 1179656 | tf_op jit(solution)/shard_map/ppermute | solution.py:28
  19.6 35.0 %collective-permute-start = (bf16[512,512]{1,0:T(8,128)(2,1)S(1)}, bf16[512,512]{1,0:T(8,128)(2,1)S(1)}, u32[]{:S(2)}, u32[]{:S(2)}) collective-permute-start(bf16[512,512]{1,0:T(8,128)(2,1)S(1)} %get-tuple-element.118), channel_id=1, source_target_pairs={{0,2},{2,0},{4,6},{6,4},{8,10},{10,8},{12,14},{14,12},{16,18},{18,... | collective-permute-start | bytes 1572872 | tf_op jit(solution)/shard_map/ppermute | solution.py:28
  20.8 33.8 %collective-permute-start.3 = (bf16[512,512]{1,0:T(8,128)(2,1)S(1)}, bf16[512,512]{1,0:T(8,128)(2,1)S(1)}, u32[]{:S(2)}, u32[]{:S(2)}) collective-permute-start(bf16[512,512]{1,0:T(8,128)(2,1)S(1)} %get-tuple-element.121), channel_id=1, source_target_pairs={{0,2},{2,0},{4,6},{6,4},{8,10},{10,8},{12,14},{14,12},{16,18},{18,... | collective-permute-start | bytes 1572872 | tf_op jit(solution)/shard_map/ppermute | solution.py:28
  21.1 24.3 %collective-permute-start.2 = (bf16[512,384]{1,0:T(8,128)(2,1)S(1)}, bf16[512,384]{1,0:T(8,128)(2,1)S(1)}, u32[]{:S(2)}, u32[]{:S(2)}) collective-permute-start(bf16[512,384]{1,0:T(8,128)(2,1)S(1)} %get-tuple-element.120), channel_id=1, source_target_pairs={{0,8},{2,10},{4,12},{6,14},{8,0},{10,2},{12,4},{14,6},{16,24},{18,... | collective-permute-start | bytes 1179656 | tf_op jit(solution)/shard_map/ppermute | solution.py:28
  22.2 24.8 %collective-permute-start.4 = (bf16[384,512]{1,0:T(8,128)(2,1)S(1)}, bf16[384,512]{1,0:T(8,128)(2,1)S(1)}, u32[]{:S(2)}, u32[]{:S(2)}) collective-permute-start(bf16[384,512]{1,0:T(8,128)(2,1)S(1)} %get-tuple-element.122), channel_id=1, source_target_pairs={{0,4},{2,6},{4,0},{6,2},{8,12},{10,14},{12,8},{14,10},{16,20},{18,... | collective-permute-start | bytes 1179656 | tf_op jit(solution)/shard_map/ppermute | solution.py:28
  35.9 17.9 %collective-permute-start.5 = (bf16[384,512]{1,0:T(8,128)(2,1)S(1)}, bf16[384,512]{1,0:T(8,128)(2,1)S(1)}, u32[]{:S(2)}, u32[]{:S(2)}) collective-permute-start(bf16[384,512]{1,0:T(8,128)(2,1)S(1)} %get-tuple-element.123), channel_id=1, source_target_pairs={{0,8},{2,10},{4,12},{6,14},{8,0},{10,2},{12,4},{14,6},{16,24},{18,... | collective-permute-start | bytes 1179656 | tf_op jit(solution)/shard_map/ppermute | solution.py:28
  56.2 15.3 %collective-permute-start.9 = (bf16[8,80,512]{2,1,0:T(8,128)(2,1)S(1)}, bf16[8,80,512]{2,1,0:T(8,128)(2,1)S(1)}, u32[]{:S(2)}, u32[]{:S(2)}) collective-permute-start(bf16[8,80,512]{2,1,0:T(8,128)(2,1)S(1)} %get-tuple-element.241.refs_0_), channel_id=1, source_target_pairs={{0,4},{2,6},{4,0},{6,2},{8,12},{10,14},{12,8},{14,10},{16,20},{18,... | collective-permute-start | bytes 1966088 | tf_op jit(solution)/shard_map/ppermute | solution.py:28
  58.0 14.7 %collective-permute-start.11 = (bf16[8,80,512]{2,1,0:T(8,128)(2,1)S(1)}, bf16[8,80,512]{2,1,0:T(8,128)(2,1)S(1)}, u32[]{:S(2)}, u32[]{:S(2)}) collective-permute-start(bf16[8,80,512]{2,1,0:T(8,128)(2,1)S(1)} %get-tuple-element.241.refs_0_), channel_id=1, source_target_pairs={{0,8},{2,10},{4,12},{6,14},{8,0},{10,2},{12,4},{14,6},{16,24},{18,... | collective-permute-start | bytes 1966088 | tf_op jit(solution)/shard_map/ppermute | solution.py:28
  58.0 14.7 %collective-permute-start.7 = (bf16[8,80,512]{2,1,0:T(8,128)(2,1)S(1)}, bf16[8,80,512]{2,1,0:T(8,128)(2,1)S(1)}, u32[]{:S(2)}, u32[]{:S(2)}) collective-permute-start(bf16[8,80,512]{2,1,0:T(8,128)(2,1)S(1)} %get-tuple-element.241.refs_0_), channel_id=1, source_target_pairs={{0,2},{2,0},{4,6},{6,4},{8,10},{10,8},{12,14},{14,12},{16,18},{18,... | collective-permute-start | bytes 1966088 | tf_op jit(solution)/shard_map/ppermute | solution.py:28
  59.0 18.4 %collective-permute-start.6 = (bf16[8,80,512]{2,1,0:T(8,128)(2,1)S(1)}, bf16[8,80,512]{2,1,0:T(8,128)(2,1)S(1)}, u32[]{:S(2)}, u32[]{:S(2)}) collective-permute-start(bf16[8,80,512]{2,1,0:T(8,128)(2,1)S(1)} %get-tuple-element.241.refs_0_), channel_id=1, source_target_pairs={{0,1},{1,0},{2,3},{3,2},{4,5},{5,4},{6,7},{7,6},{8,9},{9,8},{10,11... | collective-permute-start | bytes 1966088 | tf_op jit(solution)/shard_map/ppermute | solution.py:28
  61.3 25.1 %collective-permute-start.14 = (bf16[8,80,512]{2,1,0:T(8,128)(2,1)S(1)}, bf16[8,80,512]{2,1,0:T(8,128)(2,1)S(1)}, u32[]{:S(2)}, u32[]{:S(2)}) collective-permute-start(bf16[8,80,512]{2,1,0:T(8,128)(2,1)S(1)} %get-tuple-element.240.refs_0_), channel_id=1, source_target_pairs={{0,2},{2,0},{4,6},{6,4},{8,10},{10,8},{12,14},{14,12},{16,18},{18,... | collective-permute-start | bytes 1966088 | tf_op jit(solution)/shard_map/ppermute | solution.py:28
  71.5 17.7 %collective-permute-start.16 = (bf16[8,80,512]{2,1,0:T(8,128)(2,1)S(1)}, bf16[8,80,512]{2,1,0:T(8,128)(2,1)S(1)}, u32[]{:S(2)}, u32[]{:S(2)}) collective-permute-start(bf16[8,80,512]{2,1,0:T(8,128)(2,1)S(1)} %get-tuple-element.240.refs_0_), channel_id=1, source_target_pairs={{0,4},{2,6},{4,0},{6,2},{8,12},{10,14},{12,8},{14,10},{16,20},{18,... | collective-permute-start | bytes 1966088 | tf_op jit(solution)/shard_map/ppermute | solution.py:28
  72.7 16.5 %collective-permute-start.18 = (bf16[8,80,512]{2,1,0:T(8,128)(2,1)S(1)}, bf16[8,80,512]{2,1,0:T(8,128)(2,1)S(1)}, u32[]{:S(2)}, u32[]{:S(2)}) collective-permute-start(bf16[8,80,512]{2,1,0:T(8,128)(2,1)S(1)} %get-tuple-element.240.refs_0_), channel_id=1, source_target_pairs={{0,8},{2,10},{4,12},{6,14},{8,0},{10,2},{12,4},{14,6},{16,24},{18,... | collective-permute-start | bytes 1966088 | tf_op jit(solution)/shard_map/ppermute | solution.py:28
  72.7 17.1 %collective-permute-start.10 = (bf16[8,80,512]{2,1,0:T(8,128)(2,1)S(1)}, bf16[8,80,512]{2,1,0:T(8,128)(2,1)S(1)}, u32[]{:S(2)}, u32[]{:S(2)}) collective-permute-start(bf16[8,80,512]{2,1,0:T(8,128)(2,1)S(1)} %collective-permute-done.9.refs_4_), channel_id=1, source_target_pairs={{0,1},{1,0},{2,3},{3,2},{4,5},{5,4},{6,7},{7,6},{8,9},{9,8},{10,11... | collective-permute-start | bytes 1966088 | tf_op jit(solution)/shard_map/ppermute | solution.py:28
  77.5 12.4 %collective-permute-start.12 = (bf16[8,80,512]{2,1,0:T(8,128)(2,1)S(1)}, bf16[8,80,512]{2,1,0:T(8,128)(2,1)S(1)}, u32[]{:S(2)}, u32[]{:S(2)}) collective-permute-start(bf16[8,80,512]{2,1,0:T(8,128)(2,1)S(1)} %collective-permute-done.11.refs_6_), channel_id=1, source_target_pairs={{0,1},{1,0},{2,3},{3,2},{4,5},{5,4},{6,7},{7,6},{8,9},{9,8},{10,11... | collective-permute-start | bytes 1966088 | tf_op jit(solution)/shard_map/ppermute | solution.py:28
  95.3 12.4 %collective-permute-start.27 = (bf16[640,384]{1,0:T(8,128)(2,1)S(1)}, bf16[640,384]{1,0:T(8,128)(2,1)S(1)}, u32[]{:S(2)}, u32[]{:S(2)}) collective-permute-start(bf16[640,384]{1,0:T(8,128)(2,1)S(1)} %get-tuple-element.159), channel_id=1, source_target_pairs={{0,8},{2,10},{4,12},{6,14},{8,0},{10,2},{12,4},{14,6},{16,24},{18,... | collective-permute-start | bytes 1474568 | tf_op jit(solution)/shard_map/ppermute | solution.py:28
  96.7 15.6 %collective-permute-start.26 = (bf16[640,512]{1,0:T(8,128)(2,1)S(1)}, bf16[640,512]{1,0:T(8,128)(2,1)S(1)}, u32[]{:S(2)}, u32[]{:S(2)}) collective-permute-start(bf16[640,512]{1,0:T(8,128)(2,1)S(1)} %get-tuple-element.158), channel_id=1, source_target_pairs={{0,4},{2,6},{4,0},{6,2},{8,12},{10,14},{12,8},{14,10},{16,20},{18,... | collective-permute-start | bytes 1966088 | tf_op jit(solution)/shard_map/ppermute | solution.py:28
  96.8 14.2 %collective-permute-start.28 = (bf16[640,384]{1,0:T(8,128)(2,1)S(1)}, bf16[640,384]{1,0:T(8,128)(2,1)S(1)}, u32[]{:S(2)}, u32[]{:S(2)}) collective-permute-start(bf16[640,384]{1,0:T(8,128)(2,1)S(1)} %get-tuple-element.160), channel_id=1, source_target_pairs={{0,2},{2,0},{4,6},{6,4},{8,10},{10,8},{12,14},{14,12},{16,18},{18,... | collective-permute-start | bytes 1474568 | tf_op jit(solution)/shard_map/ppermute | solution.py:28
  100.2 26.2 %collective-permute-start.20 = (bf16[640,512]{1,0:T(8,128)(2,1)S(1)}, bf16[640,512]{1,0:T(8,128)(2,1)S(1)}, u32[]{:S(2)}, u32[]{:S(2)}) collective-permute-start(bf16[640,512]{1,0:T(8,128)(2,1)S(1)} %get-tuple-element.146), channel_id=1, source_target_pairs={{0,4},{2,6},{4,0},{6,2},{8,12},{10,14},{12,8},{14,10},{16,20},{18,... | collective-permute-start | bytes 1966088 | tf_op jit(solution)/shard_map/ppermute | solution.py:28
  101.6 16.6 %collective-permute-start.21 = (bf16[640,384]{1,0:T(8,128)(2,1)S(1)}, bf16[640,384]{1,0:T(8,128)(2,1)S(1)}, u32[]{:S(2)}, u32[]{:S(2)}) collective-permute-start(bf16[640,384]{1,0:T(8,128)(2,1)S(1)} %get-tuple-element.147), channel_id=1, source_target_pairs={{0,8},{2,10},{4,12},{6,14},{8,0},{10,2},{12,4},{14,6},{16,24},{18,... | collective-permute-start | bytes 1474568 | tf_op jit(solution)/shard_map/ppermute | solution.py:28
  107.7 10.7 %collective-permute-start.22 = (bf16[640,384]{1,0:T(8,128)(2,1)S(1)}, bf16[640,384]{1,0:T(8,128)(2,1)S(1)}, u32[]{:S(2)}, u32[]{:S(2)}) collective-permute-start(bf16[640,384]{1,0:T(8,128)(2,1)S(1)} %get-tuple-element.148), channel_id=1, source_target_pairs={{0,2},{2,0},{4,6},{6,4},{8,10},{10,8},{12,14},{14,12},{16,18},{18,... | collective-permute-start | bytes 1474568 | tf_op jit(solution)/shard_map/ppermute | solution.py:28
  112.9 15.1 %collective-permute-start.30 = (bf16[320,384]{1,0:T(8,128)(2,1)S(1)}, bf16[320,384]{1,0:T(8,128)(2,1)S(1)}, u32[]{:S(2)}, u32[]{:S(2)}) collective-permute-start(bf16[320,384]{1,0:T(8,128)(2,1)S(1)} %get-tuple-element.165), channel_id=1, source_target_pairs={{0,2},{2,0},{4,6},{6,4},{8,10},{10,8},{12,14},{14,12},{16,18},{18,... | collective-permute-start | bytes 737288 | tf_op jit(solution)/shard_map/ppermute | solution.py:28
  116.0 16.6 %collective-permute-start.29 = (bf16[320,512]{1,0:T(8,128)(2,1)S(1)}, bf16[320,512]{1,0:T(8,128)(2,1)S(1)}, u32[]{:S(2)}, u32[]{:S(2)}) collective-permute-start(bf16[320,512]{1,0:T(8,128)(2,1)S(1)} %get-tuple-element.164), channel_id=1, source_target_pairs={{0,8},{2,10},{4,12},{6,14},{8,0},{10,2},{12,4},{14,6},{16,24},{18,... | collective-permute-start | bytes 983048 | tf_op jit(solution)/shard_map/ppermute | solution.py:28
  126.7 11.2 %collective-permute-start.23 = (bf16[320,512]{1,0:T(8,128)(2,1)S(1)}, bf16[320,512]{1,0:T(8,128)(2,1)S(1)}, u32[]{:S(2)}, u32[]{:S(2)}) collective-permute-start(bf16[320,512]{1,0:T(8,128)(2,1)S(1)} %get-tuple-element.152), channel_id=1, source_target_pairs={{0,8},{2,10},{4,12},{6,14},{8,0},{10,2},{12,4},{14,6},{16,24},{18,... | collective-permute-start | bytes 983048 | tf_op jit(solution)/shard_map/ppermute | solution.py:28
  128.0 9.8 %collective-permute-start.25 = (bf16[320,384]{1,0:T(8,128)(2,1)S(1)}, bf16[320,384]{1,0:T(8,128)(2,1)S(1)}, u32[]{:S(2)}, u32[]{:S(2)}) collective-permute-start(bf16[320,384]{1,0:T(8,128)(2,1)S(1)} %get-tuple-element.154), channel_id=1, source_target_pairs={{0,4},{2,6},{4,0},{6,2},{8,12},{10,14},{12,8},{14,10},{16,20},{18,... | collective-permute-start | bytes 737288 | tf_op jit(solution)/shard_map/ppermute | solution.py:28
  139.9 9.0 %collective-permute-start.35 = (bf16[320,384]{1,0:T(8,128)(2,1)S(1)}, bf16[320,384]{1,0:T(8,128)(2,1)S(1)}, u32[]{:S(2)}, u32[]{:S(2)}) collective-permute-start(bf16[320,384]{1,0:T(8,128)(2,1)S(1)} %get-tuple-element.189.refs_10_), channel_id=1, source_target_pairs={{0,2},{2,0},{4,6},{6,4},{8,10},{10,8},{12,14},{14,12},{16,18},{18,... | collective-permute-start | bytes 737288 | tf_op jit(solution)/shard_map/ppermute | solution.py:28
  140.2 9.9 %collective-permute-start.38 = (bf16[320,384]{1,0:T(8,128)(2,1)S(1)}, bf16[320,384]{1,0:T(8,128)(2,1)S(1)}, u32[]{:S(2)}, u32[]{:S(2)}) collective-permute-start(bf16[320,384]{1,0:T(8,128)(2,1)S(1)} %get-tuple-element.193.refs_14_), channel_id=1, source_target_pairs={{0,4},{2,6},{4,0},{6,2},{8,12},{10,14},{12,8},{14,10},{16,20},{18,... | collective-permute-start | bytes 737288 | tf_op jit(solution)/shard_map/ppermute | solution.py:28
  141.7 11.9 %collective-permute-start.32 = (bf16[320,512]{1,0:T(8,128)(2,1)S(1)}, bf16[320,512]{1,0:T(8,128)(2,1)S(1)}, u32[]{:S(2)}, u32[]{:S(2)}) collective-permute-start(bf16[320,512]{1,0:T(8,128)(2,1)S(1)} %get-tuple-element.185.refs_6_), channel_id=1, source_target_pairs={{0,8},{2,10},{4,12},{6,14},{8,0},{10,2},{12,4},{14,6},{16,24},{18,... | collective-permute-start | bytes 983048 | tf_op jit(solution)/shard_map/ppermute | solution.py:28
  145.3 8.8 %collective-permute-start.39 = (bf16[320,384]{1,0:T(8,128)(2,1)S(1)}, bf16[320,384]{1,0:T(8,128)(2,1)S(1)}, u32[]{:S(2)}, u32[]{:S(2)}) collective-permute-start(bf16[320,384]{1,0:T(8,128)(2,1)S(1)} %get-tuple-element.193.refs_14_), channel_id=1, source_target_pairs={{0,2},{2,0},{4,6},{6,4},{8,10},{10,8},{12,14},{14,12},{16,18},{18,... | collective-permute-start | bytes 737288 | tf_op jit(solution)/shard_map/ppermute | solution.py:28
  148.9 10.5 %collective-permute-start.41 = (bf16[320,512]{1,0:T(8,128)(2,1)}, bf16[320,512]{1,0:T(8,128)(2,1)S(1)}, u32[]{:S(2)}, u32[]{:S(2)}) collective-permute-start(bf16[320,512]{1,0:T(8,128)(2,1)} %get-tuple-element.200.refs_6_), channel_id=1, source_target_pairs={{0,8},{2,10},{4,12},{6,14},{8,0},{10,2},{12,4},{14,6},{16,24},{18,... | collective-permute-start | bytes 983048 | tf_op jit(solution)/shard_map/ppermute | solution.py:28
  150.1 9.3 %collective-permute-start.33 = (bf16[320,512]{1,0:T(8,128)(2,1)S(1)}, bf16[320,512]{1,0:T(8,128)(2,1)S(1)}, u32[]{:S(2)}, u32[]{:S(2)}) collective-permute-start(bf16[320,512]{1,0:T(8,128)(2,1)S(1)} %get-tuple-element.185.refs_6_), channel_id=1, source_target_pairs={{0,4},{2,6},{4,0},{6,2},{8,12},{10,14},{12,8},{14,10},{16,20},{18,... | collective-permute-start | bytes 983048 | tf_op jit(solution)/shard_map/ppermute | solution.py:28
  152.4 12.3 %collective-permute-start.37 = (bf16[320,384]{1,0:T(8,128)(2,1)S(1)}, bf16[320,384]{1,0:T(8,128)(2,1)S(1)}, u32[]{:S(2)}, u32[]{:S(2)}) collective-permute-start(bf16[320,384]{1,0:T(8,128)(2,1)S(1)} %collective-permute-done.35.refs_11_), channel_id=1, source_target_pairs={{0,8},{2,10},{4,12},{6,14},{8,0},{10,2},{12,4},{14,6},{16,24},{18,... | collective-permute-start | bytes 737288 | tf_op jit(solution)/shard_map/ppermute | solution.py:28
  153.6 13.4 %collective-permute-start.34 = (bf16[320,512]{1,0:T(8,128)(2,1)S(1)}, bf16[320,512]{1,0:T(8,128)(2,1)S(1)}, u32[]{:S(2)}, u32[]{:S(2)}) collective-permute-start(bf16[320,512]{1,0:T(8,128)(2,1)S(1)} %collective-permute-done.32.refs_7_), channel_id=1, source_target_pairs={{0,4},{2,6},{4,0},{6,2},{8,12},{10,14},{12,8},{14,10},{16,20},{18,... | collective-permute-start | bytes 983048 | tf_op jit(solution)/shard_map/ppermute | solution.py:28
  154.1 11.7 %collective-permute-start.40 = (bf16[320,384]{1,0:T(8,128)(2,1)S(1)}, bf16[320,384]{1,0:T(8,128)(2,1)S(1)}, u32[]{:S(2)}, u32[]{:S(2)}) collective-permute-start(bf16[320,384]{1,0:T(8,128)(2,1)S(1)} %collective-permute-done.38.refs_15_), channel_id=1, source_target_pairs={{0,2},{2,0},{4,6},{6,4},{8,10},{10,8},{12,14},{14,12},{16,18},{18,... | collective-permute-start | bytes 737288 | tf_op jit(solution)/shard_map/ppermute | solution.py:28
  159.4 17.6 %collective-permute-start.44 = (bf16[320,512]{1,0:T(8,128)(2,1)}, bf16[320,512]{1,0:T(8,128)(2,1)}, u32[]{:S(2)}, u32[]{:S(2)}) collective-permute-start(bf16[320,512]{1,0:T(8,128)(2,1)} %get-tuple-element.200.refs_6_), channel_id=1, source_target_pairs={{0,4},{2,6},{4,0},{6,2},{8,12},{10,14},{12,8},{14,10},{16,20},{18,... | collective-permute-start | bytes 983048 | tf_op jit(solution)/shard_map/ppermute | solution.py:28
  159.4 15.9 %collective-permute-start.46 = (bf16[320,384]{1,0:T(8,128)(2,1)S(1)}, bf16[320,384]{1,0:T(8,128)(2,1)S(1)}, u32[]{:S(2)}, u32[]{:S(2)}) collective-permute-start(bf16[320,384]{1,0:T(8,128)(2,1)S(1)} %get-tuple-element.204.refs_10_), channel_id=1, source_target_pairs={{0,8},{2,10},{4,12},{6,14},{8,0},{10,2},{12,4},{14,6},{16,24},{18,... | collective-permute-start | bytes 737288 | tf_op jit(solution)/shard_map/ppermute | solution.py:28
  164.7 11.4 %collective-permute-start.48 = (bf16[320,384]{1,0:T(8,128)(2,1)S(1)}, bf16[320,384]{1,0:T(8,128)(2,1)S(1)}, u32[]{:S(2)}, u32[]{:S(2)}) collective-permute-start(bf16[320,384]{1,0:T(8,128)(2,1)S(1)} %get-tuple-element.208.refs_14_), channel_id=1, source_target_pairs={{0,2},{2,0},{4,6},{6,4},{8,10},{10,8},{12,14},{14,12},{16,18},{18,... | collective-permute-start | bytes 737288 | tf_op jit(solution)/shard_map/ppermute | solution.py:28
  165.7 12.4 %collective-permute-start.47 = (bf16[320,384]{1,0:T(8,128)(2,1)}, bf16[320,384]{1,0:T(8,128)(2,1)}, u32[]{:S(2)}, u32[]{:S(2)}) collective-permute-start(bf16[320,384]{1,0:T(8,128)(2,1)} %collective-permute-done.42.refs_11_), channel_id=1, source_target_pairs={{0,8},{2,10},{4,12},{6,14},{8,0},{10,2},{12,4},{14,6},{16,24},{18,... | collective-permute-start | bytes 737288 | tf_op jit(solution)/shard_map/ppermute | solution.py:28
  174.1 15.0 %collective-permute-start.50 = (bf16[512,512]{1,0:T(8,128)(2,1)S(1)}, bf16[512,512]{1,0:T(8,128)(2,1)S(1)}, u32[]{:S(2)}, u32[]{:S(2)}) collective-permute-start(bf16[512,512]{1,0:T(8,128)(2,1)S(1)} %get-tuple-element.197.refs_9_), channel_id=1, source_target_pairs={{0,2},{2,0},{4,6},{6,4},{8,10},{10,8},{12,14},{14,12},{16,18},{18,... | collective-permute-start | bytes 1572872 | tf_op jit(solution)/shard_map/ppermute | solution.py:28
  176.0 12.3 %collective-permute-start.51 = (bf16[384,512]{1,0:T(8,128)(2,1)}, bf16[384,512]{1,0:T(8,128)(2,1)S(1)}, u32[]{:S(2)}, u32[]{:S(2)}) collective-permute-start(bf16[384,512]{1,0:T(8,128)(2,1)} %get-tuple-element.198.refs_10_), channel_id=1, source_target_pairs={{0,4},{2,6},{4,0},{6,2},{8,12},{10,14},{12,8},{14,10},{16,20},{18,... | collective-permute-start | bytes 1179656 | tf_op jit(solution)/shard_map/ppermute | solution.py:28
  176.8 12.3 %collective-permute-start.52 = (bf16[384,512]{1,0:T(8,128)(2,1)}, bf16[384,512]{1,0:T(8,128)(2,1)}, u32[]{:S(2)}, u32[]{:S(2)}) collective-permute-start(bf16[384,512]{1,0:T(8,128)(2,1)} %get-tuple-element.199.refs_11_), channel_id=1, source_target_pairs={{0,8},{2,10},{4,12},{6,14},{8,0},{10,2},{12,4},{14,6},{16,24},{18,... | collective-permute-start | bytes 1179656 | tf_op jit(solution)/shard_map/ppermute | solution.py:28
  177.0 11.3 %collective-permute-start.49 = (bf16[320,384]{1,0:T(8,128)(2,1)}, bf16[320,384]{1,0:T(8,128)(2,1)S(1)}, u32[]{:S(2)}, u32[]{:S(2)}) collective-permute-start(bf16[320,384]{1,0:T(8,128)(2,1)} %collective-permute-done.43.refs_15_), channel_id=1, source_target_pairs={{0,2},{2,0},{4,6},{6,4},{8,10},{10,8},{12,14},{14,12},{16,18},{18,... | collective-permute-start | bytes 737288 | tf_op jit(solution)/shard_map/ppermute | solution.py:28
  178.1 10.2 %collective-permute-start.45 = (bf16[320,512]{1,0:T(8,128)(2,1)}, bf16[320,512]{1,0:T(8,128)(2,1)S(1)}, u32[]{:S(2)}, u32[]{:S(2)}) collective-permute-start(bf16[320,512]{1,0:T(8,128)(2,1)} %copy-done.41), channel_id=1, source_target_pairs={{0,4},{2,6},{4,0},{6,2},{8,12},{10,14},{12,8},{14,10},{16,20},{18,... | collective-permute-start | bytes 983048 | tf_op jit(solution)/shard_map/ppermute | solution.py:28
  215.0 21.6 %collective-permute-start.58 = (bf16[512,512]{1,0:T(8,128)(2,1)}, bf16[512,512]{1,0:T(8,128)(2,1)}, u32[]{:S(2)}, u32[]{:S(2)}) collective-permute-start(bf16[512,512]{1,0:T(8,128)(2,1)} %get-tuple-element.214.refs_3_), channel_id=1, source_target_pairs={{0,2},{2,0},{4,6},{6,4},{8,10},{10,8},{12,14},{14,12},{16,18},{18,... | collective-permute-start | bytes 1572872 | tf_op jit(solution)/shard_map/ppermute | solution.py:28
  215.5 21.1 %collective-permute-start.59 = (bf16[512,384]{1,0:T(8,128)(2,1)}, bf16[512,384]{1,0:T(8,128)(2,1)}, u32[]{:S(2)}, u32[]{:S(2)}) collective-permute-start(bf16[512,384]{1,0:T(8,128)(2,1)} %get-tuple-element.215.refs_4_), channel_id=1, source_target_pairs={{0,4},{2,6},{4,0},{6,2},{8,12},{10,14},{12,8},{14,10},{16,20},{18,... | collective-permute-start | bytes 1179656 | tf_op jit(solution)/shard_map/ppermute | solution.py:28
  215.6 21.0 %collective-permute-start.60 = (bf16[512,384]{1,0:T(8,128)(2,1)}, bf16[512,384]{1,0:T(8,128)(2,1)}, u32[]{:S(2)}, u32[]{:S(2)}) collective-permute-start(bf16[512,384]{1,0:T(8,128)(2,1)} %get-tuple-element.216.refs_5_), channel_id=1, source_target_pairs={{0,8},{2,10},{4,12},{6,14},{8,0},{10,2},{12,4},{14,6},{16,24},{18,... | collective-permute-start | bytes 1179656 | tf_op jit(solution)/shard_map/ppermute | solution.py:28
  223.2 13.4 %collective-permute-start.57 = (f32[32,512]{1,0:T(8,128)S(1)}, f32[32,512]{1,0:T(8,128)S(1)}, u32[]{:S(2)}, u32[]{:S(2)}) collective-permute-start(f32[32,512]{1,0:T(8,128)S(1)} %add.62.group_sums), channel_id=1, source_target_pairs={{0,1},{1,0},{2,3},{3,2},{4,5},{5,4},{6,7},{7,6},{8,9},{9,8},{10,11... | collective-permute-start | bytes 196616 | tf_op jit(solution)/shard_map/ppermute | solution.py:28
  (73 other events, 529.9 us)

commit v3 on v2

--- a/solution.py
+++ b/solution.py
@@ -21,6 +21,7 @@
 MASKS = (1, 2, 4)
 
 MIB = 1024 * 1024
+CUT_MIB = 14
 
 
 def swap(value, mask, axis="expert"):
@@ -97,39 +98,57 @@
 
 
 def cut_kernel(bounds, weight_in, weight_out, *refs):
-    cuts, sems = refs[:12], refs[12]
+    kept_in, kept_out, packed, sems = refs[:3], refs[3:6], refs[6:9], refs[9]
     copies = []
+    width = weight_in.shape[0]
     for k in range(3):
         low, half = bounds[k][0], (bounds[k][1] - bounds[k][0]) // 2
         side = bit(place_in_group(), k)
-        for taken in range(2):
-            at = (1 - side) if taken else side
-            part = pl.ds(pl.multiple_of(low + at * half, 128), half)
-            n = 6 * taken + k
-            copies.append(pltpu.make_async_copy(weight_in.at[:, part], cuts[n], sems.at[n]))
-            copies.append(pltpu.make_async_copy(weight_out.at[part, :], cuts[n + 3], sems.at[n + 3]))
+        kept = pl.ds(pl.multiple_of(low + side * half, 128), half)
+        copies.append((weight_in.at[:, kept], kept_in[k], 3 * k))
+        copies.append((weight_out.at[kept, :], kept_out[k], 3 * k + 1))
+        start = low + (1 - side) * half
+        at = 0
+        for n in range(half // 128):
+            part = pl.ds(pl.multiple_of(start + n * 128, 128), 128)
+            copies.append((weight_in.at[:, part], packed[k].at[at : at + width], 3 * k + 2))
+            at += width
+        for n in range(width // 128):
+            part = pl.ds(pl.multiple_of(start, 128), half)
+            source = weight_out.at[part, n * 128 : n * 128 + 128]
+            copies.append((source, packed[k].at[at : at + half], 3 * k + 2))
+            at += half
+    copies = [pltpu.make_async_copy(source, target, sems.at[n]) for n, (source, target, _) in enumerate(copies)]
     for copy in copies:
         copy.start()
     for copy in copies:
         copy.wait()
 
 
-def sums_kernel(side, by_row, *refs):
-    own, own_other, pairs, own_weights, got_weights = refs[0], refs[1], refs[2:8], refs[8:11], refs[11:14]
-    rows_out, sums_out = refs[14:17], refs[17:20]
+def got_weight(ref, by_row, half, width):
+    at = half // 128 * width if by_row else 0
+    rows = half if by_row else width
+    blocks = (width if by_row else half) // 128
+    return jnp.concatenate([ref[at + n * rows : at + (n + 1) * rows, :] for n in range(blocks)], axis=1)
+
+
+def sums_kernel(side, by_row, is_packed, *refs):
+    own, own_other, pairs, pairs_other = refs[:4]
+    own_weights, got_weights, rows_out, sums_out = refs[4:7], refs[7:10], refs[10:13], refs[13:16]
     count, width = own.shape[1], own.shape[2]
     for k in range(3):
-        pair, pair_other = pairs[2 * k : 2 * k + 2]
         first, second = 1 << (k + 1) % 3, 1 << (k + 2) % 3
         for j in range(2):
             for l in range(2):
                 chunk = flipped(place_in_group(), side * first + j * second + l * (1 << k))
                 at = (j * 2 + l) * 2 * count
                 rows_out[k][at : at + count, :width] = own[chunk]
-                rows_out[k][at : at + count, width:] = pair[chunk]
+                rows_out[k][at : at + count, width:] = pairs[k, chunk]
                 rows_out[k][at + count : at + 2 * count, :width] = own_other[chunk]
-                rows_out[k][at + count : at + 2 * count, width:] = pair_other[chunk]
-        sums = partial_sum(rows_out[k][...], own_weights[k][...], got_weights[k][...], by_row)
+                rows_out[k][at + count : at + 2 * count, width:] = pairs_other[k, chunk]
+        half = sums_out[k].shape[1]
+        got = got_weight(got_weights[k], by_row, half, width) if is_packed else got_weights[k][...]
+        sums = partial_sum(rows_out[k][...], own_weights[k][...], got, by_row)
         sums_out[k][...] = sums.astype(sums_out[k].dtype)
 
 
@@ -157,12 +176,17 @@
         pre_grad_out[k][...] = value.astype(jnp.bfloat16)
 
 
+def join_kernel(*refs):
+    for k in range(3):
+        own, got, joined = refs[k], refs[3 + k], refs[6 + k]
+        joined[: own.shape[0]] = own[...]
+        joined[own.shape[0] :] = got[...]
+
+
 def gradients(hidden_first, near_rows, far_rows, values, own_out, sent_out, sums_out):
     width = near_rows[0].shape[1] // 2
     for k in range(3):
-        pieces = values[4 * k : 4 * k + 4]
-        near = jnp.concatenate([pieces[0][...], pieces[1][...]])
-        far = jnp.concatenate([pieces[2][...], pieces[3][...]])
+        near, far = values[2 * k][...], values[2 * k + 1][...]
         if hidden_first:
             grad = dot(near, near_rows[k][...], 0, 0) + dot(far, far_rows[k][...], 0, 0)
             own_out[k][...] = grad[:, :width]
@@ -182,12 +206,12 @@
 
 
 def grad_out_kernel(*refs):
-    gradients(True, refs[:3], refs[3:6], refs[6:18], refs[18:21], refs[21:24], refs[24])
+    gradients(True, refs[:3], refs[3:6], refs[6:12], refs[12:15], refs[15:18], refs[18])
 
 
 def grad_in_kernel(*refs):
-    other_sums, hidden_prev, stats_out, sums = refs[18], refs[19], refs[26], refs[27]
-    gradients(False, refs[:3], refs[3:6], refs[6:18], refs[20:23], refs[23:26], sums)
+    other_sums, hidden_prev, stats_out, sums = refs[12], refs[13], refs[20], refs[21]
+    gradients(False, refs[:3], refs[3:6], refs[6:12], refs[14:17], refs[17:20], sums)
     collect(hidden_prev, (sums, other_sums), stats_out)
 
 
@@ -310,22 +334,27 @@
     local_in = in_weight[0]
     local_out = out_weight[0]
 
-    if all(half % 128 == 0 for half in halves):
-        cut_shapes = [shape((block_width, half), bf16) for half in halves]
-        cut_shapes += [shape((half, block_width), bf16) for half in halves]
+    is_packed = all(half % 128 == 0 for half in halves) and block_width % 128 == 0
+    if is_packed:
+        kept_shapes = [shape((block_width, half), bf16) for half in halves]
+        kept_shapes += [shape((half, block_width), bf16) for half in halves]
+        packed_shapes = [shape((2 * half * block_width // 128, 128), bf16) for half in halves]
+        copies = 6 + sum(half + block_width for half in halves) // 128
         cuts = call(
-            functools.partial(cut_kernel, bounds), 48, cut_shapes * 2, local_in, local_out,
-            scratch=[pltpu.SemaphoreType.DMA((12,))], whole=True,
+            functools.partial(cut_kernel, bounds), CUT_MIB, kept_shapes + packed_shapes, local_in, local_out,
+            scratch=[pltpu.SemaphoreType.DMA((copies,))], whole=True,
         )
+        own_weights = cuts[:3], cuts[3:6]
+        got_weights = [swap(cuts[6 + k], MASKS[k]) for k in sets]
+        got_weights = (got_weights, got_weights)
     else:
         cuts = []
         for taken in range(2):
             at = [bounds[k][0] + (1 - bits[k] if taken else bits[k]) * halves[k] for k in sets]
             cuts += [lax.dynamic_slice_in_dim(local_in, at[k], halves[k], 1) for k in sets]
             cuts += [lax.dynamic_slice_in_dim(local_out, at[k], halves[k], 0) for k in sets]
-    in_own_weights, out_own_weights = cuts[:3], cuts[3:6]
-    in_got = [swap(cuts[6 + k], MASKS[k]) for k in sets]
-    out_got = [swap(cuts[9 + k], MASKS[k]) for k in sets]
+        own_weights = cuts[:3], cuts[3:6]
+        got_weights = tuple([swap(cuts[n + k], MASKS[k]) for k in sets] for n in (6, 9))
 
     route_ids = expert_ids[:, 0]
     onehot = (route_ids[:, None] == jnp.arange(experts, dtype=jnp.int32)[None, :]).astype(jnp.int32)
@@ -342,17 +371,17 @@
 
     routed = jnp.concatenate([route(tokens), route(cotangent)], axis=2)
     got = lax.all_to_all(routed, "expert", split_axis=0, concat_axis=0, tiled=True)
-    got, in_got, out_got = lax.optimization_barrier((got, in_got, out_got))
+    got, got_weights = lax.optimization_barrier((got, got_weights))
     got = got.reshape(places // GROUP, GROUP, part_cap, 2 * block_width).transpose(1, 0, 2, 3)
     got = got.reshape(GROUP, -1, 2 * block_width)
 
-    def exchanged(own):
-        pairs = [swap(own, MASKS[k]) for k in sets]
-        return (own, swap(own, 1, "ffn")), [(pair, swap(pair, 1, "ffn")) for pair in pairs]
+    def both_cores(own, pairs):
+        pairs = jnp.stack(pairs)
+        return own, swap(own, 1, "ffn"), pairs, swap(pairs, 1, "ffn")
 
     got_tokens, got_cotangent = got[:, :, :block_width], got[:, :, block_width:]
-    own_tokens, pair_tokens = exchanged(got_tokens)
-    own_cotangent, pair_cotangent = exchanged(got_cotangent)
+    token_pairs = [swap(got_tokens, MASKS[k]) for k in sets]
+    cotangent_pairs = [swap(got_cotangent, MASKS[k]) for k in sets]
 
     def shapes(rows, dtype):
         return [shape((rows, half), dtype) for half in halves]
@@ -360,37 +389,49 @@
     count = got.shape[1] * 8
     wide = 2 * block_width
 
-    def scatter_sum(own, pairs, own_weights, got_weights, by_row):
-        operands = (*own, *pairs[0], *pairs[1], *pairs[2], *own_weights, *got_weights)
-        row_shapes = [shape((count, wide), bf16)] * 3
-        outs = call(functools.partial(sums_kernel, 1, by_row), 24, row_shapes + shapes(count, bf16), *operands)
-        far_rows, received = outs[:3], [swap(outs[3 + k], firsts[k]) for k in sets]
-        outs = call(functools.partial(sums_kernel, 0, by_row), 24, row_shapes + shapes(count, f32), *operands)
+    def far_sums(blocks, which):
+        kernel = functools.partial(sums_kernel, 1, which == 1, is_packed)
+        operands = (*blocks, *own_weights[which], *got_weights[which])
+        outs = call(kernel, 14, [shape((count, wide), bf16)] * 3 + shapes(count, bf16), *operands)
+        return operands, outs[:3], outs[3:]
+
+    def scatter_sum(operands, far_rows, sent, which):
+        received = [swap(sent[k], firsts[k]) for k in sets]
+        kernel = functools.partial(sums_kernel, 0, which == 1, is_packed)
+        outs = call(kernel, 14, [shape((count, wide), bf16)] * 3 + shapes(count, f32), *operands)
         near_rows, kept = outs[:3], outs[3:]
-        outs = call(add_kernel, 12, shapes(count // 2, f32) + shapes(count // 2, bf16), *kept, *received)
+        outs = call(add_kernel, 8, shapes(count // 2, f32) + shapes(count // 2, bf16), *kept, *received)
         return near_rows + far_rows, outs[:3], [swap(outs[3 + k], seconds[k]) for k in sets]
 
-    def gather(owns):
-        pieces = []
+    def gather(near):
+        values = []
         for k in sets:
-            near = swap(owns[k], seconds[k])
-            pieces += [owns[k], near, swap(owns[k], firsts[k]), swap(near, firsts[k])]
-        return pieces
-
-    token_rows, *pre = scatter_sum(own_tokens, pair_tokens, in_own_weights, in_got, False)
-    cotangent_rows, *back = scatter_sum(own_cotangent, pair_cotangent, out_own_weights, out_got, True)
-    outs = call(hidden_kernel, 12, shapes(count // 2, bf16) + shapes(count // 2, f32), *pre[0], *pre[1])
-    hidden, slope = gather(outs[:3]), outs[3:]
-    outs = call(pre_grad_kernel, 12, shapes(count // 2, bf16), *back[0], *back[1], *slope)
-    pre_grad = gather(outs)
-
-    hidden, near = lax.optimization_barrier((hidden, pre_grad[1::4]))
-    pre_grad[1::4] = near
+            values += [near[k], swap(near[k], firsts[k])]
+        return values
+
+    def join(owns, got):
+        return call(join_kernel, 8, shapes(count, bf16), *owns, *got)
+
+    token_operands, far_tokens, token_sums = far_sums(both_cores(got_tokens, token_pairs), 0)
+    far_tokens, cotangent_pairs = lax.optimization_barrier((far_tokens, cotangent_pairs))
+    cotangent_operands, far_cotangent, cotangent_sums = far_sums(both_cores(got_cotangent, cotangent_pairs), 1)
+    token_rows, *pre = scatter_sum(token_operands, far_tokens, token_sums, 0)
+    cotangent_rows, *back = scatter_sum(cotangent_operands, far_cotangent, cotangent_sums, 1)
+    outs = call(hidden_kernel, 8, shapes(count // 2, bf16) + shapes(count // 2, f32), *pre[0], *pre[1])
+    hidden, slope = outs[:3], outs[3:]
+    hidden_got = [swap(hidden[k], seconds[k]) for k in sets]
+    pre_grad = call(pre_grad_kernel, 8, shapes(count // 2, bf16), *back[0], *back[1], *slope)
+    pre_grad_got = [swap(pre_grad[k], seconds[k]) for k in sets]
+    hidden = gather(join(hidden, hidden_got))
+    pre_grad_near = join(pre_grad, pre_grad_got)
+    pre_grad = gather(pre_grad_near)
+
+    hidden, pre_grad[0::2] = lax.optimization_barrier((hidden, pre_grad[0::2]))
     lanes = max(block_width, *halves)
     hidden_pick = lax.dynamic_index_in_dim(hidden_states, expert, 1, keepdims=False)
     sums_shape = (6, 8, wide)
     outs = call(
-        grad_out_kernel, 24,
+        grad_out_kernel, 14,
         [shape((half, block_width), f32) for half in halves]
         + [shape((half, block_width), bf16) for half in halves]
         + [shape(sums_shape, f32)],
@@ -400,7 +441,7 @@
     got_out = [swap(out_sent[k], MASKS[k]) for k in sets]
     pre_grad, got_out = lax.optimization_barrier((pre_grad, got_out))
     outs = call(
-        grad_in_kernel, 24,
+        grad_in_kernel, 14,
         [shape((block_width, half), f32) for half in halves]
         + [shape((block_width, half), bf16) for half in halves]
         + [shape((STAT_ROWS, lanes), f32)],
@@ -437,7 +478,7 @@
     )
     norms = ffn_total(cube_total(norms))
     update_in, update_out = call(
-        functools.partial(final_kernel, bounds), 18,
+        functools.partial(final_kernel, bounds), 12,
         (shape(local_in.shape, bf16), shape(local_out.shape, bf16)),
         prev, factors, whole_sums, norms, *in_own, *out_own, *got_in, *got_out,
     )

time: 265 us -> 269 us (1.015)
  waiting for transfers between devices: 109 us -> 133 us
  starting transfers between devices: 76 us -> 61.6 us
  local copies, waits for them, and re-layouts: 35.9 us -> 30.1 us
    ppermute x66 -> x53, waiting for transfers between devices: 109 us -> 133 us  [swap(): return lax.ppermute(value, axis, pairs)]
    ppermute x66 -> x53, starting transfers between devices: 68.6 us -> 53.9 us  [swap(): return lax.ppermute(value, axis, pairs)]
    unnamed x111 -> x93, local copies, waits for them, and re-layouts: 32.9 us -> 27.8 us
    pallas_call x13 -> x15, Pallas kernels: 37.1 us -> 37.1 us  [call(): pl.pallas_call(kernel, out_shape=out_shape, in_specs=[pl.BlockSpec(memory...]
  transfers between devices with their start and end apart: 67 -> 54, of which waited for: 29 -> 30; matrix products, arithmetic and copies ran while one was open for 0% -> 0% of each run, Pallas kernels for 7% -> 5%
where the time goes in v3:
time: 269 us; the launch traced here: 268 us
  waiting for transfers between devices  133 us (49%)
  starting transfers between devices  61.6 us (23%)
  Pallas kernels  37.1 us (14%)
  local copies, waits for them, and re-layouts  30.1 us (11%)
  other arithmetic  4.19 us (2%)
    ppermute x53, waiting for transfers between devices, swap(): return lax.ppermute(value, axis, pairs)  133 us
    ppermute x53, starting transfers between devices, swap(): return lax.ppermute(value, axis, pairs)  53.9 us
    pallas_call x15, Pallas kernels, call(): pl.pallas_call(kernel, out_shape=out_shape, in_specs=[pl.BlockSpec(memory...  37.1 us
    unnamed x93, local copies, waits for them, and re-layouts  27.8 us
    all_to_all x1, starting transfers between devices, shards(): lax.all_to_all(routed, 'expert', split_axis=0, concat_axis=0, tiled=True)  7.74 us
  transfers between devices with their start and end apart: 54, of which 30 were waited for; matrix products, arithmetic and copies ran while one was open for 0% of the time, Pallas kernels for 5%

profile of v3, /device:TPU:1, one launch (start us, length us, event | category | flops | bytes accessed | tf_op | source)
XLA Modules:
  0.0 268.0 jit_solution(5311650345513590379)
XLA Ops:
  6.7 7.7 %all-to-all-start = ((bf16[16,40,1024]{2,1,0:T(8,128)(2,1)}), bf16[16,40,1024]{2,1,0:T(8,128)(2,1)}, u32[]{:S(2)}, u32[]{:S(2)}) async-start(bf16[16,40,1024]{2,1,0:T(8,128)(2,1)} %pad_maximum_fusion.2), calls=%async_computation | async-start | bytes 2621440 | tf_op jit(solution)/shard_map/all_to_all | solution.py:373
  14.5 1.7 copy-done.13
  16.2 1.5 shard_map.86
  24.5 24.1 %collective-permute-done.1.refs_8_ = bf16[3072,128]{1,0:T(8,128)(2,1)S(1)} collective-permute-done((bf16[3072,128]{1,0:T(8,128)(2,1)S(1)}, bf16[3072,128]{1,0:T(8,128)(2,1)S(1)}, u32[]{:S(2)}, u32[]{:S(2)}) %collective-permute-start.1) | collective-permute-done | bytes 786464 | tf_op jit(solution)/shard_map/ppermute | solution.py:29
  48.6 5.5 %collective-permute-done.2.refs_9_ = bf16[3072,128]{1,0:T(8,128)(2,1)S(1)} collective-permute-done((bf16[3072,128]{1,0:T(8,128)(2,1)S(1)}, bf16[3072,128]{1,0:T(8,128)(2,1)S(1)}, u32[]{:S(2)}, u32[]{:S(2)}) %collective-permute-start.2) | collective-permute-done | bytes 786464 | tf_op jit(solution)/shard_map/ppermute | solution.py:29
  55.0 1.4 copy.11
  56.6 1.5 collective-permute-start.4
  59.0 1.9 collective-permute-start.6
  60.9 10.2 %collective-permute-done.4 = bf16[8,80,512]{2,1,0:T(8,128)(2,1)S(1)} collective-permute-done((bf16[8,80,512]{2,1,0:T(8,128)(2,1)S(1)}, bf16[8,80,512]{2,1,0:T(8,128)(2,1)S(1)}, u32[]{:S(2)}, u32[]{:S(2)}) %collective-permute-start.4) | collective-permute-done | bytes 655392 | tf_op jit(solution)/shard_map/ppermute | solution.py:29
  72.4 1.5 collective-permute-done.6
  74.1 2.8 %collective-permute-start.7 = (bf16[3,8,80,512]{3,2,1,0:T(8,128)(2,1)S(1)}, bf16[3,8,80,512]{3,2,1,0:T(8,128)(2,1)S(1)}, u32[]{:S(2)}, u32[]{:S(2)}) collective-permute-start(bf16[3,8,80,512]{3,2,1,0:T(8,128)(2,1)S(1)} %pad_maximum_fusion.refs_2_), channel_id=1, source_target_pairs={{0,1},{1,0},{2,3},{3,2},{4,5},{5,4},{6,7},{7,6},{8,9},{9,8},{10,11... | collective-permute-start | bytes 5898248 | tf_op jit(solution)/shard_map/ppermute | solution.py:29
  76.9 1.5 collective-permute-start.10
  78.6 2.8 %collective-permute-done.3.refs_1_ = bf16[8,80,512]{2,1,0:T(8,128)(2,1)S(1)} collective-permute-done((bf16[8,80,512]{2,1,0:T(8,128)(2,1)S(1)}, bf16[8,80,512]{2,1,0:T(8,128)(2,1)S(1)}, u32[]{:S(2)}, u32[]{:S(2)}) %collective-permute-start.3) | collective-permute-done | bytes 655392 | tf_op jit(solution)/shard_map/ppermute | solution.py:29
  81.4 2.2 shard_map.88
  83.7 9.2 %collective-permute-done.10 = bf16[8,80,512]{2,1,0:T(8,128)(2,1)S(1)} collective-permute-done((bf16[8,80,512]{2,1,0:T(8,128)(2,1)S(1)}, bf16[8,80,512]{2,1,0:T(8,128)(2,1)S(1)}, u32[]{:S(2)}, u32[]{:S(2)}) %collective-permute-start.10) | collective-permute-done | bytes 655392 | tf_op jit(solution)/shard_map/ppermute | solution.py:29
  94.2 1.7 collective-permute-start.24
  97.9 2.2 shard_map.87
  101.1 7.9 %collective-permute-done.12.refs_4_ = bf16[640,384]{1,0:T(8,128)(2,1)S(1)} collective-permute-done((bf16[640,384]{1,0:T(8,128)(2,1)S(1)}, bf16[640,384]{1,0:T(8,128)(2,1)S(1)}, u32[]{:S(2)}, u32[]{:S(2)}) %collective-permute-start.12) | collective-permute-done | bytes 491552 | tf_op jit(solution)/shard_map/ppermute | solution.py:29
  109.1 3.2 %collective-permute-done.11.refs_3_ = bf16[640,512]{1,0:T(8,128)(2,1)S(1)} collective-permute-done((bf16[640,512]{1,0:T(8,128)(2,1)S(1)}, bf16[640,512]{1,0:T(8,128)(2,1)S(1)}, u32[]{:S(2)}, u32[]{:S(2)}) %collective-permute-start.11) | collective-permute-done | bytes 655392 | tf_op jit(solution)/shard_map/ppermute | solution.py:29
  112.6 1.5 collective-permute-start.15
  114.1 2.2 shard_map.93
  116.5 1.4 collective-permute-start.14
  119.9 16.8 %collective-permute-done.16.refs_5_ = bf16[320,384]{1,0:T(8,128)(2,1)S(1)} collective-permute-done((bf16[320,384]{1,0:T(8,128)(2,1)S(1)}, bf16[320,384]{1,0:T(8,128)(2,1)S(1)}, u32[]{:S(2)}, u32[]{:S(2)}) %collective-permute-start.16) | collective-permute-done | bytes 245792 | tf_op jit(solution)/shard_map/ppermute | solution.py:29
  139.1 2.2 shard_map.92
  141.7 1.4 collective-permute-start.28
  143.7 1.4 collective-permute-start.30
  146.3 2.3 collective-permute-done.29.refs_4_
  149.7 3.4 %collective-permute-done.28.refs_3_ = bf16[320,512]{1,0:T(8,128)(2,1)S(1)} collective-permute-done((bf16[320,512]{1,0:T(8,128)(2,1)S(1)}, bf16[320,512]{1,0:T(8,128)(2,1)S(1)}, u32[]{:S(2)}, u32[]{:S(2)}) %collective-permute-start.28) | collective-permute-done | bytes 327712 | tf_op jit(solution)/shard_map/ppermute | solution.py:29
  155.2 1.5 collective-permute-start.31
  156.6 2.4 collective-permute-done.32.refs_4_
  159.1 9.3 %collective-permute-done.33.refs_5_ = bf16[320,384]{1,0:T(8,128)(2,1)S(1)} collective-permute-done((bf16[320,384]{1,0:T(8,128)(2,1)S(1)}, bf16[320,384]{1,0:T(8,128)(2,1)S(1)}, u32[]{:S(2)}, u32[]{:S(2)}) %collective-permute-start.33) | collective-permute-done | bytes 245792 | tf_op jit(solution)/shard_map/ppermute | solution.py:29
  168.3 1.8 collective-permute-done.31.refs_3_
  171.3 5.6 %shard_map.97 = (f32[512,512]{1,0:T(8,128)S(1)}, f32[384,512]{1,0:T(8,128)S(1)}, f32[384,512]{1,0:T(8,128)S(1)}, bf16[512,512]{1,0:T(8,128)(2,1)}, bf16[384,512]...) custom-call(bf16[640,1024]{1,0:T(8,128)(2,1)S(1)} %get-tuple-element.185.refs_0_, ...), custom_call_target="tpu_custom_call" | custom-call | tf_op jit(solution)/shard_map/pallas_call | solution.py:69
  178.5 1.4 collective-permute-start.34
  179.9 1.5 collective-permute-start.37
  182.3 2.0 collective-permute-done.38.refs_10_
  185.1 1.3 collective-permute-start.39
  186.5 11.4 %collective-permute-done.39.refs_11_ = bf16[384,512]{1,0:T(8,128)(2,1)} collective-permute-done((bf16[384,512]{1,0:T(8,128)(2,1)}, bf16[384,512]{1,0:T(8,128)(2,1)}, u32[]{:S(2)}, u32[]{:S(2)}) %collective-permute-start.39) | collective-permute-done | bytes 393248 | tf_op jit(solution)/shard_map/ppermute | solution.py:29
  197.9 1.3 collective-permute-done.36.refs_11_
  210.2 8.3 %shard_map.98 = (f32[512,512]{1,0:T(8,128)S(1)}, f32[512,384]{1,0:T(8,128)S(1)}, f32[512,384]{1,0:T(8,128)S(1)}, bf16[512,512]{1,0:T(8,128)(2,1)}, bf16[512,384]...) custom-call(bf16[640,1024]{1,0:T(8,128)(2,1)S(1)} %copy-done.29, bf16[640,1024]{1,0:T(8,128)(2,1)S(1)} %copy-done.31, ...), custom_call_target="tpu_custom_call" | custom-call | tf_op jit(solution)/shard_map/pallas_call | solution.py:69
  220.3 1.7 collective-permute-start.40
  223.2 1.5 collective-permute-start.45
  227.0 5.7 %collective-permute-done.43 = f32[32,512]{1,0:T(8,128)S(1)} collective-permute-done((f32[32,512]{1,0:T(8,128)S(1)}, f32[32,512]{1,0:T(8,128)S(1)}, u32[]{:S(2)}, u32[]{:S(2)}) %collective-permute-start.43) | collective-permute-done | bytes 65568 | tf_op jit(solution)/shard_map/ppermute | solution.py:29
  232.7 7.9 %collective-permute-start.44 = (f32[32,512]{1,0:T(8,128)S(1)}, f32[32,512]{1,0:T(8,128)S(1)}, u32[]{:S(2)}, u32[]{:S(2)}) collective-permute-start(f32[32,512]{1,0:T(8,128)S(1)} %add.62.group_sums), channel_id=1, source_target_pairs={{0,1},{1,0},{2,3},{3,2},{4,5},{5,4},{6,7},{7,6},{8,9},{9,8},{10,11... | collective-permute-start | bytes 196616 | tf_op jit(solution)/shard_map/ppermute | solution.py:29
  246.0 4.0 %shard_map.99 = (f32[32,512]{1,0:T(8,128)S(1)}, f32[8,128]{1,0:T(8,128)S(1)}) custom-call(f32[32,512]{1,0:T(8,128)S(1)} %concatenate.6.prev, f32[32,512]{1,0:T(8,128)S(1)} %add.62.group_sums, f32[32,512]{1,0:T(8,128)S(1)} %add.63.whole_sums, f32[512,512]{1,0:T(8,128)S(1)} %get-tuple-element.212.refs_0_, f32[512,384]{1,0:T(8,128)S(1)} %copy-done.8, ...), custom_call_target="tpu_custom_call" | custom-call | tf_op jit(solution)/shard_map/pallas_call | solution.py:69
  255.7 1.6 collective-permute-done.51
  257.3 3.1 %collective-permute-start.52 = (f32[8,128]{1,0:T(8,128)S(1)}, f32[8,128]{1,0:T(8,128)S(1)}, u32[]{:S(2)}, u32[]{:S(2)}) collective-permute-start(f32[8,128]{1,0:T(8,128)S(1)} %add.67), channel_id=1, source_target_pairs={{0,1},{1,0},{2,3},{3,2},{4,5},{5,4},{6,7},{7,6},{8,9},{9,8},{10,11... | collective-permute-start | bytes 12296 | tf_op jit(solution)/shard_map/ppermute | solution.py:29
  262.4 5.5 %shard_map.100 = (bf16[512,2560]{1,0:T(8,128)(2,1)}, bf16[2560,512]{1,0:T(8,128)(2,1)}) custom-call(f32[32,512]{1,0:T(8,128)S(1)} %concatenate.6.prev, f32[32,512]{1,0:T(8,128)S(1)} %get-tuple-element.218.factors, f32[32,512]{1,0:T(8,128)S(1)} %add.63.whole_sums, f32[8,128]{1,0:T(8,128)S(1)} %add.68.norms, f32[512,512]{1,0:T(8,128)S(1)} %get-tuple-element.212.refs_0_, ...), custom_call_target="tpu_custom_call" | custom-call | tf_op jit(solution)/shard_map/pallas_call | solution.py:69
  (205 shorter events, 64.5 us)
Async XLA Ops:
  6.7 48.3 %all-to-all-start = ((bf16[16,40,1024]{2,1,0:T(8,128)(2,1)}), bf16[16,40,1024]{2,1,0:T(8,128)(2,1)}, u32[]{:S(2)}, u32[]{:S(2)}) async-start(bf16[16,40,1024]{2,1,0:T(8,128)(2,1)} %pad_maximum_fusion.2), calls=%async_computation | async-start | bytes 2621440 | tf_op jit(solution)/shard_map/all_to_all | solution.py:373
  20.8 34.2 %collective-permute-start = (bf16[4096,128]{1,0:T(8,128)(2,1)S(1)}, bf16[4096,128]{1,0:T(8,128)(2,1)S(1)}, u32[]{:S(2)}, u32[]{:S(2)}) collective-permute-start(bf16[4096,128]{1,0:T(8,128)(2,1)S(1)} %get-tuple-element.115), channel_id=1, source_target_pairs={{0,2},{2,0},{4,6},{6,4},{8,10},{10,8},{12,14},{14,12},{16,18},{18,... | collective-permute-start | bytes 3145736 | tf_op jit(solution)/shard_map/ppermute | solution.py:29
  22.1 26.5 %collective-permute-start.1 = (bf16[3072,128]{1,0:T(8,128)(2,1)S(1)}, bf16[3072,128]{1,0:T(8,128)(2,1)S(1)}, u32[]{:S(2)}, u32[]{:S(2)}) collective-permute-start(bf16[3072,128]{1,0:T(8,128)(2,1)S(1)} %get-tuple-element.116), channel_id=1, source_target_pairs={{0,4},{2,6},{4,0},{6,2},{8,12},{10,14},{12,8},{14,10},{16,20},{18,... | collective-permute-start | bytes 2359304 | tf_op jit(solution)/shard_map/ppermute | solution.py:29
  23.3 30.8 %collective-permute-start.2 = (bf16[3072,128]{1,0:T(8,128)(2,1)S(1)}, bf16[3072,128]{1,0:T(8,128)(2,1)S(1)}, u32[]{:S(2)}, u32[]{:S(2)}) collective-permute-start(bf16[3072,128]{1,0:T(8,128)(2,1)S(1)} %get-tuple-element.117), channel_id=1, source_target_pairs={{0,8},{2,10},{4,12},{6,14},{8,0},{10,2},{12,4},{14,6},{16,24},{18,... | collective-permute-start | bytes 2359304 | tf_op jit(solution)/shard_map/ppermute | solution.py:29
  56.6 14.5 %collective-permute-start.4 = (bf16[8,80,512]{2,1,0:T(8,128)(2,1)S(1)}, bf16[8,80,512]{2,1,0:T(8,128)(2,1)S(1)}, u32[]{:S(2)}, u32[]{:S(2)}) collective-permute-start(bf16[8,80,512]{2,1,0:T(8,128)(2,1)S(1)} %get-tuple-element.235.refs_0_), channel_id=1, source_target_pairs={{0,2},{2,0},{4,6},{6,4},{8,10},{10,8},{12,14},{14,12},{16,18},{18,... | collective-permute-start | bytes 1966088 | tf_op jit(solution)/shard_map/ppermute | solution.py:29
  58.1 14.2 %collective-permute-start.5 = (bf16[8,80,512]{2,1,0:T(8,128)(2,1)S(1)}, bf16[8,80,512]{2,1,0:T(8,128)(2,1)S(1)}, u32[]{:S(2)}, u32[]{:S(2)}) collective-permute-start(bf16[8,80,512]{2,1,0:T(8,128)(2,1)S(1)} %get-tuple-element.235.refs_0_), channel_id=1, source_target_pairs={{0,4},{2,6},{4,0},{6,2},{8,12},{10,14},{12,8},{14,10},{16,20},{18,... | collective-permute-start | bytes 1966088 | tf_op jit(solution)/shard_map/ppermute | solution.py:29
  59.0 14.8 %collective-permute-start.6 = (bf16[8,80,512]{2,1,0:T(8,128)(2,1)S(1)}, bf16[8,80,512]{2,1,0:T(8,128)(2,1)S(1)}, u32[]{:S(2)}, u32[]{:S(2)}) collective-permute-start(bf16[8,80,512]{2,1,0:T(8,128)(2,1)S(1)} %get-tuple-element.235.refs_0_), channel_id=1, source_target_pairs={{0,8},{2,10},{4,12},{6,14},{8,0},{10,2},{12,4},{14,6},{16,24},{18,... | collective-permute-start | bytes 1966088 | tf_op jit(solution)/shard_map/ppermute | solution.py:29
  74.1 7.3 %collective-permute-start.7 = (bf16[3,8,80,512]{3,2,1,0:T(8,128)(2,1)S(1)}, bf16[3,8,80,512]{3,2,1,0:T(8,128)(2,1)S(1)}, u32[]{:S(2)}, u32[]{:S(2)}) collective-permute-start(bf16[3,8,80,512]{3,2,1,0:T(8,128)(2,1)S(1)} %pad_maximum_fusion.refs_2_), channel_id=1, source_target_pairs={{0,1},{1,0},{2,3},{3,2},{4,5},{5,4},{6,7},{7,6},{8,9},{9,8},{10,11... | collective-permute-start | bytes 5898248 | tf_op jit(solution)/shard_map/ppermute | solution.py:29
  76.9 4.5 %collective-permute-start.3 = (bf16[8,80,512]{2,1,0:T(8,128)(2,1)S(1)}, bf16[8,80,512]{2,1,0:T(8,128)(2,1)S(1)}, u32[]{:S(2)}, u32[]{:S(2)}) collective-permute-start(bf16[8,80,512]{2,1,0:T(8,128)(2,1)S(1)} %get-tuple-element.235.refs_0_), channel_id=1, source_target_pairs={{0,1},{1,0},{2,3},{3,2},{4,5},{5,4},{6,7},{7,6},{8,9},{9,8},{10,11... | collective-permute-start | bytes 1966088 | tf_op jit(solution)/shard_map/ppermute | solution.py:29
  76.9 15.9 %collective-permute-start.10 = (bf16[8,80,512]{2,1,0:T(8,128)(2,1)S(1)}, bf16[8,80,512]{2,1,0:T(8,128)(2,1)S(1)}, u32[]{:S(2)}, u32[]{:S(2)}) collective-permute-start(bf16[8,80,512]{2,1,0:T(8,128)(2,1)S(1)} %get-tuple-element.234.refs_0_), channel_id=1, source_target_pairs={{0,8},{2,10},{4,12},{6,14},{8,0},{10,2},{12,4},{14,6},{16,24},{18,... | collective-permute-start | bytes 1966088 | tf_op jit(solution)/shard_map/ppermute | solution.py:29
  78.4 15.6 %collective-permute-start.8 = (bf16[8,80,512]{2,1,0:T(8,128)(2,1)S(1)}, bf16[8,80,512]{2,1,0:T(8,128)(2,1)S(1)}, u32[]{:S(2)}, u32[]{:S(2)}) collective-permute-start(bf16[8,80,512]{2,1,0:T(8,128)(2,1)S(1)} %get-tuple-element.234.refs_0_), channel_id=1, source_target_pairs={{0,2},{2,0},{4,6},{6,4},{8,10},{10,8},{12,14},{14,12},{16,18},{18,... | collective-permute-start | bytes 1966088 | tf_op jit(solution)/shard_map/ppermute | solution.py:29
  78.5 15.5 %collective-permute-start.9 = (bf16[8,80,512]{2,1,0:T(8,128)(2,1)S(1)}, bf16[8,80,512]{2,1,0:T(8,128)(2,1)S(1)}, u32[]{:S(2)}, u32[]{:S(2)}) collective-permute-start(bf16[8,80,512]{2,1,0:T(8,128)(2,1)S(1)} %get-tuple-element.234.refs_0_), channel_id=1, source_target_pairs={{0,4},{2,6},{4,0},{6,2},{8,12},{10,14},{12,8},{14,10},{16,20},{18,... | collective-permute-start | bytes 1966088 | tf_op jit(solution)/shard_map/ppermute | solution.py:29
  94.2 19.8 %collective-permute-start.24 = (bf16[3,8,80,512]{3,2,1,0:T(8,128)(2,1)S(1)}, bf16[3,8,80,512]{3,2,1,0:T(8,128)(2,1)S(1)}, u32[]{:S(2)}, u32[]{:S(2)}) collective-permute-start(bf16[3,8,80,512]{3,2,1,0:T(8,128)(2,1)S(1)} %pad_maximum_fusion.1.refs_2_), channel_id=1, source_target_pairs={{0,1},{1,0},{2,3},{3,2},{4,5},{5,4},{6,7},{7,6},{8,9},{9,8},{10,11... | collective-permute-start | bytes 5898248 | tf_op jit(solution)/shard_map/ppermute | solution.py:29
  96.0 16.3 %collective-permute-start.11 = (bf16[640,512]{1,0:T(8,128)(2,1)S(1)}, bf16[640,512]{1,0:T(8,128)(2,1)S(1)}, u32[]{:S(2)}, u32[]{:S(2)}) collective-permute-start(bf16[640,512]{1,0:T(8,128)(2,1)S(1)} %get-tuple-element.137), channel_id=1, source_target_pairs={{0,4},{2,6},{4,0},{6,2},{8,12},{10,14},{12,8},{14,10},{16,20},{18,... | collective-permute-start | bytes 1966088 | tf_op jit(solution)/shard_map/ppermute | solution.py:29
  96.0 18.0 %collective-permute-start.23 = (bf16[8,80,512]{2,1,0:T(8,128)(2,1)S(1)}, bf16[8,80,512]{2,1,0:T(8,128)(2,1)S(1)}, u32[]{:S(2)}, u32[]{:S(2)}) collective-permute-start(bf16[8,80,512]{2,1,0:T(8,128)(2,1)S(1)} %get-tuple-element.234.refs_0_), channel_id=1, source_target_pairs={{0,1},{1,0},{2,3},{3,2},{4,5},{5,4},{6,7},{7,6},{8,9},{9,8},{10,11... | collective-permute-start | bytes 1966088 | tf_op jit(solution)/shard_map/ppermute | solution.py:29
  96.4 12.7 %collective-permute-start.12 = (bf16[640,384]{1,0:T(8,128)(2,1)S(1)}, bf16[640,384]{1,0:T(8,128)(2,1)S(1)}, u32[]{:S(2)}, u32[]{:S(2)}) collective-permute-start(bf16[640,384]{1,0:T(8,128)(2,1)S(1)} %get-tuple-element.138), channel_id=1, source_target_pairs={{0,8},{2,10},{4,12},{6,14},{8,0},{10,2},{12,4},{14,6},{16,24},{18,... | collective-permute-start | bytes 1474568 | tf_op jit(solution)/shard_map/ppermute | solution.py:29
  96.6 12.5 %collective-permute-start.13 = (bf16[640,384]{1,0:T(8,128)(2,1)S(1)}, bf16[640,384]{1,0:T(8,128)(2,1)S(1)}, u32[]{:S(2)}, u32[]{:S(2)}) collective-permute-start(bf16[640,384]{1,0:T(8,128)(2,1)S(1)} %get-tuple-element.139), channel_id=1, source_target_pairs={{0,2},{2,0},{4,6},{6,4},{8,10},{10,8},{12,14},{14,12},{16,18},{18,... | collective-permute-start | bytes 1474568 | tf_op jit(solution)/shard_map/ppermute | solution.py:29
  112.6 6.7 %collective-permute-start.15 = (bf16[320,384]{1,0:T(8,128)(2,1)S(1)}, bf16[320,384]{1,0:T(8,128)(2,1)S(1)}, u32[]{:S(2)}, u32[]{:S(2)}) collective-permute-start(bf16[320,384]{1,0:T(8,128)(2,1)S(1)} %get-tuple-element.144), channel_id=1, source_target_pairs={{0,2},{2,0},{4,6},{6,4},{8,10},{10,8},{12,14},{14,12},{16,18},{18,... | collective-permute-start | bytes 737288 | tf_op jit(solution)/shard_map/ppermute | solution.py:29
  116.3 25.1 %collective-permute-start.25 = (bf16[640,512]{1,0:T(8,128)(2,1)S(1)}, bf16[640,512]{1,0:T(8,128)(2,1)S(1)}, u32[]{:S(2)}, u32[]{:S(2)}) collective-permute-start(bf16[640,512]{1,0:T(8,128)(2,1)S(1)} %get-tuple-element.164), channel_id=1, source_target_pairs={{0,4},{2,6},{4,0},{6,2},{8,12},{10,14},{12,8},{14,10},{16,20},{18,... | collective-permute-start | bytes 1966088 | tf_op jit(solution)/shard_map/ppermute | solution.py:29
  116.4 22.6 %collective-permute-start.26 = (bf16[640,384]{1,0:T(8,128)(2,1)S(1)}, bf16[640,384]{1,0:T(8,128)(2,1)S(1)}, u32[]{:S(2)}, u32[]{:S(2)}) collective-permute-start(bf16[640,384]{1,0:T(8,128)(2,1)S(1)} %get-tuple-element.165), channel_id=1, source_target_pairs={{0,8},{2,10},{4,12},{6,14},{8,0},{10,2},{12,4},{14,6},{16,24},{18,... | collective-permute-start | bytes 1474568 | tf_op jit(solution)/shard_map/ppermute | solution.py:29
  116.5 20.2 %collective-permute-start.14 = (bf16[320,512]{1,0:T(8,128)(2,1)S(1)}, bf16[320,512]{1,0:T(8,128)(2,1)S(1)}, u32[]{:S(2)}, u32[]{:S(2)}) collective-permute-start(bf16[320,512]{1,0:T(8,128)(2,1)S(1)} %get-tuple-element.143), channel_id=1, source_target_pairs={{0,8},{2,10},{4,12},{6,14},{8,0},{10,2},{12,4},{14,6},{16,24},{18,... | collective-permute-start | bytes 983048 | tf_op jit(solution)/shard_map/ppermute | solution.py:29
  117.9 23.4 %collective-permute-start.27 = (bf16[640,384]{1,0:T(8,128)(2,1)S(1)}, bf16[640,384]{1,0:T(8,128)(2,1)S(1)}, u32[]{:S(2)}, u32[]{:S(2)}) collective-permute-start(bf16[640,384]{1,0:T(8,128)(2,1)S(1)} %get-tuple-element.166), channel_id=1, source_target_pairs={{0,2},{2,0},{4,6},{6,4},{8,10},{10,8},{12,14},{14,12},{16,18},{18,... | collective-permute-start | bytes 1474568 | tf_op jit(solution)/shard_map/ppermute | solution.py:29
  119.3 17.4 %collective-permute-start.16 = (bf16[320,384]{1,0:T(8,128)(2,1)S(1)}, bf16[320,384]{1,0:T(8,128)(2,1)S(1)}, u32[]{:S(2)}, u32[]{:S(2)}) collective-permute-start(bf16[320,384]{1,0:T(8,128)(2,1)S(1)} %get-tuple-element.145), channel_id=1, source_target_pairs={{0,4},{2,6},{4,0},{6,2},{8,12},{10,14},{12,8},{14,10},{16,20},{18,... | collective-permute-start | bytes 737288 | tf_op jit(solution)/shard_map/ppermute | solution.py:29
  138.0 5.7 %collective-permute-start.18 = (bf16[320,384]{1,0:T(8,128)(2,1)S(1)}, bf16[320,384]{1,0:T(8,128)(2,1)S(1)}, u32[]{:S(2)}, u32[]{:S(2)}) collective-permute-start(bf16[320,384]{1,0:T(8,128)(2,1)S(1)} %get-tuple-element.147.refs_1_), channel_id=1, source_target_pairs={{0,2},{2,0},{4,6},{6,4},{8,10},{10,8},{12,14},{14,12},{16,18},{18,... | collective-permute-start | bytes 737288 | tf_op jit(solution)/shard_map/ppermute | solution.py:29
  138.9 7.2 %collective-permute-start.17 = (bf16[320,512]{1,0:T(8,128)(2,1)S(1)}, bf16[320,512]{1,0:T(8,128)(2,1)S(1)}, u32[]{:S(2)}, u32[]{:S(2)}) collective-permute-start(bf16[320,512]{1,0:T(8,128)(2,1)S(1)} %get-tuple-element.146.refs_0_), channel_id=1, source_target_pairs={{0,8},{2,10},{4,12},{6,14},{8,0},{10,2},{12,4},{14,6},{16,24},{18,... | collective-permute-start | bytes 983048 | tf_op jit(solution)/shard_map/ppermute | solution.py:29
  139.0 6.2 %collective-permute-start.19 = (bf16[320,384]{1,0:T(8,128)(2,1)S(1)}, bf16[320,384]{1,0:T(8,128)(2,1)S(1)}, u32[]{:S(2)}, u32[]{:S(2)}) collective-permute-start(bf16[320,384]{1,0:T(8,128)(2,1)S(1)} %get-tuple-element.148.refs_2_), channel_id=1, source_target_pairs={{0,4},{2,6},{4,0},{6,2},{8,12},{10,14},{12,8},{14,10},{16,20},{18,... | collective-permute-start | bytes 737288 | tf_op jit(solution)/shard_map/ppermute | solution.py:29
  141.7 11.4 %collective-permute-start.28 = (bf16[320,512]{1,0:T(8,128)(2,1)S(1)}, bf16[320,512]{1,0:T(8,128)(2,1)S(1)}, u32[]{:S(2)}, u32[]{:S(2)}) collective-permute-start(bf16[320,512]{1,0:T(8,128)(2,1)S(1)} %get-tuple-element.170), channel_id=1, source_target_pairs={{0,8},{2,10},{4,12},{6,14},{8,0},{10,2},{12,4},{14,6},{16,24},{18,... | collective-permute-start | bytes 983048 | tf_op jit(solution)/shard_map/ppermute | solution.py:29
  143.1 5.6 %collective-permute-start.29 = (bf16[320,384]{1,0:T(8,128)(2,1)S(1)}, bf16[320,384]{1,0:T(8,128)(2,1)S(1)}, u32[]{:S(2)}, u32[]{:S(2)}) collective-permute-start(bf16[320,384]{1,0:T(8,128)(2,1)S(1)} %get-tuple-element.171), channel_id=1, source_target_pairs={{0,2},{2,0},{4,6},{6,4},{8,10},{10,8},{12,14},{14,12},{16,18},{18,... | collective-permute-start | bytes 737288 | tf_op jit(solution)/shard_map/ppermute | solution.py:29
  143.7 6.0 %collective-permute-start.30 = (bf16[320,384]{1,0:T(8,128)(2,1)S(1)}, bf16[320,384]{1,0:T(8,128)(2,1)S(1)}, u32[]{:S(2)}, u32[]{:S(2)}) collective-permute-start(bf16[320,384]{1,0:T(8,128)(2,1)S(1)} %get-tuple-element.172), channel_id=1, source_target_pairs={{0,4},{2,6},{4,0},{6,2},{8,12},{10,14},{12,8},{14,10},{16,20},{18,... | collective-permute-start | bytes 737288 | tf_op jit(solution)/shard_map/ppermute | solution.py:29
  146.3 25.0 %collective-permute-start.20 = (bf16[640,512]{1,0:T(8,128)(2,1)S(1)}, bf16[640,512]{1,0:T(8,128)(2,1)S(1)}, u32[]{:S(2)}, u32[]{:S(2)}) collective-permute-start(bf16[640,512]{1,0:T(8,128)(2,1)S(1)} %get-tuple-element.191.refs_6_), channel_id=1, source_target_pairs={{0,4},{2,6},{4,0},{6,2},{8,12},{10,14},{12,8},{14,10},{16,20},{18,... | collective-permute-start | bytes 1966088 | tf_op jit(solution)/shard_map/ppermute | solution.py:29
  153.4 5.6 %collective-permute-start.32 = (bf16[320,384]{1,0:T(8,128)(2,1)S(1)}, bf16[320,384]{1,0:T(8,128)(2,1)S(1)}, u32[]{:S(2)}, u32[]{:S(2)}) collective-permute-start(bf16[320,384]{1,0:T(8,128)(2,1)S(1)} %get-tuple-element.177.refs_1_), channel_id=1, source_target_pairs={{0,2},{2,0},{4,6},{6,4},{8,10},{10,8},{12,14},{14,12},{16,18},{18,... | collective-permute-start | bytes 737288 | tf_op jit(solution)/shard_map/ppermute | solution.py:29
  154.0 17.3 %collective-permute-start.21 = (bf16[640,384]{1,0:T(8,128)(2,1)S(1)}, bf16[640,384]{1,0:T(8,128)(2,1)S(1)}, u32[]{:S(2)}, u32[]{:S(2)}) collective-permute-start(bf16[640,384]{1,0:T(8,128)(2,1)S(1)} %get-tuple-element.193.refs_8_), channel_id=1, source_target_pairs={{0,8},{2,10},{4,12},{6,14},{8,0},{10,2},{12,4},{14,6},{16,24},{18,... | collective-permute-start | bytes 1474568 | tf_op jit(solution)/shard_map/ppermute | solution.py:29
  154.0 17.3 %collective-permute-start.22 = (bf16[640,384]{1,0:T(8,128)(2,1)S(1)}, bf16[640,384]{1,0:T(8,128)(2,1)S(1)}, u32[]{:S(2)}, u32[]{:S(2)}) collective-permute-start(bf16[640,384]{1,0:T(8,128)(2,1)S(1)} %get-tuple-element.195.refs_10_), channel_id=1, source_target_pairs={{0,2},{2,0},{4,6},{6,4},{8,10},{10,8},{12,14},{14,12},{16,18},{18,... | collective-permute-start | bytes 1474568 | tf_op jit(solution)/shard_map/ppermute | solution.py:29
  155.2 15.0 %collective-permute-start.31 = (bf16[320,512]{1,0:T(8,128)(2,1)S(1)}, bf16[320,512]{1,0:T(8,128)(2,1)S(1)}, u32[]{:S(2)}, u32[]{:S(2)}) collective-permute-start(bf16[320,512]{1,0:T(8,128)(2,1)S(1)} %get-tuple-element.176.refs_0_), channel_id=1, source_target_pairs={{0,8},{2,10},{4,12},{6,14},{8,0},{10,2},{12,4},{14,6},{16,24},{18,... | collective-permute-start | bytes 983048 | tf_op jit(solution)/shard_map/ppermute | solution.py:29
  159.0 9.3 %collective-permute-start.33 = (bf16[320,384]{1,0:T(8,128)(2,1)S(1)}, bf16[320,384]{1,0:T(8,128)(2,1)S(1)}, u32[]{:S(2)}, u32[]{:S(2)}) collective-permute-start(bf16[320,384]{1,0:T(8,128)(2,1)S(1)} %get-tuple-element.178.refs_2_), channel_id=1, source_target_pairs={{0,4},{2,6},{4,0},{6,2},{8,12},{10,14},{12,8},{14,10},{16,20},{18,... | collective-permute-start | bytes 737288 | tf_op jit(solution)/shard_map/ppermute | solution.py:29
  177.7 6.6 %collective-permute-start.38 = (bf16[384,512]{1,0:T(8,128)(2,1)S(1)}, bf16[384,512]{1,0:T(8,128)(2,1)S(1)}, u32[]{:S(2)}, u32[]{:S(2)}) collective-permute-start(bf16[384,512]{1,0:T(8,128)(2,1)S(1)} %get-tuple-element.198.refs_10_), channel_id=1, source_target_pairs={{0,4},{2,6},{4,0},{6,2},{8,12},{10,14},{12,8},{14,10},{16,20},{18,... | collective-permute-start | bytes 1179656 | tf_op jit(solution)/shard_map/ppermute | solution.py:29
  178.5 20.8 %collective-permute-start.34 = (bf16[640,512]{1,0:T(8,128)(2,1)S(1)}, bf16[640,512]{1,0:T(8,128)(2,1)S(1)}, u32[]{:S(2)}, u32[]{:S(2)}) collective-permute-start(bf16[640,512]{1,0:T(8,128)(2,1)S(1)} %get-tuple-element.200.refs_6_), channel_id=1, source_target_pairs={{0,4},{2,6},{4,0},{6,2},{8,12},{10,14},{12,8},{14,10},{16,20},{18,... | collective-permute-start | bytes 1966088 | tf_op jit(solution)/shard_map/ppermute | solution.py:29
  179.9 19.3 %collective-permute-start.37 = (bf16[512,512]{1,0:T(8,128)(2,1)}, bf16[512,512]{1,0:T(8,128)(2,1)}, u32[]{:S(2)}, u32[]{:S(2)}) collective-permute-start(bf16[512,512]{1,0:T(8,128)(2,1)} %get-tuple-element.197.refs_9_), channel_id=1, source_target_pairs={{0,2},{2,0},{4,6},{6,4},{8,10},{10,8},{12,14},{14,12},{16,18},{18,... | collective-permute-start | bytes 1572872 | tf_op jit(solution)/shard_map/ppermute | solution.py:29
  181.4 16.5 %collective-permute-start.35 = (bf16[640,384]{1,0:T(8,128)(2,1)}, bf16[640,384]{1,0:T(8,128)(2,1)}, u32[]{:S(2)}, u32[]{:S(2)}) collective-permute-start(bf16[640,384]{1,0:T(8,128)(2,1)} %get-tuple-element.202.refs_8_), channel_id=1, source_target_pairs={{0,8},{2,10},{4,12},{6,14},{8,0},{10,2},{12,4},{14,6},{16,24},{18,... | collective-permute-start | bytes 1474568 | tf_op jit(solution)/shard_map/ppermute | solution.py:29
  181.7 17.5 %collective-permute-start.36 = (bf16[640,384]{1,0:T(8,128)(2,1)}, bf16[640,384]{1,0:T(8,128)(2,1)}, u32[]{:S(2)}, u32[]{:S(2)}) collective-permute-start(bf16[640,384]{1,0:T(8,128)(2,1)} %get-tuple-element.204.refs_10_), channel_id=1, source_target_pairs={{0,2},{2,0},{4,6},{6,4},{8,10},{10,8},{12,14},{14,12},{16,18},{18,... | collective-permute-start | bytes 1474568 | tf_op jit(solution)/shard_map/ppermute | solution.py:29
  185.1 12.8 %collective-permute-start.39 = (bf16[384,512]{1,0:T(8,128)(2,1)}, bf16[384,512]{1,0:T(8,128)(2,1)}, u32[]{:S(2)}, u32[]{:S(2)}) collective-permute-start(bf16[384,512]{1,0:T(8,128)(2,1)} %get-tuple-element.199.refs_11_), channel_id=1, source_target_pairs={{0,8},{2,10},{4,12},{6,14},{8,0},{10,2},{12,4},{14,6},{16,24},{18,... | collective-permute-start | bytes 1179656 | tf_op jit(solution)/shard_map/ppermute | solution.py:29
  220.3 4.5 %collective-permute-start.40 = (f32[32,512]{1,0:T(8,128)S(1)}, f32[32,512]{1,0:T(8,128)S(1)}, u32[]{:S(2)}, u32[]{:S(2)}) collective-permute-start(f32[32,512]{1,0:T(8,128)S(1)} %get-tuple-element.207), channel_id=1, source_target_pairs={{0,2},{2,0},{4,6},{6,4},{8,10},{10,8},{12,14},{14,12},{16,18},{18,... | collective-permute-start | bytes 196616 | tf_op jit(solution)/shard_map/ppermute | solution.py:29
  222.0 4.0 %collective-permute-start.42 = (f32[32,512]{1,0:T(8,128)S(1)}, f32[32,512]{1,0:T(8,128)S(1)}, u32[]{:S(2)}, u32[]{:S(2)}) collective-permute-start(f32[32,512]{1,0:T(8,128)S(1)} %get-tuple-element.207), channel_id=1, source_target_pairs={{0,6},{2,4},{4,2},{6,0},{8,14},{10,12},{12,10},{14,8},{16,22},{18,... | collective-permute-start | bytes 196616 | tf_op jit(solution)/shard_map/ppermute | solution.py:29
  223.2 18.3 %collective-permute-start.45 = (bf16[512,512]{1,0:T(8,128)(2,1)}, bf16[512,512]{1,0:T(8,128)(2,1)}, u32[]{:S(2)}, u32[]{:S(2)}) collective-permute-start(bf16[512,512]{1,0:T(8,128)(2,1)} %get-tuple-element.208.refs_3_), channel_id=1, source_target_pairs={{0,2},{2,0},{4,6},{6,4},{8,10},{10,8},{12,14},{14,12},{16,18},{18,... | collective-permute-start | bytes 1572872 | tf_op jit(solution)/shard_map/ppermute | solution.py:29
  224.7 16.8 %collective-permute-start.46 = (bf16[512,384]{1,0:T(8,128)(2,1)}, bf16[512,384]{1,0:T(8,128)(2,1)}, u32[]{:S(2)}, u32[]{:S(2)}) collective-permute-start(bf16[512,384]{1,0:T(8,128)(2,1)} %get-tuple-element.209.refs_4_), channel_id=1, source_target_pairs={{0,4},{2,6},{4,0},{6,2},{8,12},{10,14},{12,8},{14,10},{16,20},{18,... | collective-permute-start | bytes 1179656 | tf_op jit(solution)/shard_map/ppermute | solution.py:29
  224.8 16.7 %collective-permute-start.47 = (bf16[512,384]{1,0:T(8,128)(2,1)}, bf16[512,384]{1,0:T(8,128)(2,1)}, u32[]{:S(2)}, u32[]{:S(2)}) collective-permute-start(bf16[512,384]{1,0:T(8,128)(2,1)} %get-tuple-element.210.refs_5_), channel_id=1, source_target_pairs={{0,8},{2,10},{4,12},{6,14},{8,0},{10,2},{12,4},{14,6},{16,24},{18,... | collective-permute-start | bytes 1179656 | tf_op jit(solution)/shard_map/ppermute | solution.py:29
  226.1 6.6 %collective-permute-start.43 = (f32[32,512]{1,0:T(8,128)S(1)}, f32[32,512]{1,0:T(8,128)S(1)}, u32[]{:S(2)}, u32[]{:S(2)}) collective-permute-start(f32[32,512]{1,0:T(8,128)S(1)} %add_add_fusion), channel_id=1, source_target_pairs={{0,8},{2,10},{4,12},{6,14},{8,0},{10,2},{12,4},{14,6},{16,24},{18,... | collective-permute-start | bytes 196616 | tf_op jit(solution)/shard_map/ppermute | solution.py:29
  232.7 8.8 %collective-permute-start.44 = (f32[32,512]{1,0:T(8,128)S(1)}, f32[32,512]{1,0:T(8,128)S(1)}, u32[]{:S(2)}, u32[]{:S(2)}) collective-permute-start(f32[32,512]{1,0:T(8,128)S(1)} %add.62.group_sums), channel_id=1, source_target_pairs={{0,1},{1,0},{2,3},{3,2},{4,5},{5,4},{6,7},{7,6},{8,9},{9,8},{10,11... | collective-permute-start | bytes 196616 | tf_op jit(solution)/shard_map/ppermute | solution.py:29
  (51 other events, 303.3 us)

commit v4 on v3

--- a/solution.py
+++ b/solution.py
@@ -64,16 +64,35 @@
     )
 
 
-def call(kernel, mib, out_shape, *operands, scratch=(), whole=False):
-    space = pl.ANY if whole else pltpu.VMEM
+def call(kernel, mib, out_shape, *operands, scratch=(), streamed=(), streamed_out=(), whole=()):
+    def spec(value, n, blocks, refs):
+        if n in refs:
+            return pl.BlockSpec(memory_space=pl.ANY)
+        if n in blocks:
+            return pl.BlockSpec(value.shape, lambda: (0,) * len(value.shape))
+        return pl.BlockSpec(memory_space=pltpu.VMEM)
+
     return pl.pallas_call(
         kernel,
         out_shape=out_shape,
-        in_specs=[pl.BlockSpec(memory_space=space)] * len(operands),
-        out_specs=jax.tree.map(lambda _: pl.BlockSpec(memory_space=pltpu.VMEM), out_shape),
+        in_specs=[spec(value, n, streamed, whole) for n, value in enumerate(operands)],
+        out_specs=[spec(value, n, streamed_out, ()) for n, value in enumerate(out_shape)],
         scratch_shapes=list(scratch),
         compiler_params=pltpu.CompilerParams(vmem_limit_bytes=mib * MIB),
     )(*operands)
+
+
+def padded_width(half):
+    return -(-half // 128) * 128
+
+
+def packed_place(step, matrix, k, halves):
+    axis = (k + 1 + (step + matrix) % 2) % 3
+    return axis, padded_width(halves[(axis + 2 - step) % 3]) if matrix else 0
+
+
+def packed_widths(step, halves):
+    return [padded_width(halves[(axis + 2 - step) % 3]) + halves[(axis + 1 + step) % 3] for axis in range(3)]
 
 
 def place_in_group():
@@ -132,87 +151,123 @@
     return jnp.concatenate([ref[at + n * rows : at + (n + 1) * rows, :] for n in range(blocks)], axis=1)
 
 
-def sums_kernel(side, by_row, is_packed, *refs):
-    own, own_other, pairs, pairs_other = refs[:4]
-    own_weights, got_weights, rows_out, sums_out = refs[4:7], refs[7:10], refs[10:13], refs[13:16]
-    count, width = own.shape[1], own.shape[2]
-    for k in range(3):
-        first, second = 1 << (k + 1) % 3, 1 << (k + 2) % 3
-        for j in range(2):
-            for l in range(2):
-                chunk = flipped(place_in_group(), side * first + j * second + l * (1 << k))
-                at = (j * 2 + l) * 2 * count
-                rows_out[k][at : at + count, :width] = own[chunk]
-                rows_out[k][at : at + count, width:] = pairs[k, chunk]
-                rows_out[k][at + count : at + 2 * count, :width] = own_other[chunk]
-                rows_out[k][at + count : at + 2 * count, width:] = pairs_other[k, chunk]
-        half = sums_out[k].shape[1]
-        got = got_weight(got_weights[k], by_row, half, width) if is_packed else got_weights[k][...]
-        sums = partial_sum(rows_out[k][...], own_weights[k][...], got, by_row)
-        sums_out[k][...] = sums.astype(sums_out[k].dtype)
-
-
-def add_kernel(*refs):
-    kept, received, total_out, sent_out = refs[:3], refs[3:6], refs[6:9], refs[9:12]
-    for k in range(3):
-        middle = kept[k].shape[0] // 2
-        total_out[k][...] = kept[k][:middle] + received[k][:middle].astype(jnp.float32)
-        total = kept[k][middle:] + received[k][middle:].astype(jnp.float32)
-        sent_out[k][...] = total.astype(jnp.bfloat16)
-
-
-def hidden_kernel(*refs):
-    kept, received, hidden_out, slope_out = refs[:3], refs[3:6], refs[6:9], refs[9:12]
-    for k in range(3):
-        act_value, act_slope = gelu_pair(kept[k][...] + received[k][...].astype(jnp.float32))
-        hidden_out[k][...] = act_value.astype(jnp.bfloat16)
-        slope_out[k][...] = act_slope
-
-
-def pre_grad_kernel(*refs):
-    kept, received, slope, pre_grad_out = refs[:3], refs[3:6], refs[6:9], refs[9:12]
-    for k in range(3):
-        value = (kept[k][...] + received[k][...].astype(jnp.float32)) * slope[k][...]
-        pre_grad_out[k][...] = value.astype(jnp.bfloat16)
-
-
-def join_kernel(*refs):
-    for k in range(3):
-        own, got, joined = refs[k], refs[3 + k], refs[6 + k]
-        joined[: own.shape[0]] = own[...]
-        joined[own.shape[0] :] = got[...]
-
-
-def gradients(hidden_first, near_rows, far_rows, values, own_out, sent_out, sums_out):
-    width = near_rows[0].shape[1] // 2
-    for k in range(3):
-        near, far = values[2 * k][...], values[2 * k + 1][...]
+def sums_kernel(side, halves, is_packed, *refs):
+    own, pairs, own_weights, got_weights = refs[0], refs[1], refs[2:8], refs[8:14]
+    rows_out, sums_out = refs[14:20], refs[20:]
+    count, width = own.shape[1], own.shape[2] // 2
+    for matrix in range(2):
+        lanes = slice(matrix * width, (matrix + 1) * width)
+        for k in range(3):
+            n, half = 3 * matrix + k, halves[k]
+            axis = packed_place(0, matrix, k, halves)[0]
+            first, second = 1 << axis, 1 << (3 - axis - k)
+            for j in range(2):
+                for l in range(2):
+                    chunk = flipped(place_in_group(), side * first + j * second + l * (1 << k))
+                    at = (j * 2 + l) * count
+                    rows_out[n][at : at + count, :width] = own[chunk, :, lanes]
+                    rows_out[n][at : at + count, width:] = pairs[k, chunk, :, lanes]
+            by_row = matrix == 1
+            got = got_weight(got_weights[n], by_row, half, width) if is_packed else got_weights[n][...]
+            sums = partial_sum(rows_out[n][...], own_weights[n][...], got, by_row)
+            if side:
+                at = packed_place(0, matrix, k, halves)[1]
+                sums_out[axis][:, at : at + half] = sums.astype(jnp.bfloat16)
+            else:
+                sums_out[n][...] = sums
+
+
+def add_kernel(halves, *refs):
+    kept, received, total_out, sent_out = refs[:6], refs[6:9], refs[9:15], refs[15:18]
+    for matrix in range(2):
+        for k in range(3):
+            n, half = 3 * matrix + k, halves[k]
+            middle = kept[n].shape[0] // 2
+            axis, at = packed_place(0, matrix, k, halves)
+            total = kept[n][...] + received[axis][:, at : at + half].astype(jnp.float32)
+            total_out[n][...] = total[:middle]
+            axis, at = packed_place(1, matrix, k, halves)
+            sent_out[axis][:, at : at + half] = total[middle:].astype(jnp.bfloat16)
+
+
+def act_kernel(halves, *refs):
+    kept, received, outs = refs[:6], refs[6:9], refs[9:12]
+    for k in range(3):
+        values = []
+        for matrix in range(2):
+            axis, at = packed_place(1, matrix, k, halves)
+            values.append(kept[3 * matrix + k][...] + received[axis][:, at : at + halves[k]].astype(jnp.float32))
+        act_value, act_slope = gelu_pair(values[0])
+        for matrix, value in enumerate((act_value, values[1] * act_slope)):
+            axis, at = packed_place(0, matrix, k, halves)
+            outs[axis][:, at : at + halves[k]] = value.astype(jnp.bfloat16)
+
+
+def join_kernel(halves, *refs):
+    own, got, outs = refs[:3], refs[3:6], refs[6:9]
+    for matrix in range(2):
+        for k in range(3):
+            source, start = packed_place(0, matrix, k, halves)
+            axis, at = packed_place(1, matrix, k, halves)
+            rows = own[source].shape[0]
+            outs[axis][:rows, at : at + halves[k]] = own[source][:, start : start + halves[k]]
+            outs[axis][rows:, at : at + halves[k]] = got[source][:, start : start + halves[k]]
+
+
+def gradients(hidden_first, halves, rows, values, row_buffers, value_buffers, sems, own_out, sent_out, sums_out):
+    matrix = 0 if hidden_first else 1
+    part = row_buffers.shape[1] // 4
+    width = row_buffers.shape[2] // 2
+
+    def copies(n, parts, buffer):
+        return [
+            pltpu.make_async_copy(parts[i], buffer.at[pl.ds(i * part, part)], sems.at[n * 4 + i]) for i in range(4)
+        ]
+
+    value_copies, row_copies = {}, {}
+    for k in range(3):
+        axis = packed_place(1, matrix, k, halves)[0]
+        row_copies[k] = copies(k, rows[4 * k : 4 * k + 4], row_buffers.at[k])
+        value_copies[k] = copies(3 + axis, values[4 * axis : 4 * axis + 4], value_buffers[axis])
+        for copy in row_copies[k] + value_copies[k]:
+            copy.start()
+    for k in range(3):
+        for copy in row_copies[k] + value_copies[k]:
+            copy.wait()
+        axis, at = packed_place(1, matrix, k, halves)
+        value = value_buffers[axis][:, at : at + halves[k]]
         if hidden_first:
-            grad = dot(near, near_rows[k][...], 0, 0) + dot(far, far_rows[k][...], 0, 0)
+            grad = dot(value, row_buffers[k], 0, 0)
             own_out[k][...] = grad[:, :width]
             sent_out[k][...] = grad[:, width:].astype(jnp.bfloat16)
         else:
-            grad = dot(near_rows[k][...], near, 0, 0) + dot(far_rows[k][...], far, 0, 0)
+            grad = dot(row_buffers[k], value, 0, 0)
             own_out[k][...] = grad[:width]
             sent_out[k][...] = grad[width:].astype(jnp.bfloat16)
         square = grad * grad + EPS_ONE
         down = jnp.sum(square, axis=0, keepdims=True)
+        down = jnp.broadcast_to(down, (8, square.shape[1]))
+        if square.shape[1] % 128 == 0:
+            square = sum(square[:, n : n + 128] for n in range(0, square.shape[1], 128))
         across = dot(jnp.ones((8, square.shape[1]), jnp.float32), square, 1, 1)
-        down = jnp.broadcast_to(down, (8, square.shape[1]))
         by_width, by_hidden = (down, across) if hidden_first else (across, down)
         sums_out[k] = by_width
         sums_out[3 + k] = jnp.zeros(sums_out.shape[1:], jnp.float32)
         sums_out[3 + k, :, : by_hidden.shape[1]] = by_hidden
 
 
-def grad_out_kernel(*refs):
-    gradients(True, refs[:3], refs[3:6], refs[6:12], refs[12:15], refs[15:18], refs[18])
-
-
-def grad_in_kernel(*refs):
-    other_sums, hidden_prev, stats_out, sums = refs[12], refs[13], refs[20], refs[21]
-    gradients(False, refs[:3], refs[3:6], refs[6:12], refs[14:17], refs[17:20], sums)
-    collect(hidden_prev, (sums, other_sums), stats_out)
+def grad_out_kernel(halves, *refs):
+    rows, values, outs, buffers = refs[:12], refs[12:24], refs[24:31], refs[31:]
+    gradients(True, halves, rows, values, buffers[0], buffers[1:4], buffers[4], outs[:3], outs[3:6], outs[6])
+
+
+def grad_in_kernel(halves, *refs):
+    rows, values, other_sums, hidden_prev, outs, buffers = (
+        refs[:12], refs[12:24], refs[24], refs[25], refs[26:33], refs[33:]
+    )
+    sums = buffers[5]
+    gradients(False, halves, rows, values, buffers[0], buffers[1:4], buffers[4], outs[:3], outs[3:6], sums)
+    collect(hidden_prev, (sums, other_sums), outs[6])
 
 
 IN_WIDTH, OUT_WIDTH, IN_HIDDEN, OUT_HIDDEN, TOTALS, STAT_ROWS = 0, 8, 16, 22, 28, 32
@@ -329,8 +384,6 @@
     bounds = set_bounds(in_weight.shape[2])
     halves = [(high - low) // 2 for low, high in bounds]
     sets = range(3)
-    firsts = [MASKS[(k + 1) % 3] for k in sets]
-    seconds = [MASKS[(k + 2) % 3] for k in sets]
     local_in = in_weight[0]
     local_out = out_weight[0]
 
@@ -342,19 +395,16 @@
         copies = 6 + sum(half + block_width for half in halves) // 128
         cuts = call(
             functools.partial(cut_kernel, bounds), CUT_MIB, kept_shapes + packed_shapes, local_in, local_out,
-            scratch=[pltpu.SemaphoreType.DMA((copies,))], whole=True,
+            scratch=[pltpu.SemaphoreType.DMA((copies,))], whole=(0, 1),
         )
-        own_weights = cuts[:3], cuts[3:6]
-        got_weights = [swap(cuts[6 + k], MASKS[k]) for k in sets]
-        got_weights = (got_weights, got_weights)
+        got_weights = [swap(cuts[6 + k], MASKS[k]) for k in sets] * 2
     else:
         cuts = []
         for taken in range(2):
             at = [bounds[k][0] + (1 - bits[k] if taken else bits[k]) * halves[k] for k in sets]
             cuts += [lax.dynamic_slice_in_dim(local_in, at[k], halves[k], 1) for k in sets]
             cuts += [lax.dynamic_slice_in_dim(local_out, at[k], halves[k], 0) for k in sets]
-        own_weights = cuts[:3], cuts[3:6]
-        got_weights = tuple([swap(cuts[n + k], MASKS[k]) for k in sets] for n in (6, 9))
+        got_weights = [swap(cuts[6 + n], MASKS[n % 3]) for n in range(6)]
 
     route_ids = expert_ids[:, 0]
     onehot = (route_ids[:, None] == jnp.arange(experts, dtype=jnp.int32)[None, :]).astype(jnp.int32)
@@ -370,86 +420,88 @@
         return routed.reshape(places, part_cap, block_width)
 
     routed = jnp.concatenate([route(tokens), route(cotangent)], axis=2)
+    routed, own_weights = lax.optimization_barrier((routed, cuts[:6]))
     got = lax.all_to_all(routed, "expert", split_axis=0, concat_axis=0, tiled=True)
     got, got_weights = lax.optimization_barrier((got, got_weights))
     got = got.reshape(places // GROUP, GROUP, part_cap, 2 * block_width).transpose(1, 0, 2, 3)
     got = got.reshape(GROUP, -1, 2 * block_width)
 
-    def both_cores(own, pairs):
-        pairs = jnp.stack(pairs)
-        return own, swap(own, 1, "ffn"), pairs, swap(pairs, 1, "ffn")
-
-    got_tokens, got_cotangent = got[:, :, :block_width], got[:, :, block_width:]
-    token_pairs = [swap(got_tokens, MASKS[k]) for k in sets]
-    cotangent_pairs = [swap(got_cotangent, MASKS[k]) for k in sets]
-
-    def shapes(rows, dtype):
-        return [shape((rows, half), dtype) for half in halves]
-
-    count = got.shape[1] * 8
+    count = got.shape[1] * 4
     wide = 2 * block_width
-
-    def far_sums(blocks, which):
-        kernel = functools.partial(sums_kernel, 1, which == 1, is_packed)
-        operands = (*blocks, *own_weights[which], *got_weights[which])
-        outs = call(kernel, 14, [shape((count, wide), bf16)] * 3 + shapes(count, bf16), *operands)
-        return operands, outs[:3], outs[3:]
-
-    def scatter_sum(operands, far_rows, sent, which):
-        received = [swap(sent[k], firsts[k]) for k in sets]
-        kernel = functools.partial(sums_kernel, 0, which == 1, is_packed)
-        outs = call(kernel, 14, [shape((count, wide), bf16)] * 3 + shapes(count, f32), *operands)
-        near_rows, kept = outs[:3], outs[3:]
-        outs = call(add_kernel, 8, shapes(count // 2, f32) + shapes(count // 2, bf16), *kept, *received)
-        return near_rows + far_rows, outs[:3], [swap(outs[3 + k], seconds[k]) for k in sets]
-
-    def gather(near):
-        values = []
-        for k in sets:
-            values += [near[k], swap(near[k], firsts[k])]
-        return values
-
-    def join(owns, got):
-        return call(join_kernel, 8, shapes(count, bf16), *owns, *got)
-
-    token_operands, far_tokens, token_sums = far_sums(both_cores(got_tokens, token_pairs), 0)
-    far_tokens, cotangent_pairs = lax.optimization_barrier((far_tokens, cotangent_pairs))
-    cotangent_operands, far_cotangent, cotangent_sums = far_sums(both_cores(got_cotangent, cotangent_pairs), 1)
-    token_rows, *pre = scatter_sum(token_operands, far_tokens, token_sums, 0)
-    cotangent_rows, *back = scatter_sum(cotangent_operands, far_cotangent, cotangent_sums, 1)
-    outs = call(hidden_kernel, 8, shapes(count // 2, bf16) + shapes(count // 2, f32), *pre[0], *pre[1])
-    hidden, slope = outs[:3], outs[3:]
-    hidden_got = [swap(hidden[k], seconds[k]) for k in sets]
-    pre_grad = call(pre_grad_kernel, 8, shapes(count // 2, bf16), *back[0], *back[1], *slope)
-    pre_grad_got = [swap(pre_grad[k], seconds[k]) for k in sets]
-    hidden = gather(join(hidden, hidden_got))
-    pre_grad_near = join(pre_grad, pre_grad_got)
-    pre_grad = gather(pre_grad_near)
-
-    hidden, pre_grad[0::2] = lax.optimization_barrier((hidden, pre_grad[0::2]))
+    first_widths, second_widths = packed_widths(0, halves), packed_widths(1, halves)
+
+    def shapes(rows, widths, dtype):
+        return [shape((rows, width), dtype) for width in widths]
+
+    def along_axes(values):
+        return [swap(value, mask) for value, mask in zip(values, MASKS)]
+
+    pairs = jnp.stack([swap(got, MASKS[k]) for k in sets])
+    blocks = [(got, pairs), (swap(got, 1, "ffn"), swap(pairs, 1, "ffn"))]
+    chains = range(2)
+    row_shapes = [shape((count, wide), bf16)] * 6
+
+    def sums(chain, side, out_shapes):
+        kernel = functools.partial(sums_kernel, side, halves, is_packed)
+        outs = call(
+            kernel, 20, row_shapes + out_shapes, *blocks[chain], *own_weights, *got_weights,
+            streamed_out=range(6),
+        )
+        return outs[:6], outs[6:]
+
+    far_rows, received, near_rows, kept = [None] * 2, [None] * 2, [None] * 2, [None] * 2
+    for c in chains:
+        far_rows[c], sent = sums(c, 1, shapes(count, first_widths, bf16))
+        received[c] = along_axes(sent)
+    for c in chains:
+        near_rows[c], kept[c] = sums(c, 0, shapes(count, halves * 2, f32))
+    for c in chains:
+        out_shapes = shapes(count // 2, halves * 2, f32) + shapes(count // 2, second_widths, bf16)
+        outs = call(functools.partial(add_kernel, halves), 8, out_shapes, *kept[c], *received[c])
+        kept[c], received[c] = outs[:6], along_axes(outs[6:])
+    owns, nears, fars = [None] * 2, [None] * 2, [None] * 2
+    for c in chains:
+        out_shapes = shapes(count // 2, first_widths, bf16)
+        owns[c] = call(functools.partial(act_kernel, halves), 8, out_shapes, *kept[c], *received[c])
+        received[c] = along_axes(owns[c])
+    for c in chains:
+        out_shapes = shapes(count, second_widths, bf16)
+        nears[c] = call(functools.partial(join_kernel, halves), 8, out_shapes, *owns[c], *received[c])
+        fars[c] = along_axes(nears[c])
+
+    def parts(near, far):
+        return [value[n] for n in range(3) for chain in chains for value in (near[chain], far[chain])]
+
+    token_rows = parts([rows[:3] for rows in near_rows], [rows[:3] for rows in far_rows])
+    cotangent_rows = parts([rows[3:] for rows in near_rows], [rows[3:] for rows in far_rows])
+    values = parts(nears, fars)
+    buffers = [pltpu.VMEM((3, 4 * count, wide), bf16)]
+    buffers += [pltpu.VMEM((4 * count, width), bf16) for width in second_widths]
+    buffers += [pltpu.SemaphoreType.DMA((24,))]
+
     lanes = max(block_width, *halves)
     hidden_pick = lax.dynamic_index_in_dim(hidden_states, expert, 1, keepdims=False)
     sums_shape = (6, 8, wide)
     outs = call(
-        grad_out_kernel, 14,
+        functools.partial(grad_out_kernel, halves), 28,
         [shape((half, block_width), f32) for half in halves]
         + [shape((half, block_width), bf16) for half in halves]
         + [shape(sums_shape, f32)],
-        *cotangent_rows, *hidden,
+        *cotangent_rows, *values,
+        scratch=buffers, whole=range(24), streamed_out=range(3),
     )
     out_own, out_sent, out_sums = outs[:3], outs[3:6], outs[6]
-    got_out = [swap(out_sent[k], MASKS[k]) for k in sets]
-    pre_grad, got_out = lax.optimization_barrier((pre_grad, got_out))
+    got_out = along_axes(out_sent)
     outs = call(
-        grad_in_kernel, 14,
+        functools.partial(grad_in_kernel, halves), 28,
         [shape((block_width, half), f32) for half in halves]
         + [shape((block_width, half), bf16) for half in halves]
         + [shape((STAT_ROWS, lanes), f32)],
-        *token_rows, *pre_grad, out_sums, hidden_pick[1:2],
-        scratch=[pltpu.VMEM(sums_shape, f32)],
+        *token_rows, *values, out_sums, hidden_pick[1:2],
+        scratch=buffers + [pltpu.VMEM(sums_shape, f32)], whole=range(24), streamed_out=range(3),
     )
     in_own, in_sent, stats = outs[:3], outs[3:6], outs[6]
-    got_in = [swap(in_sent[k], MASKS[k]) for k in sets]
+    got_in = along_axes(in_sent)
 
     width_pick = lax.dynamic_index_in_dim(width_states, expert, 1, keepdims=False)
 
@@ -464,23 +516,34 @@
     prev.append(jnp.ones((STAT_ROWS - TOTALS, lanes), f32))
     prev = jnp.concatenate(prev)
 
-    def cube_total(values):
+    def totals(values):
         values = values + swap(values, 1) + swap(values, 2) + swap(values, 3)
-        return values + swap(values, 4)
-
-    group_sums = cube_total(stats)
-    whole_sums = ffn_total(group_sums)
-    whole_sums, got_in = lax.optimization_barrier((whole_sums, got_in))
+        if lax.axis_size("ffn") > 2:
+            values = values + swap(values, 4)
+            return values, ffn_total(values)
+        ends = [(e, f) for e in range(places) for f in range(2)]
+
+        def other(expert_mask, ffn_mask):
+            moves = [(e * 2 + f, (e ^ expert_mask) * 2 + (f ^ ffn_mask)) for e, f in ends]
+            return lax.ppermute(values, ("expert", "ffn"), moves)
+
+        cube = values + swap(values, 4)
+        return cube, cube + (other(0, 1) + other(4, 1))
+
+    group_sums, whole_sums = totals(stats)
+    whole_sums, got_in, got_out = lax.optimization_barrier((whole_sums, got_in, got_out))
     factors, norms = call(
-        norm_kernel, 12,
-        (shape((STAT_ROWS, lanes), f32), shape((8, 128), f32)),
+        norm_kernel, 20,
+        [shape((STAT_ROWS, lanes), f32), shape((8, 128), f32)],
         prev, group_sums, whole_sums, *in_own, *in_sent, *out_own, *out_sent,
-    )
-    norms = ffn_total(cube_total(norms))
+        streamed=range(3, 15),
+    )
+    norms = totals(norms)[1]
     update_in, update_out = call(
-        functools.partial(final_kernel, bounds), 12,
-        (shape(local_in.shape, bf16), shape(local_out.shape, bf16)),
+        functools.partial(final_kernel, bounds), 24,
+        [shape(local_in.shape, bf16), shape(local_out.shape, bf16)],
         prev, factors, whole_sums, norms, *in_own, *out_own, *got_in, *got_out,
+        streamed=range(4, 16), streamed_out=range(2),
     )
     return (update_in[None], update_out[None])
 

time: 269 us -> 303 us (1.13)
  local copies, waits for them, and re-layouts: 30.1 us -> 50.2 us
  waiting for transfers between devices: 133 us -> 142 us
  Pallas kernels: 37.1 us -> 43 us
    unnamed x93 -> x185, local copies, waits for them, and re-layouts: 27.8 us -> 48 us
    ppermute x53 -> x46, starting transfers between devices: 53.9 us -> 39.9 us  [swap(): return lax.ppermute(value, axis, pairs)]
    ppermute x0 -> x4, starting transfers between devices: none -> 12 us  [other(): return lax.ppermute(values, ('expert', 'ffn'), moves)]
    ppermute x0 -> x4, waiting for transfers between devices: none -> 6.29 us  [other(): return lax.ppermute(values, ('expert', 'ffn'), moves)]
    pallas_call x15, Pallas kernels: 37.1 us -> 43 us  [call(): pl.pallas_call(kernel, out_shape=out_shape, in_specs=[spec(value, n, stre...]
    ppermute x53 -> x46, waiting for transfers between devices: 133 us -> 136 us  [swap(): return lax.ppermute(value, axis, pairs)]
  transfers between devices with their start and end apart: 54 -> 51, of which waited for: 30 -> 27; matrix products, arithmetic and copies ran while one was open for 0% -> 0% of each run, Pallas kernels for 5% -> 4%
where the time goes in v4:
time: 303 us; the launch traced here: 301 us
  waiting for transfers between devices  142 us (47%)
  starting transfers between devices  59.4 us (20%)
  local copies, waits for them, and re-layouts  50.2 us (17%)
  Pallas kernels  43 us (14%)
  other arithmetic  4.41 us (1%)
    ppermute x46, waiting for transfers between devices, swap(): return lax.ppermute(value, axis, pairs)  136 us
    unnamed x185, local copies, waits for them, and re-layouts  48 us
    pallas_call x15, Pallas kernels, call(): pl.pallas_call(kernel, out_shape=out_shape, in_specs=[spec(value, n, stre...  43 us
    ppermute x46, starting transfers between devices, swap(): return lax.ppermute(value, axis, pairs)  39.9 us
    ppermute x4, starting transfers between devices, other(): return lax.ppermute(values, ('expert', 'ffn'), moves)  12 us
    all_to_all x1, starting transfers between devices, shards(): lax.all_to_all(routed, 'expert', split_axis=0, concat_axis=0, tiled=True)  7.47 us
    ppermute x4, waiting for transfers between devices, other(): return lax.ppermute(values, ('expert', 'ffn'), moves)  6.29 us
  transfers between devices with their start and end apart: 51, of which 27 were waited for; matrix products, arithmetic and copies ran while one was open for 0% of the time, Pallas kernels for 4%

profile of v4, /device:TPU:1, one launch (start us, length us, event | category | flops | bytes accessed | tf_op | source)
XLA Modules:
  0.0 301.4 jit_solution(11768617867235671189)
XLA Ops:
  5.5 1.2 pad_maximum_fusion.1
  8.2 2.5 shard_map.86
  14.7 7.5 %all-to-all-start = ((bf16[16,40,1024]{2,1,0:T(8,128)(2,1)}), bf16[16,40,1024]{2,1,0:T(8,128)(2,1)}, u32[]{:S(2)}, u32[]{:S(2)}) async-start(bf16[16,40,1024]{2,1,0:T(8,128)(2,1)} %pad_maximum_fusion.1), calls=%async_computation | async-start | bytes 2621440 | tf_op jit(solution)/shard_map/all_to_all | solution.py:424
  22.2 1.3 collective-permute-start
  23.5 1.2 collective-permute-start.1
  24.7 1.2 collective-permute-start.2
  25.9 29.1 %collective-permute-done.1.refs_9_.refs_12_ = bf16[3072,128]{1,0:T(8,128)(2,1)S(1)} collective-permute-done((bf16[3072,128]{1,0:T(8,128)(2,1)}, bf16[3072,128]{1,0:T(8,128)(2,1)S(1)}, u32[]{:S(2)}, u32[]{:S(2)}) %collective-permute-start.1) | collective-permute-done | bytes 786464 | tf_op jit(solution)/shard_map/ppermute | solution.py:29
  55.0 6.8 %collective-permute-done.2.refs_10_.refs_13_ = bf16[3072,128]{1,0:T(8,128)(2,1)S(1)} collective-permute-done((bf16[3072,128]{1,0:T(8,128)(2,1)}, bf16[3072,128]{1,0:T(8,128)(2,1)S(1)}, u32[]{:S(2)}, u32[]{:S(2)}) %collective-permute-start.2) | collective-permute-done | bytes 786464 | tf_op jit(solution)/shard_map/ppermute | solution.py:29
  61.8 1.4 copy.11
  63.2 1.2 collective-permute-start.3
  64.5 1.5 collective-permute-start.4
  66.0 26.2 %collective-permute-done.3 = bf16[8,80,1024]{2,1,0:T(8,128)(2,1)S(1)} collective-permute-done((bf16[8,80,1024]{2,1,0:T(8,128)(2,1)S(1)}, bf16[8,80,1024]{2,1,0:T(8,128)(2,1)S(1)}, u32[]{:S(2)}, u32[]{:S(2)}) %collective-permute-start.3) | collective-permute-done | bytes 1310752 | tf_op jit(solution)/shard_map/ppermute | solution.py:29
  94.8 3.1 %collective-permute-start.7 = (bf16[3,8,80,1024]{3,2,1,0:T(8,128)(2,1)S(1)}, bf16[3,8,80,1024]{3,2,1,0:T(8,128)(2,1)S(1)}, u32[]{:S(2)}, u32[]{:S(2)}) collective-permute-start(bf16[3,8,80,1024]{3,2,1,0:T(8,128)(2,1)S(1)} %pad_maximum_fusion.refs_1_), channel_id=1, source_target_pairs={{0,1},{1,0},{2,3},{3,2},{4,5},{5,4},{6,7},{7,6},{8,9},{9,8},{10,11... | collective-permute-start | bytes 11796488 | tf_op jit(solution)/shard_map/ppermute | solution.py:29
  98.0 2.2 shard_map.88
  105.1 2.2 shard_map.87
  107.3 8.9 %collective-permute-done.8.refs_6_ = bf16[320,768]{1,0:T(8,128)(2,1)S(1)} collective-permute-done((bf16[320,768]{1,0:T(8,128)(2,1)S(1)}, bf16[320,768]{1,0:T(8,128)(2,1)S(1)}, u32[]{:S(2)}, u32[]{:S(2)}) %collective-permute-start.8) | collective-permute-done | bytes 491552 | tf_op jit(solution)/shard_map/ppermute | solution.py:29
  116.2 2.2 collective-permute-done.10.refs_8_
  119.4 2.2 shard_map.90
  126.3 1.4 collective-permute-start.12
  128.1 15.7 %collective-permute-done.12.refs_7_ = bf16[160,896]{1,0:T(8,128)(2,1)S(1)} collective-permute-done((bf16[160,896]{1,0:T(8,128)(2,1)S(1)}, bf16[160,896]{1,0:T(8,128)(2,1)S(1)}, u32[]{:S(2)}, u32[]{:S(2)}) %collective-permute-start.12) | collective-permute-done | bytes 286752 | tf_op jit(solution)/shard_map/ppermute | solution.py:29
  145.1 1.2 collective-permute-start.15
  147.2 2.2 shard_map.89
  154.0 3.6 %collective-permute-done.21.refs_6_ = bf16[160,768]{1,0:T(8,128)(2,1)S(1)} collective-permute-done((bf16[160,768]{1,0:T(8,128)(2,1)S(1)}, bf16[160,768]{1,0:T(8,128)(2,1)S(1)}, u32[]{:S(2)}, u32[]{:S(2)}) %collective-permute-start.21) | collective-permute-done | bytes 245792 | tf_op jit(solution)/shard_map/ppermute | solution.py:29
  157.6 1.9 collective-permute-done.23.refs_8_
  160.4 1.6 collective-permute-start.26
  162.9 1.4 collective-permute-start.28
  164.3 6.9 %collective-permute-done.24.refs_3_ = bf16[160,768]{1,0:T(8,128)(2,1)S(1)} collective-permute-done((bf16[160,768]{1,0:T(8,128)(2,1)S(1)}, bf16[160,768]{1,0:T(8,128)(2,1)S(1)}, u32[]{:S(2)}, u32[]{:S(2)}) %collective-permute-start.24) | collective-permute-done | bytes 245792 | tf_op jit(solution)/shard_map/ppermute | solution.py:29
  178.2 2.9 collective-permute-done.30.refs_21_
  181.9 2.6 collective-permute-done.27.refs_15_
  184.6 3.5 %collective-permute-done.29.refs_19_ = bf16[320,896]{1,0:T(8,128)(2,1)} collective-permute-done((bf16[320,896]{1,0:T(8,128)(2,1)S(1)}, bf16[320,896]{1,0:T(8,128)(2,1)}, u32[]{:S(2)}, u32[]{:S(2)}) %collective-permute-start.29) | collective-permute-done | bytes 573472 | tf_op jit(solution)/shard_map/ppermute | solution.py:29
  188.0 5.4 %collective-permute-done.31.refs_23_ = bf16[320,896]{1,0:T(8,128)(2,1)} collective-permute-done((bf16[320,896]{1,0:T(8,128)(2,1)}, bf16[320,896]{1,0:T(8,128)(2,1)}, u32[]{:S(2)}, u32[]{:S(2)}) %collective-permute-start.31) | collective-permute-done | bytes 573472 | tf_op jit(solution)/shard_map/ppermute | solution.py:29
  211.9 9.3 %shard_map.97 = (f32[512,512]{1,0:T(8,128)S(1)}, f32[384,512]{1,0:T(8,128)S(1)}, f32[384,512]{1,0:T(8,128)S(1)}, bf16[512,512]{1,0:T(8,128)(2,1)}, bf16[384,512]...) custom-call(bf16[320,1024]{1,0:T(8,128)(2,1)S(1)} %copy-done.42, ...), custom_call_target="tpu_custom_call" | custom-call | tf_op jit(solution)/shard_map/pallas_call | solution.py:75
  222.2 1.2 copy-done.22
  224.5 9.9 %shard_map.98 = (f32[512,512]{1,0:T(8,128)S(1)}, f32[512,384]{1,0:T(8,128)S(1)}, f32[512,384]{1,0:T(8,128)S(1)}, bf16[512,512]{1,0:T(8,128)(2,1)}, bf16[512,384]...) custom-call(bf16[320,1024]{1,0:T(8,128)(2,1)S(1)} %copy-done.66, ...), custom_call_target="tpu_custom_call" | custom-call | tf_op jit(solution)/shard_map/pallas_call | solution.py:75
  237.2 1.6 collective-permute-start.34
  241.3 1.5 collective-permute-start.35
  242.7 1.5 collective-permute-start.39
  245.7 9.1 %collective-permute-start.36 = (f32[32,512]{1,0:T(8,128)S(1)}, f32[32,512]{1,0:T(8,128)S(1)}, u32[]{:S(2)}, u32[]{:S(2)}) collective-permute-start(f32[32,512]{1,0:T(8,128)S(1)} %add_add_fusion.1), channel_id=1, source_target_pairs={{0,1},{1,0},{2,3},{3,2},{4,5},{5,4},{6,7},{7,6},{8,9},{9,8},{10,11... | collective-permute-start | bytes 196616 | tf_op jit(solution)/shard_map/ppermute | solution.py:528
  256.3 2.9 collective-permute-done.37
  261.6 5.1 %collective-permute-done.40.refs_8_ = bf16[512,384]{1,0:T(8,128)(2,1)} collective-permute-done((bf16[512,384]{1,0:T(8,128)(2,1)}, bf16[512,384]{1,0:T(8,128)(2,1)}, u32[]{:S(2)}, u32[]{:S(2)}) %collective-permute-start.40) | collective-permute-done | bytes 393248 | tf_op jit(solution)/shard_map/ppermute | solution.py:29
  266.7 3.7 %collective-permute-done.42.refs_10_ = bf16[384,512]{1,0:T(8,128)(2,1)} collective-permute-done((bf16[384,512]{1,0:T(8,128)(2,1)}, bf16[384,512]{1,0:T(8,128)(2,1)}, u32[]{:S(2)}, u32[]{:S(2)}) %collective-permute-start.42) | collective-permute-done | bytes 393248 | tf_op jit(solution)/shard_map/ppermute | solution.py:29
  270.4 4.7 %collective-permute-done.43.refs_11_ = bf16[384,512]{1,0:T(8,128)(2,1)} collective-permute-done((bf16[384,512]{1,0:T(8,128)(2,1)}, bf16[384,512]{1,0:T(8,128)(2,1)}, u32[]{:S(2)}, u32[]{:S(2)}) %collective-permute-start.43) | collective-permute-done | bytes 393248 | tf_op jit(solution)/shard_map/ppermute | solution.py:29
  279.6 3.7 %shard_map.99 = (f32[32,512]{1,0:T(8,128)S(1)}, f32[8,128]{1,0:T(8,128)S(1)}) custom-call(f32[32,512]{1,0:T(8,128)S(1)} %concatenate.6.prev, f32[32,512]{1,0:T(8,128)S(1)} %get-tuple-element.249.group_sums, f32[32,512]{1,0:T(8,128)S(1)} %get-tuple-element.225.whole_sums, f32[512,512]{1,0:T(8,128)S(1)} %get-tuple-element.226.refs_0_, ...), custom_call_target="tpu_custom_call" | custom-call | tf_op jit(solution)/shard_map/pallas_call | solution.py:75
  286.2 1.9 collective-permute-done.46
  288.1 1.2 collective-permute-start.47
  289.3 2.4 collective-permute-start.48
  292.5 2.2 collective-permute-done.49
  295.9 5.6 %shard_map.100 = (bf16[512,2560]{1,0:T(8,128)(2,1)}, bf16[2560,512]{1,0:T(8,128)(2,1)}) custom-call(f32[32,512]{1,0:T(8,128)S(1)} %concatenate.6.prev, f32[32,512]{1,0:T(8,128)S(1)} %get-tuple-element.232.factors, f32[32,512]{1,0:T(8,128)S(1)} %get-tuple-element.225.whole_sums, f32[8,128]{1,0:T(8,128)S(1)} %add_add_fusion.2.norms, ...), custom_call_target="tpu_custom_call" | custom-call | tf_op jit(solution)/shard_map/pallas_call | solution.py:75
  (287 shorter events, 79.9 us)
Async XLA Ops:
  14.7 47.1 %all-to-all-start = ((bf16[16,40,1024]{2,1,0:T(8,128)(2,1)}), bf16[16,40,1024]{2,1,0:T(8,128)(2,1)}, u32[]{:S(2)}, u32[]{:S(2)}) async-start(bf16[16,40,1024]{2,1,0:T(8,128)(2,1)} %pad_maximum_fusion.1), calls=%async_computation | async-start | bytes 2621440 | tf_op jit(solution)/shard_map/all_to_all | solution.py:424
  22.2 39.6 %collective-permute-start = (bf16[4096,128]{1,0:T(8,128)(2,1)}, bf16[4096,128]{1,0:T(8,128)(2,1)S(1)}, u32[]{:S(2)}, u32[]{:S(2)}) collective-permute-start(bf16[4096,128]{1,0:T(8,128)(2,1)} %get-tuple-element.129), channel_id=1, source_target_pairs={{0,2},{2,0},{4,6},{6,4},{8,10},{10,8},{12,14},{14,12},{16,18},{18,... | collective-permute-start | bytes 3145736 | tf_op jit(solution)/shard_map/ppermute | solution.py:29
  23.5 31.5 %collective-permute-start.1 = (bf16[3072,128]{1,0:T(8,128)(2,1)}, bf16[3072,128]{1,0:T(8,128)(2,1)S(1)}, u32[]{:S(2)}, u32[]{:S(2)}) collective-permute-start(bf16[3072,128]{1,0:T(8,128)(2,1)} %get-tuple-element.130), channel_id=1, source_target_pairs={{0,4},{2,6},{4,0},{6,2},{8,12},{10,14},{12,8},{14,10},{16,20},{18,... | collective-permute-start | bytes 2359304 | tf_op jit(solution)/shard_map/ppermute | solution.py:29
  24.7 37.1 %collective-permute-start.2 = (bf16[3072,128]{1,0:T(8,128)(2,1)}, bf16[3072,128]{1,0:T(8,128)(2,1)S(1)}, u32[]{:S(2)}, u32[]{:S(2)}) collective-permute-start(bf16[3072,128]{1,0:T(8,128)(2,1)} %copy-done.87), channel_id=1, source_target_pairs={{0,8},{2,10},{4,12},{6,14},{8,0},{10,2},{12,4},{14,6},{16,24},{18,... | collective-permute-start | bytes 2359304 | tf_op jit(solution)/shard_map/ppermute | solution.py:29
  63.2 28.9 %collective-permute-start.3 = (bf16[8,80,1024]{2,1,0:T(8,128)(2,1)S(1)}, bf16[8,80,1024]{2,1,0:T(8,128)(2,1)S(1)}, u32[]{:S(2)}, u32[]{:S(2)}) collective-permute-start(bf16[8,80,1024]{2,1,0:T(8,128)(2,1)S(1)} %bitcast.32), channel_id=1, source_target_pairs={{0,2},{2,0},{4,6},{6,4},{8,10},{10,8},{12,14},{14,12},{16,18},{18,... | collective-permute-start | bytes 3932168 | tf_op jit(solution)/shard_map/ppermute | solution.py:29
  64.5 28.6 %collective-permute-start.4 = (bf16[8,80,1024]{2,1,0:T(8,128)(2,1)S(1)}, bf16[8,80,1024]{2,1,0:T(8,128)(2,1)S(1)}, u32[]{:S(2)}, u32[]{:S(2)}) collective-permute-start(bf16[8,80,1024]{2,1,0:T(8,128)(2,1)S(1)} %bitcast.33), channel_id=1, source_target_pairs={{0,4},{2,6},{4,0},{6,2},{8,12},{10,14},{12,8},{14,10},{16,20},{18,... | collective-permute-start | bytes 3932168 | tf_op jit(solution)/shard_map/ppermute | solution.py:29
  66.0 28.1 %collective-permute-start.5 = (bf16[8,80,1024]{2,1,0:T(8,128)(2,1)S(1)}, bf16[8,80,1024]{2,1,0:T(8,128)(2,1)S(1)}, u32[]{:S(2)}, u32[]{:S(2)}) collective-permute-start(bf16[8,80,1024]{2,1,0:T(8,128)(2,1)S(1)} %bitcast.34), channel_id=1, source_target_pairs={{0,8},{2,10},{4,12},{6,14},{8,0},{10,2},{12,4},{14,6},{16,24},{18,... | collective-permute-start | bytes 3932168 | tf_op jit(solution)/shard_map/ppermute | solution.py:29
  94.8 24.6 %collective-permute-start.7 = (bf16[3,8,80,1024]{3,2,1,0:T(8,128)(2,1)S(1)}, bf16[3,8,80,1024]{3,2,1,0:T(8,128)(2,1)S(1)}, u32[]{:S(2)}, u32[]{:S(2)}) collective-permute-start(bf16[3,8,80,1024]{3,2,1,0:T(8,128)(2,1)S(1)} %pad_maximum_fusion.refs_1_), channel_id=1, source_target_pairs={{0,1},{1,0},{2,3},{3,2},{4,5},{5,4},{6,7},{7,6},{8,9},{9,8},{10,11... | collective-permute-start | bytes 11796488 | tf_op jit(solution)/shard_map/ppermute | solution.py:29
  97.9 21.5 %collective-permute-start.6 = (bf16[8,80,1024]{2,1,0:T(8,128)(2,1)S(1)}, bf16[8,80,1024]{2,1,0:T(8,128)(2,1)S(1)}, u32[]{:S(2)}, u32[]{:S(2)}) collective-permute-start(bf16[8,80,1024]{2,1,0:T(8,128)(2,1)S(1)} %bitcast.35), channel_id=1, source_target_pairs={{0,1},{1,0},{2,3},{3,2},{4,5},{5,4},{6,7},{7,6},{8,9},{9,8},{10,11... | collective-permute-start | bytes 3932168 | tf_op jit(solution)/shard_map/ppermute | solution.py:29
  104.5 14.0 %collective-permute-start.10 = (bf16[320,896]{1,0:T(8,128)(2,1)S(1)}, bf16[320,896]{1,0:T(8,128)(2,1)S(1)}, u32[]{:S(2)}, u32[]{:S(2)}) collective-permute-start(bf16[320,896]{1,0:T(8,128)(2,1)S(1)} %get-tuple-element.165), channel_id=1, source_target_pairs={{0,8},{2,10},{4,12},{6,14},{8,0},{10,2},{12,4},{14,6},{16,24},{18,... | collective-permute-start | bytes 1720328 | tf_op jit(solution)/shard_map/ppermute | solution.py:29
  104.5 14.0 %collective-permute-start.9 = (bf16[320,896]{1,0:T(8,128)(2,1)S(1)}, bf16[320,896]{1,0:T(8,128)(2,1)S(1)}, u32[]{:S(2)}, u32[]{:S(2)}) collective-permute-start(bf16[320,896]{1,0:T(8,128)(2,1)S(1)} %get-tuple-element.164), channel_id=1, source_target_pairs={{0,4},{2,6},{4,0},{6,2},{8,12},{10,14},{12,8},{14,10},{16,20},{18,... | collective-permute-start | bytes 1720328 | tf_op jit(solution)/shard_map/ppermute | solution.py:29
  104.5 11.7 %collective-permute-start.8 = (bf16[320,768]{1,0:T(8,128)(2,1)S(1)}, bf16[320,768]{1,0:T(8,128)(2,1)S(1)}, u32[]{:S(2)}, u32[]{:S(2)}) collective-permute-start(bf16[320,768]{1,0:T(8,128)(2,1)S(1)} %get-tuple-element.163), channel_id=1, source_target_pairs={{0,2},{2,0},{4,6},{6,4},{8,10},{10,8},{12,14},{14,12},{16,18},{18,... | collective-permute-start | bytes 1474568 | tf_op jit(solution)/shard_map/ppermute | solution.py:29
  118.8 8.9 %collective-permute-start.11 = (bf16[160,768]{1,0:T(8,128)(2,1)S(1)}, bf16[160,768]{1,0:T(8,128)(2,1)S(1)}, u32[]{:S(2)}, u32[]{:S(2)}) collective-permute-start(bf16[160,768]{1,0:T(8,128)(2,1)S(1)} %get-tuple-element.172), channel_id=1, source_target_pairs={{0,2},{2,0},{4,6},{6,4},{8,10},{10,8},{12,14},{14,12},{16,18},{18,... | collective-permute-start | bytes 737288 | tf_op jit(solution)/shard_map/ppermute | solution.py:29
  124.1 22.1 %collective-permute-start.18 = (bf16[320,768]{1,0:T(8,128)(2,1)S(1)}, bf16[320,768]{1,0:T(8,128)(2,1)S(1)}, u32[]{:S(2)}, u32[]{:S(2)}) collective-permute-start(bf16[320,768]{1,0:T(8,128)(2,1)S(1)} %get-tuple-element.185), channel_id=1, source_target_pairs={{0,2},{2,0},{4,6},{6,4},{8,10},{10,8},{12,14},{14,12},{16,18},{18,... | collective-permute-start | bytes 1474568 | tf_op jit(solution)/shard_map/ppermute | solution.py:29
  125.1 24.3 %collective-permute-start.19 = (bf16[320,896]{1,0:T(8,128)(2,1)S(1)}, bf16[320,896]{1,0:T(8,128)(2,1)S(1)}, u32[]{:S(2)}, u32[]{:S(2)}) collective-permute-start(bf16[320,896]{1,0:T(8,128)(2,1)S(1)} %get-tuple-element.186), channel_id=1, source_target_pairs={{0,4},{2,6},{4,0},{6,2},{8,12},{10,14},{12,8},{14,10},{16,20},{18,... | collective-permute-start | bytes 1720328 | tf_op jit(solution)/shard_map/ppermute | solution.py:29
  125.1 24.3 %collective-permute-start.20 = (bf16[320,896]{1,0:T(8,128)(2,1)S(1)}, bf16[320,896]{1,0:T(8,128)(2,1)S(1)}, u32[]{:S(2)}, u32[]{:S(2)}) collective-permute-start(bf16[320,896]{1,0:T(8,128)(2,1)S(1)} %get-tuple-element.187), channel_id=1, source_target_pairs={{0,8},{2,10},{4,12},{6,14},{8,0},{10,2},{12,4},{14,6},{16,24},{18,... | collective-permute-start | bytes 1720328 | tf_op jit(solution)/shard_map/ppermute | solution.py:29
  126.3 17.5 %collective-permute-start.12 = (bf16[160,896]{1,0:T(8,128)(2,1)S(1)}, bf16[160,896]{1,0:T(8,128)(2,1)S(1)}, u32[]{:S(2)}, u32[]{:S(2)}) collective-permute-start(bf16[160,896]{1,0:T(8,128)(2,1)S(1)} %get-tuple-element.173), channel_id=1, source_target_pairs={{0,4},{2,6},{4,0},{6,2},{8,12},{10,14},{12,8},{14,10},{16,20},{18,... | collective-permute-start | bytes 860168 | tf_op jit(solution)/shard_map/ppermute | solution.py:29
  127.7 16.0 %collective-permute-start.13 = (bf16[160,896]{1,0:T(8,128)(2,1)S(1)}, bf16[160,896]{1,0:T(8,128)(2,1)S(1)}, u32[]{:S(2)}, u32[]{:S(2)}) collective-permute-start(bf16[160,896]{1,0:T(8,128)(2,1)S(1)} %get-tuple-element.174), channel_id=1, source_target_pairs={{0,8},{2,10},{4,12},{6,14},{8,0},{10,2},{12,4},{14,6},{16,24},{18,... | collective-permute-start | bytes 860168 | tf_op jit(solution)/shard_map/ppermute | solution.py:29
  144.5 7.8 %collective-permute-start.14 = (bf16[160,768]{1,0:T(8,128)(2,1)S(1)}, bf16[160,768]{1,0:T(8,128)(2,1)S(1)}, u32[]{:S(2)}, u32[]{:S(2)}) collective-permute-start(bf16[160,768]{1,0:T(8,128)(2,1)S(1)} %get-tuple-element.175.refs_0_), channel_id=1, source_target_pairs={{0,2},{2,0},{4,6},{6,4},{8,10},{10,8},{12,14},{14,12},{16,18},{18,... | collective-permute-start | bytes 737288 | tf_op jit(solution)/shard_map/ppermute | solution.py:29
  145.1 8.2 %collective-permute-start.15 = (bf16[160,896]{1,0:T(8,128)(2,1)S(1)}, bf16[160,896]{1,0:T(8,128)(2,1)S(1)}, u32[]{:S(2)}, u32[]{:S(2)}) collective-permute-start(bf16[160,896]{1,0:T(8,128)(2,1)S(1)} %get-tuple-element.176.refs_1_), channel_id=1, source_target_pairs={{0,4},{2,6},{4,0},{6,2},{8,12},{10,14},{12,8},{14,10},{16,20},{18,... | collective-permute-start | bytes 860168 | tf_op jit(solution)/shard_map/ppermute | solution.py:29
  146.3 7.0 %collective-permute-start.16 = (bf16[160,896]{1,0:T(8,128)(2,1)S(1)}, bf16[160,896]{1,0:T(8,128)(2,1)S(1)}, u32[]{:S(2)}, u32[]{:S(2)}) collective-permute-start(bf16[160,896]{1,0:T(8,128)(2,1)S(1)} %get-tuple-element.177.refs_2_), channel_id=1, source_target_pairs={{0,8},{2,10},{4,12},{6,14},{8,0},{10,2},{12,4},{14,6},{16,24},{18,... | collective-permute-start | bytes 860168 | tf_op jit(solution)/shard_map/ppermute | solution.py:29
  151.4 6.3 %collective-permute-start.22 = (bf16[160,896]{1,0:T(8,128)(2,1)S(1)}, bf16[160,896]{1,0:T(8,128)(2,1)S(1)}, u32[]{:S(2)}, u32[]{:S(2)}) collective-permute-start(bf16[160,896]{1,0:T(8,128)(2,1)S(1)} %get-tuple-element.195), channel_id=1, source_target_pairs={{0,4},{2,6},{4,0},{6,2},{8,12},{10,14},{12,8},{14,10},{16,20},{18,... | collective-permute-start | bytes 860168 | tf_op jit(solution)/shard_map/ppermute | solution.py:29
  151.6 7.9 %collective-permute-start.23 = (bf16[160,896]{1,0:T(8,128)(2,1)S(1)}, bf16[160,896]{1,0:T(8,128)(2,1)S(1)}, u32[]{:S(2)}, u32[]{:S(2)}) collective-permute-start(bf16[160,896]{1,0:T(8,128)(2,1)S(1)} %get-tuple-element.196), channel_id=1, source_target_pairs={{0,8},{2,10},{4,12},{6,14},{8,0},{10,2},{12,4},{14,6},{16,24},{18,... | collective-permute-start | bytes 860168 | tf_op jit(solution)/shard_map/ppermute | solution.py:29
  152.3 5.3 %collective-permute-start.21 = (bf16[160,768]{1,0:T(8,128)(2,1)S(1)}, bf16[160,768]{1,0:T(8,128)(2,1)S(1)}, u32[]{:S(2)}, u32[]{:S(2)}) collective-permute-start(bf16[160,768]{1,0:T(8,128)(2,1)S(1)} %get-tuple-element.194), channel_id=1, source_target_pairs={{0,2},{2,0},{4,6},{6,4},{8,10},{10,8},{12,14},{14,12},{16,18},{18,... | collective-permute-start | bytes 737288 | tf_op jit(solution)/shard_map/ppermute | solution.py:29
  153.4 22.1 %collective-permute-start.17 = (bf16[320,768]{1,0:T(8,128)(2,1)S(1)}, bf16[320,768]{1,0:T(8,128)(2,1)S(1)}, u32[]{:S(2)}, u32[]{:S(2)}) collective-permute-start(bf16[320,768]{1,0:T(8,128)(2,1)S(1)} %get-tuple-element.178.refs_12_), channel_id=1, source_target_pairs={{0,2},{2,0},{4,6},{6,4},{8,10},{10,8},{12,14},{14,12},{16,18},{18,... | collective-permute-start | bytes 1474568 | tf_op jit(solution)/shard_map/ppermute | solution.py:29
  160.3 11.5 %collective-permute-start.25 = (bf16[160,896]{1,0:T(8,128)(2,1)S(1)}, bf16[160,896]{1,0:T(8,128)(2,1)S(1)}, u32[]{:S(2)}, u32[]{:S(2)}) collective-permute-start(bf16[160,896]{1,0:T(8,128)(2,1)S(1)} %get-tuple-element.198.refs_1_), channel_id=1, source_target_pairs={{0,4},{2,6},{4,0},{6,2},{8,12},{10,14},{12,8},{14,10},{16,20},{18,... | collective-permute-start | bytes 860168 | tf_op jit(solution)/shard_map/ppermute | solution.py:29
  160.4 11.4 %collective-permute-start.26 = (bf16[160,896]{1,0:T(8,128)(2,1)S(1)}, bf16[160,896]{1,0:T(8,128)(2,1)S(1)}, u32[]{:S(2)}, u32[]{:S(2)}) collective-permute-start(bf16[160,896]{1,0:T(8,128)(2,1)S(1)} %get-tuple-element.199.refs_2_), channel_id=1, source_target_pairs={{0,8},{2,10},{4,12},{6,14},{8,0},{10,2},{12,4},{14,6},{16,24},{18,... | collective-permute-start | bytes 860168 | tf_op jit(solution)/shard_map/ppermute | solution.py:29
  162.0 9.3 %collective-permute-start.24 = (bf16[160,768]{1,0:T(8,128)(2,1)S(1)}, bf16[160,768]{1,0:T(8,128)(2,1)S(1)}, u32[]{:S(2)}, u32[]{:S(2)}) collective-permute-start(bf16[160,768]{1,0:T(8,128)(2,1)S(1)} %get-tuple-element.197.refs_0_), channel_id=1, source_target_pairs={{0,2},{2,0},{4,6},{6,4},{8,10},{10,8},{12,14},{14,12},{16,18},{18,... | collective-permute-start | bytes 737288 | tf_op jit(solution)/shard_map/ppermute | solution.py:29
  162.9 14.4 %collective-permute-start.28 = (bf16[320,896]{1,0:T(8,128)(2,1)S(1)}, bf16[320,896]{1,0:T(8,128)(2,1)S(1)}, u32[]{:S(2)}, u32[]{:S(2)}) collective-permute-start(bf16[320,896]{1,0:T(8,128)(2,1)S(1)} %get-tuple-element.201.refs_16_), channel_id=1, source_target_pairs={{0,4},{2,6},{4,0},{6,2},{8,12},{10,14},{12,8},{14,10},{16,20},{18,... | collective-permute-start | bytes 1720328 | tf_op jit(solution)/shard_map/ppermute | solution.py:29
  171.2 9.9 %collective-permute-start.30 = (bf16[320,896]{1,0:T(8,128)(2,1)S(1)}, bf16[320,896]{1,0:T(8,128)(2,1)S(1)}, u32[]{:S(2)}, u32[]{:S(2)}) collective-permute-start(bf16[320,896]{1,0:T(8,128)(2,1)S(1)} %get-tuple-element.203.refs_20_), channel_id=1, source_target_pairs={{0,8},{2,10},{4,12},{6,14},{8,0},{10,2},{12,4},{14,6},{16,24},{18,... | collective-permute-start | bytes 1720328 | tf_op jit(solution)/shard_map/ppermute | solution.py:29
  172.9 15.2 %collective-permute-start.29 = (bf16[320,896]{1,0:T(8,128)(2,1)S(1)}, bf16[320,896]{1,0:T(8,128)(2,1)}, u32[]{:S(2)}, u32[]{:S(2)}) collective-permute-start(bf16[320,896]{1,0:T(8,128)(2,1)S(1)} %get-tuple-element.202.refs_18_), channel_id=1, source_target_pairs={{0,4},{2,6},{4,0},{6,2},{8,12},{10,14},{12,8},{14,10},{16,20},{18,... | collective-permute-start | bytes 1720328 | tf_op jit(solution)/shard_map/ppermute | solution.py:29
  174.6 18.9 %collective-permute-start.31 = (bf16[320,896]{1,0:T(8,128)(2,1)}, bf16[320,896]{1,0:T(8,128)(2,1)}, u32[]{:S(2)}, u32[]{:S(2)}) collective-permute-start(bf16[320,896]{1,0:T(8,128)(2,1)} %get-tuple-element.204.refs_22_), channel_id=1, source_target_pairs={{0,8},{2,10},{4,12},{6,14},{8,0},{10,2},{12,4},{14,6},{16,24},{18,... | collective-permute-start | bytes 1720328 | tf_op jit(solution)/shard_map/ppermute | solution.py:29
  176.4 8.2 %collective-permute-start.27 = (bf16[320,768]{1,0:T(8,128)(2,1)}, bf16[320,768]{1,0:T(8,128)(2,1)}, u32[]{:S(2)}, u32[]{:S(2)}) collective-permute-start(bf16[320,768]{1,0:T(8,128)(2,1)} %get-tuple-element.200.refs_14_), channel_id=1, source_target_pairs={{0,2},{2,0},{4,6},{6,4},{8,10},{10,8},{12,14},{14,12},{16,18},{18,... | collective-permute-start | bytes 1474568 | tf_op jit(solution)/shard_map/ppermute | solution.py:29
  236.2 3.1 %collective-permute-start.32 = (f32[32,512]{1,0:T(8,128)S(1)}, f32[32,512]{1,0:T(8,128)S(1)}, u32[]{:S(2)}, u32[]{:S(2)}) collective-permute-start(f32[32,512]{1,0:T(8,128)S(1)} %get-tuple-element.218), channel_id=1, source_target_pairs={{0,2},{2,0},{4,6},{6,4},{8,10},{10,8},{12,14},{14,12},{16,18},{18,... | collective-permute-start | bytes 196616 | tf_op jit(solution)/shard_map/ppermute | solution.py:29
  237.2 3.1 %collective-permute-start.33 = (f32[32,512]{1,0:T(8,128)S(1)}, f32[32,512]{1,0:T(8,128)S(1)}, u32[]{:S(2)}, u32[]{:S(2)}) collective-permute-start(f32[32,512]{1,0:T(8,128)S(1)} %get-tuple-element.218), channel_id=1, source_target_pairs={{0,4},{2,6},{4,0},{6,2},{8,12},{10,14},{12,8},{14,10},{16,20},{18,... | collective-permute-start | bytes 196616 | tf_op jit(solution)/shard_map/ppermute | solution.py:29
  237.2 4.0 %collective-permute-start.34 = (f32[32,512]{1,0:T(8,128)S(1)}, f32[32,512]{1,0:T(8,128)S(1)}, u32[]{:S(2)}, u32[]{:S(2)}) collective-permute-start(f32[32,512]{1,0:T(8,128)S(1)} %get-tuple-element.218), channel_id=1, source_target_pairs={{0,6},{2,4},{4,2},{6,0},{8,14},{10,12},{12,10},{14,8},{16,22},{18,... | collective-permute-start | bytes 196616 | tf_op jit(solution)/shard_map/ppermute | solution.py:29
  241.3 13.5 %collective-permute-start.35 = (f32[32,512]{1,0:T(8,128)S(1)}, f32[32,512]{1,0:T(8,128)S(1)}, u32[]{:S(2)}, u32[]{:S(2)}) collective-permute-start(f32[32,512]{1,0:T(8,128)S(1)} %add_add_fusion.1), channel_id=1, source_target_pairs={{0,8},{2,10},{4,12},{6,14},{8,0},{10,2},{12,4},{14,6},{16,24},{18,... | collective-permute-start | bytes 196616 | tf_op jit(solution)/shard_map/ppermute | solution.py:29
  242.7 16.6 %collective-permute-start.39 = (bf16[512,384]{1,0:T(8,128)(2,1)S(1)}, bf16[512,384]{1,0:T(8,128)(2,1)S(1)}, u32[]{:S(2)}, u32[]{:S(2)}) collective-permute-start(bf16[512,384]{1,0:T(8,128)(2,1)S(1)} %get-tuple-element.220.refs_4_), channel_id=1, source_target_pairs={{0,4},{2,6},{4,0},{6,2},{8,12},{10,14},{12,8},{14,10},{16,20},{18,... | collective-permute-start | bytes 1179656 | tf_op jit(solution)/shard_map/ppermute | solution.py:29
  244.2 30.9 %collective-permute-start.38 = (bf16[512,512]{1,0:T(8,128)(2,1)}, bf16[512,512]{1,0:T(8,128)(2,1)}, u32[]{:S(2)}, u32[]{:S(2)}) collective-permute-start(bf16[512,512]{1,0:T(8,128)(2,1)} %get-tuple-element.219.refs_3_), channel_id=1, source_target_pairs={{0,2},{2,0},{4,6},{6,4},{8,10},{10,8},{12,14},{14,12},{16,18},{18,... | collective-permute-start | bytes 1572872 | tf_op jit(solution)/shard_map/ppermute | solution.py:29
  244.7 30.4 %collective-permute-start.41 = (bf16[512,512]{1,0:T(8,128)(2,1)}, bf16[512,512]{1,0:T(8,128)(2,1)}, u32[]{:S(2)}, u32[]{:S(2)}) collective-permute-start(bf16[512,512]{1,0:T(8,128)(2,1)} %get-tuple-element.222.refs_9_), channel_id=1, source_target_pairs={{0,2},{2,0},{4,6},{6,4},{8,10},{10,8},{12,14},{14,12},{16,18},{18,... | collective-permute-start | bytes 1572872 | tf_op jit(solution)/shard_map/ppermute | solution.py:29
  245.7 10.0 %collective-permute-start.36 = (f32[32,512]{1,0:T(8,128)S(1)}, f32[32,512]{1,0:T(8,128)S(1)}, u32[]{:S(2)}, u32[]{:S(2)}) collective-permute-start(f32[32,512]{1,0:T(8,128)S(1)} %add_add_fusion.1), channel_id=1, source_target_pairs={{0,1},{1,0},{2,3},{3,2},{4,5},{5,4},{6,7},{7,6},{8,9},{9,8},{10,11... | collective-permute-start | bytes 196616 | tf_op jit(solution)/shard_map/ppermute | solution.py:528
  254.8 4.4 %collective-permute-start.37 = (f32[32,512]{1,0:T(8,128)S(1)}, f32[32,512]{1,0:T(8,128)S(1)}, u32[]{:S(2)}, u32[]{:S(2)}) collective-permute-start(f32[32,512]{1,0:T(8,128)S(1)} %add_add_fusion.1), channel_id=1, source_target_pairs={{0,9},{1,8},{2,11},{3,10},{4,13},{5,12},{6,15},{7,14},{8,1},{9,0},... | collective-permute-start | bytes 196616 | tf_op jit(solution)/shard_map/ppermute | solution.py:528
  255.7 11.0 %collective-permute-start.40 = (bf16[512,384]{1,0:T(8,128)(2,1)}, bf16[512,384]{1,0:T(8,128)(2,1)}, u32[]{:S(2)}, u32[]{:S(2)}) collective-permute-start(bf16[512,384]{1,0:T(8,128)(2,1)} %get-tuple-element.221.refs_5_), channel_id=1, source_target_pairs={{0,8},{2,10},{4,12},{6,14},{8,0},{10,2},{12,4},{14,6},{16,24},{18,... | collective-permute-start | bytes 1179656 | tf_op jit(solution)/shard_map/ppermute | solution.py:29
  259.1 11.3 %collective-permute-start.42 = (bf16[384,512]{1,0:T(8,128)(2,1)}, bf16[384,512]{1,0:T(8,128)(2,1)}, u32[]{:S(2)}, u32[]{:S(2)}) collective-permute-start(bf16[384,512]{1,0:T(8,128)(2,1)} %get-tuple-element.223.refs_10_), channel_id=1, source_target_pairs={{0,4},{2,6},{4,0},{6,2},{8,12},{10,14},{12,8},{14,10},{16,20},{18,... | collective-permute-start | bytes 1179656 | tf_op jit(solution)/shard_map/ppermute | solution.py:29
  260.1 15.1 %collective-permute-start.43 = (bf16[384,512]{1,0:T(8,128)(2,1)}, bf16[384,512]{1,0:T(8,128)(2,1)}, u32[]{:S(2)}, u32[]{:S(2)}) collective-permute-start(bf16[384,512]{1,0:T(8,128)(2,1)} %get-tuple-element.224.refs_11_), channel_id=1, source_target_pairs={{0,8},{2,10},{4,12},{6,14},{8,0},{10,2},{12,4},{14,6},{16,24},{18,... | collective-permute-start | bytes 1179656 | tf_op jit(solution)/shard_map/ppermute | solution.py:29
  284.7 3.4 %collective-permute-start.46 = (f32[8,128]{1,0:T(8,128)S(1)}, f32[8,128]{1,0:T(8,128)S(1)}, u32[]{:S(2)}, u32[]{:S(2)}) collective-permute-start(f32[8,128]{1,0:T(8,128)S(1)} %get-tuple-element.233), channel_id=1, source_target_pairs={{0,6},{2,4},{4,2},{6,0},{8,14},{10,12},{12,10},{14,8},{16,22},{18,... | collective-permute-start | bytes 12296 | tf_op jit(solution)/shard_map/ppermute | solution.py:29
  288.1 4.0 %collective-permute-start.47 = (f32[8,128]{1,0:T(8,128)S(1)}, f32[8,128]{1,0:T(8,128)S(1)}, u32[]{:S(2)}, u32[]{:S(2)}) collective-permute-start(f32[8,128]{1,0:T(8,128)S(1)} %add_add_fusion.3), channel_id=1, source_target_pairs={{0,8},{2,10},{4,12},{6,14},{8,0},{10,2},{12,4},{14,6},{16,24},{18,... | collective-permute-start | bytes 12296 | tf_op jit(solution)/shard_map/ppermute | solution.py:29
  289.3 3.2 %collective-permute-start.48 = (f32[8,128]{1,0:T(8,128)S(1)}, f32[8,128]{1,0:T(8,128)S(1)}, u32[]{:S(2)}, u32[]{:S(2)}) collective-permute-start(f32[8,128]{1,0:T(8,128)S(1)} %add_add_fusion.3), channel_id=1, source_target_pairs={{0,1},{1,0},{2,3},{3,2},{4,5},{5,4},{6,7},{7,6},{8,9},{9,8},{10,11... | collective-permute-start | bytes 12296 | tf_op jit(solution)/shard_map/ppermute | solution.py:528
  (94 other events, 614.6 us)

commit v5 on v4

--- a/solution.py
+++ b/solution.py
@@ -21,7 +21,7 @@
 MASKS = (1, 2, 4)
 
 MIB = 1024 * 1024
-CUT_MIB = 14
+CUT_MIB = 44
 
 
 def swap(value, mask, axis="expert"):
@@ -226,9 +226,13 @@
 
     value_copies, row_copies = {}, {}
     for k in range(3):
-        axis = packed_place(1, matrix, k, halves)[0]
+        axis, at = packed_place(1, matrix, k, halves)
         row_copies[k] = copies(k, rows[4 * k : 4 * k + 4], row_buffers.at[k])
-        value_copies[k] = copies(3 + axis, values[4 * axis : 4 * axis + 4], value_buffers[axis])
+        parts, buffer = values[4 * axis : 4 * axis + 4], value_buffers[axis]
+        if all(half % 128 == 0 for half in halves):
+            parts = [value.at[:, at : at + halves[k]] for value in parts]
+            buffer = buffer.at[:, at : at + halves[k]]
+        value_copies[k] = copies(3 + axis, parts, buffer)
         for copy in row_copies[k] + value_copies[k]:
             copy.start()
     for k in range(3):
@@ -420,7 +424,6 @@
         return routed.reshape(places, part_cap, block_width)
 
     routed = jnp.concatenate([route(tokens), route(cotangent)], axis=2)
-    routed, own_weights = lax.optimization_barrier((routed, cuts[:6]))
     got = lax.all_to_all(routed, "expert", split_axis=0, concat_axis=0, tiled=True)
     got, got_weights = lax.optimization_barrier((got, got_weights))
     got = got.reshape(places // GROUP, GROUP, part_cap, 2 * block_width).transpose(1, 0, 2, 3)
@@ -444,7 +447,7 @@
     def sums(chain, side, out_shapes):
         kernel = functools.partial(sums_kernel, side, halves, is_packed)
         outs = call(
-            kernel, 20, row_shapes + out_shapes, *blocks[chain], *own_weights, *got_weights,
+            kernel, 40, row_shapes + out_shapes, *blocks[chain], *cuts[:6], *got_weights,
             streamed_out=range(6),
         )
         return outs[:6], outs[6:]
@@ -483,7 +486,7 @@
     hidden_pick = lax.dynamic_index_in_dim(hidden_states, expert, 1, keepdims=False)
     sums_shape = (6, 8, wide)
     outs = call(
-        functools.partial(grad_out_kernel, halves), 28,
+        functools.partial(grad_out_kernel, halves), 56,
         [shape((half, block_width), f32) for half in halves]
         + [shape((half, block_width), bf16) for half in halves]
         + [shape(sums_shape, f32)],
@@ -493,7 +496,7 @@
     out_own, out_sent, out_sums = outs[:3], outs[3:6], outs[6]
     got_out = along_axes(out_sent)
     outs = call(
-        functools.partial(grad_in_kernel, halves), 28,
+        functools.partial(grad_in_kernel, halves), 56,
         [shape((block_width, half), f32) for half in halves]
         + [shape((block_width, half), bf16) for half in halves]
         + [shape((STAT_ROWS, lanes), f32)],
@@ -530,17 +533,18 @@
         cube = values + swap(values, 4)
         return cube, cube + (other(0, 1) + other(4, 1))
 
+    stats, got_out = lax.optimization_barrier((stats, got_out))
     group_sums, whole_sums = totals(stats)
-    whole_sums, got_in, got_out = lax.optimization_barrier((whole_sums, got_in, got_out))
+    whole_sums, got_in = lax.optimization_barrier((whole_sums, got_in))
     factors, norms = call(
-        norm_kernel, 20,
+        norm_kernel, 52,
         [shape((STAT_ROWS, lanes), f32), shape((8, 128), f32)],
         prev, group_sums, whole_sums, *in_own, *in_sent, *out_own, *out_sent,
         streamed=range(3, 15),
     )
     norms = totals(norms)[1]
     update_in, update_out = call(
-        functools.partial(final_kernel, bounds), 24,
+        functools.partial(final_kernel, bounds), 52,
         [shape(local_in.shape, bf16), shape(local_out.shape, bf16)],
         prev, factors, whole_sums, norms, *in_own, *out_own, *got_in, *got_out,
         streamed=range(4, 16), streamed_out=range(2),

time: 303 us -> 262 us (0.86)
  local copies, waits for them, and re-layouts: 50.2 us -> 15.7 us
  waiting for transfers between devices: 142 us -> 122 us
  Pallas kernels: 43 us -> 50.5 us
  starting transfers between devices: 59.4 us -> 64.4 us
    unnamed x185 -> x113, local copies, waits for them, and re-layouts: 48 us -> 12.9 us
    ppermute x46, waiting for transfers between devices: 136 us -> 117 us  [swap(): return lax.ppermute(value, axis, pairs)]
    pallas_call x15, Pallas kernels: 43 us -> 50.5 us  [call(): pl.pallas_call(kernel, out_shape=out_shape, in_specs=[spec(value, n, stre...]
    ppermute x4, starting transfers between devices: 12 us -> 17.3 us  [other(): return lax.ppermute(values, ('expert', 'ffn'), moves)]
  transfers between devices with their start and end apart: 51 -> 51, of which waited for: 27 -> 20; matrix products, arithmetic and copies ran while one was open for 0% -> 1% of each run, Pallas kernels for 4% -> 12%
where the time goes in v5:
time: 262 us; the launch traced here: 261 us
  waiting for transfers between devices  122 us (47%)
  starting transfers between devices  64.4 us (25%)
  Pallas kernels  50.5 us (19%)
  local copies, waits for them, and re-layouts  15.7 us (6%)
  other arithmetic  6.69 us (3%)
    ppermute x46, waiting for transfers between devices, swap(): return lax.ppermute(value, axis, pairs)  117 us
    pallas_call x15, Pallas kernels, call(): pl.pallas_call(kernel, out_shape=out_shape, in_specs=[spec(value, n, stre...  50.5 us
    ppermute x46, starting transfers between devices, swap(): return lax.ppermute(value, axis, pairs)  39.4 us
    ppermute x4, starting transfers between devices, other(): return lax.ppermute(values, ('expert', 'ffn'), moves)  17.3 us
    unnamed x113, local copies, waits for them, and re-layouts  12.9 us
    all_to_all x1, starting transfers between devices, shards(): lax.all_to_all(routed, 'expert', split_axis=0, concat_axis=0, tiled=True)  7.74 us
  transfers between devices with their start and end apart: 51, of which 20 were waited for; matrix products, arithmetic and copies ran while one was open for 1% of the time, Pallas kernels for 12%

profile of v5, /device:TPU:1, one launch (start us, length us, event | category | flops | bytes accessed | tf_op | source)
XLA Modules:
  0.0 261.1 jit_solution(13262168267260075204)
XLA Ops:
  5.5 1.2 pad_maximum_fusion.1
  6.7 7.7 %all-to-all-start = ((bf16[16,40,1024]{2,1,0:T(8,128)(2,1)}), bf16[16,40,1024]{2,1,0:T(8,128)(2,1)}, u32[]{:S(2)}, u32[]{:S(2)}) async-start(bf16[16,40,1024]{2,1,0:T(8,128)(2,1)} %pad_maximum_fusion.1), calls=%async_computation | async-start | bytes 2621440 | tf_op jit(solution)/shard_map/all_to_all | solution.py:427
  14.5 2.1 shard_map.86
  19.7 1.3 collective-permute-start
  21.0 1.2 collective-permute-start.1
  22.2 1.2 collective-permute-start.2
  23.4 24.3 %collective-permute-done.1.refs_9_.refs_12_ = bf16[3072,128]{1,0:T(8,128)(2,1)S(1)} collective-permute-done((bf16[3072,128]{1,0:T(8,128)(2,1)S(1)}, bf16[3072,128]{1,0:T(8,128)(2,1)S(1)}, u32[]{:S(2)}, u32[]{:S(2)}) %collective-permute-start.1) | collective-permute-done | bytes 786464 | tf_op jit(solution)/shard_map/ppermute | solution.py:29
  47.7 6.4 %collective-permute-done.2.refs_10_.refs_13_ = bf16[3072,128]{1,0:T(8,128)(2,1)S(1)} collective-permute-done((bf16[3072,128]{1,0:T(8,128)(2,1)S(1)}, bf16[3072,128]{1,0:T(8,128)(2,1)S(1)}, u32[]{:S(2)}, u32[]{:S(2)}) %collective-permute-start.2) | collective-permute-done | bytes 786464 | tf_op jit(solution)/shard_map/ppermute | solution.py:29
  54.1 1.4 copy.11
  55.5 1.2 collective-permute-start.3
  56.8 1.6 collective-permute-start.4
  59.2 25.0 %collective-permute-done.3 = bf16[8,80,1024]{2,1,0:T(8,128)(2,1)S(1)} collective-permute-done((bf16[8,80,1024]{2,1,0:T(8,128)(2,1)S(1)}, bf16[8,80,1024]{2,1,0:T(8,128)(2,1)S(1)}, u32[]{:S(2)}, u32[]{:S(2)}) %collective-permute-start.3) | collective-permute-done | bytes 1310752 | tf_op jit(solution)/shard_map/ppermute | solution.py:29
  85.1 1.4 collective-permute-done.5
  86.5 2.1 pad_maximum_fusion.refs_1_
  88.6 3.0 %collective-permute-start.7 = (bf16[3,8,80,1024]{3,2,1,0:T(8,128)(2,1)}, bf16[3,8,80,1024]{3,2,1,0:T(8,128)(2,1)}, u32[]{:S(2)}, u32[]{:S(2)}) collective-permute-start(bf16[3,8,80,1024]{3,2,1,0:T(8,128)(2,1)} %pad_maximum_fusion.refs_1_), channel_id=1, source_target_pairs={{0,1},{1,0},{2,3},{3,2},{4,5},{5,4},{6,7},{7,6},{8,9},{9,8},{10,11... | collective-permute-start | bytes 11796488 | tf_op jit(solution)/shard_map/ppermute | solution.py:29
  91.7 4.3 %shard_map.88 = (bf16[320,1024]{1,0:T(8,128)(2,1)S(1)}, bf16[320,1024]{1,0:T(8,128)(2,1)S(1)}, bf16[320,1024]{1,0:T(8,128)(2,1)S(1)}, bf16[320,1024]{1,0:T(8,128...) custom-call(bf16[8,80,1024]{2,1,0:T(8,128)(2,1)S(1)} %bitcast.36, ...), custom_call_target="tpu_custom_call" | custom-call | tf_op jit(solution)/shard_map/pallas_call | solution.py:75
  99.6 4.3 %shard_map.87 = (bf16[320,1024]{1,0:T(8,128)(2,1)S(1)}, bf16[320,1024]{1,0:T(8,128)(2,1)S(1)}, bf16[320,1024]{1,0:T(8,128)(2,1)S(1)}, bf16[320,1024]{1,0:T(8,128...) custom-call(bf16[8,80,1024]{2,1,0:T(8,128)(2,1)S(1)} %bitcast.37, ...), custom_call_target="tpu_custom_call" | custom-call | tf_op jit(solution)/shard_map/pallas_call | solution.py:75
  104.0 7.0 %collective-permute-done.8.refs_6_ = bf16[320,768]{1,0:T(8,128)(2,1)S(1)} collective-permute-done((bf16[320,768]{1,0:T(8,128)(2,1)S(1)}, bf16[320,768]{1,0:T(8,128)(2,1)S(1)}, u32[]{:S(2)}, u32[]{:S(2)}) %collective-permute-start.8) | collective-permute-done | bytes 491552 | tf_op jit(solution)/shard_map/ppermute | solution.py:29
  111.0 1.6 collective-permute-done.10.refs_8_
  113.6 4.3 %shard_map.90 = (bf16[320,1024]{1,0:T(8,128)(2,1)S(1)}, bf16[320,1024]{1,0:T(8,128)(2,1)S(1)}, bf16[320,1024]{1,0:T(8,128)(2,1)S(1)}, bf16[320,1024]{1,0:T(8,128...) custom-call(bf16[8,80,1024]{2,1,0:T(8,128)(2,1)S(1)} %collective-per, ...), custom_call_target="tpu_custom_call" | custom-call | tf_op jit(solution)/shard_map/pallas_call | solution.py:75
  120.4 1.4 collective-permute-start.18
  122.5 1.5 collective-permute-start.12
  124.7 15.5 %collective-permute-done.12.refs_7_ = bf16[160,896]{1,0:T(8,128)(2,1)S(1)} collective-permute-done((bf16[160,896]{1,0:T(8,128)(2,1)S(1)}, bf16[160,896]{1,0:T(8,128)(2,1)S(1)}, u32[]{:S(2)}, u32[]{:S(2)}) %collective-permute-start.12) | collective-permute-done | bytes 286752 | tf_op jit(solution)/shard_map/ppermute | solution.py:29
  143.2 4.3 %shard_map.89 = (bf16[320,1024]{1,0:T(8,128)(2,1)S(1)}, bf16[320,1024]{1,0:T(8,128)(2,1)S(1)}, bf16[320,1024]{1,0:T(8,128)(2,1)S(1)}, bf16[320,1024]{1,0:T(8,128...) custom-call(bf16[8,80,1024]{2,1,0:T(8,128)(2,1)S(1)} %collective-per, ...), custom_call_target="tpu_custom_call" | custom-call | tf_op jit(solution)/shard_map/pallas_call | solution.py:75
  150.3 1.4 collective-permute-start.21
  152.0 3.3 %collective-permute-done.21.refs_6_ = bf16[160,768]{1,0:T(8,128)(2,1)S(1)} collective-permute-done((bf16[160,768]{1,0:T(8,128)(2,1)S(1)}, bf16[160,768]{1,0:T(8,128)(2,1)S(1)}, u32[]{:S(2)}, u32[]{:S(2)}) %collective-permute-start.21) | collective-permute-done | bytes 245792 | tf_op jit(solution)/shard_map/ppermute | solution.py:29
  156.1 1.2 collective-permute-start.25
  157.3 1.3 collective-permute-start.26
  159.7 9.1 %collective-permute-done.24.refs_3_ = bf16[160,768]{1,0:T(8,128)(2,1)S(1)} collective-permute-done((bf16[160,768]{1,0:T(8,128)(2,1)S(1)}, bf16[160,768]{1,0:T(8,128)(2,1)S(1)}, u32[]{:S(2)}, u32[]{:S(2)}) %collective-permute-start.24) | collective-permute-done | bytes 245792 | tf_op jit(solution)/shard_map/ppermute | solution.py:29
  171.6 1.4 collective-permute-start.27
  173.0 6.6 %collective-permute-done.30.refs_21_ = bf16[320,896]{1,0:T(8,128)(2,1)S(1)} collective-permute-done((bf16[320,896]{1,0:T(8,128)(2,1)S(1)}, bf16[320,896]{1,0:T(8,128)(2,1)S(1)}, u32[]{:S(2)}, u32[]{:S(2)}) %collective-permute-start.30) | collective-permute-done | bytes 573472 | tf_op jit(solution)/shard_map/ppermute | solution.py:29
  179.6 5.7 %collective-permute-done.29.refs_19_ = bf16[320,896]{1,0:T(8,128)(2,1)S(1)} collective-permute-done((bf16[320,896]{1,0:T(8,128)(2,1)S(1)}, bf16[320,896]{1,0:T(8,128)(2,1)S(1)}, u32[]{:S(2)}, u32[]{:S(2)}) %collective-permute-start.29) | collective-permute-done | bytes 573472 | tf_op jit(solution)/shard_map/ppermute | solution.py:29
  185.3 6.6 %collective-permute-done.31.refs_23_ = bf16[320,896]{1,0:T(8,128)(2,1)S(1)} collective-permute-done((bf16[320,896]{1,0:T(8,128)(2,1)S(1)}, bf16[320,896]{1,0:T(8,128)(2,1)S(1)}, u32[]{:S(2)}, u32[]{:S(2)}) %collective-permute-start.31) | collective-permute-done | bytes 573472 | tf_op jit(solution)/shard_map/ppermute | solution.py:29
  192.7 7.6 %shard_map.97 = (f32[512,512]{1,0:T(8,128)}, f32[384,512]{1,0:T(8,128)}, f32[384,512]{1,0:T(8,128)}, bf16[512,512]{1,0:T(8,128)(2,1)}, bf16[384,512]{1,0:T(8,128...) custom-call(bf16[320,1024]{1,0:T(8,128)(2,1)} %copy-done.20, bf16[320,1024]{1,0:T(8,128)(2,1)} %copy-done.17, ...), custom_call_target="tpu_custom_call" | custom-call | tf_op jit(solution)/shard_map/pallas_call | solution.py:75
  200.4 1.5 collective-permute-start.32
  203.1 9.9 %shard_map.98 = (f32[512,512]{1,0:T(8,128)}, f32[512,384]{1,0:T(8,128)}, f32[512,384]{1,0:T(8,128)}, bf16[512,512]{1,0:T(8,128)(2,1)}, bf16[512,384]{1,0:T(8,128...) custom-call(bf16[320,1024]{1,0:T(8,128)(2,1)} %copy-done.32, bf16[320,1024]{1,0:T(8,128)(2,1)} %copy-done.29, ...), custom_call_target="tpu_custom_call" | custom-call | tf_op jit(solution)/shard_map/pallas_call | solution.py:75
  213.6 1.5 collective-permute-start.36
  216.4 1.5 collective-permute-start.42
  221.0 8.8 %collective-permute-start.39 = (f32[32,512]{1,0:T(8,128)S(1)}, f32[32,512]{1,0:T(8,128)S(1)}, u32[]{:S(2)}, u32[]{:S(2)}) collective-permute-start(f32[32,512]{1,0:T(8,128)S(1)} %add_add_fusion.1), channel_id=1, source_target_pairs={{0,1},{1,0},{2,3},{3,2},{4,5},{5,4},{6,7},{7,6},{8,9},{9,8},{10,11... | collective-permute-start | bytes 196616 | tf_op jit(solution)/shard_map/ppermute | solution.py:531
  229.9 4.9 %collective-permute-start.40 = (f32[32,512]{1,0:T(8,128)S(1)}, f32[32,512]{1,0:T(8,128)S(1)}, u32[]{:S(2)}, u32[]{:S(2)}) collective-permute-start(f32[32,512]{1,0:T(8,128)S(1)} %add_add_fusion.1), channel_id=1, source_target_pairs={{0,9},{1,8},{2,11},{3,10},{4,13},{5,12},{6,15},{7,14},{8,1},{9,0},... | collective-permute-start | bytes 196616 | tf_op jit(solution)/shard_map/ppermute | solution.py:531
  234.9 2.2 collective-permute-done.40
  238.2 4.8 %shard_map.99 = (f32[32,512]{1,0:T(8,128)S(1)}, f32[8,128]{1,0:T(8,128)S(1)}) custom-call(f32[32,512]{1,0:T(8,128)S(1)} %concatenate.6.prev, f32[32,512]{1,0:T(8,128)S(1)} %get-tuple-element.237.group_sums, f32[32,512]{1,0:T(8,128)S(1)} %get-tuple-element.213.whole_sums, f32[512,512]{1,0:T(8,128)} %get-tuple-element.214.refs_0_, ...), custom_call_target="tpu_custom_call" | custom-call | tf_op jit(solution)/shard_map/pallas_call | solution.py:75
  243.0 1.7 collective-permute-start.44
  244.7 1.2 collective-permute-start.46
  246.0 1.2 collective-permute-done.45
  248.6 2.9 %collective-permute-start.48 = (f32[8,128]{1,0:T(8,128)S(1)}, f32[8,128]{1,0:T(8,128)S(1)}, u32[]{:S(2)}, u32[]{:S(2)}) collective-permute-start(f32[8,128]{1,0:T(8,128)S(1)} %add_add_fusion.3), channel_id=1, source_target_pairs={{0,1},{1,0},{2,3},{3,2},{4,5},{5,4},{6,7},{7,6},{8,9},{9,8},{10,11... | collective-permute-start | bytes 12296 | tf_op jit(solution)/shard_map/ppermute | solution.py:531
  252.3 2.2 collective-permute-done.49
  254.5 6.6 %shard_map.100 = (bf16[512,2560]{1,0:T(8,128)(2,1)}, bf16[2560,512]{1,0:T(8,128)(2,1)}) custom-call(f32[32,512]{1,0:T(8,128)S(1)} %concatenate.6.prev, f32[32,512]{1,0:T(8,128)S(1)} %get-tuple-element.220.factors, f32[32,512]{1,0:T(8,128)S(1)} %get-tuple-element.213.whole_sums, f32[8,128]{1,0:T(8,128)S(1)} %add_add_fusion.2.norms, ...), custom_call_target="tpu_custom_call" | custom-call | tf_op jit(solution)/shard_map/pallas_call | solution.py:75
  (215 shorter events, 39.2 us)
Async XLA Ops:
  6.7 47.4 %all-to-all-start = ((bf16[16,40,1024]{2,1,0:T(8,128)(2,1)}), bf16[16,40,1024]{2,1,0:T(8,128)(2,1)}, u32[]{:S(2)}, u32[]{:S(2)}) async-start(bf16[16,40,1024]{2,1,0:T(8,128)(2,1)} %pad_maximum_fusion.1), calls=%async_computation | async-start | bytes 2621440 | tf_op jit(solution)/shard_map/all_to_all | solution.py:427
  19.7 34.4 %collective-permute-start = (bf16[4096,128]{1,0:T(8,128)(2,1)S(1)}, bf16[4096,128]{1,0:T(8,128)(2,1)S(1)}, u32[]{:S(2)}, u32[]{:S(2)}) collective-permute-start(bf16[4096,128]{1,0:T(8,128)(2,1)S(1)} %get-tuple-element.116), channel_id=1, source_target_pairs={{0,2},{2,0},{4,6},{6,4},{8,10},{10,8},{12,14},{14,12},{16,18},{18,... | collective-permute-start | bytes 3145736 | tf_op jit(solution)/shard_map/ppermute | solution.py:29
  21.0 26.7 %collective-permute-start.1 = (bf16[3072,128]{1,0:T(8,128)(2,1)S(1)}, bf16[3072,128]{1,0:T(8,128)(2,1)S(1)}, u32[]{:S(2)}, u32[]{:S(2)}) collective-permute-start(bf16[3072,128]{1,0:T(8,128)(2,1)S(1)} %get-tuple-element.117), channel_id=1, source_target_pairs={{0,4},{2,6},{4,0},{6,2},{8,12},{10,14},{12,8},{14,10},{16,20},{18,... | collective-permute-start | bytes 2359304 | tf_op jit(solution)/shard_map/ppermute | solution.py:29
  22.2 31.9 %collective-permute-start.2 = (bf16[3072,128]{1,0:T(8,128)(2,1)S(1)}, bf16[3072,128]{1,0:T(8,128)(2,1)S(1)}, u32[]{:S(2)}, u32[]{:S(2)}) collective-permute-start(bf16[3072,128]{1,0:T(8,128)(2,1)S(1)} %get-tuple-element.118), channel_id=1, source_target_pairs={{0,8},{2,10},{4,12},{6,14},{8,0},{10,2},{12,4},{14,6},{16,24},{18,... | collective-permute-start | bytes 2359304 | tf_op jit(solution)/shard_map/ppermute | solution.py:29
  55.5 28.6 %collective-permute-start.3 = (bf16[8,80,1024]{2,1,0:T(8,128)(2,1)S(1)}, bf16[8,80,1024]{2,1,0:T(8,128)(2,1)S(1)}, u32[]{:S(2)}, u32[]{:S(2)}) collective-permute-start(bf16[8,80,1024]{2,1,0:T(8,128)(2,1)S(1)} %bitcast.32), channel_id=1, source_target_pairs={{0,2},{2,0},{4,6},{6,4},{8,10},{10,8},{12,14},{14,12},{16,18},{18,... | collective-permute-start | bytes 3932168 | tf_op jit(solution)/shard_map/ppermute | solution.py:29
  56.8 28.3 %collective-permute-start.4 = (bf16[8,80,1024]{2,1,0:T(8,128)(2,1)S(1)}, bf16[8,80,1024]{2,1,0:T(8,128)(2,1)S(1)}, u32[]{:S(2)}, u32[]{:S(2)}) collective-permute-start(bf16[8,80,1024]{2,1,0:T(8,128)(2,1)S(1)} %bitcast.33), channel_id=1, source_target_pairs={{0,4},{2,6},{4,0},{6,2},{8,12},{10,14},{12,8},{14,10},{16,20},{18,... | collective-permute-start | bytes 3932168 | tf_op jit(solution)/shard_map/ppermute | solution.py:29
  58.4 28.2 %collective-permute-start.5 = (bf16[8,80,1024]{2,1,0:T(8,128)(2,1)S(1)}, bf16[8,80,1024]{2,1,0:T(8,128)(2,1)S(1)}, u32[]{:S(2)}, u32[]{:S(2)}) collective-permute-start(bf16[8,80,1024]{2,1,0:T(8,128)(2,1)S(1)} %bitcast.34), channel_id=1, source_target_pairs={{0,8},{2,10},{4,12},{6,14},{8,0},{10,2},{12,4},{14,6},{16,24},{18,... | collective-permute-start | bytes 3932168 | tf_op jit(solution)/shard_map/ppermute | solution.py:29
  88.6 24.9 %collective-permute-start.7 = (bf16[3,8,80,1024]{3,2,1,0:T(8,128)(2,1)}, bf16[3,8,80,1024]{3,2,1,0:T(8,128)(2,1)}, u32[]{:S(2)}, u32[]{:S(2)}) collective-permute-start(bf16[3,8,80,1024]{3,2,1,0:T(8,128)(2,1)} %pad_maximum_fusion.refs_1_), channel_id=1, source_target_pairs={{0,1},{1,0},{2,3},{3,2},{4,5},{5,4},{6,7},{7,6},{8,9},{9,8},{10,11... | collective-permute-start | bytes 11796488 | tf_op jit(solution)/shard_map/ppermute | solution.py:29
  91.7 21.9 %collective-permute-start.6 = (bf16[8,80,1024]{2,1,0:T(8,128)(2,1)S(1)}, bf16[8,80,1024]{2,1,0:T(8,128)(2,1)S(1)}, u32[]{:S(2)}, u32[]{:S(2)}) collective-permute-start(bf16[8,80,1024]{2,1,0:T(8,128)(2,1)S(1)} %bitcast.35), channel_id=1, source_target_pairs={{0,1},{1,0},{2,3},{3,2},{4,5},{5,4},{6,7},{7,6},{8,9},{9,8},{10,11... | collective-permute-start | bytes 3932168 | tf_op jit(solution)/shard_map/ppermute | solution.py:29
  98.5 14.1 %collective-permute-start.10 = (bf16[320,896]{1,0:T(8,128)(2,1)S(1)}, bf16[320,896]{1,0:T(8,128)(2,1)S(1)}, u32[]{:S(2)}, u32[]{:S(2)}) collective-permute-start(bf16[320,896]{1,0:T(8,128)(2,1)S(1)} %get-tuple-element.152), channel_id=1, source_target_pairs={{0,8},{2,10},{4,12},{6,14},{8,0},{10,2},{12,4},{14,6},{16,24},{18,... | collective-permute-start | bytes 1720328 | tf_op jit(solution)/shard_map/ppermute | solution.py:29
  99.4 13.7 %collective-permute-start.9 = (bf16[320,896]{1,0:T(8,128)(2,1)S(1)}, bf16[320,896]{1,0:T(8,128)(2,1)S(1)}, u32[]{:S(2)}, u32[]{:S(2)}) collective-permute-start(bf16[320,896]{1,0:T(8,128)(2,1)S(1)} %get-tuple-element.151), channel_id=1, source_target_pairs={{0,4},{2,6},{4,0},{6,2},{8,12},{10,14},{12,8},{14,10},{16,20},{18,... | collective-permute-start | bytes 1720328 | tf_op jit(solution)/shard_map/ppermute | solution.py:29
  99.4 11.7 %collective-permute-start.8 = (bf16[320,768]{1,0:T(8,128)(2,1)S(1)}, bf16[320,768]{1,0:T(8,128)(2,1)S(1)}, u32[]{:S(2)}, u32[]{:S(2)}) collective-permute-start(bf16[320,768]{1,0:T(8,128)(2,1)S(1)} %get-tuple-element.150), channel_id=1, source_target_pairs={{0,2},{2,0},{4,6},{6,4},{8,10},{10,8},{12,14},{14,12},{16,18},{18,... | collective-permute-start | bytes 1474568 | tf_op jit(solution)/shard_map/ppermute | solution.py:29
  113.4 10.5 %collective-permute-start.11 = (bf16[160,768]{1,0:T(8,128)(2,1)S(1)}, bf16[160,768]{1,0:T(8,128)(2,1)S(1)}, u32[]{:S(2)}, u32[]{:S(2)}) collective-permute-start(bf16[160,768]{1,0:T(8,128)(2,1)S(1)} %get-tuple-element.159), channel_id=1, source_target_pairs={{0,2},{2,0},{4,6},{6,4},{8,10},{10,8},{12,14},{14,12},{16,18},{18,... | collective-permute-start | bytes 737288 | tf_op jit(solution)/shard_map/ppermute | solution.py:29
  120.4 21.8 %collective-permute-start.18 = (bf16[320,768]{1,0:T(8,128)(2,1)S(1)}, bf16[320,768]{1,0:T(8,128)(2,1)S(1)}, u32[]{:S(2)}, u32[]{:S(2)}) collective-permute-start(bf16[320,768]{1,0:T(8,128)(2,1)S(1)} %get-tuple-element.172), channel_id=1, source_target_pairs={{0,2},{2,0},{4,6},{6,4},{8,10},{10,8},{12,14},{14,12},{16,18},{18,... | collective-permute-start | bytes 1474568 | tf_op jit(solution)/shard_map/ppermute | solution.py:29
  121.8 25.8 %collective-permute-start.19 = (bf16[320,896]{1,0:T(8,128)(2,1)S(1)}, bf16[320,896]{1,0:T(8,128)(2,1)S(1)}, u32[]{:S(2)}, u32[]{:S(2)}) collective-permute-start(bf16[320,896]{1,0:T(8,128)(2,1)S(1)} %get-tuple-element.173), channel_id=1, source_target_pairs={{0,4},{2,6},{4,0},{6,2},{8,12},{10,14},{12,8},{14,10},{16,20},{18,... | collective-permute-start | bytes 1720328 | tf_op jit(solution)/shard_map/ppermute | solution.py:29
  121.8 25.8 %collective-permute-start.20 = (bf16[320,896]{1,0:T(8,128)(2,1)S(1)}, bf16[320,896]{1,0:T(8,128)(2,1)S(1)}, u32[]{:S(2)}, u32[]{:S(2)}) collective-permute-start(bf16[320,896]{1,0:T(8,128)(2,1)S(1)} %get-tuple-element.174), channel_id=1, source_target_pairs={{0,8},{2,10},{4,12},{6,14},{8,0},{10,2},{12,4},{14,6},{16,24},{18,... | collective-permute-start | bytes 1720328 | tf_op jit(solution)/shard_map/ppermute | solution.py:29
  122.5 17.7 %collective-permute-start.12 = (bf16[160,896]{1,0:T(8,128)(2,1)S(1)}, bf16[160,896]{1,0:T(8,128)(2,1)S(1)}, u32[]{:S(2)}, u32[]{:S(2)}) collective-permute-start(bf16[160,896]{1,0:T(8,128)(2,1)S(1)} %get-tuple-element.160), channel_id=1, source_target_pairs={{0,4},{2,6},{4,0},{6,2},{8,12},{10,14},{12,8},{14,10},{16,20},{18,... | collective-permute-start | bytes 860168 | tf_op jit(solution)/shard_map/ppermute | solution.py:29
  123.9 16.3 %collective-permute-start.13 = (bf16[160,896]{1,0:T(8,128)(2,1)S(1)}, bf16[160,896]{1,0:T(8,128)(2,1)S(1)}, u32[]{:S(2)}, u32[]{:S(2)}) collective-permute-start(bf16[160,896]{1,0:T(8,128)(2,1)S(1)} %get-tuple-element.161), channel_id=1, source_target_pairs={{0,8},{2,10},{4,12},{6,14},{8,0},{10,2},{12,4},{14,6},{16,24},{18,... | collective-permute-start | bytes 860168 | tf_op jit(solution)/shard_map/ppermute | solution.py:29
  140.9 9.4 %collective-permute-start.14 = (bf16[160,768]{1,0:T(8,128)(2,1)S(1)}, bf16[160,768]{1,0:T(8,128)(2,1)S(1)}, u32[]{:S(2)}, u32[]{:S(2)}) collective-permute-start(bf16[160,768]{1,0:T(8,128)(2,1)S(1)} %get-tuple-element.162.refs_0_), channel_id=1, source_target_pairs={{0,2},{2,0},{4,6},{6,4},{8,10},{10,8},{12,14},{14,12},{16,18},{18,... | collective-permute-start | bytes 737288 | tf_op jit(solution)/shard_map/ppermute | solution.py:29
  141.1 10.6 %collective-permute-start.15 = (bf16[160,896]{1,0:T(8,128)(2,1)S(1)}, bf16[160,896]{1,0:T(8,128)(2,1)S(1)}, u32[]{:S(2)}, u32[]{:S(2)}) collective-permute-start(bf16[160,896]{1,0:T(8,128)(2,1)S(1)} %get-tuple-element.163.refs_1_), channel_id=1, source_target_pairs={{0,4},{2,6},{4,0},{6,2},{8,12},{10,14},{12,8},{14,10},{16,20},{18,... | collective-permute-start | bytes 860168 | tf_op jit(solution)/shard_map/ppermute | solution.py:29
  142.3 9.4 %collective-permute-start.16 = (bf16[160,896]{1,0:T(8,128)(2,1)S(1)}, bf16[160,896]{1,0:T(8,128)(2,1)S(1)}, u32[]{:S(2)}, u32[]{:S(2)}) collective-permute-start(bf16[160,896]{1,0:T(8,128)(2,1)S(1)} %get-tuple-element.164.refs_2_), channel_id=1, source_target_pairs={{0,8},{2,10},{4,12},{6,14},{8,0},{10,2},{12,4},{14,6},{16,24},{18,... | collective-permute-start | bytes 860168 | tf_op jit(solution)/shard_map/ppermute | solution.py:29
  149.5 5.8 %collective-permute-start.22 = (bf16[160,896]{1,0:T(8,128)(2,1)S(1)}, bf16[160,896]{1,0:T(8,128)(2,1)S(1)}, u32[]{:S(2)}, u32[]{:S(2)}) collective-permute-start(bf16[160,896]{1,0:T(8,128)(2,1)S(1)} %get-tuple-element.182), channel_id=1, source_target_pairs={{0,4},{2,6},{4,0},{6,2},{8,12},{10,14},{12,8},{14,10},{16,20},{18,... | collective-permute-start | bytes 860168 | tf_op jit(solution)/shard_map/ppermute | solution.py:29
  149.8 5.6 %collective-permute-start.23 = (bf16[160,896]{1,0:T(8,128)(2,1)S(1)}, bf16[160,896]{1,0:T(8,128)(2,1)S(1)}, u32[]{:S(2)}, u32[]{:S(2)}) collective-permute-start(bf16[160,896]{1,0:T(8,128)(2,1)S(1)} %get-tuple-element.183), channel_id=1, source_target_pairs={{0,8},{2,10},{4,12},{6,14},{8,0},{10,2},{12,4},{14,6},{16,24},{18,... | collective-permute-start | bytes 860168 | tf_op jit(solution)/shard_map/ppermute | solution.py:29
  150.3 5.0 %collective-permute-start.21 = (bf16[160,768]{1,0:T(8,128)(2,1)S(1)}, bf16[160,768]{1,0:T(8,128)(2,1)S(1)}, u32[]{:S(2)}, u32[]{:S(2)}) collective-permute-start(bf16[160,768]{1,0:T(8,128)(2,1)S(1)} %get-tuple-element.181), channel_id=1, source_target_pairs={{0,2},{2,0},{4,6},{6,4},{8,10},{10,8},{12,14},{14,12},{16,18},{18,... | collective-permute-start | bytes 737288 | tf_op jit(solution)/shard_map/ppermute | solution.py:29
  151.9 19.8 %collective-permute-start.17 = (bf16[320,768]{1,0:T(8,128)(2,1)S(1)}, bf16[320,768]{1,0:T(8,128)(2,1)S(1)}, u32[]{:S(2)}, u32[]{:S(2)}) collective-permute-start(bf16[320,768]{1,0:T(8,128)(2,1)S(1)} %get-tuple-element.165.refs_12_), channel_id=1, source_target_pairs={{0,2},{2,0},{4,6},{6,4},{8,10},{10,8},{12,14},{14,12},{16,18},{18,... | collective-permute-start | bytes 1474568 | tf_op jit(solution)/shard_map/ppermute | solution.py:29
  156.1 13.9 %collective-permute-start.25 = (bf16[160,896]{1,0:T(8,128)(2,1)S(1)}, bf16[160,896]{1,0:T(8,128)(2,1)S(1)}, u32[]{:S(2)}, u32[]{:S(2)}) collective-permute-start(bf16[160,896]{1,0:T(8,128)(2,1)S(1)} %get-tuple-element.185.refs_1_), channel_id=1, source_target_pairs={{0,4},{2,6},{4,0},{6,2},{8,12},{10,14},{12,8},{14,10},{16,20},{18,... | collective-permute-start | bytes 860168 | tf_op jit(solution)/shard_map/ppermute | solution.py:29
  157.3 12.6 %collective-permute-start.26 = (bf16[160,896]{1,0:T(8,128)(2,1)S(1)}, bf16[160,896]{1,0:T(8,128)(2,1)S(1)}, u32[]{:S(2)}, u32[]{:S(2)}) collective-permute-start(bf16[160,896]{1,0:T(8,128)(2,1)S(1)} %get-tuple-element.186.refs_2_), channel_id=1, source_target_pairs={{0,8},{2,10},{4,12},{6,14},{8,0},{10,2},{12,4},{14,6},{16,24},{18,... | collective-permute-start | bytes 860168 | tf_op jit(solution)/shard_map/ppermute | solution.py:29
  158.6 10.2 %collective-permute-start.24 = (bf16[160,768]{1,0:T(8,128)(2,1)S(1)}, bf16[160,768]{1,0:T(8,128)(2,1)S(1)}, u32[]{:S(2)}, u32[]{:S(2)}) collective-permute-start(bf16[160,768]{1,0:T(8,128)(2,1)S(1)} %get-tuple-element.184.refs_0_), channel_id=1, source_target_pairs={{0,2},{2,0},{4,6},{6,4},{8,10},{10,8},{12,14},{14,12},{16,18},{18,... | collective-permute-start | bytes 737288 | tf_op jit(solution)/shard_map/ppermute | solution.py:29
  159.7 13.4 %collective-permute-start.28 = (bf16[320,896]{1,0:T(8,128)(2,1)S(1)}, bf16[320,896]{1,0:T(8,128)(2,1)S(1)}, u32[]{:S(2)}, u32[]{:S(2)}) collective-permute-start(bf16[320,896]{1,0:T(8,128)(2,1)S(1)} %get-tuple-element.188.refs_16_), channel_id=1, source_target_pairs={{0,4},{2,6},{4,0},{6,2},{8,12},{10,14},{12,8},{14,10},{16,20},{18,... | collective-permute-start | bytes 1720328 | tf_op jit(solution)/shard_map/ppermute | solution.py:29
  168.8 10.8 %collective-permute-start.30 = (bf16[320,896]{1,0:T(8,128)(2,1)S(1)}, bf16[320,896]{1,0:T(8,128)(2,1)S(1)}, u32[]{:S(2)}, u32[]{:S(2)}) collective-permute-start(bf16[320,896]{1,0:T(8,128)(2,1)S(1)} %get-tuple-element.190.refs_20_), channel_id=1, source_target_pairs={{0,8},{2,10},{4,12},{6,14},{8,0},{10,2},{12,4},{14,6},{16,24},{18,... | collective-permute-start | bytes 1720328 | tf_op jit(solution)/shard_map/ppermute | solution.py:29
  170.2 15.1 %collective-permute-start.29 = (bf16[320,896]{1,0:T(8,128)(2,1)S(1)}, bf16[320,896]{1,0:T(8,128)(2,1)S(1)}, u32[]{:S(2)}, u32[]{:S(2)}) collective-permute-start(bf16[320,896]{1,0:T(8,128)(2,1)S(1)} %get-tuple-element.189.refs_18_), channel_id=1, source_target_pairs={{0,4},{2,6},{4,0},{6,2},{8,12},{10,14},{12,8},{14,10},{16,20},{18,... | collective-permute-start | bytes 1720328 | tf_op jit(solution)/shard_map/ppermute | solution.py:29
  171.1 20.8 %collective-permute-start.31 = (bf16[320,896]{1,0:T(8,128)(2,1)S(1)}, bf16[320,896]{1,0:T(8,128)(2,1)S(1)}, u32[]{:S(2)}, u32[]{:S(2)}) collective-permute-start(bf16[320,896]{1,0:T(8,128)(2,1)S(1)} %get-tuple-element.191.refs_22_), channel_id=1, source_target_pairs={{0,8},{2,10},{4,12},{6,14},{8,0},{10,2},{12,4},{14,6},{16,24},{18,... | collective-permute-start | bytes 1720328 | tf_op jit(solution)/shard_map/ppermute | solution.py:29
  171.6 8.0 %collective-permute-start.27 = (bf16[320,768]{1,0:T(8,128)(2,1)S(1)}, bf16[320,768]{1,0:T(8,128)(2,1)S(1)}, u32[]{:S(2)}, u32[]{:S(2)}) collective-permute-start(bf16[320,768]{1,0:T(8,128)(2,1)S(1)} %get-tuple-element.187.refs_14_), channel_id=1, source_target_pairs={{0,2},{2,0},{4,6},{6,4},{8,10},{10,8},{12,14},{14,12},{16,18},{18,... | collective-permute-start | bytes 1474568 | tf_op jit(solution)/shard_map/ppermute | solution.py:29
  200.4 12.7 %collective-permute-start.32 = (bf16[512,512]{1,0:T(8,128)(2,1)}, bf16[512,512]{1,0:T(8,128)(2,1)S(1)}, u32[]{:S(2)}, u32[]{:S(2)}) collective-permute-start(bf16[512,512]{1,0:T(8,128)(2,1)} %get-tuple-element.206.refs_9_), channel_id=1, source_target_pairs={{0,2},{2,0},{4,6},{6,4},{8,10},{10,8},{12,14},{14,12},{16,18},{18,... | collective-permute-start | bytes 1572872 | tf_op jit(solution)/shard_map/ppermute | solution.py:29
  201.8 11.3 %collective-permute-start.33 = (bf16[384,512]{1,0:T(8,128)(2,1)}, bf16[384,512]{1,0:T(8,128)(2,1)S(1)}, u32[]{:S(2)}, u32[]{:S(2)}) collective-permute-start(bf16[384,512]{1,0:T(8,128)(2,1)} %get-tuple-element.207.refs_10_), channel_id=1, source_target_pairs={{0,4},{2,6},{4,0},{6,2},{8,12},{10,14},{12,8},{14,10},{16,20},{18,... | collective-permute-start | bytes 1179656 | tf_op jit(solution)/shard_map/ppermute | solution.py:29
  201.8 11.3 %collective-permute-start.34 = (bf16[384,512]{1,0:T(8,128)(2,1)}, bf16[384,512]{1,0:T(8,128)(2,1)S(1)}, u32[]{:S(2)}, u32[]{:S(2)}) collective-permute-start(bf16[384,512]{1,0:T(8,128)(2,1)} %get-tuple-element.208.refs_11_), channel_id=1, source_target_pairs={{0,8},{2,10},{4,12},{6,14},{8,0},{10,2},{12,4},{14,6},{16,24},{18,... | collective-permute-start | bytes 1179656 | tf_op jit(solution)/shard_map/ppermute | solution.py:29
  213.2 4.7 %collective-permute-start.35 = (f32[32,512]{1,0:T(8,128)}, f32[32,512]{1,0:T(8,128)S(1)}, u32[]{:S(2)}, u32[]{:S(2)}) collective-permute-start(f32[32,512]{1,0:T(8,128)} %get-tuple-element.209), channel_id=1, source_target_pairs={{0,2},{2,0},{4,6},{6,4},{8,10},{10,8},{12,14},{14,12},{16,18},{18,... | collective-permute-start | bytes 196616 | tf_op jit(solution)/shard_map/ppermute | solution.py:29
  213.6 4.7 %collective-permute-start.36 = (f32[32,512]{1,0:T(8,128)}, f32[32,512]{1,0:T(8,128)S(1)}, u32[]{:S(2)}, u32[]{:S(2)}) collective-permute-start(f32[32,512]{1,0:T(8,128)} %get-tuple-element.209), channel_id=1, source_target_pairs={{0,4},{2,6},{4,0},{6,2},{8,12},{10,14},{12,8},{14,10},{16,20},{18,... | collective-permute-start | bytes 196616 | tf_op jit(solution)/shard_map/ppermute | solution.py:29
  215.1 4.3 %collective-permute-start.37 = (f32[32,512]{1,0:T(8,128)}, f32[32,512]{1,0:T(8,128)S(1)}, u32[]{:S(2)}, u32[]{:S(2)}) collective-permute-start(f32[32,512]{1,0:T(8,128)} %get-tuple-element.209), channel_id=1, source_target_pairs={{0,6},{2,4},{4,2},{6,0},{8,14},{10,12},{12,10},{14,8},{16,22},{18,... | collective-permute-start | bytes 196616 | tf_op jit(solution)/shard_map/ppermute | solution.py:29
  215.9 21.2 %collective-permute-start.41 = (bf16[512,512]{1,0:T(8,128)(2,1)}, bf16[512,512]{1,0:T(8,128)(2,1)}, u32[]{:S(2)}, u32[]{:S(2)}) collective-permute-start(bf16[512,512]{1,0:T(8,128)(2,1)} %get-tuple-element.210.refs_3_), channel_id=1, source_target_pairs={{0,2},{2,0},{4,6},{6,4},{8,10},{10,8},{12,14},{14,12},{16,18},{18,... | collective-permute-start | bytes 1572872 | tf_op jit(solution)/shard_map/ppermute | solution.py:29
  216.4 20.7 %collective-permute-start.42 = (bf16[512,384]{1,0:T(8,128)(2,1)}, bf16[512,384]{1,0:T(8,128)(2,1)S(1)}, u32[]{:S(2)}, u32[]{:S(2)}) collective-permute-start(bf16[512,384]{1,0:T(8,128)(2,1)} %get-tuple-element.211.refs_4_), channel_id=1, source_target_pairs={{0,4},{2,6},{4,0},{6,2},{8,12},{10,14},{12,8},{14,10},{16,20},{18,... | collective-permute-start | bytes 1179656 | tf_op jit(solution)/shard_map/ppermute | solution.py:29
  217.8 19.3 %collective-permute-start.43 = (bf16[512,384]{1,0:T(8,128)(2,1)}, bf16[512,384]{1,0:T(8,128)(2,1)S(1)}, u32[]{:S(2)}, u32[]{:S(2)}) collective-permute-start(bf16[512,384]{1,0:T(8,128)(2,1)} %get-tuple-element.212.refs_5_), channel_id=1, source_target_pairs={{0,8},{2,10},{4,12},{6,14},{8,0},{10,2},{12,4},{14,6},{16,24},{18,... | collective-permute-start | bytes 1179656 | tf_op jit(solution)/shard_map/ppermute | solution.py:29
  220.2 9.7 %collective-permute-start.38 = (f32[32,512]{1,0:T(8,128)S(1)}, f32[32,512]{1,0:T(8,128)S(1)}, u32[]{:S(2)}, u32[]{:S(2)}) collective-permute-start(f32[32,512]{1,0:T(8,128)S(1)} %add_add_fusion.1), channel_id=1, source_target_pairs={{0,8},{2,10},{4,12},{6,14},{8,0},{10,2},{12,4},{14,6},{16,24},{18,... | collective-permute-start | bytes 196616 | tf_op jit(solution)/shard_map/ppermute | solution.py:29
  221.0 13.8 %collective-permute-start.39 = (f32[32,512]{1,0:T(8,128)S(1)}, f32[32,512]{1,0:T(8,128)S(1)}, u32[]{:S(2)}, u32[]{:S(2)}) collective-permute-start(f32[32,512]{1,0:T(8,128)S(1)} %add_add_fusion.1), channel_id=1, source_target_pairs={{0,1},{1,0},{2,3},{3,2},{4,5},{5,4},{6,7},{7,6},{8,9},{9,8},{10,11... | collective-permute-start | bytes 196616 | tf_op jit(solution)/shard_map/ppermute | solution.py:531
  229.9 7.2 %collective-permute-start.40 = (f32[32,512]{1,0:T(8,128)S(1)}, f32[32,512]{1,0:T(8,128)S(1)}, u32[]{:S(2)}, u32[]{:S(2)}) collective-permute-start(f32[32,512]{1,0:T(8,128)S(1)} %add_add_fusion.1), channel_id=1, source_target_pairs={{0,9},{1,8},{2,11},{3,10},{4,13},{5,12},{6,15},{7,14},{8,1},{9,0},... | collective-permute-start | bytes 196616 | tf_op jit(solution)/shard_map/ppermute | solution.py:531
  244.7 3.4 %collective-permute-start.46 = (f32[8,128]{1,0:T(8,128)S(1)}, f32[8,128]{1,0:T(8,128)S(1)}, u32[]{:S(2)}, u32[]{:S(2)}) collective-permute-start(f32[8,128]{1,0:T(8,128)S(1)} %get-tuple-element.221), channel_id=1, source_target_pairs={{0,6},{2,4},{4,2},{6,0},{8,14},{10,12},{12,10},{14,8},{16,22},{18,... | collective-permute-start | bytes 12296 | tf_op jit(solution)/shard_map/ppermute | solution.py:29
  248.1 4.1 %collective-permute-start.47 = (f32[8,128]{1,0:T(8,128)S(1)}, f32[8,128]{1,0:T(8,128)S(1)}, u32[]{:S(2)}, u32[]{:S(2)}) collective-permute-start(f32[8,128]{1,0:T(8,128)S(1)} %add_add_fusion.3), channel_id=1, source_target_pairs={{0,8},{2,10},{4,12},{6,14},{8,0},{10,2},{12,4},{14,6},{16,24},{18,... | collective-permute-start | bytes 12296 | tf_op jit(solution)/shard_map/ppermute | solution.py:29
  248.6 3.7 %collective-permute-start.48 = (f32[8,128]{1,0:T(8,128)S(1)}, f32[8,128]{1,0:T(8,128)S(1)}, u32[]{:S(2)}, u32[]{:S(2)}) collective-permute-start(f32[8,128]{1,0:T(8,128)S(1)} %add_add_fusion.3), channel_id=1, source_target_pairs={{0,1},{1,0},{2,3},{3,2},{4,5},{5,4},{6,7},{7,6},{8,9},{9,8},{10,11... | collective-permute-start | bytes 12296 | tf_op jit(solution)/shard_map/ppermute | solution.py:531
  (58 other events, 513.2 us)

commit v6 on v5

--- a/solution.py
+++ b/solution.py
@@ -21,7 +21,7 @@
 MASKS = (1, 2, 4)
 
 MIB = 1024 * 1024
-CUT_MIB = 44
+CUT_MIB = 8
 
 
 def swap(value, mask, axis="expert"):
@@ -64,10 +64,10 @@
     )
 
 
-def call(kernel, mib, out_shape, *operands, scratch=(), streamed=(), streamed_out=(), whole=()):
+def call(kernel, mib, out_shape, *operands, scratch=(), streamed=(), streamed_out=(), whole=(), whole_out=()):
     def spec(value, n, blocks, refs):
         if n in refs:
-            return pl.BlockSpec(memory_space=pl.ANY)
+            return pl.BlockSpec(memory_space=pltpu.HBM)
         if n in blocks:
             return pl.BlockSpec(value.shape, lambda: (0,) * len(value.shape))
         return pl.BlockSpec(memory_space=pltpu.VMEM)
@@ -76,7 +76,7 @@
         kernel,
         out_shape=out_shape,
         in_specs=[spec(value, n, streamed, whole) for n, value in enumerate(operands)],
-        out_specs=[spec(value, n, streamed_out, ()) for n, value in enumerate(out_shape)],
+        out_specs=[spec(value, n, streamed_out, whole_out) for n, value in enumerate(out_shape)],
         scratch_shapes=list(scratch),
         compiler_params=pltpu.CompilerParams(vmem_limit_bytes=mib * MIB),
     )(*operands)
@@ -153,7 +153,8 @@
 
 def sums_kernel(side, halves, is_packed, *refs):
     own, pairs, own_weights, got_weights = refs[0], refs[1], refs[2:8], refs[8:14]
-    rows_out, sums_out = refs[14:20], refs[20:]
+    rows_out, sums_out, all_rows, sems = refs[14:20], refs[20:-2], refs[-2], refs[-1]
+    copies = [pltpu.make_async_copy(all_rows.at[n], rows_out[n], sems.at[n]) for n in range(6)]
     count, width = own.shape[1], own.shape[2] // 2
     for matrix in range(2):
         lanes = slice(matrix * width, (matrix + 1) * width)
@@ -165,16 +166,19 @@
                 for l in range(2):
                     chunk = flipped(place_in_group(), side * first + j * second + l * (1 << k))
                     at = (j * 2 + l) * count
-                    rows_out[n][at : at + count, :width] = own[chunk, :, lanes]
-                    rows_out[n][at : at + count, width:] = pairs[k, chunk, :, lanes]
+                    all_rows[n, at : at + count, :width] = own[chunk, :, lanes]
+                    all_rows[n, at : at + count, width:] = pairs[k, chunk, :, lanes]
+            copies[n].start()
             by_row = matrix == 1
             got = got_weight(got_weights[n], by_row, half, width) if is_packed else got_weights[n][...]
-            sums = partial_sum(rows_out[n][...], own_weights[n][...], got, by_row)
+            sums = partial_sum(all_rows[n], own_weights[n][...], got, by_row)
             if side:
                 at = packed_place(0, matrix, k, halves)[1]
                 sums_out[axis][:, at : at + half] = sums.astype(jnp.bfloat16)
             else:
                 sums_out[n][...] = sums
+    for copy in copies:
+        copy.wait()
 
 
 def add_kernel(halves, *refs):
@@ -447,8 +451,8 @@
     def sums(chain, side, out_shapes):
         kernel = functools.partial(sums_kernel, side, halves, is_packed)
         outs = call(
-            kernel, 40, row_shapes + out_shapes, *blocks[chain], *cuts[:6], *got_weights,
-            streamed_out=range(6),
+            kernel, 14, row_shapes + out_shapes, *blocks[chain], *cuts[:6], *got_weights,
+            scratch=[pltpu.VMEM((6, count, wide), bf16), pltpu.SemaphoreType.DMA((6,))], whole_out=range(6),
         )
         return outs[:6], outs[6:]
 
@@ -456,8 +460,10 @@
     for c in chains:
         far_rows[c], sent = sums(c, 1, shapes(count, first_widths, bf16))
         received[c] = along_axes(sent)
+    blocks, sent = lax.optimization_barrier((blocks, sent))
     for c in chains:
         near_rows[c], kept[c] = sums(c, 0, shapes(count, halves * 2, f32))
+    kept = lax.optimization_barrier(kept)
     for c in chains:
         out_shapes = shapes(count // 2, halves * 2, f32) + shapes(count // 2, second_widths, bf16)
         outs = call(functools.partial(add_kernel, halves), 8, out_shapes, *kept[c], *received[c])

time: 262 us -> 267 us (1.019)
  local copies, waits for them, and re-layouts: 15.7 us -> 27.5 us
  waiting for transfers between devices: 122 us -> 116 us
    unnamed x113 -> x115, local copies, waits for them, and re-layouts: 12.9 us -> 24.7 us
    ppermute x46, waiting for transfers between devices: 117 us -> 111 us  [swap(): return lax.ppermute(value, axis, pairs)]
  transfers between devices with their start and end apart: 51 -> 51, of which waited for: 20 -> 26; matrix products, arithmetic and copies ran while one was open for 1% -> 1% of each run, Pallas kernels for 12% -> 12%
where the time goes in v6:
time: 267 us
  waiting for transfers between devices  116 us (43%)
  starting transfers between devices  64.8 us (24%)
  Pallas kernels  50.9 us (19%)
  local copies, waits for them, and re-layouts  27.5 us (10%)
  other arithmetic  5.07 us (2%)
    ppermute x46, waiting for transfers between devices, swap(): return lax.ppermute(value, axis, pairs)  111 us
    pallas_call x15, Pallas kernels, call(): pl.pallas_call(kernel, out_shape=out_shape, in_specs=[spec(value, n, stre...  50.9 us
    ppermute x46, starting transfers between devices, swap(): return lax.ppermute(value, axis, pairs)  38.6 us
    unnamed x115, local copies, waits for them, and re-layouts  24.7 us
    ppermute x4, starting transfers between devices, other(): return lax.ppermute(values, ('expert', 'ffn'), moves)  18.4 us
    all_to_all x1, starting transfers between devices, shards(): lax.all_to_all(routed, 'expert', split_axis=0, concat_axis=0, tiled=True)  7.74 us
  transfers between devices with their start and end apart: 51, of which 26 were waited for; matrix products, arithmetic and copies ran while one was open for 1% of the time, Pallas kernels for 12%

profile of v6, /device:TPU:1, one launch (start us, length us, event | category | flops | bytes accessed | tf_op | source)
XLA Modules:
  0.0 266.7 jit_solution(9713267114366181989)
XLA Ops:
  5.5 1.2 pad_maximum_fusion.1
  6.7 7.7 %all-to-all-start = ((bf16[16,40,1024]{2,1,0:T(8,128)(2,1)}), bf16[16,40,1024]{2,1,0:T(8,128)(2,1)}, u32[]{:S(2)}, u32[]{:S(2)}) async-start(bf16[16,40,1024]{2,1,0:T(8,128)(2,1)} %pad_maximum_fusion.1), calls=%async_computation | async-start | bytes 2621440 | tf_op jit(solution)/shard_map/all_to_all | solution.py:431
  14.5 1.7 copy-done.11
  16.2 1.3 shard_map.86
  20.6 1.3 collective-permute-start
  24.3 24.2 %collective-permute-done.1.refs_9_.refs_12_ = bf16[3072,128]{1,0:T(8,128)(2,1)S(1)} collective-permute-done((bf16[3072,128]{1,0:T(8,128)(2,1)S(1)}, bf16[3072,128]{1,0:T(8,128)(2,1)S(1)}, u32[]{:S(2)}, u32[]{:S(2)}) %collective-permute-start.1) | collective-permute-done | bytes 786464 | tf_op jit(solution)/shard_map/ppermute | solution.py:29
  48.5 5.6 %collective-permute-done.2.refs_10_.refs_13_ = bf16[3072,128]{1,0:T(8,128)(2,1)S(1)} collective-permute-done((bf16[3072,128]{1,0:T(8,128)(2,1)S(1)}, bf16[3072,128]{1,0:T(8,128)(2,1)S(1)}, u32[]{:S(2)}, u32[]{:S(2)}) %collective-permute-start.2) | collective-permute-done | bytes 786464 | tf_op jit(solution)/shard_map/ppermute | solution.py:29
  54.8 1.4 copy.11
  56.2 1.5 collective-permute-start.3
  58.8 1.6 collective-permute-start.5
  60.4 24.3 %collective-permute-done.3 = bf16[8,80,1024]{2,1,0:T(8,128)(2,1)S(1)} collective-permute-done((bf16[8,80,1024]{2,1,0:T(8,128)(2,1)S(1)}, bf16[8,80,1024]{2,1,0:T(8,128)(2,1)S(1)}, u32[]{:S(2)}, u32[]{:S(2)}) %collective-permute-start.3) | collective-permute-done | bytes 1310752 | tf_op jit(solution)/shard_map/ppermute | solution.py:29
  84.7 1.3 collective-permute-done.4
  86.0 1.3 collective-permute-done.5
  87.7 3.0 %collective-permute-start.7 = (bf16[3,8,80,1024]{3,2,1,0:T(8,128)(2,1)S(1)}, bf16[3,8,80,1024]{3,2,1,0:T(8,128)(2,1)S(1)}, u32[]{:S(2)}, u32[]{:S(2)}) collective-permute-start(bf16[3,8,80,1024]{3,2,1,0:T(8,128)(2,1)S(1)} %pad_maximum_fusion.refs_1_), channel_id=1, source_target_pairs={{0,1},{1,0},{2,3},{3,2},{4,5},{5,4},{6,7},{7,6},{8,9},{9,8},{10,11... | collective-permute-start | bytes 11796488 | tf_op jit(solution)/shard_map/ppermute | solution.py:29
  90.8 4.6 %shard_map.89 = (bf16[320,1024]{1,0:T(8,128)(2,1)S(1)}, bf16[320,1024]{1,0:T(8,128)(2,1)S(1)}, bf16[320,1024]{1,0:T(8,128)(2,1)S(1)}, bf16[320,1024]{1,0:T(8,128...) custom-call(bf16[8,80,1024]{2,1,0:T(8,128)(2,1)S(1)} %bitcast.36, ...), custom_call_target="tpu_custom_call" | custom-call | tf_op jit(solution)/shard_map/pallas_call | solution.py:75
  100.5 1.5 collective-permute-start.10
  102.1 4.6 %shard_map.87 = (bf16[320,1024]{1,0:T(8,128)(2,1)S(1)}, bf16[320,1024]{1,0:T(8,128)(2,1)S(1)}, bf16[320,1024]{1,0:T(8,128)(2,1)S(1)}, bf16[320,1024]{1,0:T(8,128...) custom-call(bf16[8,80,1024]{2,1,0:T(8,128)(2,1)S(1)} %collective-per, ...), custom_call_target="tpu_custom_call" | custom-call | tf_op jit(solution)/shard_map/pallas_call | solution.py:75
  111.8 4.5 %shard_map.90 = (bf16[320,1024]{1,0:T(8,128)(2,1)S(1)}, bf16[320,1024]{1,0:T(8,128)(2,1)S(1)}, bf16[320,1024]{1,0:T(8,128)(2,1)S(1)}, bf16[320,1024]{1,0:T(8,128...) custom-call(bf16[8,80,1024]{2,1,0:T(8,128)(2,1)S(1)} %collective-per, ...), custom_call_target="tpu_custom_call" | custom-call | tf_op jit(solution)/shard_map/pallas_call | solution.py:75
  121.6 4.7 %shard_map.88 = (bf16[320,1024]{1,0:T(8,128)(2,1)S(1)}, bf16[320,1024]{1,0:T(8,128)(2,1)S(1)}, bf16[320,1024]{1,0:T(8,128)(2,1)S(1)}, bf16[320,1024]{1,0:T(8,128...) custom-call(bf16[8,80,1024]{2,1,0:T(8,128)(2,1)S(1)} %bitcast.37, ...), custom_call_target="tpu_custom_call" | custom-call | tf_op jit(solution)/shard_map/pallas_call | solution.py:75
  128.2 1.3 collective-permute-start.11
  129.7 1.4 collective-permute-start.19
  131.4 2.7 %collective-permute-done.11.refs_6_ = bf16[160,768]{1,0:T(8,128)(2,1)S(1)} collective-permute-done((bf16[160,768]{1,0:T(8,128)(2,1)S(1)}, bf16[160,768]{1,0:T(8,128)(2,1)S(1)}, u32[]{:S(2)}, u32[]{:S(2)}) %collective-permute-start.11) | collective-permute-done | bytes 245792 | tf_op jit(solution)/shard_map/ppermute | solution.py:29
  134.4 13.8 %collective-permute-done.12.refs_7_ = bf16[160,896]{1,0:T(8,128)(2,1)S(1)} collective-permute-done((bf16[160,896]{1,0:T(8,128)(2,1)S(1)}, bf16[160,896]{1,0:T(8,128)(2,1)S(1)}, u32[]{:S(2)}, u32[]{:S(2)}) %collective-permute-start.12) | collective-permute-done | bytes 286752 | tf_op jit(solution)/shard_map/ppermute | solution.py:29
  150.0 1.4 collective-permute-start.14
  152.1 1.2 collective-permute-start.22
  153.3 1.4 collective-permute-start.23
  155.1 1.4 collective-permute-start.21
  157.8 4.1 %collective-permute-done.21.refs_6_ = bf16[160,768]{1,0:T(8,128)(2,1)S(1)} collective-permute-done((bf16[160,768]{1,0:T(8,128)(2,1)S(1)}, bf16[160,768]{1,0:T(8,128)(2,1)S(1)}, u32[]{:S(2)}, u32[]{:S(2)}) %collective-permute-start.21) | collective-permute-done | bytes 245792 | tf_op jit(solution)/shard_map/ppermute | solution.py:29
  165.5 9.8 %collective-permute-done.24.refs_3_ = bf16[160,768]{1,0:T(8,128)(2,1)S(1)} collective-permute-done((bf16[160,768]{1,0:T(8,128)(2,1)S(1)}, bf16[160,768]{1,0:T(8,128)(2,1)S(1)}, u32[]{:S(2)}, u32[]{:S(2)}) %collective-permute-start.24) | collective-permute-done | bytes 245792 | tf_op jit(solution)/shard_map/ppermute | solution.py:29
  177.4 1.4 collective-permute-start.27
  178.8 5.6 %collective-permute-done.30.refs_21_ = bf16[320,896]{1,0:T(8,128)(2,1)S(1)} collective-permute-done((bf16[320,896]{1,0:T(8,128)(2,1)S(1)}, bf16[320,896]{1,0:T(8,128)(2,1)S(1)}, u32[]{:S(2)}, u32[]{:S(2)}) %collective-permute-start.30) | collective-permute-done | bytes 573472 | tf_op jit(solution)/shard_map/ppermute | solution.py:29
  185.5 5.5 %collective-permute-done.29.refs_19_ = bf16[320,896]{1,0:T(8,128)(2,1)S(1)} collective-permute-done((bf16[320,896]{1,0:T(8,128)(2,1)S(1)}, bf16[320,896]{1,0:T(8,128)(2,1)S(1)}, u32[]{:S(2)}, u32[]{:S(2)}) %collective-permute-start.29) | collective-permute-done | bytes 573472 | tf_op jit(solution)/shard_map/ppermute | solution.py:29
  191.0 5.6 %collective-permute-done.31.refs_23_ = bf16[320,896]{1,0:T(8,128)(2,1)S(1)} collective-permute-done((bf16[320,896]{1,0:T(8,128)(2,1)S(1)}, bf16[320,896]{1,0:T(8,128)(2,1)S(1)}, u32[]{:S(2)}, u32[]{:S(2)}) %collective-permute-start.31) | collective-permute-done | bytes 573472 | tf_op jit(solution)/shard_map/ppermute | solution.py:29
  197.5 7.5 %shard_map.97 = (f32[512,512]{1,0:T(8,128)}, f32[384,512]{1,0:T(8,128)}, f32[384,512]{1,0:T(8,128)}, bf16[512,512]{1,0:T(8,128)(2,1)}, bf16[384,512]{1,0:T(8,128...) custom-call(bf16[320,1024]{1,0:T(8,128)(2,1)} %copy-done.27, bf16[320,1024]{1,0:T(8,128)(2,1)} %copy-done.18, ...), custom_call_target="tpu_custom_call" | custom-call | tf_op jit(solution)/shard_map/pallas_call | solution.py:75
  205.0 1.4 collective-permute-start.32
  206.4 1.2 collective-permute-start.33
  208.3 9.9 %shard_map.98 = (f32[512,512]{1,0:T(8,128)}, f32[512,384]{1,0:T(8,128)}, f32[512,384]{1,0:T(8,128)}, bf16[512,512]{1,0:T(8,128)(2,1)}, bf16[512,384]{1,0:T(8,128...) custom-call(bf16[320,1024]{1,0:T(8,128)(2,1)} %copy-done.39, bf16[320,1024]{1,0:T(8,128)(2,1)} %copy-done.30, ...), custom_call_target="tpu_custom_call" | custom-call | tf_op jit(solution)/shard_map/pallas_call | solution.py:75
  219.0 2.0 collective-permute-start.37
  221.7 1.4 collective-permute-start.43
  224.1 1.2 collective-permute-start.38
  225.4 9.2 %collective-permute-start.39 = (f32[32,512]{1,0:T(8,128)S(1)}, f32[32,512]{1,0:T(8,128)S(1)}, u32[]{:S(2)}, u32[]{:S(2)}) collective-permute-start(f32[32,512]{1,0:T(8,128)S(1)} %add_add_fusion.1), channel_id=1, source_target_pairs={{0,1},{1,0},{2,3},{3,2},{4,5},{5,4},{6,7},{7,6},{8,9},{9,8},{10,11... | collective-permute-start | bytes 196616 | tf_op jit(solution)/shard_map/ppermute | solution.py:537
  234.7 5.5 %collective-permute-start.40 = (f32[32,512]{1,0:T(8,128)S(1)}, f32[32,512]{1,0:T(8,128)S(1)}, u32[]{:S(2)}, u32[]{:S(2)}) collective-permute-start(f32[32,512]{1,0:T(8,128)S(1)} %add_add_fusion.1), channel_id=1, source_target_pairs={{0,9},{1,8},{2,11},{3,10},{4,13},{5,12},{6,15},{7,14},{8,1},{9,0},... | collective-permute-start | bytes 196616 | tf_op jit(solution)/shard_map/ppermute | solution.py:537
  240.4 2.6 collective-permute-done.40
  244.1 4.8 %shard_map.99 = (f32[32,512]{1,0:T(8,128)S(1)}, f32[8,128]{1,0:T(8,128)S(1)}) custom-call(f32[32,512]{1,0:T(8,128)S(1)} %concatenate.6.prev, f32[32,512]{1,0:T(8,128)S(1)} %get-tuple-element.269.group_sums, f32[32,512]{1,0:T(8,128)S(1)} %get-tuple-element.245.whole_sums, f32[512,512]{1,0:T(8,128)} %get-tuple-element.246.refs_0_, ...), custom_call_target="tpu_custom_call" | custom-call | tf_op jit(solution)/shard_map/pallas_call | solution.py:75
  250.3 1.3 collective-permute-start.46
  253.6 3.4 %collective-permute-start.48 = (f32[8,128]{1,0:T(8,128)S(1)}, f32[8,128]{1,0:T(8,128)S(1)}, u32[]{:S(2)}, u32[]{:S(2)}) collective-permute-start(f32[8,128]{1,0:T(8,128)S(1)} %add_add_fusion.3), channel_id=1, source_target_pairs={{0,1},{1,0},{2,3},{3,2},{4,5},{5,4},{6,7},{7,6},{8,9},{9,8},{10,11... | collective-permute-start | bytes 12296 | tf_op jit(solution)/shard_map/ppermute | solution.py:537
  257.9 2.2 collective-permute-done.49
  260.1 6.6 %shard_map.100 = (bf16[512,2560]{1,0:T(8,128)(2,1)}, bf16[2560,512]{1,0:T(8,128)(2,1)}) custom-call(f32[32,512]{1,0:T(8,128)S(1)} %concatenate.6.prev, f32[32,512]{1,0:T(8,128)S(1)} %get-tuple-element.252.factors, f32[32,512]{1,0:T(8,128)S(1)} %get-tuple-element.245.whole_sums, f32[8,128]{1,0:T(8,128)S(1)} %add_add_fusion.2.norms, ...), custom_call_target="tpu_custom_call" | custom-call | tf_op jit(solution)/shard_map/pallas_call | solution.py:75
  (217 shorter events, 51.0 us)
Async XLA Ops:
  6.7 48.1 %all-to-all-start = ((bf16[16,40,1024]{2,1,0:T(8,128)(2,1)}), bf16[16,40,1024]{2,1,0:T(8,128)(2,1)}, u32[]{:S(2)}, u32[]{:S(2)}) async-start(bf16[16,40,1024]{2,1,0:T(8,128)(2,1)} %pad_maximum_fusion.1), calls=%async_computation | async-start | bytes 2621440 | tf_op jit(solution)/shard_map/all_to_all | solution.py:431
  20.6 34.2 %collective-permute-start = (bf16[4096,128]{1,0:T(8,128)(2,1)S(1)}, bf16[4096,128]{1,0:T(8,128)(2,1)S(1)}, u32[]{:S(2)}, u32[]{:S(2)}) collective-permute-start(bf16[4096,128]{1,0:T(8,128)(2,1)S(1)} %get-tuple-element.132), channel_id=1, source_target_pairs={{0,2},{2,0},{4,6},{6,4},{8,10},{10,8},{12,14},{14,12},{16,18},{18,... | collective-permute-start | bytes 3145736 | tf_op jit(solution)/shard_map/ppermute | solution.py:29
  21.9 26.6 %collective-permute-start.1 = (bf16[3072,128]{1,0:T(8,128)(2,1)S(1)}, bf16[3072,128]{1,0:T(8,128)(2,1)S(1)}, u32[]{:S(2)}, u32[]{:S(2)}) collective-permute-start(bf16[3072,128]{1,0:T(8,128)(2,1)S(1)} %get-tuple-element.133), channel_id=1, source_target_pairs={{0,4},{2,6},{4,0},{6,2},{8,12},{10,14},{12,8},{14,10},{16,20},{18,... | collective-permute-start | bytes 2359304 | tf_op jit(solution)/shard_map/ppermute | solution.py:29
  23.1 31.0 %collective-permute-start.2 = (bf16[3072,128]{1,0:T(8,128)(2,1)S(1)}, bf16[3072,128]{1,0:T(8,128)(2,1)S(1)}, u32[]{:S(2)}, u32[]{:S(2)}) collective-permute-start(bf16[3072,128]{1,0:T(8,128)(2,1)S(1)} %get-tuple-element.134), channel_id=1, source_target_pairs={{0,8},{2,10},{4,12},{6,14},{8,0},{10,2},{12,4},{14,6},{16,24},{18,... | collective-permute-start | bytes 2359304 | tf_op jit(solution)/shard_map/ppermute | solution.py:29
  56.2 28.5 %collective-permute-start.3 = (bf16[8,80,1024]{2,1,0:T(8,128)(2,1)S(1)}, bf16[8,80,1024]{2,1,0:T(8,128)(2,1)S(1)}, u32[]{:S(2)}, u32[]{:S(2)}) collective-permute-start(bf16[8,80,1024]{2,1,0:T(8,128)(2,1)S(1)} %bitcast.32), channel_id=1, source_target_pairs={{0,2},{2,0},{4,6},{6,4},{8,10},{10,8},{12,14},{14,12},{16,18},{18,... | collective-permute-start | bytes 3932168 | tf_op jit(solution)/shard_map/ppermute | solution.py:29
  57.7 28.2 %collective-permute-start.4 = (bf16[8,80,1024]{2,1,0:T(8,128)(2,1)S(1)}, bf16[8,80,1024]{2,1,0:T(8,128)(2,1)S(1)}, u32[]{:S(2)}, u32[]{:S(2)}) collective-permute-start(bf16[8,80,1024]{2,1,0:T(8,128)(2,1)S(1)} %bitcast.33), channel_id=1, source_target_pairs={{0,4},{2,6},{4,0},{6,2},{8,12},{10,14},{12,8},{14,10},{16,20},{18,... | collective-permute-start | bytes 3932168 | tf_op jit(solution)/shard_map/ppermute | solution.py:29
  58.8 28.4 %collective-permute-start.5 = (bf16[8,80,1024]{2,1,0:T(8,128)(2,1)S(1)}, bf16[8,80,1024]{2,1,0:T(8,128)(2,1)S(1)}, u32[]{:S(2)}, u32[]{:S(2)}) collective-permute-start(bf16[8,80,1024]{2,1,0:T(8,128)(2,1)S(1)} %bitcast.34), channel_id=1, source_target_pairs={{0,8},{2,10},{4,12},{6,14},{8,0},{10,2},{12,4},{14,6},{16,24},{18,... | collective-permute-start | bytes 3932168 | tf_op jit(solution)/shard_map/ppermute | solution.py:29
  87.7 14.4 %collective-permute-start.7 = (bf16[3,8,80,1024]{3,2,1,0:T(8,128)(2,1)S(1)}, bf16[3,8,80,1024]{3,2,1,0:T(8,128)(2,1)S(1)}, u32[]{:S(2)}, u32[]{:S(2)}) collective-permute-start(bf16[3,8,80,1024]{3,2,1,0:T(8,128)(2,1)S(1)} %pad_maximum_fusion.refs_1_), channel_id=1, source_target_pairs={{0,1},{1,0},{2,3},{3,2},{4,5},{5,4},{6,7},{7,6},{8,9},{9,8},{10,11... | collective-permute-start | bytes 11796488 | tf_op jit(solution)/shard_map/ppermute | solution.py:29
  90.7 11.4 %collective-permute-start.6 = (bf16[8,80,1024]{2,1,0:T(8,128)(2,1)S(1)}, bf16[8,80,1024]{2,1,0:T(8,128)(2,1)S(1)}, u32[]{:S(2)}, u32[]{:S(2)}) collective-permute-start(bf16[8,80,1024]{2,1,0:T(8,128)(2,1)S(1)} %bitcast.35), channel_id=1, source_target_pairs={{0,1},{1,0},{2,3},{3,2},{4,5},{5,4},{6,7},{7,6},{8,9},{9,8},{10,11... | collective-permute-start | bytes 3932168 | tf_op jit(solution)/shard_map/ppermute | solution.py:29
  100.5 25.9 %collective-permute-start.10 = (bf16[320,896]{1,0:T(8,128)(2,1)S(1)}, bf16[320,896]{1,0:T(8,128)(2,1)S(1)}, u32[]{:S(2)}, u32[]{:S(2)}) collective-permute-start(bf16[320,896]{1,0:T(8,128)(2,1)S(1)} %get-tuple-element.187), channel_id=1, source_target_pairs={{0,8},{2,10},{4,12},{6,14},{8,0},{10,2},{12,4},{14,6},{16,24},{18,... | collective-permute-start | bytes 1720328 | tf_op jit(solution)/shard_map/ppermute | solution.py:29
  102.0 24.4 %collective-permute-start.9 = (bf16[320,896]{1,0:T(8,128)(2,1)S(1)}, bf16[320,896]{1,0:T(8,128)(2,1)S(1)}, u32[]{:S(2)}, u32[]{:S(2)}) collective-permute-start(bf16[320,896]{1,0:T(8,128)(2,1)S(1)} %get-tuple-element.186), channel_id=1, source_target_pairs={{0,4},{2,6},{4,0},{6,2},{8,12},{10,14},{12,8},{14,10},{16,20},{18,... | collective-permute-start | bytes 1720328 | tf_op jit(solution)/shard_map/ppermute | solution.py:29
  102.0 24.4 %collective-permute-start.8 = (bf16[320,768]{1,0:T(8,128)(2,1)S(1)}, bf16[320,768]{1,0:T(8,128)(2,1)S(1)}, u32[]{:S(2)}, u32[]{:S(2)}) collective-permute-start(bf16[320,768]{1,0:T(8,128)(2,1)S(1)} %get-tuple-element.185), channel_id=1, source_target_pairs={{0,2},{2,0},{4,6},{6,4},{8,10},{10,8},{12,14},{14,12},{16,18},{18,... | collective-permute-start | bytes 1474568 | tf_op jit(solution)/shard_map/ppermute | solution.py:29
  128.2 5.9 %collective-permute-start.11 = (bf16[160,768]{1,0:T(8,128)(2,1)S(1)}, bf16[160,768]{1,0:T(8,128)(2,1)S(1)}, u32[]{:S(2)}, u32[]{:S(2)}) collective-permute-start(bf16[160,768]{1,0:T(8,128)(2,1)S(1)} %get-tuple-element.194), channel_id=1, source_target_pairs={{0,2},{2,0},{4,6},{6,4},{8,10},{10,8},{12,14},{14,12},{16,18},{18,... | collective-permute-start | bytes 737288 | tf_op jit(solution)/shard_map/ppermute | solution.py:29
  129.5 22.2 %collective-permute-start.18 = (bf16[320,768]{1,0:T(8,128)(2,1)S(1)}, bf16[320,768]{1,0:T(8,128)(2,1)S(1)}, u32[]{:S(2)}, u32[]{:S(2)}) collective-permute-start(bf16[320,768]{1,0:T(8,128)(2,1)S(1)} %get-tuple-element.148), channel_id=1, source_target_pairs={{0,2},{2,0},{4,6},{6,4},{8,10},{10,8},{12,14},{14,12},{16,18},{18,... | collective-permute-start | bytes 1474568 | tf_op jit(solution)/shard_map/ppermute | solution.py:29
  129.7 22.1 %collective-permute-start.19 = (bf16[320,896]{1,0:T(8,128)(2,1)S(1)}, bf16[320,896]{1,0:T(8,128)(2,1)S(1)}, u32[]{:S(2)}, u32[]{:S(2)}) collective-permute-start(bf16[320,896]{1,0:T(8,128)(2,1)S(1)} %get-tuple-element.149), channel_id=1, source_target_pairs={{0,4},{2,6},{4,0},{6,2},{8,12},{10,14},{12,8},{14,10},{16,20},{18,... | collective-permute-start | bytes 1720328 | tf_op jit(solution)/shard_map/ppermute | solution.py:29
  131.1 20.7 %collective-permute-start.20 = (bf16[320,896]{1,0:T(8,128)(2,1)S(1)}, bf16[320,896]{1,0:T(8,128)(2,1)S(1)}, u32[]{:S(2)}, u32[]{:S(2)}) collective-permute-start(bf16[320,896]{1,0:T(8,128)(2,1)S(1)} %get-tuple-element.150), channel_id=1, source_target_pairs={{0,8},{2,10},{4,12},{6,14},{8,0},{10,2},{12,4},{14,6},{16,24},{18,... | collective-permute-start | bytes 1720328 | tf_op jit(solution)/shard_map/ppermute | solution.py:29
  131.4 16.8 %collective-permute-start.12 = (bf16[160,896]{1,0:T(8,128)(2,1)S(1)}, bf16[160,896]{1,0:T(8,128)(2,1)S(1)}, u32[]{:S(2)}, u32[]{:S(2)}) collective-permute-start(bf16[160,896]{1,0:T(8,128)(2,1)S(1)} %get-tuple-element.195), channel_id=1, source_target_pairs={{0,4},{2,6},{4,0},{6,2},{8,12},{10,14},{12,8},{14,10},{16,20},{18,... | collective-permute-start | bytes 860168 | tf_op jit(solution)/shard_map/ppermute | solution.py:29
  134.1 15.2 %collective-permute-start.13 = (bf16[160,896]{1,0:T(8,128)(2,1)S(1)}, bf16[160,896]{1,0:T(8,128)(2,1)S(1)}, u32[]{:S(2)}, u32[]{:S(2)}) collective-permute-start(bf16[160,896]{1,0:T(8,128)(2,1)S(1)} %get-tuple-element.196), channel_id=1, source_target_pairs={{0,8},{2,10},{4,12},{6,14},{8,0},{10,2},{12,4},{14,6},{16,24},{18,... | collective-permute-start | bytes 860168 | tf_op jit(solution)/shard_map/ppermute | solution.py:29
  150.0 5.1 %collective-permute-start.14 = (bf16[160,768]{1,0:T(8,128)(2,1)S(1)}, bf16[160,768]{1,0:T(8,128)(2,1)S(1)}, u32[]{:S(2)}, u32[]{:S(2)}) collective-permute-start(bf16[160,768]{1,0:T(8,128)(2,1)S(1)} %get-tuple-element.197.refs_0_), channel_id=1, source_target_pairs={{0,2},{2,0},{4,6},{6,4},{8,10},{10,8},{12,14},{14,12},{16,18},{18,... | collective-permute-start | bytes 737288 | tf_op jit(solution)/shard_map/ppermute | solution.py:29
  151.5 5.8 %collective-permute-start.15 = (bf16[160,896]{1,0:T(8,128)(2,1)S(1)}, bf16[160,896]{1,0:T(8,128)(2,1)S(1)}, u32[]{:S(2)}, u32[]{:S(2)}) collective-permute-start(bf16[160,896]{1,0:T(8,128)(2,1)S(1)} %get-tuple-element.198.refs_1_), channel_id=1, source_target_pairs={{0,4},{2,6},{4,0},{6,2},{8,12},{10,14},{12,8},{14,10},{16,20},{18,... | collective-permute-start | bytes 860168 | tf_op jit(solution)/shard_map/ppermute | solution.py:29
  151.8 5.8 %collective-permute-start.16 = (bf16[160,896]{1,0:T(8,128)(2,1)S(1)}, bf16[160,896]{1,0:T(8,128)(2,1)S(1)}, u32[]{:S(2)}, u32[]{:S(2)}) collective-permute-start(bf16[160,896]{1,0:T(8,128)(2,1)S(1)} %get-tuple-element.199.refs_2_), channel_id=1, source_target_pairs={{0,8},{2,10},{4,12},{6,14},{8,0},{10,2},{12,4},{14,6},{16,24},{18,... | collective-permute-start | bytes 860168 | tf_op jit(solution)/shard_map/ppermute | solution.py:29
  152.1 10.3 %collective-permute-start.22 = (bf16[160,896]{1,0:T(8,128)(2,1)S(1)}, bf16[160,896]{1,0:T(8,128)(2,1)S(1)}, u32[]{:S(2)}, u32[]{:S(2)}) collective-permute-start(bf16[160,896]{1,0:T(8,128)(2,1)S(1)} %get-tuple-element.214), channel_id=1, source_target_pairs={{0,4},{2,6},{4,0},{6,2},{8,12},{10,14},{12,8},{14,10},{16,20},{18,... | collective-permute-start | bytes 860168 | tf_op jit(solution)/shard_map/ppermute | solution.py:29
  153.3 9.3 %collective-permute-start.23 = (bf16[160,896]{1,0:T(8,128)(2,1)S(1)}, bf16[160,896]{1,0:T(8,128)(2,1)S(1)}, u32[]{:S(2)}, u32[]{:S(2)}) collective-permute-start(bf16[160,896]{1,0:T(8,128)(2,1)S(1)} %get-tuple-element.215), channel_id=1, source_target_pairs={{0,8},{2,10},{4,12},{6,14},{8,0},{10,2},{12,4},{14,6},{16,24},{18,... | collective-permute-start | bytes 860168 | tf_op jit(solution)/shard_map/ppermute | solution.py:29
  155.1 6.7 %collective-permute-start.21 = (bf16[160,768]{1,0:T(8,128)(2,1)S(1)}, bf16[160,768]{1,0:T(8,128)(2,1)S(1)}, u32[]{:S(2)}, u32[]{:S(2)}) collective-permute-start(bf16[160,768]{1,0:T(8,128)(2,1)S(1)} %get-tuple-element.213), channel_id=1, source_target_pairs={{0,2},{2,0},{4,6},{6,4},{8,10},{10,8},{12,14},{14,12},{16,18},{18,... | collective-permute-start | bytes 737288 | tf_op jit(solution)/shard_map/ppermute | solution.py:29
  157.7 19.7 %collective-permute-start.17 = (bf16[320,768]{1,0:T(8,128)(2,1)S(1)}, bf16[320,768]{1,0:T(8,128)(2,1)S(1)}, u32[]{:S(2)}, u32[]{:S(2)}) collective-permute-start(bf16[320,768]{1,0:T(8,128)(2,1)S(1)} %get-tuple-element.200.refs_12_), channel_id=1, source_target_pairs={{0,2},{2,0},{4,6},{6,4},{8,10},{10,8},{12,14},{14,12},{16,18},{18,... | collective-permute-start | bytes 1474568 | tf_op jit(solution)/shard_map/ppermute | solution.py:29
  163.4 12.3 %collective-permute-start.25 = (bf16[160,896]{1,0:T(8,128)(2,1)S(1)}, bf16[160,896]{1,0:T(8,128)(2,1)S(1)}, u32[]{:S(2)}, u32[]{:S(2)}) collective-permute-start(bf16[160,896]{1,0:T(8,128)(2,1)S(1)} %get-tuple-element.217.refs_1_), channel_id=1, source_target_pairs={{0,4},{2,6},{4,0},{6,2},{8,12},{10,14},{12,8},{14,10},{16,20},{18,... | collective-permute-start | bytes 860168 | tf_op jit(solution)/shard_map/ppermute | solution.py:29
  164.3 11.3 %collective-permute-start.26 = (bf16[160,896]{1,0:T(8,128)(2,1)S(1)}, bf16[160,896]{1,0:T(8,128)(2,1)S(1)}, u32[]{:S(2)}, u32[]{:S(2)}) collective-permute-start(bf16[160,896]{1,0:T(8,128)(2,1)S(1)} %get-tuple-element.218.refs_2_), channel_id=1, source_target_pairs={{0,8},{2,10},{4,12},{6,14},{8,0},{10,2},{12,4},{14,6},{16,24},{18,... | collective-permute-start | bytes 860168 | tf_op jit(solution)/shard_map/ppermute | solution.py:29
  164.4 11.0 %collective-permute-start.24 = (bf16[160,768]{1,0:T(8,128)(2,1)S(1)}, bf16[160,768]{1,0:T(8,128)(2,1)S(1)}, u32[]{:S(2)}, u32[]{:S(2)}) collective-permute-start(bf16[160,768]{1,0:T(8,128)(2,1)S(1)} %get-tuple-element.216.refs_0_), channel_id=1, source_target_pairs={{0,2},{2,0},{4,6},{6,4},{8,10},{10,8},{12,14},{14,12},{16,18},{18,... | collective-permute-start | bytes 737288 | tf_op jit(solution)/shard_map/ppermute | solution.py:29
  164.8 14.0 %collective-permute-start.28 = (bf16[320,896]{1,0:T(8,128)(2,1)S(1)}, bf16[320,896]{1,0:T(8,128)(2,1)S(1)}, u32[]{:S(2)}, u32[]{:S(2)}) collective-permute-start(bf16[320,896]{1,0:T(8,128)(2,1)S(1)} %get-tuple-element.220.refs_16_), channel_id=1, source_target_pairs={{0,4},{2,6},{4,0},{6,2},{8,12},{10,14},{12,8},{14,10},{16,20},{18,... | collective-permute-start | bytes 1720328 | tf_op jit(solution)/shard_map/ppermute | solution.py:29
  175.3 9.0 %collective-permute-start.30 = (bf16[320,896]{1,0:T(8,128)(2,1)S(1)}, bf16[320,896]{1,0:T(8,128)(2,1)S(1)}, u32[]{:S(2)}, u32[]{:S(2)}) collective-permute-start(bf16[320,896]{1,0:T(8,128)(2,1)S(1)} %get-tuple-element.222.refs_20_), channel_id=1, source_target_pairs={{0,8},{2,10},{4,12},{6,14},{8,0},{10,2},{12,4},{14,6},{16,24},{18,... | collective-permute-start | bytes 1720328 | tf_op jit(solution)/shard_map/ppermute | solution.py:29
  175.9 15.1 %collective-permute-start.29 = (bf16[320,896]{1,0:T(8,128)(2,1)S(1)}, bf16[320,896]{1,0:T(8,128)(2,1)S(1)}, u32[]{:S(2)}, u32[]{:S(2)}) collective-permute-start(bf16[320,896]{1,0:T(8,128)(2,1)S(1)} %get-tuple-element.221.refs_18_), channel_id=1, source_target_pairs={{0,4},{2,6},{4,0},{6,2},{8,12},{10,14},{12,8},{14,10},{16,20},{18,... | collective-permute-start | bytes 1720328 | tf_op jit(solution)/shard_map/ppermute | solution.py:29
  176.2 20.4 %collective-permute-start.31 = (bf16[320,896]{1,0:T(8,128)(2,1)S(1)}, bf16[320,896]{1,0:T(8,128)(2,1)S(1)}, u32[]{:S(2)}, u32[]{:S(2)}) collective-permute-start(bf16[320,896]{1,0:T(8,128)(2,1)S(1)} %get-tuple-element.223.refs_22_), channel_id=1, source_target_pairs={{0,8},{2,10},{4,12},{6,14},{8,0},{10,2},{12,4},{14,6},{16,24},{18,... | collective-permute-start | bytes 1720328 | tf_op jit(solution)/shard_map/ppermute | solution.py:29
  177.4 8.2 %collective-permute-start.27 = (bf16[320,768]{1,0:T(8,128)(2,1)S(1)}, bf16[320,768]{1,0:T(8,128)(2,1)S(1)}, u32[]{:S(2)}, u32[]{:S(2)}) collective-permute-start(bf16[320,768]{1,0:T(8,128)(2,1)S(1)} %get-tuple-element.219.refs_14_), channel_id=1, source_target_pairs={{0,2},{2,0},{4,6},{6,4},{8,10},{10,8},{12,14},{14,12},{16,18},{18,... | collective-permute-start | bytes 1474568 | tf_op jit(solution)/shard_map/ppermute | solution.py:29
  205.0 13.3 %collective-permute-start.32 = (bf16[512,512]{1,0:T(8,128)(2,1)}, bf16[512,512]{1,0:T(8,128)(2,1)S(1)}, u32[]{:S(2)}, u32[]{:S(2)}) collective-permute-start(bf16[512,512]{1,0:T(8,128)(2,1)} %get-tuple-element.238.refs_9_), channel_id=1, source_target_pairs={{0,2},{2,0},{4,6},{6,4},{8,10},{10,8},{12,14},{14,12},{16,18},{18,... | collective-permute-start | bytes 1572872 | tf_op jit(solution)/shard_map/ppermute | solution.py:29
  206.4 11.8 %collective-permute-start.33 = (bf16[384,512]{1,0:T(8,128)(2,1)}, bf16[384,512]{1,0:T(8,128)(2,1)S(1)}, u32[]{:S(2)}, u32[]{:S(2)}) collective-permute-start(bf16[384,512]{1,0:T(8,128)(2,1)} %get-tuple-element.239.refs_10_), channel_id=1, source_target_pairs={{0,4},{2,6},{4,0},{6,2},{8,12},{10,14},{12,8},{14,10},{16,20},{18,... | collective-permute-start | bytes 1179656 | tf_op jit(solution)/shard_map/ppermute | solution.py:29
  207.6 10.6 %collective-permute-start.34 = (bf16[384,512]{1,0:T(8,128)(2,1)}, bf16[384,512]{1,0:T(8,128)(2,1)S(1)}, u32[]{:S(2)}, u32[]{:S(2)}) collective-permute-start(bf16[384,512]{1,0:T(8,128)(2,1)} %get-tuple-element.240.refs_11_), channel_id=1, source_target_pairs={{0,8},{2,10},{4,12},{6,14},{8,0},{10,2},{12,4},{14,6},{16,24},{18,... | collective-permute-start | bytes 1179656 | tf_op jit(solution)/shard_map/ppermute | solution.py:29
  218.2 3.5 %collective-permute-start.35 = (f32[32,512]{1,0:T(8,128)}, f32[32,512]{1,0:T(8,128)S(1)}, u32[]{:S(2)}, u32[]{:S(2)}) collective-permute-start(f32[32,512]{1,0:T(8,128)} %get-tuple-element.241), channel_id=1, source_target_pairs={{0,2},{2,0},{4,6},{6,4},{8,10},{10,8},{12,14},{14,12},{16,18},{18,... | collective-permute-start | bytes 196616 | tf_op jit(solution)/shard_map/ppermute | solution.py:29
  218.7 4.4 %collective-permute-start.36 = (f32[32,512]{1,0:T(8,128)}, f32[32,512]{1,0:T(8,128)S(1)}, u32[]{:S(2)}, u32[]{:S(2)}) collective-permute-start(f32[32,512]{1,0:T(8,128)} %get-tuple-element.241), channel_id=1, source_target_pairs={{0,4},{2,6},{4,0},{6,2},{8,12},{10,14},{12,8},{14,10},{16,20},{18,... | collective-permute-start | bytes 196616 | tf_op jit(solution)/shard_map/ppermute | solution.py:29
  219.0 4.2 %collective-permute-start.37 = (f32[32,512]{1,0:T(8,128)}, f32[32,512]{1,0:T(8,128)S(1)}, u32[]{:S(2)}, u32[]{:S(2)}) collective-permute-start(f32[32,512]{1,0:T(8,128)} %get-tuple-element.241), channel_id=1, source_target_pairs={{0,6},{2,4},{4,2},{6,0},{8,14},{10,12},{12,10},{14,8},{16,22},{18,... | collective-permute-start | bytes 196616 | tf_op jit(solution)/shard_map/ppermute | solution.py:29
  221.0 22.0 %collective-permute-start.41 = (bf16[512,512]{1,0:T(8,128)(2,1)}, bf16[512,512]{1,0:T(8,128)(2,1)}, u32[]{:S(2)}, u32[]{:S(2)}) collective-permute-start(bf16[512,512]{1,0:T(8,128)(2,1)} %get-tuple-element.242.refs_3_), channel_id=1, source_target_pairs={{0,2},{2,0},{4,6},{6,4},{8,10},{10,8},{12,14},{14,12},{16,18},{18,... | collective-permute-start | bytes 1572872 | tf_op jit(solution)/shard_map/ppermute | solution.py:29
  221.5 21.5 %collective-permute-start.42 = (bf16[512,384]{1,0:T(8,128)(2,1)}, bf16[512,384]{1,0:T(8,128)(2,1)S(1)}, u32[]{:S(2)}, u32[]{:S(2)}) collective-permute-start(bf16[512,384]{1,0:T(8,128)(2,1)} %get-tuple-element.243.refs_4_), channel_id=1, source_target_pairs={{0,4},{2,6},{4,0},{6,2},{8,12},{10,14},{12,8},{14,10},{16,20},{18,... | collective-permute-start | bytes 1179656 | tf_op jit(solution)/shard_map/ppermute | solution.py:29
  221.7 21.3 %collective-permute-start.43 = (bf16[512,384]{1,0:T(8,128)(2,1)}, bf16[512,384]{1,0:T(8,128)(2,1)S(1)}, u32[]{:S(2)}, u32[]{:S(2)}) collective-permute-start(bf16[512,384]{1,0:T(8,128)(2,1)} %get-tuple-element.244.refs_5_), channel_id=1, source_target_pairs={{0,8},{2,10},{4,12},{6,14},{8,0},{10,2},{12,4},{14,6},{16,24},{18,... | collective-permute-start | bytes 1179656 | tf_op jit(solution)/shard_map/ppermute | solution.py:29
  224.1 10.6 %collective-permute-start.38 = (f32[32,512]{1,0:T(8,128)S(1)}, f32[32,512]{1,0:T(8,128)S(1)}, u32[]{:S(2)}, u32[]{:S(2)}) collective-permute-start(f32[32,512]{1,0:T(8,128)S(1)} %add_add_fusion.1), channel_id=1, source_target_pairs={{0,8},{2,10},{4,12},{6,14},{8,0},{10,2},{12,4},{14,6},{16,24},{18,... | collective-permute-start | bytes 196616 | tf_op jit(solution)/shard_map/ppermute | solution.py:29
  225.4 15.0 %collective-permute-start.39 = (f32[32,512]{1,0:T(8,128)S(1)}, f32[32,512]{1,0:T(8,128)S(1)}, u32[]{:S(2)}, u32[]{:S(2)}) collective-permute-start(f32[32,512]{1,0:T(8,128)S(1)} %add_add_fusion.1), channel_id=1, source_target_pairs={{0,1},{1,0},{2,3},{3,2},{4,5},{5,4},{6,7},{7,6},{8,9},{9,8},{10,11... | collective-permute-start | bytes 196616 | tf_op jit(solution)/shard_map/ppermute | solution.py:537
  234.7 8.3 %collective-permute-start.40 = (f32[32,512]{1,0:T(8,128)S(1)}, f32[32,512]{1,0:T(8,128)S(1)}, u32[]{:S(2)}, u32[]{:S(2)}) collective-permute-start(f32[32,512]{1,0:T(8,128)S(1)} %add_add_fusion.1), channel_id=1, source_target_pairs={{0,9},{1,8},{2,11},{3,10},{4,13},{5,12},{6,15},{7,14},{8,1},{9,0},... | collective-permute-start | bytes 196616 | tf_op jit(solution)/shard_map/ppermute | solution.py:537
  250.3 3.4 %collective-permute-start.46 = (f32[8,128]{1,0:T(8,128)S(1)}, f32[8,128]{1,0:T(8,128)S(1)}, u32[]{:S(2)}, u32[]{:S(2)}) collective-permute-start(f32[8,128]{1,0:T(8,128)S(1)} %get-tuple-element.253), channel_id=1, source_target_pairs={{0,6},{2,4},{4,2},{6,0},{8,14},{10,12},{12,10},{14,8},{16,22},{18,... | collective-permute-start | bytes 12296 | tf_op jit(solution)/shard_map/ppermute | solution.py:29
  253.6 3.7 %collective-permute-start.47 = (f32[8,128]{1,0:T(8,128)S(1)}, f32[8,128]{1,0:T(8,128)S(1)}, u32[]{:S(2)}, u32[]{:S(2)}) collective-permute-start(f32[8,128]{1,0:T(8,128)S(1)} %add_add_fusion.3), channel_id=1, source_target_pairs={{0,8},{2,10},{4,12},{6,14},{8,0},{10,2},{12,4},{14,6},{16,24},{18,... | collective-permute-start | bytes 12296 | tf_op jit(solution)/shard_map/ppermute | solution.py:29
  253.6 4.3 %collective-permute-start.48 = (f32[8,128]{1,0:T(8,128)S(1)}, f32[8,128]{1,0:T(8,128)S(1)}, u32[]{:S(2)}, u32[]{:S(2)}) collective-permute-start(f32[8,128]{1,0:T(8,128)S(1)} %add_add_fusion.3), channel_id=1, source_target_pairs={{0,1},{1,0},{2,3},{3,2},{4,5},{5,4},{6,7},{7,6},{8,9},{9,8},{10,11... | collective-permute-start | bytes 12296 | tf_op jit(solution)/shard_map/ppermute | solution.py:537
  (59 other events, 374.2 us)

commit v7 on v5

--- a/solution.py
+++ b/solution.py
@@ -21,7 +21,7 @@
 MASKS = (1, 2, 4)
 
 MIB = 1024 * 1024
-CUT_MIB = 44
+CUT_MIB = 8
 
 
 def swap(value, mask, axis="expert"):
@@ -67,7 +67,7 @@
 def call(kernel, mib, out_shape, *operands, scratch=(), streamed=(), streamed_out=(), whole=()):
     def spec(value, n, blocks, refs):
         if n in refs:
-            return pl.BlockSpec(memory_space=pl.ANY)
+            return pl.BlockSpec(memory_space=pltpu.HBM)
         if n in blocks:
             return pl.BlockSpec(value.shape, lambda: (0,) * len(value.shape))
         return pl.BlockSpec(memory_space=pltpu.VMEM)
@@ -151,25 +151,30 @@
     return jnp.concatenate([ref[at + n * rows : at + (n + 1) * rows, :] for n in range(blocks)], axis=1)
 
 
+def assemble(rows, start, own, pair, lanes, k, axis, side):
+    count, width = own.shape[1], rows.shape[1] // 2
+    first, second = 1 << axis, 1 << (3 - axis - k)
+    for j in range(2):
+        for l in range(2):
+            chunk = flipped(place_in_group(), side * first + j * second + l * (1 << k))
+            at = start + (j * 2 + l) * count
+            rows[at : at + count, :width] = own[chunk, :, lanes]
+            rows[at : at + count, width:] = pair[chunk, :, lanes]
+
+
 def sums_kernel(side, halves, is_packed, *refs):
     own, pairs, own_weights, got_weights = refs[0], refs[1], refs[2:8], refs[8:14]
-    rows_out, sums_out = refs[14:20], refs[20:]
-    count, width = own.shape[1], own.shape[2] // 2
+    sums_out, rows = refs[14:-1], refs[-1]
+    width = own.shape[2] // 2
     for matrix in range(2):
         lanes = slice(matrix * width, (matrix + 1) * width)
         for k in range(3):
             n, half = 3 * matrix + k, halves[k]
             axis = packed_place(0, matrix, k, halves)[0]
-            first, second = 1 << axis, 1 << (3 - axis - k)
-            for j in range(2):
-                for l in range(2):
-                    chunk = flipped(place_in_group(), side * first + j * second + l * (1 << k))
-                    at = (j * 2 + l) * count
-                    rows_out[n][at : at + count, :width] = own[chunk, :, lanes]
-                    rows_out[n][at : at + count, width:] = pairs[k, chunk, :, lanes]
+            assemble(rows.at[n], 0, own, pairs.at[k], lanes, k, axis, side)
             by_row = matrix == 1
             got = got_weight(got_weights[n], by_row, half, width) if is_packed else got_weights[n][...]
-            sums = partial_sum(rows_out[n][...], own_weights[n][...], got, by_row)
+            sums = partial_sum(rows[n], own_weights[n][...], got, by_row)
             if side:
                 at = packed_place(0, matrix, k, halves)[1]
                 sums_out[axis][:, at : at + half] = sums.astype(jnp.bfloat16)
@@ -214,38 +219,44 @@
             outs[axis][rows:, at : at + halves[k]] = got[source][:, start : start + halves[k]]
 
 
-def gradients(hidden_first, halves, rows, values, row_buffers, value_buffers, sems, own_out, sent_out, sums_out):
+def gradients(hidden_first, halves, blocks, values, buffers, own_out, sent_out, sums_out):
+    own_buffer, pair_buffer, rows, value_buffers, sems = buffers[0], buffers[1], buffers[2], buffers[3:6], buffers[6]
     matrix = 0 if hidden_first else 1
-    part = row_buffers.shape[1] // 4
-    width = row_buffers.shape[2] // 2
-
-    def copies(n, parts, buffer):
-        return [
-            pltpu.make_async_copy(parts[i], buffer.at[pl.ds(i * part, part)], sems.at[n * 4 + i]) for i in range(4)
-        ]
-
-    value_copies, row_copies = {}, {}
+    part = rows.shape[0] // 4
+    width = rows.shape[1] // 2
+    lanes = slice(width, 2 * width) if hidden_first else slice(0, width)
+    set_copies = []
     for k in range(3):
         axis, at = packed_place(1, matrix, k, halves)
-        row_copies[k] = copies(k, rows[4 * k : 4 * k + 4], row_buffers.at[k])
         parts, buffer = values[4 * axis : 4 * axis + 4], value_buffers[axis]
         if all(half % 128 == 0 for half in halves):
             parts = [value.at[:, at : at + halves[k]] for value in parts]
             buffer = buffer.at[:, at : at + halves[k]]
-        value_copies[k] = copies(3 + axis, parts, buffer)
-        for copy in row_copies[k] + value_copies[k]:
+        moves = [(parts[i], buffer.at[pl.ds(i * part, part)]) for i in range(4)]
+        for chain in range(2):
+            moves.append((blocks[2 * chain + 1].at[k, :, :, lanes], pair_buffer.at[chain, k]))
+            if k == 0:
+                moves.append((blocks[2 * chain].at[:, :, lanes], own_buffer.at[chain]))
+        copies = [pltpu.make_async_copy(*move, sems.at[k * 8 + n]) for n, move in enumerate(moves)]
+        for copy in copies:
             copy.start()
-    for k in range(3):
-        for copy in row_copies[k] + value_copies[k]:
+        set_copies.append(copies)
+    for k in range(3):
+        for copy in set_copies[k]:
             copy.wait()
+        axis = packed_place(0, 1 - matrix, k, halves)[0]
+        for chain in range(2):
+            for side in range(2):
+                start = (2 * chain + side) * part
+                assemble(rows, start, own_buffer.at[chain], pair_buffer.at[chain, k], slice(None), k, axis, side)
         axis, at = packed_place(1, matrix, k, halves)
         value = value_buffers[axis][:, at : at + halves[k]]
         if hidden_first:
-            grad = dot(value, row_buffers[k], 0, 0)
+            grad = dot(value, rows[...], 0, 0)
             own_out[k][...] = grad[:, :width]
             sent_out[k][...] = grad[:, width:].astype(jnp.bfloat16)
         else:
-            grad = dot(row_buffers[k], value, 0, 0)
+            grad = dot(rows[...], value, 0, 0)
             own_out[k][...] = grad[:width]
             sent_out[k][...] = grad[width:].astype(jnp.bfloat16)
         square = grad * grad + EPS_ONE
@@ -261,16 +272,16 @@
 
 
 def grad_out_kernel(halves, *refs):
-    rows, values, outs, buffers = refs[:12], refs[12:24], refs[24:31], refs[31:]
-    gradients(True, halves, rows, values, buffers[0], buffers[1:4], buffers[4], outs[:3], outs[3:6], outs[6])
+    blocks, values, outs, buffers = refs[:4], refs[4:16], refs[16:23], refs[23:]
+    gradients(True, halves, blocks, values, buffers, outs[:3], outs[3:6], outs[6])
 
 
 def grad_in_kernel(halves, *refs):
-    rows, values, other_sums, hidden_prev, outs, buffers = (
-        refs[:12], refs[12:24], refs[24], refs[25], refs[26:33], refs[33:]
-    )
-    sums = buffers[5]
-    gradients(False, halves, rows, values, buffers[0], buffers[1:4], buffers[4], outs[:3], outs[3:6], sums)
+    blocks, values, other_sums, hidden_prev, outs, buffers = (
+        refs[:4], refs[4:16], refs[16], refs[17], refs[18:25], refs[25:]
+    )
+    sums = buffers[-1]
+    gradients(False, halves, blocks, values, buffers[:-1], outs[:3], outs[3:6], sums)
     collect(hidden_prev, (sums, other_sums), outs[6])
 
 
@@ -442,22 +453,17 @@
     pairs = jnp.stack([swap(got, MASKS[k]) for k in sets])
     blocks = [(got, pairs), (swap(got, 1, "ffn"), swap(pairs, 1, "ffn"))]
     chains = range(2)
-    row_shapes = [shape((count, wide), bf16)] * 6
-
     def sums(chain, side, out_shapes):
-        kernel = functools.partial(sums_kernel, side, halves, is_packed)
-        outs = call(
-            kernel, 40, row_shapes + out_shapes, *blocks[chain], *cuts[:6], *got_weights,
-            streamed_out=range(6),
+        return call(
+            functools.partial(sums_kernel, side, halves, is_packed), 14,
+            out_shapes, *blocks[chain], *cuts[:6], *got_weights,
+            scratch=[pltpu.VMEM((6, count, wide), bf16)],
         )
-        return outs[:6], outs[6:]
-
-    far_rows, received, near_rows, kept = [None] * 2, [None] * 2, [None] * 2, [None] * 2
-    for c in chains:
-        far_rows[c], sent = sums(c, 1, shapes(count, first_widths, bf16))
-        received[c] = along_axes(sent)
-    for c in chains:
-        near_rows[c], kept[c] = sums(c, 0, shapes(count, halves * 2, f32))
+
+    sent = [sums(c, 1, shapes(count, first_widths, bf16)) for c in chains]
+    received = [along_axes(values) for values in sent]
+    blocks, sent = lax.optimization_barrier((blocks, sent))
+    kept = lax.optimization_barrier([sums(c, 0, shapes(count, halves * 2, f32)) for c in chains])
     for c in chains:
         out_shapes = shapes(count // 2, halves * 2, f32) + shapes(count // 2, second_widths, bf16)
         outs = call(functools.partial(add_kernel, halves), 8, out_shapes, *kept[c], *received[c])
@@ -475,10 +481,10 @@
     def parts(near, far):
         return [value[n] for n in range(3) for chain in chains for value in (near[chain], far[chain])]
 
-    token_rows = parts([rows[:3] for rows in near_rows], [rows[:3] for rows in far_rows])
-    cotangent_rows = parts([rows[3:] for rows in near_rows], [rows[3:] for rows in far_rows])
     values = parts(nears, fars)
-    buffers = [pltpu.VMEM((3, 4 * count, wide), bf16)]
+    all_blocks = [value for chain in chains for value in blocks[chain]]
+    chunks = got.shape[:2] + (block_width,)
+    buffers = [pltpu.VMEM((2, *chunks), bf16), pltpu.VMEM((2, 3, *chunks), bf16), pltpu.VMEM((4 * count, wide), bf16)]
     buffers += [pltpu.VMEM((4 * count, width), bf16) for width in second_widths]
     buffers += [pltpu.SemaphoreType.DMA((24,))]
 
@@ -490,8 +496,8 @@
         [shape((half, block_width), f32) for half in halves]
         + [shape((half, block_width), bf16) for half in halves]
         + [shape(sums_shape, f32)],
-        *cotangent_rows, *values,
-        scratch=buffers, whole=range(24), streamed_out=range(3),
+        *all_blocks, *values,
+        scratch=buffers, whole=range(16), streamed_out=range(3),
     )
     out_own, out_sent, out_sums = outs[:3], outs[3:6], outs[6]
     got_out = along_axes(out_sent)
@@ -500,8 +506,8 @@
         [shape((block_width, half), f32) for half in halves]
         + [shape((block_width, half), bf16) for half in halves]
         + [shape((STAT_ROWS, lanes), f32)],
-        *token_rows, *values, out_sums, hidden_pick[1:2],
-        scratch=buffers + [pltpu.VMEM(sums_shape, f32)], whole=range(24), streamed_out=range(3),
+        *all_blocks, *values, out_sums, hidden_pick[1:2],
+        scratch=buffers + [pltpu.VMEM(sums_shape, f32)], whole=range(16), streamed_out=range(3),
     )
     in_own, in_sent, stats = outs[:3], outs[3:6], outs[6]
     got_in = along_axes(in_sent)

time: 262 us -> 247 us (0.943)
  Pallas kernels: 50.5 us -> 41.7 us
  local copies, waits for them, and re-layouts: 15.7 us -> 10.8 us
    pallas_call x15, Pallas kernels: 50.5 us -> 41.7 us  [call(): pl.pallas_call(kernel, out_shape=out_shape, in_specs=[spec(value, n, stre...]
    unnamed x113 -> x75, local copies, waits for them, and re-layouts: 12.9 us -> 8.08 us
  transfers between devices with their start and end apart: 51 -> 51, of which waited for: 20 -> 27; matrix products, arithmetic and copies ran while one was open for 1% -> 1% of each run, Pallas kernels for 12% -> 9%
where the time goes in v7:
time: 247 us; the launch traced here: 246 us
  waiting for transfers between devices  122 us (49%)
  starting transfers between devices  64.3 us (26%)
  Pallas kernels  41.7 us (17%)
  local copies, waits for them, and re-layouts  10.8 us (4%)
  other arithmetic  5.25 us (2%)
    ppermute x46, waiting for transfers between devices, swap(): return lax.ppermute(value, axis, pairs)  117 us
    pallas_call x15, Pallas kernels, call(): pl.pallas_call(kernel, out_shape=out_shape, in_specs=[spec(value, n, stre...  41.7 us
    ppermute x46, starting transfers between devices, swap(): return lax.ppermute(value, axis, pairs)  39.3 us
    ppermute x4, starting transfers between devices, other(): return lax.ppermute(values, ('expert', 'ffn'), moves)  17.3 us
    unnamed x75, local copies, waits for them, and re-layouts  8.08 us
    all_to_all x1, starting transfers between devices, shards(): lax.all_to_all(routed, 'expert', split_axis=0, concat_axis=0, tiled=True)  7.74 us
    ppermute x4, waiting for transfers between devices, other(): return lax.ppermute(values, ('expert', 'ffn'), moves)  4.95 us
  transfers between devices with their start and end apart: 51, of which 27 were waited for; matrix products, arithmetic and copies ran while one was open for 1% of the time, Pallas kernels for 9%

profile of v7, /device:TPU:1, one launch (start us, length us, event | category | flops | bytes accessed | tf_op | source)
XLA Modules:
  0.0 246.3 jit_solution(2742495856598219531)
XLA Ops:
  6.7 7.7 %all-to-all-start = ((bf16[16,40,1024]{2,1,0:T(8,128)(2,1)}), bf16[16,40,1024]{2,1,0:T(8,128)(2,1)}, u32[]{:S(2)}, u32[]{:S(2)}) async-start(bf16[16,40,1024]{2,1,0:T(8,128)(2,1)} %pad_maximum_fusion.1), calls=%async_computation | async-start | bytes 2621440 | tf_op jit(solution)/shard_map/all_to_all | solution.py:438
  14.5 1.7 copy-done.15
  16.2 1.3 shard_map.86
  20.6 1.3 collective-permute-start
  24.3 24.2 %collective-permute-done.1.refs_9_.refs_12_ = bf16[3072,128]{1,0:T(8,128)(2,1)S(1)} collective-permute-done((bf16[3072,128]{1,0:T(8,128)(2,1)S(1)}, bf16[3072,128]{1,0:T(8,128)(2,1)S(1)}, u32[]{:S(2)}, u32[]{:S(2)}) %collective-permute-start.1) | collective-permute-done | bytes 786464 | tf_op jit(solution)/shard_map/ppermute | solution.py:29
  48.4 5.6 %collective-permute-done.2.refs_10_.refs_13_ = bf16[3072,128]{1,0:T(8,128)(2,1)S(1)} collective-permute-done((bf16[3072,128]{1,0:T(8,128)(2,1)S(1)}, bf16[3072,128]{1,0:T(8,128)(2,1)S(1)}, u32[]{:S(2)}, u32[]{:S(2)}) %collective-permute-start.2) | collective-permute-done | bytes 786464 | tf_op jit(solution)/shard_map/ppermute | solution.py:29
  54.8 1.4 copy.11
  56.2 1.5 collective-permute-start.3
  58.8 1.6 collective-permute-start.5
  60.4 24.3 %collective-permute-done.3 = bf16[8,80,1024]{2,1,0:T(8,128)(2,1)S(1)} collective-permute-done((bf16[8,80,1024]{2,1,0:T(8,128)(2,1)S(1)}, bf16[8,80,1024]{2,1,0:T(8,128)(2,1)S(1)}, u32[]{:S(2)}, u32[]{:S(2)}) %collective-permute-start.3) | collective-permute-done | bytes 1310752 | tf_op jit(solution)/shard_map/ppermute | solution.py:29
  84.7 1.3 collective-permute-done.4
  86.0 1.3 collective-permute-done.5
  87.9 3.0 %collective-permute-start.7 = (bf16[3,8,80,1024]{3,2,1,0:T(8,128)(2,1)S(1)}, bf16[3,8,80,1024]{3,2,1,0:T(8,128)(2,1)S(1)}, u32[]{:S(2)}, u32[]{:S(2)}) collective-permute-start(bf16[3,8,80,1024]{3,2,1,0:T(8,128)(2,1)S(1)} %pad_maximum_fusion.refs_1_), channel_id=1, source_target_pairs={{0,1},{1,0},{2,3},{3,2},{4,5},{5,4},{6,7},{7,6},{8,9},{9,8},{10,11... | collective-permute-start | bytes 11796488 | tf_op jit(solution)/shard_map/ppermute | solution.py:29
  91.0 2.2 shard_map.87
  93.2 1.5 collective-permute-start.10
  94.9 4.3 %collective-permute-done.6.refs_0_.refs_2_ = bf16[8,80,1024]{2,1,0:T(8,128)(2,1)S(1)} collective-permute-done((bf16[8,80,1024]{2,1,0:T(8,128)(2,1)S(1)}, bf16[8,80,1024]{2,1,0:T(8,128)(2,1)S(1)}, u32[]{:S(2)}, u32[]{:S(2)}) %collective-permute-start.6) | collective-permute-done | bytes 1310752 | tf_op jit(solution)/shard_map/ppermute | solution.py:29
  99.2 2.2 shard_map.88
  101.6 2.2 shard_map.90
  103.8 2.2 shard_map.89
  108.9 1.4 collective-permute-start.18
  110.6 1.4 collective-permute-start.12
  112.1 2.5 %collective-permute-done.11.refs_6_ = bf16[160,768]{1,0:T(8,128)(2,1)S(1)} collective-permute-done((bf16[160,768]{1,0:T(8,128)(2,1)S(1)}, bf16[160,768]{1,0:T(8,128)(2,1)S(1)}, u32[]{:S(2)}, u32[]{:S(2)}) %collective-permute-start.11) | collective-permute-done | bytes 245792 | tf_op jit(solution)/shard_map/ppermute | solution.py:29
  115.1 13.5 %collective-permute-done.12.refs_7_ = bf16[160,896]{1,0:T(8,128)(2,1)S(1)} collective-permute-done((bf16[160,896]{1,0:T(8,128)(2,1)S(1)}, bf16[160,896]{1,0:T(8,128)(2,1)S(1)}, u32[]{:S(2)}, u32[]{:S(2)}) %collective-permute-start.12) | collective-permute-done | bytes 286752 | tf_op jit(solution)/shard_map/ppermute | solution.py:29
  132.8 1.7 collective-permute-done.14.refs_3_
  135.0 1.5 collective-permute-done.16.refs_5_
  136.7 1.5 collective-permute-start.17
  138.1 3.0 %collective-permute-done.21.refs_6_ = bf16[160,768]{1,0:T(8,128)(2,1)S(1)} collective-permute-done((bf16[160,768]{1,0:T(8,128)(2,1)S(1)}, bf16[160,768]{1,0:T(8,128)(2,1)S(1)}, u32[]{:S(2)}, u32[]{:S(2)}) %collective-permute-start.21) | collective-permute-done | bytes 245792 | tf_op jit(solution)/shard_map/ppermute | solution.py:29
  141.9 1.5 collective-permute-start.25
  145.6 9.1 %collective-permute-done.24.refs_3_ = bf16[160,768]{1,0:T(8,128)(2,1)S(1)} collective-permute-done((bf16[160,768]{1,0:T(8,128)(2,1)S(1)}, bf16[160,768]{1,0:T(8,128)(2,1)S(1)}, u32[]{:S(2)}, u32[]{:S(2)}) %collective-permute-start.24) | collective-permute-done | bytes 245792 | tf_op jit(solution)/shard_map/ppermute | solution.py:29
  155.5 1.2 collective-permute-start.29
  157.7 7.5 %collective-permute-done.30.refs_13_ = bf16[320,896]{1,0:T(8,128)(2,1)S(1)} collective-permute-done((bf16[320,896]{1,0:T(8,128)(2,1)S(1)}, bf16[320,896]{1,0:T(8,128)(2,1)S(1)}, u32[]{:S(2)}, u32[]{:S(2)}) %collective-permute-start.30) | collective-permute-done | bytes 573472 | tf_op jit(solution)/shard_map/ppermute | solution.py:29
  165.6 5.0 %collective-permute-done.29.refs_11_ = bf16[320,896]{1,0:T(8,128)(2,1)S(1)} collective-permute-done((bf16[320,896]{1,0:T(8,128)(2,1)S(1)}, bf16[320,896]{1,0:T(8,128)(2,1)S(1)}, u32[]{:S(2)}, u32[]{:S(2)}) %collective-permute-start.29) | collective-permute-done | bytes 573472 | tf_op jit(solution)/shard_map/ppermute | solution.py:29
  170.6 6.8 %collective-permute-done.31.refs_15_ = bf16[320,896]{1,0:T(8,128)(2,1)S(1)} collective-permute-done((bf16[320,896]{1,0:T(8,128)(2,1)S(1)}, bf16[320,896]{1,0:T(8,128)(2,1)S(1)}, u32[]{:S(2)}, u32[]{:S(2)}) %collective-permute-start.31) | collective-permute-done | bytes 573472 | tf_op jit(solution)/shard_map/ppermute | solution.py:29
  178.3 7.9 %shard_map.97 = (f32[512,512]{1,0:T(8,128)}, f32[384,512]{1,0:T(8,128)}, f32[384,512]{1,0:T(8,128)}, bf16[512,512]{1,0:T(8,128)(2,1)}, bf16[384,512]{1,0:T(8,128...) custom-call(bf16[8,80,1024]{2,1,0:T(8,128)(2,1)} %bitcast.38, bf16[3,8,80,1024]{3,2,1,0:T(8,128)(2,1)} %copy-done.2, ...), custom_call_target="tpu_custom_call" | custom-call | tf_op jit(solution)/shard_map/pallas_call | solution.py:75
  187.5 9.9 %shard_map.98 = (f32[512,512]{1,0:T(8,128)}, f32[512,384]{1,0:T(8,128)}, f32[512,384]{1,0:T(8,128)}, bf16[512,512]{1,0:T(8,128)(2,1)}, bf16[512,384]{1,0:T(8,128...) custom-call(bf16[8,80,1024]{2,1,0:T(8,128)(2,1)} %bitcast.39, bf16[3,8,80,1024]{3,2,1,0:T(8,128)(2,1)} %copy-done.2, ...), custom_call_target="tpu_custom_call" | custom-call | tf_op jit(solution)/shard_map/pallas_call | solution.py:75
  197.5 1.5 collective-permute-start.35
  200.3 1.5 collective-permute-start.41
  202.7 1.5 collective-permute-start.43
  205.1 1.5 collective-permute-start.38
  206.9 8.4 %collective-permute-start.39 = (f32[32,512]{1,0:T(8,128)S(1)}, f32[32,512]{1,0:T(8,128)S(1)}, u32[]{:S(2)}, u32[]{:S(2)}) collective-permute-start(f32[32,512]{1,0:T(8,128)S(1)} %add_add_fusion.1), channel_id=1, source_target_pairs={{0,1},{1,0},{2,3},{3,2},{4,5},{5,4},{6,7},{7,6},{8,9},{9,8},{10,11... | collective-permute-start | bytes 196616 | tf_op jit(solution)/shard_map/ppermute | solution.py:537
  215.3 5.2 %collective-permute-start.40 = (f32[32,512]{1,0:T(8,128)S(1)}, f32[32,512]{1,0:T(8,128)S(1)}, u32[]{:S(2)}, u32[]{:S(2)}) collective-permute-start(f32[32,512]{1,0:T(8,128)S(1)} %add_add_fusion.1), channel_id=1, source_target_pairs={{0,9},{1,8},{2,11},{3,10},{4,13},{5,12},{6,15},{7,14},{8,1},{9,0},... | collective-permute-start | bytes 196616 | tf_op jit(solution)/shard_map/ppermute | solution.py:537
  220.7 2.3 collective-permute-done.40
  224.1 4.8 %shard_map.99 = (f32[32,512]{1,0:T(8,128)S(1)}, f32[8,128]{1,0:T(8,128)S(1)}) custom-call(f32[32,512]{1,0:T(8,128)S(1)} %concatenate.6.prev, f32[32,512]{1,0:T(8,128)S(1)} %get-tuple-element.221.group_sums, f32[32,512]{1,0:T(8,128)S(1)} %get-tuple-element.197.whole_sums, f32[512,512]{1,0:T(8,128)} %get-tuple-element.198.refs_0_, ...), custom_call_target="tpu_custom_call" | custom-call | tf_op jit(solution)/shard_map/pallas_call | solution.py:75
  230.0 1.6 collective-permute-start.46
  231.7 1.7 collective-permute-done.46
  233.5 3.2 %collective-permute-start.48 = (f32[8,128]{1,0:T(8,128)S(1)}, f32[8,128]{1,0:T(8,128)S(1)}, u32[]{:S(2)}, u32[]{:S(2)}) collective-permute-start(f32[8,128]{1,0:T(8,128)S(1)} %add_add_fusion.3), channel_id=1, source_target_pairs={{0,1},{1,0},{2,3},{3,2},{4,5},{5,4},{6,7},{7,6},{8,9},{9,8},{10,11... | collective-permute-start | bytes 12296 | tf_op jit(solution)/shard_map/ppermute | solution.py:537
  237.5 2.2 collective-permute-done.49
  239.7 6.6 %shard_map.100 = (bf16[512,2560]{1,0:T(8,128)(2,1)}, bf16[2560,512]{1,0:T(8,128)(2,1)}) custom-call(f32[32,512]{1,0:T(8,128)S(1)} %concatenate.6.prev, f32[32,512]{1,0:T(8,128)S(1)} %get-tuple-element.204.factors, f32[32,512]{1,0:T(8,128)S(1)} %get-tuple-element.197.whole_sums, f32[8,128]{1,0:T(8,128)S(1)} %add_add_fusion.2.norms, ...), custom_call_target="tpu_custom_call" | custom-call | tf_op jit(solution)/shard_map/pallas_call | solution.py:75
  (177 shorter events, 36.8 us)
Async XLA Ops:
  6.7 48.1 %all-to-all-start = ((bf16[16,40,1024]{2,1,0:T(8,128)(2,1)}), bf16[16,40,1024]{2,1,0:T(8,128)(2,1)}, u32[]{:S(2)}, u32[]{:S(2)}) async-start(bf16[16,40,1024]{2,1,0:T(8,128)(2,1)} %pad_maximum_fusion.1), calls=%async_computation | async-start | bytes 2621440 | tf_op jit(solution)/shard_map/all_to_all | solution.py:438
  20.6 34.2 %collective-permute-start = (bf16[4096,128]{1,0:T(8,128)(2,1)S(1)}, bf16[4096,128]{1,0:T(8,128)(2,1)S(1)}, u32[]{:S(2)}, u32[]{:S(2)}) collective-permute-start(bf16[4096,128]{1,0:T(8,128)(2,1)S(1)} %get-tuple-element.108), channel_id=1, source_target_pairs={{0,2},{2,0},{4,6},{6,4},{8,10},{10,8},{12,14},{14,12},{16,18},{18,... | collective-permute-start | bytes 3145736 | tf_op jit(solution)/shard_map/ppermute | solution.py:29
  21.9 26.6 %collective-permute-start.1 = (bf16[3072,128]{1,0:T(8,128)(2,1)S(1)}, bf16[3072,128]{1,0:T(8,128)(2,1)S(1)}, u32[]{:S(2)}, u32[]{:S(2)}) collective-permute-start(bf16[3072,128]{1,0:T(8,128)(2,1)S(1)} %get-tuple-element.109), channel_id=1, source_target_pairs={{0,4},{2,6},{4,0},{6,2},{8,12},{10,14},{12,8},{14,10},{16,20},{18,... | collective-permute-start | bytes 2359304 | tf_op jit(solution)/shard_map/ppermute | solution.py:29
  23.1 31.0 %collective-permute-start.2 = (bf16[3072,128]{1,0:T(8,128)(2,1)S(1)}, bf16[3072,128]{1,0:T(8,128)(2,1)S(1)}, u32[]{:S(2)}, u32[]{:S(2)}) collective-permute-start(bf16[3072,128]{1,0:T(8,128)(2,1)S(1)} %get-tuple-element.110), channel_id=1, source_target_pairs={{0,8},{2,10},{4,12},{6,14},{8,0},{10,2},{12,4},{14,6},{16,24},{18,... | collective-permute-start | bytes 2359304 | tf_op jit(solution)/shard_map/ppermute | solution.py:29
  56.2 28.5 %collective-permute-start.3 = (bf16[8,80,1024]{2,1,0:T(8,128)(2,1)S(1)}, bf16[8,80,1024]{2,1,0:T(8,128)(2,1)S(1)}, u32[]{:S(2)}, u32[]{:S(2)}) collective-permute-start(bf16[8,80,1024]{2,1,0:T(8,128)(2,1)S(1)} %bitcast.32), channel_id=1, source_target_pairs={{0,2},{2,0},{4,6},{6,4},{8,10},{10,8},{12,14},{14,12},{16,18},{18,... | collective-permute-start | bytes 3932168 | tf_op jit(solution)/shard_map/ppermute | solution.py:29
  57.7 28.2 %collective-permute-start.4 = (bf16[8,80,1024]{2,1,0:T(8,128)(2,1)S(1)}, bf16[8,80,1024]{2,1,0:T(8,128)(2,1)S(1)}, u32[]{:S(2)}, u32[]{:S(2)}) collective-permute-start(bf16[8,80,1024]{2,1,0:T(8,128)(2,1)S(1)} %bitcast.33), channel_id=1, source_target_pairs={{0,4},{2,6},{4,0},{6,2},{8,12},{10,14},{12,8},{14,10},{16,20},{18,... | collective-permute-start | bytes 3932168 | tf_op jit(solution)/shard_map/ppermute | solution.py:29
  58.8 28.4 %collective-permute-start.5 = (bf16[8,80,1024]{2,1,0:T(8,128)(2,1)S(1)}, bf16[8,80,1024]{2,1,0:T(8,128)(2,1)S(1)}, u32[]{:S(2)}, u32[]{:S(2)}) collective-permute-start(bf16[8,80,1024]{2,1,0:T(8,128)(2,1)S(1)} %bitcast.34), channel_id=1, source_target_pairs={{0,8},{2,10},{4,12},{6,14},{8,0},{10,2},{12,4},{14,6},{16,24},{18,... | collective-permute-start | bytes 3932168 | tf_op jit(solution)/shard_map/ppermute | solution.py:29
  87.9 11.3 %collective-permute-start.7 = (bf16[3,8,80,1024]{3,2,1,0:T(8,128)(2,1)S(1)}, bf16[3,8,80,1024]{3,2,1,0:T(8,128)(2,1)S(1)}, u32[]{:S(2)}, u32[]{:S(2)}) collective-permute-start(bf16[3,8,80,1024]{3,2,1,0:T(8,128)(2,1)S(1)} %pad_maximum_fusion.refs_1_), channel_id=1, source_target_pairs={{0,1},{1,0},{2,3},{3,2},{4,5},{5,4},{6,7},{7,6},{8,9},{9,8},{10,11... | collective-permute-start | bytes 11796488 | tf_op jit(solution)/shard_map/ppermute | solution.py:29
  90.9 8.3 %collective-permute-start.6 = (bf16[8,80,1024]{2,1,0:T(8,128)(2,1)S(1)}, bf16[8,80,1024]{2,1,0:T(8,128)(2,1)S(1)}, u32[]{:S(2)}, u32[]{:S(2)}) collective-permute-start(bf16[8,80,1024]{2,1,0:T(8,128)(2,1)S(1)} %bitcast.35), channel_id=1, source_target_pairs={{0,1},{1,0},{2,3},{3,2},{4,5},{5,4},{6,7},{7,6},{8,9},{9,8},{10,11... | collective-permute-start | bytes 3932168 | tf_op jit(solution)/shard_map/ppermute | solution.py:29
  93.2 14.1 %collective-permute-start.10 = (bf16[320,896]{1,0:T(8,128)(2,1)S(1)}, bf16[320,896]{1,0:T(8,128)(2,1)S(1)}, u32[]{:S(2)}, u32[]{:S(2)}) collective-permute-start(bf16[320,896]{1,0:T(8,128)(2,1)S(1)} %get-tuple-element.126), channel_id=1, source_target_pairs={{0,8},{2,10},{4,12},{6,14},{8,0},{10,2},{12,4},{14,6},{16,24},{18,... | collective-permute-start | bytes 1720328 | tf_op jit(solution)/shard_map/ppermute | solution.py:29
  94.8 13.7 %collective-permute-start.9 = (bf16[320,896]{1,0:T(8,128)(2,1)S(1)}, bf16[320,896]{1,0:T(8,128)(2,1)S(1)}, u32[]{:S(2)}, u32[]{:S(2)}) collective-permute-start(bf16[320,896]{1,0:T(8,128)(2,1)S(1)} %get-tuple-element.125), channel_id=1, source_target_pairs={{0,4},{2,6},{4,0},{6,2},{8,12},{10,14},{12,8},{14,10},{16,20},{18,... | collective-permute-start | bytes 1720328 | tf_op jit(solution)/shard_map/ppermute | solution.py:29
  94.8 11.6 %collective-permute-start.8 = (bf16[320,768]{1,0:T(8,128)(2,1)S(1)}, bf16[320,768]{1,0:T(8,128)(2,1)S(1)}, u32[]{:S(2)}, u32[]{:S(2)}) collective-permute-start(bf16[320,768]{1,0:T(8,128)(2,1)S(1)} %get-tuple-element.124), channel_id=1, source_target_pairs={{0,2},{2,0},{4,6},{6,4},{8,10},{10,8},{12,14},{14,12},{16,18},{18,... | collective-permute-start | bytes 1474568 | tf_op jit(solution)/shard_map/ppermute | solution.py:29
  108.8 5.8 %collective-permute-start.11 = (bf16[160,768]{1,0:T(8,128)(2,1)S(1)}, bf16[160,768]{1,0:T(8,128)(2,1)S(1)}, u32[]{:S(2)}, u32[]{:S(2)}) collective-permute-start(bf16[160,768]{1,0:T(8,128)(2,1)S(1)} %get-tuple-element.158), channel_id=1, source_target_pairs={{0,2},{2,0},{4,6},{6,4},{8,10},{10,8},{12,14},{14,12},{16,18},{18,... | collective-permute-start | bytes 737288 | tf_op jit(solution)/shard_map/ppermute | solution.py:29
  108.9 21.8 %collective-permute-start.18 = (bf16[320,768]{1,0:T(8,128)(2,1)S(1)}, bf16[320,768]{1,0:T(8,128)(2,1)S(1)}, u32[]{:S(2)}, u32[]{:S(2)}) collective-permute-start(bf16[320,768]{1,0:T(8,128)(2,1)S(1)} %get-tuple-element.127), channel_id=1, source_target_pairs={{0,2},{2,0},{4,6},{6,4},{8,10},{10,8},{12,14},{14,12},{16,18},{18,... | collective-permute-start | bytes 1474568 | tf_op jit(solution)/shard_map/ppermute | solution.py:29
  110.3 21.0 %collective-permute-start.19 = (bf16[320,896]{1,0:T(8,128)(2,1)S(1)}, bf16[320,896]{1,0:T(8,128)(2,1)S(1)}, u32[]{:S(2)}, u32[]{:S(2)}) collective-permute-start(bf16[320,896]{1,0:T(8,128)(2,1)S(1)} %get-tuple-element.128), channel_id=1, source_target_pairs={{0,4},{2,6},{4,0},{6,2},{8,12},{10,14},{12,8},{14,10},{16,20},{18,... | collective-permute-start | bytes 1720328 | tf_op jit(solution)/shard_map/ppermute | solution.py:29
  110.3 21.0 %collective-permute-start.20 = (bf16[320,896]{1,0:T(8,128)(2,1)S(1)}, bf16[320,896]{1,0:T(8,128)(2,1)S(1)}, u32[]{:S(2)}, u32[]{:S(2)}) collective-permute-start(bf16[320,896]{1,0:T(8,128)(2,1)S(1)} %get-tuple-element.129), channel_id=1, source_target_pairs={{0,8},{2,10},{4,12},{6,14},{8,0},{10,2},{12,4},{14,6},{16,24},{18,... | collective-permute-start | bytes 1720328 | tf_op jit(solution)/shard_map/ppermute | solution.py:29
  110.6 18.0 %collective-permute-start.12 = (bf16[160,896]{1,0:T(8,128)(2,1)S(1)}, bf16[160,896]{1,0:T(8,128)(2,1)S(1)}, u32[]{:S(2)}, u32[]{:S(2)}) collective-permute-start(bf16[160,896]{1,0:T(8,128)(2,1)S(1)} %get-tuple-element.159), channel_id=1, source_target_pairs={{0,4},{2,6},{4,0},{6,2},{8,12},{10,14},{12,8},{14,10},{16,20},{18,... | collective-permute-start | bytes 860168 | tf_op jit(solution)/shard_map/ppermute | solution.py:29
  114.6 14.1 %collective-permute-start.13 = (bf16[160,896]{1,0:T(8,128)(2,1)S(1)}, bf16[160,896]{1,0:T(8,128)(2,1)S(1)}, u32[]{:S(2)}, u32[]{:S(2)}) collective-permute-start(bf16[160,896]{1,0:T(8,128)(2,1)S(1)} %get-tuple-element.160), channel_id=1, source_target_pairs={{0,8},{2,10},{4,12},{6,14},{8,0},{10,2},{12,4},{14,6},{16,24},{18,... | collective-permute-start | bytes 860168 | tf_op jit(solution)/shard_map/ppermute | solution.py:29
  129.4 5.1 %collective-permute-start.14 = (bf16[160,768]{1,0:T(8,128)(2,1)S(1)}, bf16[160,768]{1,0:T(8,128)(2,1)S(1)}, u32[]{:S(2)}, u32[]{:S(2)}) collective-permute-start(bf16[160,768]{1,0:T(8,128)(2,1)S(1)} %get-tuple-element.161.refs_0_), channel_id=1, source_target_pairs={{0,2},{2,0},{4,6},{6,4},{8,10},{10,8},{12,14},{14,12},{16,18},{18,... | collective-permute-start | bytes 737288 | tf_op jit(solution)/shard_map/ppermute | solution.py:29
  129.5 5.5 %collective-permute-start.15 = (bf16[160,896]{1,0:T(8,128)(2,1)S(1)}, bf16[160,896]{1,0:T(8,128)(2,1)S(1)}, u32[]{:S(2)}, u32[]{:S(2)}) collective-permute-start(bf16[160,896]{1,0:T(8,128)(2,1)S(1)} %get-tuple-element.162.refs_1_), channel_id=1, source_target_pairs={{0,4},{2,6},{4,0},{6,2},{8,12},{10,14},{12,8},{14,10},{16,20},{18,... | collective-permute-start | bytes 860168 | tf_op jit(solution)/shard_map/ppermute | solution.py:29
  130.7 5.8 %collective-permute-start.16 = (bf16[160,896]{1,0:T(8,128)(2,1)S(1)}, bf16[160,896]{1,0:T(8,128)(2,1)S(1)}, u32[]{:S(2)}, u32[]{:S(2)}) collective-permute-start(bf16[160,896]{1,0:T(8,128)(2,1)S(1)} %get-tuple-element.163.refs_2_), channel_id=1, source_target_pairs={{0,8},{2,10},{4,12},{6,14},{8,0},{10,2},{12,4},{14,6},{16,24},{18,... | collective-permute-start | bytes 860168 | tf_op jit(solution)/shard_map/ppermute | solution.py:29
  131.6 9.5 %collective-permute-start.22 = (bf16[160,896]{1,0:T(8,128)(2,1)S(1)}, bf16[160,896]{1,0:T(8,128)(2,1)S(1)}, u32[]{:S(2)}, u32[]{:S(2)}) collective-permute-start(bf16[160,896]{1,0:T(8,128)(2,1)S(1)} %get-tuple-element.178), channel_id=1, source_target_pairs={{0,4},{2,6},{4,0},{6,2},{8,12},{10,14},{12,8},{14,10},{16,20},{18,... | collective-permute-start | bytes 860168 | tf_op jit(solution)/shard_map/ppermute | solution.py:29
  131.9 9.2 %collective-permute-start.23 = (bf16[160,896]{1,0:T(8,128)(2,1)S(1)}, bf16[160,896]{1,0:T(8,128)(2,1)S(1)}, u32[]{:S(2)}, u32[]{:S(2)}) collective-permute-start(bf16[160,896]{1,0:T(8,128)(2,1)S(1)} %get-tuple-element.179), channel_id=1, source_target_pairs={{0,8},{2,10},{4,12},{6,14},{8,0},{10,2},{12,4},{14,6},{16,24},{18,... | collective-permute-start | bytes 860168 | tf_op jit(solution)/shard_map/ppermute | solution.py:29
  134.5 6.6 %collective-permute-start.21 = (bf16[160,768]{1,0:T(8,128)(2,1)S(1)}, bf16[160,768]{1,0:T(8,128)(2,1)S(1)}, u32[]{:S(2)}, u32[]{:S(2)}) collective-permute-start(bf16[160,768]{1,0:T(8,128)(2,1)S(1)} %get-tuple-element.177), channel_id=1, source_target_pairs={{0,2},{2,0},{4,6},{6,4},{8,10},{10,8},{12,14},{14,12},{16,18},{18,... | collective-permute-start | bytes 737288 | tf_op jit(solution)/shard_map/ppermute | solution.py:29
  136.7 20.9 %collective-permute-start.17 = (bf16[320,768]{1,0:T(8,128)(2,1)S(1)}, bf16[320,768]{1,0:T(8,128)(2,1)S(1)}, u32[]{:S(2)}, u32[]{:S(2)}) collective-permute-start(bf16[320,768]{1,0:T(8,128)(2,1)S(1)} %get-tuple-element.164.refs_4_), channel_id=1, source_target_pairs={{0,2},{2,0},{4,6},{6,4},{8,10},{10,8},{12,14},{14,12},{16,18},{18,... | collective-permute-start | bytes 1474568 | tf_op jit(solution)/shard_map/ppermute | solution.py:29
  141.9 13.4 %collective-permute-start.25 = (bf16[160,896]{1,0:T(8,128)(2,1)S(1)}, bf16[160,896]{1,0:T(8,128)(2,1)S(1)}, u32[]{:S(2)}, u32[]{:S(2)}) collective-permute-start(bf16[160,896]{1,0:T(8,128)(2,1)S(1)} %get-tuple-element.181.refs_1_), channel_id=1, source_target_pairs={{0,4},{2,6},{4,0},{6,2},{8,12},{10,14},{12,8},{14,10},{16,20},{18,... | collective-permute-start | bytes 860168 | tf_op jit(solution)/shard_map/ppermute | solution.py:29
  143.4 11.9 %collective-permute-start.26 = (bf16[160,896]{1,0:T(8,128)(2,1)S(1)}, bf16[160,896]{1,0:T(8,128)(2,1)S(1)}, u32[]{:S(2)}, u32[]{:S(2)}) collective-permute-start(bf16[160,896]{1,0:T(8,128)(2,1)S(1)} %get-tuple-element.182.refs_2_), channel_id=1, source_target_pairs={{0,8},{2,10},{4,12},{6,14},{8,0},{10,2},{12,4},{14,6},{16,24},{18,... | collective-permute-start | bytes 860168 | tf_op jit(solution)/shard_map/ppermute | solution.py:29
  143.7 11.0 %collective-permute-start.24 = (bf16[160,768]{1,0:T(8,128)(2,1)S(1)}, bf16[160,768]{1,0:T(8,128)(2,1)S(1)}, u32[]{:S(2)}, u32[]{:S(2)}) collective-permute-start(bf16[160,768]{1,0:T(8,128)(2,1)S(1)} %get-tuple-element.180.refs_0_), channel_id=1, source_target_pairs={{0,2},{2,0},{4,6},{6,4},{8,10},{10,8},{12,14},{14,12},{16,18},{18,... | collective-permute-start | bytes 737288 | tf_op jit(solution)/shard_map/ppermute | solution.py:29
  144.7 13.0 %collective-permute-start.28 = (bf16[320,896]{1,0:T(8,128)(2,1)S(1)}, bf16[320,896]{1,0:T(8,128)(2,1)S(1)}, u32[]{:S(2)}, u32[]{:S(2)}) collective-permute-start(bf16[320,896]{1,0:T(8,128)(2,1)S(1)} %get-tuple-element.184.refs_8_), channel_id=1, source_target_pairs={{0,4},{2,6},{4,0},{6,2},{8,12},{10,14},{12,8},{14,10},{16,20},{18,... | collective-permute-start | bytes 1720328 | tf_op jit(solution)/shard_map/ppermute | solution.py:29
  154.7 10.5 %collective-permute-start.30 = (bf16[320,896]{1,0:T(8,128)(2,1)S(1)}, bf16[320,896]{1,0:T(8,128)(2,1)S(1)}, u32[]{:S(2)}, u32[]{:S(2)}) collective-permute-start(bf16[320,896]{1,0:T(8,128)(2,1)S(1)} %get-tuple-element.186.refs_12_), channel_id=1, source_target_pairs={{0,8},{2,10},{4,12},{6,14},{8,0},{10,2},{12,4},{14,6},{16,24},{18,... | collective-permute-start | bytes 1720328 | tf_op jit(solution)/shard_map/ppermute | solution.py:29
  155.5 15.1 %collective-permute-start.29 = (bf16[320,896]{1,0:T(8,128)(2,1)S(1)}, bf16[320,896]{1,0:T(8,128)(2,1)S(1)}, u32[]{:S(2)}, u32[]{:S(2)}) collective-permute-start(bf16[320,896]{1,0:T(8,128)(2,1)S(1)} %get-tuple-element.185.refs_10_), channel_id=1, source_target_pairs={{0,4},{2,6},{4,0},{6,2},{8,12},{10,14},{12,8},{14,10},{16,20},{18,... | collective-permute-start | bytes 1720328 | tf_op jit(solution)/shard_map/ppermute | solution.py:29
  156.7 20.7 %collective-permute-start.31 = (bf16[320,896]{1,0:T(8,128)(2,1)S(1)}, bf16[320,896]{1,0:T(8,128)(2,1)S(1)}, u32[]{:S(2)}, u32[]{:S(2)}) collective-permute-start(bf16[320,896]{1,0:T(8,128)(2,1)S(1)} %get-tuple-element.187.refs_14_), channel_id=1, source_target_pairs={{0,8},{2,10},{4,12},{6,14},{8,0},{10,2},{12,4},{14,6},{16,24},{18,... | collective-permute-start | bytes 1720328 | tf_op jit(solution)/shard_map/ppermute | solution.py:29
  157.6 8.0 %collective-permute-start.27 = (bf16[320,768]{1,0:T(8,128)(2,1)S(1)}, bf16[320,768]{1,0:T(8,128)(2,1)S(1)}, u32[]{:S(2)}, u32[]{:S(2)}) collective-permute-start(bf16[320,768]{1,0:T(8,128)(2,1)S(1)} %get-tuple-element.183.refs_6_), channel_id=1, source_target_pairs={{0,2},{2,0},{4,6},{6,4},{8,10},{10,8},{12,14},{14,12},{16,18},{18,... | collective-permute-start | bytes 1474568 | tf_op jit(solution)/shard_map/ppermute | solution.py:29
  186.3 11.2 %collective-permute-start.32 = (bf16[512,512]{1,0:T(8,128)(2,1)}, bf16[512,512]{1,0:T(8,128)(2,1)S(1)}, u32[]{:S(2)}, u32[]{:S(2)}) collective-permute-start(bf16[512,512]{1,0:T(8,128)(2,1)} %get-tuple-element.190.refs_9_), channel_id=1, source_target_pairs={{0,2},{2,0},{4,6},{6,4},{8,10},{10,8},{12,14},{14,12},{16,18},{18,... | collective-permute-start | bytes 1572872 | tf_op jit(solution)/shard_map/ppermute | solution.py:29
  186.4 11.1 %collective-permute-start.33 = (bf16[384,512]{1,0:T(8,128)(2,1)}, bf16[384,512]{1,0:T(8,128)(2,1)S(1)}, u32[]{:S(2)}, u32[]{:S(2)}) collective-permute-start(bf16[384,512]{1,0:T(8,128)(2,1)} %get-tuple-element.191.refs_10_), channel_id=1, source_target_pairs={{0,4},{2,6},{4,0},{6,2},{8,12},{10,14},{12,8},{14,10},{16,20},{18,... | collective-permute-start | bytes 1179656 | tf_op jit(solution)/shard_map/ppermute | solution.py:29
  186.4 11.1 %collective-permute-start.34 = (bf16[384,512]{1,0:T(8,128)(2,1)}, bf16[384,512]{1,0:T(8,128)(2,1)S(1)}, u32[]{:S(2)}, u32[]{:S(2)}) collective-permute-start(bf16[384,512]{1,0:T(8,128)(2,1)} %get-tuple-element.192.refs_11_), channel_id=1, source_target_pairs={{0,8},{2,10},{4,12},{6,14},{8,0},{10,2},{12,4},{14,6},{16,24},{18,... | collective-permute-start | bytes 1179656 | tf_op jit(solution)/shard_map/ppermute | solution.py:29
  197.5 5.2 %collective-permute-start.35 = (f32[32,512]{1,0:T(8,128)}, f32[32,512]{1,0:T(8,128)S(1)}, u32[]{:S(2)}, u32[]{:S(2)}) collective-permute-start(f32[32,512]{1,0:T(8,128)} %get-tuple-element.193), channel_id=1, source_target_pairs={{0,2},{2,0},{4,6},{6,4},{8,10},{10,8},{12,14},{14,12},{16,18},{18,... | collective-permute-start | bytes 196616 | tf_op jit(solution)/shard_map/ppermute | solution.py:29
  199.0 5.2 %collective-permute-start.36 = (f32[32,512]{1,0:T(8,128)}, f32[32,512]{1,0:T(8,128)S(1)}, u32[]{:S(2)}, u32[]{:S(2)}) collective-permute-start(f32[32,512]{1,0:T(8,128)} %get-tuple-element.193), channel_id=1, source_target_pairs={{0,4},{2,6},{4,0},{6,2},{8,12},{10,14},{12,8},{14,10},{16,20},{18,... | collective-permute-start | bytes 196616 | tf_op jit(solution)/shard_map/ppermute | solution.py:29
  200.0 4.2 %collective-permute-start.37 = (f32[32,512]{1,0:T(8,128)}, f32[32,512]{1,0:T(8,128)S(1)}, u32[]{:S(2)}, u32[]{:S(2)}) collective-permute-start(f32[32,512]{1,0:T(8,128)} %get-tuple-element.193), channel_id=1, source_target_pairs={{0,6},{2,4},{4,2},{6,0},{8,14},{10,12},{12,10},{14,8},{16,22},{18,... | collective-permute-start | bytes 196616 | tf_op jit(solution)/shard_map/ppermute | solution.py:29
  200.3 22.8 %collective-permute-start.41 = (bf16[512,512]{1,0:T(8,128)(2,1)}, bf16[512,512]{1,0:T(8,128)(2,1)}, u32[]{:S(2)}, u32[]{:S(2)}) collective-permute-start(bf16[512,512]{1,0:T(8,128)(2,1)} %get-tuple-element.194.refs_3_), channel_id=1, source_target_pairs={{0,2},{2,0},{4,6},{6,4},{8,10},{10,8},{12,14},{14,12},{16,18},{18,... | collective-permute-start | bytes 1572872 | tf_op jit(solution)/shard_map/ppermute | solution.py:29
  201.7 21.3 %collective-permute-start.42 = (bf16[512,384]{1,0:T(8,128)(2,1)}, bf16[512,384]{1,0:T(8,128)(2,1)S(1)}, u32[]{:S(2)}, u32[]{:S(2)}) collective-permute-start(bf16[512,384]{1,0:T(8,128)(2,1)} %get-tuple-element.195.refs_4_), channel_id=1, source_target_pairs={{0,4},{2,6},{4,0},{6,2},{8,12},{10,14},{12,8},{14,10},{16,20},{18,... | collective-permute-start | bytes 1179656 | tf_op jit(solution)/shard_map/ppermute | solution.py:29
  202.7 20.3 %collective-permute-start.43 = (bf16[512,384]{1,0:T(8,128)(2,1)}, bf16[512,384]{1,0:T(8,128)(2,1)S(1)}, u32[]{:S(2)}, u32[]{:S(2)}) collective-permute-start(bf16[512,384]{1,0:T(8,128)(2,1)} %get-tuple-element.196.refs_5_), channel_id=1, source_target_pairs={{0,8},{2,10},{4,12},{6,14},{8,0},{10,2},{12,4},{14,6},{16,24},{18,... | collective-permute-start | bytes 1179656 | tf_op jit(solution)/shard_map/ppermute | solution.py:29
  205.1 10.2 %collective-permute-start.38 = (f32[32,512]{1,0:T(8,128)S(1)}, f32[32,512]{1,0:T(8,128)S(1)}, u32[]{:S(2)}, u32[]{:S(2)}) collective-permute-start(f32[32,512]{1,0:T(8,128)S(1)} %add_add_fusion.1), channel_id=1, source_target_pairs={{0,8},{2,10},{4,12},{6,14},{8,0},{10,2},{12,4},{14,6},{16,24},{18,... | collective-permute-start | bytes 196616 | tf_op jit(solution)/shard_map/ppermute | solution.py:29
  206.9 13.8 %collective-permute-start.39 = (f32[32,512]{1,0:T(8,128)S(1)}, f32[32,512]{1,0:T(8,128)S(1)}, u32[]{:S(2)}, u32[]{:S(2)}) collective-permute-start(f32[32,512]{1,0:T(8,128)S(1)} %add_add_fusion.1), channel_id=1, source_target_pairs={{0,1},{1,0},{2,3},{3,2},{4,5},{5,4},{6,7},{7,6},{8,9},{9,8},{10,11... | collective-permute-start | bytes 196616 | tf_op jit(solution)/shard_map/ppermute | solution.py:537
  215.3 7.7 %collective-permute-start.40 = (f32[32,512]{1,0:T(8,128)S(1)}, f32[32,512]{1,0:T(8,128)S(1)}, u32[]{:S(2)}, u32[]{:S(2)}) collective-permute-start(f32[32,512]{1,0:T(8,128)S(1)} %add_add_fusion.1), channel_id=1, source_target_pairs={{0,9},{1,8},{2,11},{3,10},{4,13},{5,12},{6,15},{7,14},{8,1},{9,0},... | collective-permute-start | bytes 196616 | tf_op jit(solution)/shard_map/ppermute | solution.py:537
  230.0 3.4 %collective-permute-start.46 = (f32[8,128]{1,0:T(8,128)S(1)}, f32[8,128]{1,0:T(8,128)S(1)}, u32[]{:S(2)}, u32[]{:S(2)}) collective-permute-start(f32[8,128]{1,0:T(8,128)S(1)} %get-tuple-element.205), channel_id=1, source_target_pairs={{0,6},{2,4},{4,2},{6,0},{8,14},{10,12},{12,10},{14,8},{16,22},{18,... | collective-permute-start | bytes 12296 | tf_op jit(solution)/shard_map/ppermute | solution.py:29
  233.4 3.7 %collective-permute-start.47 = (f32[8,128]{1,0:T(8,128)S(1)}, f32[8,128]{1,0:T(8,128)S(1)}, u32[]{:S(2)}, u32[]{:S(2)}) collective-permute-start(f32[8,128]{1,0:T(8,128)S(1)} %add_add_fusion.3), channel_id=1, source_target_pairs={{0,8},{2,10},{4,12},{6,14},{8,0},{10,2},{12,4},{14,6},{16,24},{18,... | collective-permute-start | bytes 12296 | tf_op jit(solution)/shard_map/ppermute | solution.py:29
  233.5 4.0 %collective-permute-start.48 = (f32[8,128]{1,0:T(8,128)S(1)}, f32[8,128]{1,0:T(8,128)S(1)}, u32[]{:S(2)}, u32[]{:S(2)}) collective-permute-start(f32[8,128]{1,0:T(8,128)S(1)} %add_add_fusion.3), channel_id=1, source_target_pairs={{0,1},{1,0},{2,3},{3,2},{4,5},{5,4},{6,7},{7,6},{8,9},{9,8},{10,11... | collective-permute-start | bytes 12296 | tf_op jit(solution)/shard_map/ppermute | solution.py:537
  (39 other events, 438.7 us)

commit v8 on v7

--- a/solution.py
+++ b/solution.py
@@ -114,6 +114,25 @@
     width = rows.shape[1] // 2
     contract = 1 if by_row else 0
     return dot(rows[:, :width], own_weight, 1, contract) + dot(rows[:, width:], got_weight, 1, contract)
+
+
+def route_kernel(part_cap, ids, tokens, cotangent, out):
+    rows, experts, groups = ids.shape[0], out.shape[0], out.shape[1]
+    width = out.shape[3] // 2
+    part = lax.rem(lax.axis_index("ffn"), 2)
+    onehot = lax.broadcasted_iota(jnp.int32, (rows, 128), 1) == ids[...]
+    earlier = lax.broadcasted_iota(jnp.int32, (rows, rows), 0) > lax.broadcasted_iota(jnp.int32, (rows, rows), 1)
+    before = dot(earlier.astype(jnp.float32), onehot.astype(jnp.float32), 1, 0)
+    slot = jnp.sum(jnp.where(onehot, before, 0.0), axis=1, keepdims=True).astype(jnp.int32) - part * part_cap
+    target = jnp.where((slot >= 0) & (slot < part_cap), ids[...] * part_cap + slot, -1)
+    select = lax.broadcasted_iota(jnp.int32, (rows, experts * part_cap), 1) == target
+    select = select.astype(jnp.float32).astype(jnp.bfloat16)
+    for n, values in enumerate((tokens, cotangent)):
+        routed = dot(select, values[...], 0, 0)
+        for e in range(experts):
+            mine = routed[e * part_cap : (e + 1) * part_cap].astype(jnp.bfloat16)
+            for b in range(groups):
+                out[e, b, :, n * width : (n + 1) * width] = mine[:, b * width : (b + 1) * width]
 
 
 def cut_kernel(bounds, weight_in, weight_out, *refs):
@@ -316,9 +335,18 @@
     return jnp.transpose(jnp.broadcast_to(row, (8, row.shape[1])))[:, 0:1]
 
 
+def fetch(sources, buffers, sems):
+    copies = [pltpu.make_async_copy(sources[n], buffers[n], sems.at[n]) for n in range(12)]
+    for k in range(3):
+        for copy in copies[k::3]:
+            copy.start()
+    return [copies[k::3] for k in range(3)]
+
+
 def norm_kernel(prev, group_sums, whole_sums, *refs):
-    own_in, sent_in, own_out, sent_out = refs[:3], refs[3:6], refs[6:9], refs[9:12]
-    factors_out, norms_out = refs[12], refs[13]
+    factors_out, norms_out, buffers = refs[12], refs[13], refs[14:26]
+    copies = fetch(refs[:12], buffers, refs[26])
+    own_in, sent_in, own_out, sent_out = buffers[:3], buffers[3:6], buffers[6:9], buffers[9:12]
     place = place_in_group()
     width = own_in[0].shape[0]
     row = lax.broadcasted_iota(jnp.int32, prev.shape, 0)
@@ -327,6 +355,8 @@
     factors_out[...] = DECAY_RATE * prev[...] + (1.0 - DECAY_RATE) * mean
     norm_in, norm_out = 0.0, 0.0
     for k in range(3):
+        for copy in copies[k]:
+            copy.wait()
         half = own_in[k].shape[1]
         partner = flipped(place, 1 << k)
         own_row = stat_row(factors_out, IN_WIDTH + place)[:, :width]
@@ -349,8 +379,9 @@
 
 
 def final_kernel(bounds, prev, factors, whole_sums, norms, *refs):
-    own_in, own_out, got_in, got_out = refs[:3], refs[3:6], refs[6:9], refs[9:12]
-    update_in, update_out = refs[12:]
+    update_in, update_out, buffers = refs[12], refs[13], refs[14:26]
+    copies = fetch(refs[:12], buffers, refs[26])
+    own_in, own_out, got_in, got_out = buffers[:3], buffers[3:6], buffers[6:9], buffers[9:12]
     place = place_in_group()
     width = update_in.shape[0]
     count = float(D) * float(FF)
@@ -363,6 +394,8 @@
     width_in = upright(lax.rsqrt(stat_row(factors, IN_WIDTH + place)[:, :width]) * factor_in)
     width_out = lax.rsqrt(stat_row(factors, OUT_WIDTH + place)[:, :width]) * factor_out
     for k in range(3):
+        for copy in copies[k]:
+            copy.wait()
         low, half = bounds[k][0], (bounds[k][1] - bounds[k][0]) // 2
         own_bit = bit(place, k)
         if half % 128:
@@ -421,20 +454,12 @@
             cuts += [lax.dynamic_slice_in_dim(local_out, at[k], halves[k], 0) for k in sets]
         got_weights = [swap(cuts[6 + n], MASKS[n % 3]) for n in range(6)]
 
-    route_ids = expert_ids[:, 0]
-    onehot = (route_ids[:, None] == jnp.arange(experts, dtype=jnp.int32)[None, :]).astype(jnp.int32)
-    before = jnp.cumsum(onehot, axis=0) - onehot
-    slot_index = jnp.sum(before * onehot, axis=1) - part * part_cap
-    valid = (slot_index >= 0) & (slot_index < part_cap)
-    target = jnp.where(valid, route_ids * part_cap + slot_index, -1)
-    select = (jnp.arange(experts * part_cap, dtype=jnp.int32)[:, None] == target[None, :]).astype(bf16)
-
-    def route(values):
-        routed = dot(select, values, 1, 0).astype(bf16)
-        routed = routed.reshape(experts, part_cap, GROUP, block_width).transpose(0, 2, 1, 3)
-        return routed.reshape(places, part_cap, block_width)
-
-    routed = jnp.concatenate([route(tokens), route(cotangent)], axis=2)
+    routed_shape = shape((experts, GROUP, part_cap, 2 * block_width), bf16)
+    (routed,) = call(
+        functools.partial(route_kernel, part_cap), 12, [routed_shape], expert_ids, tokens, cotangent,
+        streamed=range(3),
+    )
+    routed = routed.reshape(places, part_cap, 2 * block_width)
     got = lax.all_to_all(routed, "expert", split_axis=0, concat_axis=0, tiled=True)
     got, got_weights = lax.optimization_barrier((got, got_weights))
     got = got.reshape(places // GROUP, GROUP, part_cap, 2 * block_width).transpose(1, 0, 2, 3)
@@ -510,7 +535,6 @@
         scratch=buffers + [pltpu.VMEM(sums_shape, f32)], whole=range(16), streamed_out=range(3),
     )
     in_own, in_sent, stats = outs[:3], outs[3:6], outs[6]
-    got_in = along_axes(in_sent)
 
     width_pick = lax.dynamic_index_in_dim(width_states, expert, 1, keepdims=False)
 
@@ -525,6 +549,10 @@
     prev.append(jnp.ones((STAT_ROWS - TOTALS, lanes), f32))
     prev = jnp.concatenate(prev)
 
+    def fetched(*groups):
+        arrays = [value for group in groups for value in group]
+        return [pltpu.VMEM(value.shape, value.dtype) for value in arrays] + [pltpu.SemaphoreType.DMA((len(arrays),))]
+
     def totals(values):
         values = values + swap(values, 1) + swap(values, 2) + swap(values, 3)
         if lax.axis_size("ffn") > 2:
@@ -541,19 +569,21 @@
 
     stats, got_out = lax.optimization_barrier((stats, got_out))
     group_sums, whole_sums = totals(stats)
-    whole_sums, got_in = lax.optimization_barrier((whole_sums, got_in))
+    in_sent, whole_sums = lax.optimization_barrier((in_sent, whole_sums))
+    got_in = along_axes(in_sent)
     factors, norms = call(
         norm_kernel, 52,
         [shape((STAT_ROWS, lanes), f32), shape((8, 128), f32)],
         prev, group_sums, whole_sums, *in_own, *in_sent, *out_own, *out_sent,
-        streamed=range(3, 15),
-    )
+        scratch=fetched(in_own, in_sent, out_own, out_sent), whole=range(3, 15),
+    )
+    norms, got_in = lax.optimization_barrier((norms, got_in))
     norms = totals(norms)[1]
     update_in, update_out = call(
         functools.partial(final_kernel, bounds), 52,
         [shape(local_in.shape, bf16), shape(local_out.shape, bf16)],
         prev, factors, whole_sums, norms, *in_own, *out_own, *got_in, *got_out,
-        streamed=range(4, 16), streamed_out=range(2),
+        scratch=fetched(in_own, out_own, got_in, got_out), whole=range(4, 16), streamed_out=range(2),
     )
     return (update_in[None], update_out[None])
 

time: 247 us -> 250 us (1.012)
  waiting for transfers between devices: 122 us -> 132 us
  starting transfers between devices: 64.3 us -> 56.9 us
  other arithmetic: 5.25 us -> 1.55 us
  local copies, waits for them, and re-layouts: 10.8 us -> 14.2 us
    ppermute x46, waiting for transfers between devices: 117 us -> 126 us  [swap(): return lax.ppermute(value, axis, pairs)]
    ppermute x4, starting transfers between devices: 17.3 us -> 11.8 us  [other(): return lax.ppermute(values, ('expert', 'ffn'), moves)]
    unnamed x75 -> x76, local copies, waits for them, and re-layouts: 8.08 us -> 11.9 us
    pallas_call x15 -> x16, Pallas kernels: 41.7 us -> 42.7 us  [call(): pl.pallas_call(kernel, out_shape=out_shape, in_specs=[spec(value, n, stre...]
  transfers between devices with their start and end apart: 51 -> 51, of which waited for: 27 -> 32; matrix products, arithmetic and copies ran while one was open for 1% -> 0% of each run, Pallas kernels for 9% -> 11%
where the time goes in v8:
time: 250 us; the launch traced here: 249 us
  waiting for transfers between devices  132 us (53%)
  starting transfers between devices  56.9 us (23%)
  Pallas kernels  42.7 us (17%)
  local copies, waits for them, and re-layouts  14.2 us (6%)
    ppermute x46, waiting for transfers between devices, swap(): return lax.ppermute(value, axis, pairs)  126 us
    pallas_call x16, Pallas kernels, call(): pl.pallas_call(kernel, out_shape=out_shape, in_specs=[spec(value, n, stre...  42.7 us
    ppermute x46, starting transfers between devices, swap(): return lax.ppermute(value, axis, pairs)  37.7 us
    unnamed x76, local copies, waits for them, and re-layouts  11.9 us
    ppermute x4, starting transfers between devices, other(): return lax.ppermute(values, ('expert', 'ffn'), moves)  11.8 us
    all_to_all x1, starting transfers between devices, shards(): lax.all_to_all(routed, 'expert', split_axis=0, concat_axis=0, tiled=True)  7.45 us
    ppermute x4, waiting for transfers between devices, other(): return lax.ppermute(values, ('expert', 'ffn'), moves)  6.24 us
  transfers between devices with their start and end apart: 51, of which 32 were waited for; matrix products, arithmetic and copies ran while one was open for 0% of the time, Pallas kernels for 11%

profile of v8, /device:TPU:1, one launch (start us, length us, event | category | flops | bytes accessed | tf_op | source)
XLA Modules:
  0.0 249.2 jit_solution(3607850910122843954)
XLA Ops:
  1.4 1.2 copy-done.23
  2.7 1.2 copy-done.24
  3.9 2.0 shard_map.86
  5.9 7.5 %all-to-all-start = ((bf16[16,40,1024]{2,1,0:T(8,128)(2,1)}), bf16[16,40,1024]{2,1,0:T(8,128)(2,1)}, u32[]{:S(2)}, u32[]{:S(2)}) async-start(bf16[16,40,1024]{2,1,0:T(8,128)(2,1)} %bitcast), calls=%async_computation | async-start | bytes 2621440 | tf_op jit(solution)/shard_map/all_to_all | solution.py:463
  13.3 1.7 copy-done.16
  15.1 1.3 shard_map.87
  20.2 1.3 collective-permute-start
  23.9 23.5 %collective-permute-done.1.refs_9_.refs_12_ = bf16[3072,128]{1,0:T(8,128)(2,1)S(1)} collective-permute-done((bf16[3072,128]{1,0:T(8,128)(2,1)S(1)}, bf16[3072,128]{1,0:T(8,128)(2,1)S(1)}, u32[]{:S(2)}, u32[]{:S(2)}) %collective-permute-start.1) | collective-permute-done | bytes 786464 | tf_op jit(solution)/shard_map/ppermute | solution.py:29
  47.4 5.5 %collective-permute-done.2.refs_10_.refs_13_ = bf16[3072,128]{1,0:T(8,128)(2,1)S(1)} collective-permute-done((bf16[3072,128]{1,0:T(8,128)(2,1)S(1)}, bf16[3072,128]{1,0:T(8,128)(2,1)S(1)}, u32[]{:S(2)}, u32[]{:S(2)}) %collective-permute-start.2) | collective-permute-done | bytes 786464 | tf_op jit(solution)/shard_map/ppermute | solution.py:29
  52.9 1.7 collective-permute-done.refs_8_.refs_11_
  54.7 1.4 copy.11
  56.1 1.5 collective-permute-start.3
  58.0 1.9 collective-permute-start.5
  59.9 24.9 %collective-permute-done.3 = bf16[8,80,1024]{2,1,0:T(8,128)(2,1)S(1)} collective-permute-done((bf16[8,80,1024]{2,1,0:T(8,128)(2,1)S(1)}, bf16[8,80,1024]{2,1,0:T(8,128)(2,1)S(1)}, u32[]{:S(2)}, u32[]{:S(2)}) %collective-permute-start.3) | collective-permute-done | bytes 1310752 | tf_op jit(solution)/shard_map/ppermute | solution.py:29
  84.8 1.2 collective-permute-done.4
  87.5 2.9 %collective-permute-start.7 = (bf16[3,8,80,1024]{3,2,1,0:T(8,128)(2,1)S(1)}, bf16[3,8,80,1024]{3,2,1,0:T(8,128)(2,1)S(1)}, u32[]{:S(2)}, u32[]{:S(2)}) collective-permute-start(bf16[3,8,80,1024]{3,2,1,0:T(8,128)(2,1)S(1)} %pad_maximum_fusion.refs_1_), channel_id=1, source_target_pairs={{0,1},{1,0},{2,3},{3,2},{4,5},{5,4},{6,7},{7,6},{8,9},{9,8},{10,11... | collective-permute-start | bytes 11796488 | tf_op jit(solution)/shard_map/ppermute | solution.py:29
  90.5 2.2 shard_map.88
  92.7 1.5 collective-permute-start.10
  94.7 4.0 %collective-permute-done.6.refs_0_.refs_2_ = bf16[8,80,1024]{2,1,0:T(8,128)(2,1)S(1)} collective-permute-done((bf16[8,80,1024]{2,1,0:T(8,128)(2,1)S(1)}, bf16[8,80,1024]{2,1,0:T(8,128)(2,1)S(1)}, u32[]{:S(2)}, u32[]{:S(2)}) %collective-permute-start.6) | collective-permute-done | bytes 1310752 | tf_op jit(solution)/shard_map/ppermute | solution.py:29
  98.7 2.2 shard_map.89
  101.1 2.2 shard_map.91
  103.3 2.2 shard_map.90
  110.3 1.2 collective-permute-start.12
  111.5 2.4 collective-permute-done.11.refs_6_
  114.4 13.5 %collective-permute-done.12.refs_7_ = bf16[160,896]{1,0:T(8,128)(2,1)S(1)} collective-permute-done((bf16[160,896]{1,0:T(8,128)(2,1)S(1)}, bf16[160,896]{1,0:T(8,128)(2,1)S(1)}, u32[]{:S(2)}, u32[]{:S(2)}) %collective-permute-start.12) | collective-permute-done | bytes 286752 | tf_op jit(solution)/shard_map/ppermute | solution.py:29
  132.4 1.3 collective-permute-done.14.refs_3_
  134.6 1.5 collective-permute-done.16.refs_5_
  137.4 3.1 %collective-permute-done.21.refs_6_ = bf16[160,768]{1,0:T(8,128)(2,1)S(1)} collective-permute-done((bf16[160,768]{1,0:T(8,128)(2,1)S(1)}, bf16[160,768]{1,0:T(8,128)(2,1)S(1)}, u32[]{:S(2)}, u32[]{:S(2)}) %collective-permute-start.21) | collective-permute-done | bytes 245792 | tf_op jit(solution)/shard_map/ppermute | solution.py:29
  141.4 1.3 collective-permute-start.25
  144.8 9.2 %collective-permute-done.24.refs_3_ = bf16[160,768]{1,0:T(8,128)(2,1)S(1)} collective-permute-done((bf16[160,768]{1,0:T(8,128)(2,1)S(1)}, bf16[160,768]{1,0:T(8,128)(2,1)S(1)}, u32[]{:S(2)}, u32[]{:S(2)}) %collective-permute-start.24) | collective-permute-done | bytes 245792 | tf_op jit(solution)/shard_map/ppermute | solution.py:29
  154.7 1.3 collective-permute-start.29
  157.3 7.6 %collective-permute-done.30.refs_13_ = bf16[320,896]{1,0:T(8,128)(2,1)S(1)} collective-permute-done((bf16[320,896]{1,0:T(8,128)(2,1)S(1)}, bf16[320,896]{1,0:T(8,128)(2,1)S(1)}, u32[]{:S(2)}, u32[]{:S(2)}) %collective-permute-start.30) | collective-permute-done | bytes 573472 | tf_op jit(solution)/shard_map/ppermute | solution.py:29
  164.8 5.0 %collective-permute-done.29.refs_11_ = bf16[320,896]{1,0:T(8,128)(2,1)S(1)} collective-permute-done((bf16[320,896]{1,0:T(8,128)(2,1)S(1)}, bf16[320,896]{1,0:T(8,128)(2,1)S(1)}, u32[]{:S(2)}, u32[]{:S(2)}) %collective-permute-start.29) | collective-permute-done | bytes 573472 | tf_op jit(solution)/shard_map/ppermute | solution.py:29
  169.8 7.3 %collective-permute-done.31.refs_15_ = bf16[320,896]{1,0:T(8,128)(2,1)S(1)} collective-permute-done((bf16[320,896]{1,0:T(8,128)(2,1)S(1)}, bf16[320,896]{1,0:T(8,128)(2,1)S(1)}, u32[]{:S(2)}, u32[]{:S(2)}) %collective-permute-start.31) | collective-permute-done | bytes 573472 | tf_op jit(solution)/shard_map/ppermute | solution.py:29
  178.0 7.9 %shard_map.98 = (f32[512,512]{1,0:T(8,128)}, f32[384,512]{1,0:T(8,128)}, f32[384,512]{1,0:T(8,128)}, bf16[512,512]{1,0:T(8,128)(2,1)}, bf16[384,512]{1,0:T(8,128...) custom-call(bf16[8,80,1024]{2,1,0:T(8,128)(2,1)} %bitcast.23, bf16[3,8,80,1024]{3,2,1,0:T(8,128)(2,1)} %copy-done.1, ...), custom_call_target="tpu_custom_call" | custom-call | tf_op jit(solution)/shard_map/pallas_call | solution.py:75
  187.0 10.0 %shard_map.99 = (f32[512,512]{1,0:T(8,128)}, f32[512,384]{1,0:T(8,128)}, f32[512,384]{1,0:T(8,128)}, bf16[512,512]{1,0:T(8,128)(2,1)}, bf16[512,384]{1,0:T(8,128...) custom-call(bf16[8,80,1024]{2,1,0:T(8,128)(2,1)} %bitcast.24, bf16[3,8,80,1024]{3,2,1,0:T(8,128)(2,1)} %copy-done.1, ...), custom_call_target="tpu_custom_call" | custom-call | tf_op jit(solution)/shard_map/pallas_call | solution.py:75
  198.2 1.5 collective-permute-start.36
  201.5 2.3 collective-permute-done.37
  204.7 1.5 collective-permute-start.38
  206.2 8.2 %collective-permute-start.39 = (f32[32,512]{1,0:T(8,128)S(1)}, f32[32,512]{1,0:T(8,128)S(1)}, u32[]{:S(2)}, u32[]{:S(2)}) collective-permute-start(f32[32,512]{1,0:T(8,128)S(1)} %add_add_fusion.1), channel_id=1, source_target_pairs={{0,1},{1,0},{2,3},{3,2},{4,5},{5,4},{6,7},{7,6},{8,9},{9,8},{10,11... | collective-permute-start | bytes 196616 | tf_op jit(solution)/shard_map/ppermute | solution.py:565
  215.4 2.8 %collective-permute-done.40 = f32[32,512]{1,0:T(8,128)S(1)} collective-permute-done((f32[32,512]{1,0:T(8,128)S(1)}, f32[32,512]{1,0:T(8,128)S(1)}, u32[]{:S(2)}, u32[]{:S(2)}) %collective-permute-start.40) | collective-permute-done | bytes 65568 | tf_op jit(solution)/shard_map/ppermute | solution.py:565
  222.4 4.4 %shard_map.100 = (f32[32,512]{1,0:T(8,128)S(1)}, f32[8,128]{1,0:T(8,128)S(1)}) custom-call(f32[32,512]{1,0:T(8,128)S(1)} %concatenate.3.prev, f32[32,512]{1,0:T(8,128)S(1)} %get-tuple-element.229.group_sums, f32[32,512]{1,0:T(8,128)S(1)} %get-tuple-element.201.whole_sums, f32[512,512]{1,0:T(8,128)} %get-tuple-element.202.refs_0_, ...), custom_call_target="tpu_custom_call" | custom-call | tf_op jit(solution)/shard_map/pallas_call | solution.py:75
  226.9 2.5 %collective-permute-done.42.refs_7_ = bf16[512,384]{1,0:T(8,128)(2,1)S(1)} collective-permute-done((bf16[512,384]{1,0:T(8,128)(2,1)}, bf16[512,384]{1,0:T(8,128)(2,1)S(1)}, u32[]{:S(2)}, u32[]{:S(2)}) %collective-permute-start.42) | collective-permute-done | bytes 393248 | tf_op jit(solution)/shard_map/ppermute | solution.py:29
  229.4 2.7 %collective-permute-done.41.refs_6_ = bf16[512,512]{1,0:T(8,128)(2,1)} collective-permute-done((bf16[512,512]{1,0:T(8,128)(2,1)}, bf16[512,512]{1,0:T(8,128)(2,1)}, u32[]{:S(2)}, u32[]{:S(2)}) %collective-permute-start.41) | collective-permute-done | bytes 524320 | tf_op jit(solution)/shard_map/ppermute | solution.py:29
  232.8 2.0 collective-permute-start.46
  236.9 3.1 %collective-permute-start.48 = (f32[8,128]{1,0:T(8,128)S(1)}, f32[8,128]{1,0:T(8,128)S(1)}, u32[]{:S(2)}, u32[]{:S(2)}) collective-permute-start(f32[8,128]{1,0:T(8,128)S(1)} %add_add_fusion.3), channel_id=1, source_target_pairs={{0,1},{1,0},{2,3},{3,2},{4,5},{5,4},{6,7},{7,6},{8,9},{9,8},{10,11... | collective-permute-start | bytes 12296 | tf_op jit(solution)/shard_map/ppermute | solution.py:565
  240.8 2.2 collective-permute-done.49
  243.0 6.0 %shard_map.101 = (bf16[512,2560]{1,0:T(8,128)(2,1)}, bf16[2560,512]{1,0:T(8,128)(2,1)}) custom-call(f32[32,512]{1,0:T(8,128)S(1)} %concatenate.3.prev, f32[32,512]{1,0:T(8,128)S(1)} %get-tuple-element.211.factors, f32[32,512]{1,0:T(8,128)S(1)} %get-tuple-element.201.whole_sums, f32[8,128]{1,0:T(8,128)S(1)} %add_add_fusion.2.norms, ...), custom_call_target="tpu_custom_call" | custom-call | tf_op jit(solution)/shard_map/pallas_call | solution.py:75
  (170 shorter events, 41.1 us)
Async XLA Ops:
  5.9 48.8 %all-to-all-start = ((bf16[16,40,1024]{2,1,0:T(8,128)(2,1)}), bf16[16,40,1024]{2,1,0:T(8,128)(2,1)}, u32[]{:S(2)}, u32[]{:S(2)}) async-start(bf16[16,40,1024]{2,1,0:T(8,128)(2,1)} %bitcast), calls=%async_computation | async-start | bytes 2621440 | tf_op jit(solution)/shard_map/all_to_all | solution.py:463
  20.2 34.4 %collective-permute-start = (bf16[4096,128]{1,0:T(8,128)(2,1)S(1)}, bf16[4096,128]{1,0:T(8,128)(2,1)S(1)}, u32[]{:S(2)}, u32[]{:S(2)}) collective-permute-start(bf16[4096,128]{1,0:T(8,128)(2,1)S(1)} %get-tuple-element.112), channel_id=1, source_target_pairs={{0,2},{2,0},{4,6},{6,4},{8,10},{10,8},{12,14},{14,12},{16,18},{18,... | collective-permute-start | bytes 3145736 | tf_op jit(solution)/shard_map/ppermute | solution.py:29
  21.6 25.9 %collective-permute-start.1 = (bf16[3072,128]{1,0:T(8,128)(2,1)S(1)}, bf16[3072,128]{1,0:T(8,128)(2,1)S(1)}, u32[]{:S(2)}, u32[]{:S(2)}) collective-permute-start(bf16[3072,128]{1,0:T(8,128)(2,1)S(1)} %get-tuple-element.113), channel_id=1, source_target_pairs={{0,4},{2,6},{4,0},{6,2},{8,12},{10,14},{12,8},{14,10},{16,20},{18,... | collective-permute-start | bytes 2359304 | tf_op jit(solution)/shard_map/ppermute | solution.py:29
  22.7 30.2 %collective-permute-start.2 = (bf16[3072,128]{1,0:T(8,128)(2,1)S(1)}, bf16[3072,128]{1,0:T(8,128)(2,1)S(1)}, u32[]{:S(2)}, u32[]{:S(2)}) collective-permute-start(bf16[3072,128]{1,0:T(8,128)(2,1)S(1)} %get-tuple-element.114), channel_id=1, source_target_pairs={{0,8},{2,10},{4,12},{6,14},{8,0},{10,2},{12,4},{14,6},{16,24},{18,... | collective-permute-start | bytes 2359304 | tf_op jit(solution)/shard_map/ppermute | solution.py:29
  56.1 28.7 %collective-permute-start.3 = (bf16[8,80,1024]{2,1,0:T(8,128)(2,1)S(1)}, bf16[8,80,1024]{2,1,0:T(8,128)(2,1)S(1)}, u32[]{:S(2)}, u32[]{:S(2)}) collective-permute-start(bf16[8,80,1024]{2,1,0:T(8,128)(2,1)S(1)} %bitcast.17), channel_id=1, source_target_pairs={{0,2},{2,0},{4,6},{6,4},{8,10},{10,8},{12,14},{14,12},{16,18},{18,... | collective-permute-start | bytes 3932168 | tf_op jit(solution)/shard_map/ppermute | solution.py:29
  57.6 28.4 %collective-permute-start.4 = (bf16[8,80,1024]{2,1,0:T(8,128)(2,1)S(1)}, bf16[8,80,1024]{2,1,0:T(8,128)(2,1)S(1)}, u32[]{:S(2)}, u32[]{:S(2)}) collective-permute-start(bf16[8,80,1024]{2,1,0:T(8,128)(2,1)S(1)} %bitcast.18), channel_id=1, source_target_pairs={{0,4},{2,6},{4,0},{6,2},{8,12},{10,14},{12,8},{14,10},{16,20},{18,... | collective-permute-start | bytes 3932168 | tf_op jit(solution)/shard_map/ppermute | solution.py:29
  58.0 28.8 %collective-permute-start.5 = (bf16[8,80,1024]{2,1,0:T(8,128)(2,1)S(1)}, bf16[8,80,1024]{2,1,0:T(8,128)(2,1)S(1)}, u32[]{:S(2)}, u32[]{:S(2)}) collective-permute-start(bf16[8,80,1024]{2,1,0:T(8,128)(2,1)S(1)} %bitcast.19), channel_id=1, source_target_pairs={{0,8},{2,10},{4,12},{6,14},{8,0},{10,2},{12,4},{14,6},{16,24},{18,... | collective-permute-start | bytes 3932168 | tf_op jit(solution)/shard_map/ppermute | solution.py:29
  87.5 11.2 %collective-permute-start.7 = (bf16[3,8,80,1024]{3,2,1,0:T(8,128)(2,1)S(1)}, bf16[3,8,80,1024]{3,2,1,0:T(8,128)(2,1)S(1)}, u32[]{:S(2)}, u32[]{:S(2)}) collective-permute-start(bf16[3,8,80,1024]{3,2,1,0:T(8,128)(2,1)S(1)} %pad_maximum_fusion.refs_1_), channel_id=1, source_target_pairs={{0,1},{1,0},{2,3},{3,2},{4,5},{5,4},{6,7},{7,6},{8,9},{9,8},{10,11... | collective-permute-start | bytes 11796488 | tf_op jit(solution)/shard_map/ppermute | solution.py:29
  90.4 8.3 %collective-permute-start.6 = (bf16[8,80,1024]{2,1,0:T(8,128)(2,1)S(1)}, bf16[8,80,1024]{2,1,0:T(8,128)(2,1)S(1)}, u32[]{:S(2)}, u32[]{:S(2)}) collective-permute-start(bf16[8,80,1024]{2,1,0:T(8,128)(2,1)S(1)} %bitcast.20), channel_id=1, source_target_pairs={{0,1},{1,0},{2,3},{3,2},{4,5},{5,4},{6,7},{7,6},{8,9},{9,8},{10,11... | collective-permute-start | bytes 3932168 | tf_op jit(solution)/shard_map/ppermute | solution.py:29
  92.7 14.0 %collective-permute-start.10 = (bf16[320,896]{1,0:T(8,128)(2,1)S(1)}, bf16[320,896]{1,0:T(8,128)(2,1)S(1)}, u32[]{:S(2)}, u32[]{:S(2)}) collective-permute-start(bf16[320,896]{1,0:T(8,128)(2,1)S(1)} %get-tuple-element.130), channel_id=1, source_target_pairs={{0,8},{2,10},{4,12},{6,14},{8,0},{10,2},{12,4},{14,6},{16,24},{18,... | collective-permute-start | bytes 1720328 | tf_op jit(solution)/shard_map/ppermute | solution.py:29
  94.3 13.6 %collective-permute-start.9 = (bf16[320,896]{1,0:T(8,128)(2,1)S(1)}, bf16[320,896]{1,0:T(8,128)(2,1)S(1)}, u32[]{:S(2)}, u32[]{:S(2)}) collective-permute-start(bf16[320,896]{1,0:T(8,128)(2,1)S(1)} %get-tuple-element.129), channel_id=1, source_target_pairs={{0,4},{2,6},{4,0},{6,2},{8,12},{10,14},{12,8},{14,10},{16,20},{18,... | collective-permute-start | bytes 1720328 | tf_op jit(solution)/shard_map/ppermute | solution.py:29
  94.3 11.5 %collective-permute-start.8 = (bf16[320,768]{1,0:T(8,128)(2,1)S(1)}, bf16[320,768]{1,0:T(8,128)(2,1)S(1)}, u32[]{:S(2)}, u32[]{:S(2)}) collective-permute-start(bf16[320,768]{1,0:T(8,128)(2,1)S(1)} %get-tuple-element.128), channel_id=1, source_target_pairs={{0,2},{2,0},{4,6},{6,4},{8,10},{10,8},{12,14},{14,12},{16,18},{18,... | collective-permute-start | bytes 1474568 | tf_op jit(solution)/shard_map/ppermute | solution.py:29
  108.2 5.7 %collective-permute-start.11 = (bf16[160,768]{1,0:T(8,128)(2,1)S(1)}, bf16[160,768]{1,0:T(8,128)(2,1)S(1)}, u32[]{:S(2)}, u32[]{:S(2)}) collective-permute-start(bf16[160,768]{1,0:T(8,128)(2,1)S(1)} %get-tuple-element.162), channel_id=1, source_target_pairs={{0,2},{2,0},{4,6},{6,4},{8,10},{10,8},{12,14},{14,12},{16,18},{18,... | collective-permute-start | bytes 737288 | tf_op jit(solution)/shard_map/ppermute | solution.py:29
  108.6 21.7 %collective-permute-start.18 = (bf16[320,768]{1,0:T(8,128)(2,1)S(1)}, bf16[320,768]{1,0:T(8,128)(2,1)S(1)}, u32[]{:S(2)}, u32[]{:S(2)}) collective-permute-start(bf16[320,768]{1,0:T(8,128)(2,1)S(1)} %get-tuple-element.131), channel_id=1, source_target_pairs={{0,2},{2,0},{4,6},{6,4},{8,10},{10,8},{12,14},{14,12},{16,18},{18,... | collective-permute-start | bytes 1474568 | tf_op jit(solution)/shard_map/ppermute | solution.py:29
  109.7 21.2 %collective-permute-start.19 = (bf16[320,896]{1,0:T(8,128)(2,1)S(1)}, bf16[320,896]{1,0:T(8,128)(2,1)S(1)}, u32[]{:S(2)}, u32[]{:S(2)}) collective-permute-start(bf16[320,896]{1,0:T(8,128)(2,1)S(1)} %get-tuple-element.132), channel_id=1, source_target_pairs={{0,4},{2,6},{4,0},{6,2},{8,12},{10,14},{12,8},{14,10},{16,20},{18,... | collective-permute-start | bytes 1720328 | tf_op jit(solution)/shard_map/ppermute | solution.py:29
  109.7 21.2 %collective-permute-start.20 = (bf16[320,896]{1,0:T(8,128)(2,1)S(1)}, bf16[320,896]{1,0:T(8,128)(2,1)S(1)}, u32[]{:S(2)}, u32[]{:S(2)}) collective-permute-start(bf16[320,896]{1,0:T(8,128)(2,1)S(1)} %get-tuple-element.133), channel_id=1, source_target_pairs={{0,8},{2,10},{4,12},{6,14},{8,0},{10,2},{12,4},{14,6},{16,24},{18,... | collective-permute-start | bytes 1720328 | tf_op jit(solution)/shard_map/ppermute | solution.py:29
  110.3 17.6 %collective-permute-start.12 = (bf16[160,896]{1,0:T(8,128)(2,1)S(1)}, bf16[160,896]{1,0:T(8,128)(2,1)S(1)}, u32[]{:S(2)}, u32[]{:S(2)}) collective-permute-start(bf16[160,896]{1,0:T(8,128)(2,1)S(1)} %get-tuple-element.163), channel_id=1, source_target_pairs={{0,4},{2,6},{4,0},{6,2},{8,12},{10,14},{12,8},{14,10},{16,20},{18,... | collective-permute-start | bytes 860168 | tf_op jit(solution)/shard_map/ppermute | solution.py:29
  113.8 14.1 %collective-permute-start.13 = (bf16[160,896]{1,0:T(8,128)(2,1)S(1)}, bf16[160,896]{1,0:T(8,128)(2,1)S(1)}, u32[]{:S(2)}, u32[]{:S(2)}) collective-permute-start(bf16[160,896]{1,0:T(8,128)(2,1)S(1)} %get-tuple-element.164), channel_id=1, source_target_pairs={{0,8},{2,10},{4,12},{6,14},{8,0},{10,2},{12,4},{14,6},{16,24},{18,... | collective-permute-start | bytes 860168 | tf_op jit(solution)/shard_map/ppermute | solution.py:29
  128.7 5.1 %collective-permute-start.14 = (bf16[160,768]{1,0:T(8,128)(2,1)S(1)}, bf16[160,768]{1,0:T(8,128)(2,1)S(1)}, u32[]{:S(2)}, u32[]{:S(2)}) collective-permute-start(bf16[160,768]{1,0:T(8,128)(2,1)S(1)} %get-tuple-element.165.refs_0_), channel_id=1, source_target_pairs={{0,2},{2,0},{4,6},{6,4},{8,10},{10,8},{12,14},{14,12},{16,18},{18,... | collective-permute-start | bytes 737288 | tf_op jit(solution)/shard_map/ppermute | solution.py:29
  129.2 5.5 %collective-permute-start.15 = (bf16[160,896]{1,0:T(8,128)(2,1)S(1)}, bf16[160,896]{1,0:T(8,128)(2,1)S(1)}, u32[]{:S(2)}, u32[]{:S(2)}) collective-permute-start(bf16[160,896]{1,0:T(8,128)(2,1)S(1)} %get-tuple-element.166.refs_1_), channel_id=1, source_target_pairs={{0,4},{2,6},{4,0},{6,2},{8,12},{10,14},{12,8},{14,10},{16,20},{18,... | collective-permute-start | bytes 860168 | tf_op jit(solution)/shard_map/ppermute | solution.py:29
  130.3 5.8 %collective-permute-start.16 = (bf16[160,896]{1,0:T(8,128)(2,1)S(1)}, bf16[160,896]{1,0:T(8,128)(2,1)S(1)}, u32[]{:S(2)}, u32[]{:S(2)}) collective-permute-start(bf16[160,896]{1,0:T(8,128)(2,1)S(1)} %get-tuple-element.167.refs_2_), channel_id=1, source_target_pairs={{0,8},{2,10},{4,12},{6,14},{8,0},{10,2},{12,4},{14,6},{16,24},{18,... | collective-permute-start | bytes 860168 | tf_op jit(solution)/shard_map/ppermute | solution.py:29
  131.2 9.3 %collective-permute-start.22 = (bf16[160,896]{1,0:T(8,128)(2,1)S(1)}, bf16[160,896]{1,0:T(8,128)(2,1)S(1)}, u32[]{:S(2)}, u32[]{:S(2)}) collective-permute-start(bf16[160,896]{1,0:T(8,128)(2,1)S(1)} %get-tuple-element.182), channel_id=1, source_target_pairs={{0,4},{2,6},{4,0},{6,2},{8,12},{10,14},{12,8},{14,10},{16,20},{18,... | collective-permute-start | bytes 860168 | tf_op jit(solution)/shard_map/ppermute | solution.py:29
  131.5 9.1 %collective-permute-start.23 = (bf16[160,896]{1,0:T(8,128)(2,1)S(1)}, bf16[160,896]{1,0:T(8,128)(2,1)S(1)}, u32[]{:S(2)}, u32[]{:S(2)}) collective-permute-start(bf16[160,896]{1,0:T(8,128)(2,1)S(1)} %get-tuple-element.183), channel_id=1, source_target_pairs={{0,8},{2,10},{4,12},{6,14},{8,0},{10,2},{12,4},{14,6},{16,24},{18,... | collective-permute-start | bytes 860168 | tf_op jit(solution)/shard_map/ppermute | solution.py:29
  133.8 6.7 %collective-permute-start.21 = (bf16[160,768]{1,0:T(8,128)(2,1)S(1)}, bf16[160,768]{1,0:T(8,128)(2,1)S(1)}, u32[]{:S(2)}, u32[]{:S(2)}) collective-permute-start(bf16[160,768]{1,0:T(8,128)(2,1)S(1)} %get-tuple-element.181), channel_id=1, source_target_pairs={{0,2},{2,0},{4,6},{6,4},{8,10},{10,8},{12,14},{14,12},{16,18},{18,... | collective-permute-start | bytes 737288 | tf_op jit(solution)/shard_map/ppermute | solution.py:29
  136.3 20.5 %collective-permute-start.17 = (bf16[320,768]{1,0:T(8,128)(2,1)S(1)}, bf16[320,768]{1,0:T(8,128)(2,1)S(1)}, u32[]{:S(2)}, u32[]{:S(2)}) collective-permute-start(bf16[320,768]{1,0:T(8,128)(2,1)S(1)} %get-tuple-element.168.refs_4_), channel_id=1, source_target_pairs={{0,2},{2,0},{4,6},{6,4},{8,10},{10,8},{12,14},{14,12},{16,18},{18,... | collective-permute-start | bytes 1474568 | tf_op jit(solution)/shard_map/ppermute | solution.py:29
  141.4 13.1 %collective-permute-start.25 = (bf16[160,896]{1,0:T(8,128)(2,1)S(1)}, bf16[160,896]{1,0:T(8,128)(2,1)S(1)}, u32[]{:S(2)}, u32[]{:S(2)}) collective-permute-start(bf16[160,896]{1,0:T(8,128)(2,1)S(1)} %get-tuple-element.185.refs_1_), channel_id=1, source_target_pairs={{0,4},{2,6},{4,0},{6,2},{8,12},{10,14},{12,8},{14,10},{16,20},{18,... | collective-permute-start | bytes 860168 | tf_op jit(solution)/shard_map/ppermute | solution.py:29
  142.7 11.8 %collective-permute-start.26 = (bf16[160,896]{1,0:T(8,128)(2,1)S(1)}, bf16[160,896]{1,0:T(8,128)(2,1)S(1)}, u32[]{:S(2)}, u32[]{:S(2)}) collective-permute-start(bf16[160,896]{1,0:T(8,128)(2,1)S(1)} %get-tuple-element.186.refs_2_), channel_id=1, source_target_pairs={{0,8},{2,10},{4,12},{6,14},{8,0},{10,2},{12,4},{14,6},{16,24},{18,... | collective-permute-start | bytes 860168 | tf_op jit(solution)/shard_map/ppermute | solution.py:29
  143.1 10.9 %collective-permute-start.24 = (bf16[160,768]{1,0:T(8,128)(2,1)S(1)}, bf16[160,768]{1,0:T(8,128)(2,1)S(1)}, u32[]{:S(2)}, u32[]{:S(2)}) collective-permute-start(bf16[160,768]{1,0:T(8,128)(2,1)S(1)} %get-tuple-element.184.refs_0_), channel_id=1, source_target_pairs={{0,2},{2,0},{4,6},{6,4},{8,10},{10,8},{12,14},{14,12},{16,18},{18,... | collective-permute-start | bytes 737288 | tf_op jit(solution)/shard_map/ppermute | solution.py:29
  143.6 13.6 %collective-permute-start.28 = (bf16[320,896]{1,0:T(8,128)(2,1)S(1)}, bf16[320,896]{1,0:T(8,128)(2,1)S(1)}, u32[]{:S(2)}, u32[]{:S(2)}) collective-permute-start(bf16[320,896]{1,0:T(8,128)(2,1)S(1)} %get-tuple-element.188.refs_8_), channel_id=1, source_target_pairs={{0,4},{2,6},{4,0},{6,2},{8,12},{10,14},{12,8},{14,10},{16,20},{18,... | collective-permute-start | bytes 1720328 | tf_op jit(solution)/shard_map/ppermute | solution.py:29
  154.0 10.9 %collective-permute-start.30 = (bf16[320,896]{1,0:T(8,128)(2,1)S(1)}, bf16[320,896]{1,0:T(8,128)(2,1)S(1)}, u32[]{:S(2)}, u32[]{:S(2)}) collective-permute-start(bf16[320,896]{1,0:T(8,128)(2,1)S(1)} %get-tuple-element.190.refs_12_), channel_id=1, source_target_pairs={{0,8},{2,10},{4,12},{6,14},{8,0},{10,2},{12,4},{14,6},{16,24},{18,... | collective-permute-start | bytes 1720328 | tf_op jit(solution)/shard_map/ppermute | solution.py:29
  154.7 15.1 %collective-permute-start.29 = (bf16[320,896]{1,0:T(8,128)(2,1)S(1)}, bf16[320,896]{1,0:T(8,128)(2,1)S(1)}, u32[]{:S(2)}, u32[]{:S(2)}) collective-permute-start(bf16[320,896]{1,0:T(8,128)(2,1)S(1)} %get-tuple-element.189.refs_10_), channel_id=1, source_target_pairs={{0,4},{2,6},{4,0},{6,2},{8,12},{10,14},{12,8},{14,10},{16,20},{18,... | collective-permute-start | bytes 1720328 | tf_op jit(solution)/shard_map/ppermute | solution.py:29
  155.9 21.2 %collective-permute-start.31 = (bf16[320,896]{1,0:T(8,128)(2,1)S(1)}, bf16[320,896]{1,0:T(8,128)(2,1)S(1)}, u32[]{:S(2)}, u32[]{:S(2)}) collective-permute-start(bf16[320,896]{1,0:T(8,128)(2,1)S(1)} %get-tuple-element.191.refs_14_), channel_id=1, source_target_pairs={{0,8},{2,10},{4,12},{6,14},{8,0},{10,2},{12,4},{14,6},{16,24},{18,... | collective-permute-start | bytes 1720328 | tf_op jit(solution)/shard_map/ppermute | solution.py:29
  156.8 8.0 %collective-permute-start.27 = (bf16[320,768]{1,0:T(8,128)(2,1)S(1)}, bf16[320,768]{1,0:T(8,128)(2,1)S(1)}, u32[]{:S(2)}, u32[]{:S(2)}) collective-permute-start(bf16[320,768]{1,0:T(8,128)(2,1)S(1)} %get-tuple-element.187.refs_6_), channel_id=1, source_target_pairs={{0,2},{2,0},{4,6},{6,4},{8,10},{10,8},{12,14},{14,12},{16,18},{18,... | collective-permute-start | bytes 1474568 | tf_op jit(solution)/shard_map/ppermute | solution.py:29
  185.9 11.1 %collective-permute-start.32 = (bf16[512,512]{1,0:T(8,128)(2,1)}, bf16[512,512]{1,0:T(8,128)(2,1)S(1)}, u32[]{:S(2)}, u32[]{:S(2)}) collective-permute-start(bf16[512,512]{1,0:T(8,128)(2,1)} %get-tuple-element.194.refs_9_), channel_id=1, source_target_pairs={{0,2},{2,0},{4,6},{6,4},{8,10},{10,8},{12,14},{14,12},{16,18},{18,... | collective-permute-start | bytes 1572872 | tf_op jit(solution)/shard_map/ppermute | solution.py:29
  186.4 10.6 %collective-permute-start.33 = (bf16[384,512]{1,0:T(8,128)(2,1)}, bf16[384,512]{1,0:T(8,128)(2,1)S(1)}, u32[]{:S(2)}, u32[]{:S(2)}) collective-permute-start(bf16[384,512]{1,0:T(8,128)(2,1)} %get-tuple-element.195.refs_10_), channel_id=1, source_target_pairs={{0,4},{2,6},{4,0},{6,2},{8,12},{10,14},{12,8},{14,10},{16,20},{18,... | collective-permute-start | bytes 1179656 | tf_op jit(solution)/shard_map/ppermute | solution.py:29
  186.4 10.6 %collective-permute-start.34 = (bf16[384,512]{1,0:T(8,128)(2,1)}, bf16[384,512]{1,0:T(8,128)(2,1)S(1)}, u32[]{:S(2)}, u32[]{:S(2)}) collective-permute-start(bf16[384,512]{1,0:T(8,128)(2,1)} %get-tuple-element.196.refs_11_), channel_id=1, source_target_pairs={{0,8},{2,10},{4,12},{6,14},{8,0},{10,2},{12,4},{14,6},{16,24},{18,... | collective-permute-start | bytes 1179656 | tf_op jit(solution)/shard_map/ppermute | solution.py:29
  197.1 3.7 %collective-permute-start.35 = (f32[32,512]{1,0:T(8,128)}, f32[32,512]{1,0:T(8,128)S(1)}, u32[]{:S(2)}, u32[]{:S(2)}) collective-permute-start(f32[32,512]{1,0:T(8,128)} %get-tuple-element.197), channel_id=1, source_target_pairs={{0,2},{2,0},{4,6},{6,4},{8,10},{10,8},{12,14},{14,12},{16,18},{18,... | collective-permute-start | bytes 196616 | tf_op jit(solution)/shard_map/ppermute | solution.py:29
  198.2 3.4 %collective-permute-start.36 = (f32[32,512]{1,0:T(8,128)}, f32[32,512]{1,0:T(8,128)S(1)}, u32[]{:S(2)}, u32[]{:S(2)}) collective-permute-start(f32[32,512]{1,0:T(8,128)} %get-tuple-element.197), channel_id=1, source_target_pairs={{0,4},{2,6},{4,0},{6,2},{8,12},{10,14},{12,8},{14,10},{16,20},{18,... | collective-permute-start | bytes 196616 | tf_op jit(solution)/shard_map/ppermute | solution.py:29
  199.6 4.2 %collective-permute-start.37 = (f32[32,512]{1,0:T(8,128)}, f32[32,512]{1,0:T(8,128)S(1)}, u32[]{:S(2)}, u32[]{:S(2)}) collective-permute-start(f32[32,512]{1,0:T(8,128)} %get-tuple-element.197), channel_id=1, source_target_pairs={{0,6},{2,4},{4,2},{6,0},{8,14},{10,12},{12,10},{14,8},{16,22},{18,... | collective-permute-start | bytes 196616 | tf_op jit(solution)/shard_map/ppermute | solution.py:29
  204.7 9.8 %collective-permute-start.38 = (f32[32,512]{1,0:T(8,128)S(1)}, f32[32,512]{1,0:T(8,128)S(1)}, u32[]{:S(2)}, u32[]{:S(2)}) collective-permute-start(f32[32,512]{1,0:T(8,128)S(1)} %add_add_fusion.1), channel_id=1, source_target_pairs={{0,8},{2,10},{4,12},{6,14},{8,0},{10,2},{12,4},{14,6},{16,24},{18,... | collective-permute-start | bytes 196616 | tf_op jit(solution)/shard_map/ppermute | solution.py:29
  206.2 9.1 %collective-permute-start.39 = (f32[32,512]{1,0:T(8,128)S(1)}, f32[32,512]{1,0:T(8,128)S(1)}, u32[]{:S(2)}, u32[]{:S(2)}) collective-permute-start(f32[32,512]{1,0:T(8,128)S(1)} %add_add_fusion.1), channel_id=1, source_target_pairs={{0,1},{1,0},{2,3},{3,2},{4,5},{5,4},{6,7},{7,6},{8,9},{9,8},{10,11... | collective-permute-start | bytes 196616 | tf_op jit(solution)/shard_map/ppermute | solution.py:565
  214.5 3.7 %collective-permute-start.40 = (f32[32,512]{1,0:T(8,128)S(1)}, f32[32,512]{1,0:T(8,128)S(1)}, u32[]{:S(2)}, u32[]{:S(2)}) collective-permute-start(f32[32,512]{1,0:T(8,128)S(1)} %add_add_fusion.1), channel_id=1, source_target_pairs={{0,9},{1,8},{2,11},{3,10},{4,13},{5,12},{6,15},{7,14},{8,1},{9,0},... | collective-permute-start | bytes 196616 | tf_op jit(solution)/shard_map/ppermute | solution.py:565
  218.2 13.9 %collective-permute-start.41 = (bf16[512,512]{1,0:T(8,128)(2,1)}, bf16[512,512]{1,0:T(8,128)(2,1)}, u32[]{:S(2)}, u32[]{:S(2)}) collective-permute-start(bf16[512,512]{1,0:T(8,128)(2,1)} %get-tuple-element.205.refs_3_), channel_id=1, source_target_pairs={{0,2},{2,0},{4,6},{6,4},{8,10},{10,8},{12,14},{14,12},{16,18},{18,... | collective-permute-start | bytes 1572872 | tf_op jit(solution)/shard_map/ppermute | solution.py:29
  218.7 10.7 %collective-permute-start.42 = (bf16[512,384]{1,0:T(8,128)(2,1)}, bf16[512,384]{1,0:T(8,128)(2,1)S(1)}, u32[]{:S(2)}, u32[]{:S(2)}) collective-permute-start(bf16[512,384]{1,0:T(8,128)(2,1)} %get-tuple-element.206.refs_4_), channel_id=1, source_target_pairs={{0,4},{2,6},{4,0},{6,2},{8,12},{10,14},{12,8},{14,10},{16,20},{18,... | collective-permute-start | bytes 1179656 | tf_op jit(solution)/shard_map/ppermute | solution.py:29
  219.1 10.3 %collective-permute-start.43 = (bf16[512,384]{1,0:T(8,128)(2,1)}, bf16[512,384]{1,0:T(8,128)(2,1)S(1)}, u32[]{:S(2)}, u32[]{:S(2)}) collective-permute-start(bf16[512,384]{1,0:T(8,128)(2,1)} %get-tuple-element.207.refs_5_), channel_id=1, source_target_pairs={{0,8},{2,10},{4,12},{6,14},{8,0},{10,2},{12,4},{14,6},{16,24},{18,... | collective-permute-start | bytes 1179656 | tf_op jit(solution)/shard_map/ppermute | solution.py:29
  232.8 3.4 %collective-permute-start.46 = (f32[8,128]{1,0:T(8,128)S(1)}, f32[8,128]{1,0:T(8,128)S(1)}, u32[]{:S(2)}, u32[]{:S(2)}) collective-permute-start(f32[8,128]{1,0:T(8,128)S(1)} %get-tuple-element.213), channel_id=1, source_target_pairs={{0,6},{2,4},{4,2},{6,0},{8,14},{10,12},{12,10},{14,8},{16,22},{18,... | collective-permute-start | bytes 12296 | tf_op jit(solution)/shard_map/ppermute | solution.py:29
  236.1 4.3 %collective-permute-start.47 = (f32[8,128]{1,0:T(8,128)S(1)}, f32[8,128]{1,0:T(8,128)S(1)}, u32[]{:S(2)}, u32[]{:S(2)}) collective-permute-start(f32[8,128]{1,0:T(8,128)S(1)} %add_add_fusion.3), channel_id=1, source_target_pairs={{0,8},{2,10},{4,12},{6,14},{8,0},{10,2},{12,4},{14,6},{16,24},{18,... | collective-permute-start | bytes 12296 | tf_op jit(solution)/shard_map/ppermute | solution.py:29
  236.9 3.9 %collective-permute-start.48 = (f32[8,128]{1,0:T(8,128)S(1)}, f32[8,128]{1,0:T(8,128)S(1)}, u32[]{:S(2)}, u32[]{:S(2)}) collective-permute-start(f32[8,128]{1,0:T(8,128)S(1)} %add_add_fusion.3), channel_id=1, source_target_pairs={{0,1},{1,0},{2,3},{3,2},{4,5},{5,4},{6,7},{7,6},{8,9},{9,8},{10,11... | collective-permute-start | bytes 12296 | tf_op jit(solution)/shard_map/ppermute | solution.py:565
  (40 other events, 722.3 us)

commit v9 on v8

--- a/solution.py
+++ b/solution.py
@@ -21,7 +21,7 @@
 MASKS = (1, 2, 4)
 
 MIB = 1024 * 1024
-CUT_MIB = 8
+PACK_MIB = 44
 
 
 def swap(value, mask, axis="expert"):
@@ -135,32 +135,39 @@
                 out[e, b, :, n * width : (n + 1) * width] = mine[:, b * width : (b + 1) * width]
 
 
-def cut_kernel(bounds, weight_in, weight_out, *refs):
-    kept_in, kept_out, packed, sems = refs[:3], refs[3:6], refs[6:9], refs[9]
-    copies = []
-    width = weight_in.shape[0]
-    for k in range(3):
-        low, half = bounds[k][0], (bounds[k][1] - bounds[k][0]) // 2
-        side = bit(place_in_group(), k)
-        kept = pl.ds(pl.multiple_of(low + side * half, 128), half)
-        copies.append((weight_in.at[:, kept], kept_in[k], 3 * k))
-        copies.append((weight_out.at[kept, :], kept_out[k], 3 * k + 1))
-        start = low + (1 - side) * half
-        at = 0
-        for n in range(half // 128):
-            part = pl.ds(pl.multiple_of(start + n * 128, 128), 128)
-            copies.append((weight_in.at[:, part], packed[k].at[at : at + width], 3 * k + 2))
-            at += width
-        for n in range(width // 128):
-            part = pl.ds(pl.multiple_of(start, 128), half)
-            source = weight_out.at[part, n * 128 : n * 128 + 128]
-            copies.append((source, packed[k].at[at : at + half], 3 * k + 2))
-            at += half
-    copies = [pltpu.make_async_copy(source, target, sems.at[n]) for n, (source, target, _) in enumerate(copies)]
+def run_copies(moves, sems):
+    copies = [pltpu.make_async_copy(source, target, sems.at[n]) for n, (source, target) in enumerate(moves)]
     for copy in copies:
         copy.start()
     for copy in copies:
         copy.wait()
+
+
+def keep_kernel(bounds, weight_in, weight_out, *refs):
+    moves = []
+    for k in range(3):
+        low, half = bounds[k][0], (bounds[k][1] - bounds[k][0]) // 2
+        kept = pl.ds(pl.multiple_of(low + bit(place_in_group(), k) * half, 128), half)
+        moves += [(weight_in.at[:, kept], refs[k]), (weight_out.at[kept, :], refs[3 + k])]
+    run_copies(moves, refs[6])
+
+
+def pack_kernel(bounds, weight_in, weight_out, *refs):
+    packed, moves = refs[:3], []
+    width = weight_in.shape[0]
+    for k in range(3):
+        low, half = bounds[k][0], (bounds[k][1] - bounds[k][0]) // 2
+        start = low + (1 - bit(place_in_group(), k)) * half
+        at = 0
+        for n in range(half // 128):
+            part = pl.ds(pl.multiple_of(start + n * 128, 128), 128)
+            moves.append((weight_in.at[:, part], packed[k].at[at : at + width]))
+            at += width
+        for n in range(width // 128):
+            part = pl.ds(pl.multiple_of(start, 128), half)
+            moves.append((weight_out.at[part, n * 128 : n * 128 + 128], packed[k].at[at : at + half]))
+            at += half
+    run_copies(moves, refs[3])
 
 
 def got_weight(ref, by_row, half, width):
@@ -437,15 +444,13 @@
 
     is_packed = all(half % 128 == 0 for half in halves) and block_width % 128 == 0
     if is_packed:
-        kept_shapes = [shape((block_width, half), bf16) for half in halves]
-        kept_shapes += [shape((half, block_width), bf16) for half in halves]
         packed_shapes = [shape((2 * half * block_width // 128, 128), bf16) for half in halves]
-        copies = 6 + sum(half + block_width for half in halves) // 128
+        copies = sum(half + block_width for half in halves) // 128
         cuts = call(
-            functools.partial(cut_kernel, bounds), CUT_MIB, kept_shapes + packed_shapes, local_in, local_out,
+            functools.partial(pack_kernel, bounds), PACK_MIB, packed_shapes, local_in, local_out,
             scratch=[pltpu.SemaphoreType.DMA((copies,))], whole=(0, 1),
         )
-        got_weights = [swap(cuts[6 + k], MASKS[k]) for k in sets] * 2
+        got_weights = [swap(cuts[k], MASKS[k]) for k in sets] * 2
     else:
         cuts = []
         for taken in range(2):
@@ -461,7 +466,14 @@
     )
     routed = routed.reshape(places, part_cap, 2 * block_width)
     got = lax.all_to_all(routed, "expert", split_axis=0, concat_axis=0, tiled=True)
-    got, got_weights = lax.optimization_barrier((got, got_weights))
+    got, got_weights, local_in, local_out = lax.optimization_barrier((got, got_weights, local_in, local_out))
+    if is_packed:
+        kept_shapes = [shape((block_width, half), bf16) for half in halves]
+        kept_shapes += [shape((half, block_width), bf16) for half in halves]
+        cuts = call(
+            functools.partial(keep_kernel, bounds), PACK_MIB, kept_shapes, local_in, local_out,
+            scratch=[pltpu.SemaphoreType.DMA((6,))], whole=(0, 1),
+        )
     got = got.reshape(places // GROUP, GROUP, part_cap, 2 * block_width).transpose(1, 0, 2, 3)
     got = got.reshape(GROUP, -1, 2 * block_width)
 
@@ -553,11 +565,12 @@
         arrays = [value for group in groups for value in group]
         return [pltpu.VMEM(value.shape, value.dtype) for value in arrays] + [pltpu.SemaphoreType.DMA((len(arrays),))]
 
-    def totals(values):
+    def totals(values, others):
         values = values + swap(values, 1) + swap(values, 2) + swap(values, 3)
+        values, others = lax.optimization_barrier((values, others))
         if lax.axis_size("ffn") > 2:
             values = values + swap(values, 4)
-            return values, ffn_total(values)
+            return values, ffn_total(values), others
         ends = [(e, f) for e in range(places) for f in range(2)]
 
         def other(expert_mask, ffn_mask):
@@ -565,10 +578,10 @@
             return lax.ppermute(values, ("expert", "ffn"), moves)
 
         cube = values + swap(values, 4)
-        return cube, cube + (other(0, 1) + other(4, 1))
+        return cube, cube + (other(0, 1) + other(4, 1)), others
 
     stats, got_out = lax.optimization_barrier((stats, got_out))
-    group_sums, whole_sums = totals(stats)
+    group_sums, whole_sums, got_out = totals(stats, got_out)
     in_sent, whole_sums = lax.optimization_barrier((in_sent, whole_sums))
     got_in = along_axes(in_sent)
     factors, norms = call(
@@ -577,8 +590,7 @@
         prev, group_sums, whole_sums, *in_own, *in_sent, *out_own, *out_sent,
         scratch=fetched(in_own, in_sent, out_own, out_sent), whole=range(3, 15),
     )
-    norms, got_in = lax.optimization_barrier((norms, got_in))
-    norms = totals(norms)[1]
+    norms, got_in = totals(norms, got_in)[1:]
     update_in, update_out = call(
         functools.partial(final_kernel, bounds), 52,
         [shape(local_in.shape, bf16), shape(local_out.shape, bf16)],

time: 250 us -> 251 us (level)
  Pallas kernels: 42.7 us -> 47.9 us
  starting transfers between devices: 56.9 us -> 53.3 us
    pallas_call x16 -> x17, Pallas kernels: 42.7 us -> 47.9 us  [call(): pl.pallas_call(kernel, out_shape=out_shape, in_specs=[spec(value, n, stre...]
    unnamed x76 -> x58, local copies, waits for them, and re-layouts: 11.9 us -> 9.23 us
  transfers between devices with their start and end apart: 51 -> 51, of which waited for: 32 -> 29; matrix products, arithmetic and copies ran while one was open for 0% -> 0% of each run, Pallas kernels for 11% -> 13%
where the time goes in v9:
time: 251 us
  waiting for transfers between devices  134 us (53%)
  starting transfers between devices  53.3 us (21%)
  Pallas kernels  47.9 us (19%)
  local copies, waits for them, and re-layouts  12.7 us (5%)
    ppermute x46, waiting for transfers between devices, swap(): return lax.ppermute(value, axis, pairs)  128 us
    pallas_call x17, Pallas kernels, call(): pl.pallas_call(kernel, out_shape=out_shape, in_specs=[spec(value, n, stre...  47.9 us
    ppermute x46, starting transfers between devices, swap(): return lax.ppermute(value, axis, pairs)  35.2 us
    ppermute x4, starting transfers between devices, other(): return lax.ppermute(values, ('expert', 'ffn'), moves)  10.6 us
    unnamed x58, local copies, waits for them, and re-layouts  9.23 us
    all_to_all x1, starting transfers between devices, shards(): lax.all_to_all(routed, 'expert', split_axis=0, concat_axis=0, tiled=True)  7.45 us
    ppermute x4, waiting for transfers between devices, other(): return lax.ppermute(values, ('expert', 'ffn'), moves)  6.19 us
  transfers between devices with their start and end apart: 51, of which 29 were waited for; matrix products, arithmetic and copies ran while one was open for 0% of the time, Pallas kernels for 13%

profile of v9, /device:TPU:1, one launch (start us, length us, event | category | flops | bytes accessed | tf_op | source)
XLA Modules:
  0.0 250.6 jit_solution(12193147903696792365)
XLA Ops:
  1.4 1.2 copy-done.14
  2.7 1.2 copy-done.15
  5.9 7.5 %all-to-all-start = ((bf16[16,40,1024]{2,1,0:T(8,128)(2,1)}), bf16[16,40,1024]{2,1,0:T(8,128)(2,1)}, u32[]{:S(2)}, u32[]{:S(2)}) async-start(bf16[16,40,1024]{2,1,0:T(8,128)(2,1)} %bitcast.21), calls=%async_computation | async-start | bytes 2621440 | tf_op jit(solution)/shard_map/all_to_all | solution.py:468
  13.3 1.7 copy-done.5
  15.8 1.4 collective-permute-start
  19.5 26.7 %collective-permute-done.1.refs_9_.refs_12_ = bf16[3072,128]{1,0:T(8,128)(2,1)S(1)} collective-permute-done((bf16[3072,128]{1,0:T(8,128)(2,1)S(1)}, bf16[3072,128]{1,0:T(8,128)(2,1)S(1)}, u32[]{:S(2)}, u32[]{:S(2)}) %collective-permute-start.1) | collective-permute-done | bytes 786464 | tf_op jit(solution)/shard_map/ppermute | solution.py:29
  46.2 6.7 %collective-permute-done.2.refs_10_.refs_13_ = bf16[3072,128]{1,0:T(8,128)(2,1)S(1)} collective-permute-done((bf16[3072,128]{1,0:T(8,128)(2,1)S(1)}, bf16[3072,128]{1,0:T(8,128)(2,1)S(1)}, u32[]{:S(2)}, u32[]{:S(2)}) %collective-permute-start.2) | collective-permute-done | bytes 786464 | tf_op jit(solution)/shard_map/ppermute | solution.py:29
  53.0 2.5 copy.11
  56.6 1.6 collective-permute-start.4
  58.2 26.3 %collective-permute-done.3 = bf16[8,80,1024]{2,1,0:T(8,128)(2,1)S(1)} collective-permute-done((bf16[8,80,1024]{2,1,0:T(8,128)(2,1)}, bf16[8,80,1024]{2,1,0:T(8,128)(2,1)S(1)}, u32[]{:S(2)}, u32[]{:S(2)}) %collective-permute-start.3) | collective-permute-done | bytes 1310752 | tf_op jit(solution)/shard_map/ppermute | solution.py:29
  87.1 3.1 %collective-permute-start.7 = (bf16[3,8,80,1024]{3,2,1,0:T(8,128)(2,1)S(1)}, bf16[3,8,80,1024]{3,2,1,0:T(8,128)(2,1)S(1)}, u32[]{:S(2)}, u32[]{:S(2)}) collective-permute-start(bf16[3,8,80,1024]{3,2,1,0:T(8,128)(2,1)S(1)} %pad_maximum_fusion.refs_1_), channel_id=1, source_target_pairs={{0,1},{1,0},{2,3},{3,2},{4,5},{5,4},{6,7},{7,6},{8,9},{9,8},{10,11... | collective-permute-start | bytes 11796488 | tf_op jit(solution)/shard_map/ppermute | solution.py:29
  91.3 3.5 %shard_map.89 = (bf16[320,768]{1,0:T(8,128)(2,1)S(1)}, bf16[320,896]{1,0:T(8,128)(2,1)S(1)}, bf16[320,896]{1,0:T(8,128)(2,1)S(1)}) custom-call(bf16[8,80,1024]{2,1,0:T(8,128)(2,1)} %bitcast.5.refs_0_, bf16[3,8,80,1024]{3,2,1,0:T(8,128)(2,1)S(1)} %pad_maximum_fusion.refs_1_, bf16[512,512]{1,0:T(8,128)(2,1)S(1)} %get-tuple-element.124.refs_2_, ...), custom_call_target="tpu_custom_call" | custom-call | tf_op jit(solution)/shard_map/pallas_call | solution.py:75
  95.7 3.0 %collective-permute-done.6.refs_0_.refs_2_ = bf16[8,80,1024]{2,1,0:T(8,128)(2,1)} collective-permute-done((bf16[8,80,1024]{2,1,0:T(8,128)(2,1)}, bf16[8,80,1024]{2,1,0:T(8,128)(2,1)}, u32[]{:S(2)}, u32[]{:S(2)}) %collective-permute-start.6) | collective-permute-done | bytes 1310752 | tf_op jit(solution)/shard_map/ppermute | solution.py:29
  98.7 4.5 %shard_map.90 = (bf16[320,768]{1,0:T(8,128)(2,1)S(1)}, bf16[320,896]{1,0:T(8,128)(2,1)S(1)}, bf16[320,896]{1,0:T(8,128)(2,1)S(1)}) custom-call(bf16[8,80,1024]{2,1,0:T(8,128)(2,1)} %collective-permute-done.6.refs_0_.refs_2_, bf16[3,8,80,1024]{3,2,1,0:T(8,128)(2,1)S(1)} %collective-permute-done.7.refs_1_.refs_3_, ...), custom_call_target="tpu_custom_call" | custom-call | tf_op jit(solution)/shard_map/pallas_call | solution.py:75
  103.1 3.5 %shard_map.92 = (f32[320,512]{1,0:T(8,128)S(1)}, f32[320,384]{1,0:T(8,128)S(1)}, f32[320,384]{1,0:T(8,128)S(1)}, f32[320,512]{1,0:T(8,128)S(1)}, f32[320,384]{1,0:T(8,128)S(1)}, /*index=5*/f32[320,384]{1,0:T(8,128)S(1)}) custom-call(bf16[8,80,1024]{2,1,0:T(8,128)(2,1)} %collective-permute-done.6.refs_0_.refs_2_, ...), custom_call_target="tpu_custom_call" | custom-call | tf_op jit(solution)/shard_map/pallas_call | solution.py:75
  106.7 3.5 %shard_map.91 = (f32[320,512]{1,0:T(8,128)S(1)}, f32[320,384]{1,0:T(8,128)S(1)}, f32[320,384]{1,0:T(8,128)S(1)}, f32[320,512]{1,0:T(8,128)S(1)}, f32[320,384]{1,0:T(8,128)S(1)}, /*index=5*/f32[320,384]{1,0:T(8,128)S(1)}) custom-call(bf16[8,80,1024]{2,1,0:T(8,128)(2,1)} %bitcast.5.refs_0_, bf16[3,8,80,1024]{3,2,1,0:T(8,128)(2,1)S(1)} %pad_maximum_fusion.refs_1_, ...), custom_call_target="tpu_custom_call" | custom-call | tf_op jit(solution)/shard_map/pallas_call | solution.py:75
  112.1 1.4 collective-permute-start.12
  113.5 3.9 %collective-permute-done.11.refs_6_ = bf16[160,768]{1,0:T(8,128)(2,1)S(1)} collective-permute-done((bf16[160,768]{1,0:T(8,128)(2,1)S(1)}, bf16[160,768]{1,0:T(8,128)(2,1)S(1)}, u32[]{:S(2)}, u32[]{:S(2)}) %collective-permute-start.11) | collective-permute-done | bytes 245792 | tf_op jit(solution)/shard_map/ppermute | solution.py:29
  117.4 14.0 %collective-permute-done.12.refs_7_ = bf16[160,896]{1,0:T(8,128)(2,1)S(1)} collective-permute-done((bf16[160,896]{1,0:T(8,128)(2,1)S(1)}, bf16[160,896]{1,0:T(8,128)(2,1)S(1)}, u32[]{:S(2)}, u32[]{:S(2)}) %collective-permute-start.12) | collective-permute-done | bytes 286752 | tf_op jit(solution)/shard_map/ppermute | solution.py:29
  132.2 1.2 collective-permute-start.15
  134.1 1.4 collective-permute-start.23
  135.6 1.7 collective-permute-done.14.refs_3_
  138.1 1.2 collective-permute-done.16.refs_5_
  139.4 1.5 collective-permute-start.17
  140.9 1.9 collective-permute-done.21.refs_6_
  142.8 1.2 collective-permute-done.22.refs_7_
  146.0 1.7 collective-permute-start.24
  148.7 8.8 %collective-permute-done.24.refs_3_ = bf16[160,768]{1,0:T(8,128)(2,1)S(1)} collective-permute-done((bf16[160,768]{1,0:T(8,128)(2,1)S(1)}, bf16[160,768]{1,0:T(8,128)(2,1)S(1)}, u32[]{:S(2)}, u32[]{:S(2)}) %collective-permute-start.24) | collective-permute-done | bytes 245792 | tf_op jit(solution)/shard_map/ppermute | solution.py:29
  157.7 1.2 collective-permute-start.29
  158.9 1.5 collective-permute-start.31
  161.1 6.7 %collective-permute-done.30.refs_13_ = bf16[320,896]{1,0:T(8,128)(2,1)S(1)} collective-permute-done((bf16[320,896]{1,0:T(8,128)(2,1)S(1)}, bf16[320,896]{1,0:T(8,128)(2,1)S(1)}, u32[]{:S(2)}, u32[]{:S(2)}) %collective-permute-start.30) | collective-permute-done | bytes 573472 | tf_op jit(solution)/shard_map/ppermute | solution.py:29
  168.4 5.0 %collective-permute-done.29.refs_11_ = bf16[320,896]{1,0:T(8,128)(2,1)S(1)} collective-permute-done((bf16[320,896]{1,0:T(8,128)(2,1)S(1)}, bf16[320,896]{1,0:T(8,128)(2,1)S(1)}, u32[]{:S(2)}, u32[]{:S(2)}) %collective-permute-start.29) | collective-permute-done | bytes 573472 | tf_op jit(solution)/shard_map/ppermute | solution.py:29
  173.4 6.7 %collective-permute-done.31.refs_15_ = bf16[320,896]{1,0:T(8,128)(2,1)S(1)} collective-permute-done((bf16[320,896]{1,0:T(8,128)(2,1)S(1)}, bf16[320,896]{1,0:T(8,128)(2,1)S(1)}, u32[]{:S(2)}, u32[]{:S(2)}) %collective-permute-start.31) | collective-permute-done | bytes 573472 | tf_op jit(solution)/shard_map/ppermute | solution.py:29
  181.0 7.9 %shard_map.99 = (f32[512,512]{1,0:T(8,128)}, f32[384,512]{1,0:T(8,128)}, f32[384,512]{1,0:T(8,128)}, bf16[512,512]{1,0:T(8,128)(2,1)}, bf16[384,512]{1,0:T(8,128...) custom-call(bf16[8,80,1024]{2,1,0:T(8,128)(2,1)} %bitcast.5.refs_0_, bf16[3,8,80,1024]{3,2,1,0:T(8,128)(2,1)} %copy-done.1, ...), custom_call_target="tpu_custom_call" | custom-call | tf_op jit(solution)/shard_map/pallas_call | solution.py:75
  190.6 10.0 %shard_map.100 = (f32[512,512]{1,0:T(8,128)}, f32[512,384]{1,0:T(8,128)}, f32[512,384]{1,0:T(8,128)}, bf16[512,512]{1,0:T(8,128)(2,1)}, bf16[512,384]{1,0:T(8,12...) custom-call(bf16[8,80,1024]{2,1,0:T(8,128)(2,1)} %bitcast.5.refs_0_, bf16[3,8,80,1024]{3,2,1,0:T(8,128)(2,1)} %copy-done.1, ...), custom_call_target="tpu_custom_call" | custom-call | tf_op jit(solution)/shard_map/pallas_call | solution.py:75
  200.6 1.5 collective-permute-start.35
  204.0 1.4 collective-permute-done.36
  205.4 1.4 collective-permute-done.37
  207.7 1.5 collective-permute-start.38
  209.2 7.9 %collective-permute-start.39 = (f32[32,512]{1,0:T(8,128)S(1)}, f32[32,512]{1,0:T(8,128)S(1)}, u32[]{:S(2)}, u32[]{:S(2)}) collective-permute-start(f32[32,512]{1,0:T(8,128)S(1)} %add_add_fusion.1), channel_id=1, source_target_pairs={{0,1},{1,0},{2,3},{3,2},{4,5},{5,4},{6,7},{7,6},{8,9},{9,8},{10,11... | collective-permute-start | bytes 196616 | tf_op jit(solution)/shard_map/ppermute | solution.py:578
  218.1 2.8 %collective-permute-done.40 = f32[32,512]{1,0:T(8,128)S(1)} collective-permute-done((f32[32,512]{1,0:T(8,128)S(1)}, f32[32,512]{1,0:T(8,128)S(1)}, u32[]{:S(2)}, u32[]{:S(2)}) %collective-permute-start.40) | collective-permute-done | bytes 65568 | tf_op jit(solution)/shard_map/ppermute | solution.py:578
  225.5 4.4 %shard_map.101 = (f32[32,512]{1,0:T(8,128)S(1)}, f32[8,128]{1,0:T(8,128)S(1)}) custom-call(f32[32,512]{1,0:T(8,128)S(1)} %concatenate.3.prev, f32[32,512]{1,0:T(8,128)S(1)} %get-tuple-element.241.group_sums, f32[32,512]{1,0:T(8,128)S(1)} %get-tuple-element.213.whole_sums, f32[512,512]{1,0:T(8,128)} %get-tuple-element.214.refs_0_, ...), custom_call_target="tpu_custom_call" | custom-call | tf_op jit(solution)/shard_map/pallas_call | solution.py:75
  230.0 1.5 collective-permute-start.41
  231.8 3.1 %collective-permute-done.41 = f32[8,128]{1,0:T(8,128)S(1)} collective-permute-done((f32[8,128]{1,0:T(8,128)S(1)}, f32[8,128]{1,0:T(8,128)S(1)}, u32[]{:S(2)}, u32[]{:S(2)}) %collective-permute-start.41) | collective-permute-done | bytes 4128 | tf_op jit(solution)/shard_map/ppermute | solution.py:29
  235.8 2.4 collective-permute-done.43
  239.2 2.2 collective-permute-start.48
  242.2 2.2 collective-permute-done.49
  244.4 6.0 %shard_map.102 = (bf16[512,2560]{1,0:T(8,128)(2,1)}, bf16[2560,512]{1,0:T(8,128)(2,1)}) custom-call(f32[32,512]{1,0:T(8,128)S(1)} %concatenate.3.prev, f32[32,512]{1,0:T(8,128)S(1)} %get-tuple-element.223.factors, f32[32,512]{1,0:T(8,128)S(1)} %get-tuple-element.213.whole_sums, f32[8,128]{1,0:T(8,128)S(1)} %add_add_fusion.2.norms, ...), custom_call_target="tpu_custom_call" | custom-call | tf_op jit(solution)/shard_map/pallas_call | solution.py:75
  (153 shorter events, 34.0 us)
Async XLA Ops:
  5.9 47.1 %all-to-all-start = ((bf16[16,40,1024]{2,1,0:T(8,128)(2,1)}), bf16[16,40,1024]{2,1,0:T(8,128)(2,1)}, u32[]{:S(2)}, u32[]{:S(2)}) async-start(bf16[16,40,1024]{2,1,0:T(8,128)(2,1)} %bitcast.21), calls=%async_computation | async-start | bytes 2621440 | tf_op jit(solution)/shard_map/all_to_all | solution.py:468
  15.8 37.2 %collective-permute-start = (bf16[4096,128]{1,0:T(8,128)(2,1)S(1)}, bf16[4096,128]{1,0:T(8,128)(2,1)S(1)}, u32[]{:S(2)}, u32[]{:S(2)}) collective-permute-start(bf16[4096,128]{1,0:T(8,128)(2,1)S(1)} %get-tuple-element.118), channel_id=1, source_target_pairs={{0,2},{2,0},{4,6},{6,4},{8,10},{10,8},{12,14},{14,12},{16,18},{18,... | collective-permute-start | bytes 3145736 | tf_op jit(solution)/shard_map/ppermute | solution.py:29
  17.2 29.1 %collective-permute-start.1 = (bf16[3072,128]{1,0:T(8,128)(2,1)S(1)}, bf16[3072,128]{1,0:T(8,128)(2,1)S(1)}, u32[]{:S(2)}, u32[]{:S(2)}) collective-permute-start(bf16[3072,128]{1,0:T(8,128)(2,1)S(1)} %get-tuple-element.119), channel_id=1, source_target_pairs={{0,4},{2,6},{4,0},{6,2},{8,12},{10,14},{12,8},{14,10},{16,20},{18,... | collective-permute-start | bytes 2359304 | tf_op jit(solution)/shard_map/ppermute | solution.py:29
  18.4 34.6 %collective-permute-start.2 = (bf16[3072,128]{1,0:T(8,128)(2,1)S(1)}, bf16[3072,128]{1,0:T(8,128)(2,1)S(1)}, u32[]{:S(2)}, u32[]{:S(2)}) collective-permute-start(bf16[3072,128]{1,0:T(8,128)(2,1)S(1)} %get-tuple-element.120), channel_id=1, source_target_pairs={{0,8},{2,10},{4,12},{6,14},{8,0},{10,2},{12,4},{14,6},{16,24},{18,... | collective-permute-start | bytes 2359304 | tf_op jit(solution)/shard_map/ppermute | solution.py:29
  55.5 29.0 %collective-permute-start.3 = (bf16[8,80,1024]{2,1,0:T(8,128)(2,1)}, bf16[8,80,1024]{2,1,0:T(8,128)(2,1)S(1)}, u32[]{:S(2)}, u32[]{:S(2)}) collective-permute-start(bf16[8,80,1024]{2,1,0:T(8,128)(2,1)} %bitcast.5.refs_0_), channel_id=1, source_target_pairs={{0,2},{2,0},{4,6},{6,4},{8,10},{10,8},{12,14},{14,12},{16,18},{18,... | collective-permute-start | bytes 3932168 | tf_op jit(solution)/shard_map/ppermute | solution.py:29
  56.6 29.0 %collective-permute-start.4 = (bf16[8,80,1024]{2,1,0:T(8,128)(2,1)}, bf16[8,80,1024]{2,1,0:T(8,128)(2,1)S(1)}, u32[]{:S(2)}, u32[]{:S(2)}) collective-permute-start(bf16[8,80,1024]{2,1,0:T(8,128)(2,1)} %bitcast.5.refs_0_), channel_id=1, source_target_pairs={{0,4},{2,6},{4,0},{6,2},{8,12},{10,14},{12,8},{14,10},{16,20},{18,... | collective-permute-start | bytes 3932168 | tf_op jit(solution)/shard_map/ppermute | solution.py:29
  58.2 28.4 %collective-permute-start.5 = (bf16[8,80,1024]{2,1,0:T(8,128)(2,1)}, bf16[8,80,1024]{2,1,0:T(8,128)(2,1)S(1)}, u32[]{:S(2)}, u32[]{:S(2)}) collective-permute-start(bf16[8,80,1024]{2,1,0:T(8,128)(2,1)} %bitcast.5.refs_0_), channel_id=1, source_target_pairs={{0,8},{2,10},{4,12},{6,14},{8,0},{10,2},{12,4},{14,6},{16,24},{18,... | collective-permute-start | bytes 3932168 | tf_op jit(solution)/shard_map/ppermute | solution.py:29
  87.1 11.6 %collective-permute-start.7 = (bf16[3,8,80,1024]{3,2,1,0:T(8,128)(2,1)S(1)}, bf16[3,8,80,1024]{3,2,1,0:T(8,128)(2,1)S(1)}, u32[]{:S(2)}, u32[]{:S(2)}) collective-permute-start(bf16[3,8,80,1024]{3,2,1,0:T(8,128)(2,1)S(1)} %pad_maximum_fusion.refs_1_), channel_id=1, source_target_pairs={{0,1},{1,0},{2,3},{3,2},{4,5},{5,4},{6,7},{7,6},{8,9},{9,8},{10,11... | collective-permute-start | bytes 11796488 | tf_op jit(solution)/shard_map/ppermute | solution.py:29
  90.2 8.5 %collective-permute-start.6 = (bf16[8,80,1024]{2,1,0:T(8,128)(2,1)}, bf16[8,80,1024]{2,1,0:T(8,128)(2,1)}, u32[]{:S(2)}, u32[]{:S(2)}) collective-permute-start(bf16[8,80,1024]{2,1,0:T(8,128)(2,1)} %bitcast.5.refs_0_), channel_id=1, source_target_pairs={{0,1},{1,0},{2,3},{3,2},{4,5},{5,4},{6,7},{7,6},{8,9},{9,8},{10,11... | collective-permute-start | bytes 3932168 | tf_op jit(solution)/shard_map/ppermute | solution.py:29
  94.9 15.4 %collective-permute-start.10 = (bf16[320,896]{1,0:T(8,128)(2,1)S(1)}, bf16[320,896]{1,0:T(8,128)(2,1)S(1)}, u32[]{:S(2)}, u32[]{:S(2)}) collective-permute-start(bf16[320,896]{1,0:T(8,128)(2,1)S(1)} %get-tuple-element.138), channel_id=1, source_target_pairs={{0,8},{2,10},{4,12},{6,14},{8,0},{10,2},{12,4},{14,6},{16,24},{18,... | collective-permute-start | bytes 1720328 | tf_op jit(solution)/shard_map/ppermute | solution.py:29
  95.1 15.1 %collective-permute-start.9 = (bf16[320,896]{1,0:T(8,128)(2,1)S(1)}, bf16[320,896]{1,0:T(8,128)(2,1)S(1)}, u32[]{:S(2)}, u32[]{:S(2)}) collective-permute-start(bf16[320,896]{1,0:T(8,128)(2,1)S(1)} %get-tuple-element.137), channel_id=1, source_target_pairs={{0,4},{2,6},{4,0},{6,2},{8,12},{10,14},{12,8},{14,10},{16,20},{18,... | collective-permute-start | bytes 1720328 | tf_op jit(solution)/shard_map/ppermute | solution.py:29
  95.3 14.9 %collective-permute-start.8 = (bf16[320,768]{1,0:T(8,128)(2,1)S(1)}, bf16[320,768]{1,0:T(8,128)(2,1)S(1)}, u32[]{:S(2)}, u32[]{:S(2)}) collective-permute-start(bf16[320,768]{1,0:T(8,128)(2,1)S(1)} %get-tuple-element.136), channel_id=1, source_target_pairs={{0,2},{2,0},{4,6},{6,4},{8,10},{10,8},{12,14},{14,12},{16,18},{18,... | collective-permute-start | bytes 1474568 | tf_op jit(solution)/shard_map/ppermute | solution.py:29
  110.5 6.9 %collective-permute-start.11 = (bf16[160,768]{1,0:T(8,128)(2,1)S(1)}, bf16[160,768]{1,0:T(8,128)(2,1)S(1)}, u32[]{:S(2)}, u32[]{:S(2)}) collective-permute-start(bf16[160,768]{1,0:T(8,128)(2,1)S(1)} %get-tuple-element.170), channel_id=1, source_target_pairs={{0,2},{2,0},{4,6},{6,4},{8,10},{10,8},{12,14},{14,12},{16,18},{18,... | collective-permute-start | bytes 737288 | tf_op jit(solution)/shard_map/ppermute | solution.py:29
  111.0 22.5 %collective-permute-start.18 = (bf16[320,768]{1,0:T(8,128)(2,1)S(1)}, bf16[320,768]{1,0:T(8,128)(2,1)S(1)}, u32[]{:S(2)}, u32[]{:S(2)}) collective-permute-start(bf16[320,768]{1,0:T(8,128)(2,1)S(1)} %get-tuple-element.139), channel_id=1, source_target_pairs={{0,2},{2,0},{4,6},{6,4},{8,10},{10,8},{12,14},{14,12},{16,18},{18,... | collective-permute-start | bytes 1474568 | tf_op jit(solution)/shard_map/ppermute | solution.py:29
  112.0 21.5 %collective-permute-start.19 = (bf16[320,896]{1,0:T(8,128)(2,1)S(1)}, bf16[320,896]{1,0:T(8,128)(2,1)S(1)}, u32[]{:S(2)}, u32[]{:S(2)}) collective-permute-start(bf16[320,896]{1,0:T(8,128)(2,1)S(1)} %get-tuple-element.140), channel_id=1, source_target_pairs={{0,4},{2,6},{4,0},{6,2},{8,12},{10,14},{12,8},{14,10},{16,20},{18,... | collective-permute-start | bytes 1720328 | tf_op jit(solution)/shard_map/ppermute | solution.py:29
  112.1 21.5 %collective-permute-start.20 = (bf16[320,896]{1,0:T(8,128)(2,1)S(1)}, bf16[320,896]{1,0:T(8,128)(2,1)S(1)}, u32[]{:S(2)}, u32[]{:S(2)}) collective-permute-start(bf16[320,896]{1,0:T(8,128)(2,1)S(1)} %get-tuple-element.141), channel_id=1, source_target_pairs={{0,8},{2,10},{4,12},{6,14},{8,0},{10,2},{12,4},{14,6},{16,24},{18,... | collective-permute-start | bytes 1720328 | tf_op jit(solution)/shard_map/ppermute | solution.py:29
  112.1 19.3 %collective-permute-start.12 = (bf16[160,896]{1,0:T(8,128)(2,1)S(1)}, bf16[160,896]{1,0:T(8,128)(2,1)S(1)}, u32[]{:S(2)}, u32[]{:S(2)}) collective-permute-start(bf16[160,896]{1,0:T(8,128)(2,1)S(1)} %get-tuple-element.171), channel_id=1, source_target_pairs={{0,4},{2,6},{4,0},{6,2},{8,12},{10,14},{12,8},{14,10},{16,20},{18,... | collective-permute-start | bytes 860168 | tf_op jit(solution)/shard_map/ppermute | solution.py:29
  117.4 14.0 %collective-permute-start.13 = (bf16[160,896]{1,0:T(8,128)(2,1)S(1)}, bf16[160,896]{1,0:T(8,128)(2,1)S(1)}, u32[]{:S(2)}, u32[]{:S(2)}) collective-permute-start(bf16[160,896]{1,0:T(8,128)(2,1)S(1)} %get-tuple-element.172), channel_id=1, source_target_pairs={{0,8},{2,10},{4,12},{6,14},{8,0},{10,2},{12,4},{14,6},{16,24},{18,... | collective-permute-start | bytes 860168 | tf_op jit(solution)/shard_map/ppermute | solution.py:29
  132.2 5.1 %collective-permute-start.14 = (bf16[160,768]{1,0:T(8,128)(2,1)S(1)}, bf16[160,768]{1,0:T(8,128)(2,1)S(1)}, u32[]{:S(2)}, u32[]{:S(2)}) collective-permute-start(bf16[160,768]{1,0:T(8,128)(2,1)S(1)} %get-tuple-element.173.refs_0_), channel_id=1, source_target_pairs={{0,2},{2,0},{4,6},{6,4},{8,10},{10,8},{12,14},{14,12},{16,18},{18,... | collective-permute-start | bytes 737288 | tf_op jit(solution)/shard_map/ppermute | solution.py:29
  132.2 5.8 %collective-permute-start.15 = (bf16[160,896]{1,0:T(8,128)(2,1)S(1)}, bf16[160,896]{1,0:T(8,128)(2,1)S(1)}, u32[]{:S(2)}, u32[]{:S(2)}) collective-permute-start(bf16[160,896]{1,0:T(8,128)(2,1)S(1)} %get-tuple-element.174.refs_1_), channel_id=1, source_target_pairs={{0,4},{2,6},{4,0},{6,2},{8,12},{10,14},{12,8},{14,10},{16,20},{18,... | collective-permute-start | bytes 860168 | tf_op jit(solution)/shard_map/ppermute | solution.py:29
  133.5 5.8 %collective-permute-start.16 = (bf16[160,896]{1,0:T(8,128)(2,1)S(1)}, bf16[160,896]{1,0:T(8,128)(2,1)S(1)}, u32[]{:S(2)}, u32[]{:S(2)}) collective-permute-start(bf16[160,896]{1,0:T(8,128)(2,1)S(1)} %get-tuple-element.175.refs_2_), channel_id=1, source_target_pairs={{0,8},{2,10},{4,12},{6,14},{8,0},{10,2},{12,4},{14,6},{16,24},{18,... | collective-permute-start | bytes 860168 | tf_op jit(solution)/shard_map/ppermute | solution.py:29
  133.8 10.2 %collective-permute-start.22 = (bf16[160,896]{1,0:T(8,128)(2,1)S(1)}, bf16[160,896]{1,0:T(8,128)(2,1)S(1)}, u32[]{:S(2)}, u32[]{:S(2)}) collective-permute-start(bf16[160,896]{1,0:T(8,128)(2,1)S(1)} %get-tuple-element.190), channel_id=1, source_target_pairs={{0,4},{2,6},{4,0},{6,2},{8,12},{10,14},{12,8},{14,10},{16,20},{18,... | collective-permute-start | bytes 860168 | tf_op jit(solution)/shard_map/ppermute | solution.py:29
  134.1 10.5 %collective-permute-start.23 = (bf16[160,896]{1,0:T(8,128)(2,1)S(1)}, bf16[160,896]{1,0:T(8,128)(2,1)S(1)}, u32[]{:S(2)}, u32[]{:S(2)}) collective-permute-start(bf16[160,896]{1,0:T(8,128)(2,1)S(1)} %get-tuple-element.191), channel_id=1, source_target_pairs={{0,8},{2,10},{4,12},{6,14},{8,0},{10,2},{12,4},{14,6},{16,24},{18,... | collective-permute-start | bytes 860168 | tf_op jit(solution)/shard_map/ppermute | solution.py:29
  137.3 5.6 %collective-permute-start.21 = (bf16[160,768]{1,0:T(8,128)(2,1)S(1)}, bf16[160,768]{1,0:T(8,128)(2,1)S(1)}, u32[]{:S(2)}, u32[]{:S(2)}) collective-permute-start(bf16[160,768]{1,0:T(8,128)(2,1)S(1)} %get-tuple-element.189), channel_id=1, source_target_pairs={{0,2},{2,0},{4,6},{6,4},{8,10},{10,8},{12,14},{14,12},{16,18},{18,... | collective-permute-start | bytes 737288 | tf_op jit(solution)/shard_map/ppermute | solution.py:29
  139.4 20.9 %collective-permute-start.17 = (bf16[320,768]{1,0:T(8,128)(2,1)S(1)}, bf16[320,768]{1,0:T(8,128)(2,1)S(1)}, u32[]{:S(2)}, u32[]{:S(2)}) collective-permute-start(bf16[320,768]{1,0:T(8,128)(2,1)S(1)} %get-tuple-element.176.refs_4_), channel_id=1, source_target_pairs={{0,2},{2,0},{4,6},{6,4},{8,10},{10,8},{12,14},{14,12},{16,18},{18,... | collective-permute-start | bytes 1474568 | tf_op jit(solution)/shard_map/ppermute | solution.py:29
  145.4 12.1 %collective-permute-start.25 = (bf16[160,896]{1,0:T(8,128)(2,1)S(1)}, bf16[160,896]{1,0:T(8,128)(2,1)S(1)}, u32[]{:S(2)}, u32[]{:S(2)}) collective-permute-start(bf16[160,896]{1,0:T(8,128)(2,1)S(1)} %get-tuple-element.193.refs_1_), channel_id=1, source_target_pairs={{0,4},{2,6},{4,0},{6,2},{8,12},{10,14},{12,8},{14,10},{16,20},{18,... | collective-permute-start | bytes 860168 | tf_op jit(solution)/shard_map/ppermute | solution.py:29
  146.0 11.5 %collective-permute-start.26 = (bf16[160,896]{1,0:T(8,128)(2,1)S(1)}, bf16[160,896]{1,0:T(8,128)(2,1)S(1)}, u32[]{:S(2)}, u32[]{:S(2)}) collective-permute-start(bf16[160,896]{1,0:T(8,128)(2,1)S(1)} %get-tuple-element.194.refs_2_), channel_id=1, source_target_pairs={{0,8},{2,10},{4,12},{6,14},{8,0},{10,2},{12,4},{14,6},{16,24},{18,... | collective-permute-start | bytes 860168 | tf_op jit(solution)/shard_map/ppermute | solution.py:29
  146.0 11.5 %collective-permute-start.24 = (bf16[160,768]{1,0:T(8,128)(2,1)S(1)}, bf16[160,768]{1,0:T(8,128)(2,1)S(1)}, u32[]{:S(2)}, u32[]{:S(2)}) collective-permute-start(bf16[160,768]{1,0:T(8,128)(2,1)S(1)} %get-tuple-element.192.refs_0_), channel_id=1, source_target_pairs={{0,2},{2,0},{4,6},{6,4},{8,10},{10,8},{12,14},{14,12},{16,18},{18,... | collective-permute-start | bytes 737288 | tf_op jit(solution)/shard_map/ppermute | solution.py:29
  147.7 13.4 %collective-permute-start.28 = (bf16[320,896]{1,0:T(8,128)(2,1)S(1)}, bf16[320,896]{1,0:T(8,128)(2,1)S(1)}, u32[]{:S(2)}, u32[]{:S(2)}) collective-permute-start(bf16[320,896]{1,0:T(8,128)(2,1)S(1)} %get-tuple-element.196.refs_8_), channel_id=1, source_target_pairs={{0,4},{2,6},{4,0},{6,2},{8,12},{10,14},{12,8},{14,10},{16,20},{18,... | collective-permute-start | bytes 1720328 | tf_op jit(solution)/shard_map/ppermute | solution.py:29
  157.5 10.3 %collective-permute-start.30 = (bf16[320,896]{1,0:T(8,128)(2,1)S(1)}, bf16[320,896]{1,0:T(8,128)(2,1)S(1)}, u32[]{:S(2)}, u32[]{:S(2)}) collective-permute-start(bf16[320,896]{1,0:T(8,128)(2,1)S(1)} %get-tuple-element.198.refs_12_), channel_id=1, source_target_pairs={{0,8},{2,10},{4,12},{6,14},{8,0},{10,2},{12,4},{14,6},{16,24},{18,... | collective-permute-start | bytes 1720328 | tf_op jit(solution)/shard_map/ppermute | solution.py:29
  157.7 15.7 %collective-permute-start.29 = (bf16[320,896]{1,0:T(8,128)(2,1)S(1)}, bf16[320,896]{1,0:T(8,128)(2,1)S(1)}, u32[]{:S(2)}, u32[]{:S(2)}) collective-permute-start(bf16[320,896]{1,0:T(8,128)(2,1)S(1)} %get-tuple-element.197.refs_10_), channel_id=1, source_target_pairs={{0,4},{2,6},{4,0},{6,2},{8,12},{10,14},{12,8},{14,10},{16,20},{18,... | collective-permute-start | bytes 1720328 | tf_op jit(solution)/shard_map/ppermute | solution.py:29
  158.9 21.2 %collective-permute-start.31 = (bf16[320,896]{1,0:T(8,128)(2,1)S(1)}, bf16[320,896]{1,0:T(8,128)(2,1)S(1)}, u32[]{:S(2)}, u32[]{:S(2)}) collective-permute-start(bf16[320,896]{1,0:T(8,128)(2,1)S(1)} %get-tuple-element.199.refs_14_), channel_id=1, source_target_pairs={{0,8},{2,10},{4,12},{6,14},{8,0},{10,2},{12,4},{14,6},{16,24},{18,... | collective-permute-start | bytes 1720328 | tf_op jit(solution)/shard_map/ppermute | solution.py:29
  160.4 8.0 %collective-permute-start.27 = (bf16[320,768]{1,0:T(8,128)(2,1)S(1)}, bf16[320,768]{1,0:T(8,128)(2,1)S(1)}, u32[]{:S(2)}, u32[]{:S(2)}) collective-permute-start(bf16[320,768]{1,0:T(8,128)(2,1)S(1)} %get-tuple-element.195.refs_6_), channel_id=1, source_target_pairs={{0,2},{2,0},{4,6},{6,4},{8,10},{10,8},{12,14},{14,12},{16,18},{18,... | collective-permute-start | bytes 1474568 | tf_op jit(solution)/shard_map/ppermute | solution.py:29
  188.9 11.7 %collective-permute-start.32 = (bf16[512,512]{1,0:T(8,128)(2,1)}, bf16[512,512]{1,0:T(8,128)(2,1)S(1)}, u32[]{:S(2)}, u32[]{:S(2)}) collective-permute-start(bf16[512,512]{1,0:T(8,128)(2,1)} %get-tuple-element.202.refs_9_), channel_id=1, source_target_pairs={{0,2},{2,0},{4,6},{6,4},{8,10},{10,8},{12,14},{14,12},{16,18},{18,... | collective-permute-start | bytes 1572872 | tf_op jit(solution)/shard_map/ppermute | solution.py:29
  189.0 11.6 %collective-permute-start.33 = (bf16[384,512]{1,0:T(8,128)(2,1)}, bf16[384,512]{1,0:T(8,128)(2,1)S(1)}, u32[]{:S(2)}, u32[]{:S(2)}) collective-permute-start(bf16[384,512]{1,0:T(8,128)(2,1)} %get-tuple-element.203.refs_10_), channel_id=1, source_target_pairs={{0,4},{2,6},{4,0},{6,2},{8,12},{10,14},{12,8},{14,10},{16,20},{18,... | collective-permute-start | bytes 1179656 | tf_op jit(solution)/shard_map/ppermute | solution.py:29
  190.0 10.6 %collective-permute-start.34 = (bf16[384,512]{1,0:T(8,128)(2,1)}, bf16[384,512]{1,0:T(8,128)(2,1)S(1)}, u32[]{:S(2)}, u32[]{:S(2)}) collective-permute-start(bf16[384,512]{1,0:T(8,128)(2,1)} %get-tuple-element.204.refs_11_), channel_id=1, source_target_pairs={{0,8},{2,10},{4,12},{6,14},{8,0},{10,2},{12,4},{14,6},{16,24},{18,... | collective-permute-start | bytes 1179656 | tf_op jit(solution)/shard_map/ppermute | solution.py:29
  200.6 3.4 %collective-permute-start.35 = (f32[32,512]{1,0:T(8,128)}, f32[32,512]{1,0:T(8,128)S(1)}, u32[]{:S(2)}, u32[]{:S(2)}) collective-permute-start(f32[32,512]{1,0:T(8,128)} %get-tuple-element.205), channel_id=1, source_target_pairs={{0,2},{2,0},{4,6},{6,4},{8,10},{10,8},{12,14},{14,12},{16,18},{18,... | collective-permute-start | bytes 196616 | tf_op jit(solution)/shard_map/ppermute | solution.py:29
  202.6 4.2 %collective-permute-start.37 = (f32[32,512]{1,0:T(8,128)}, f32[32,512]{1,0:T(8,128)S(1)}, u32[]{:S(2)}, u32[]{:S(2)}) collective-permute-start(f32[32,512]{1,0:T(8,128)} %get-tuple-element.205), channel_id=1, source_target_pairs={{0,6},{2,4},{4,2},{6,0},{8,14},{10,12},{12,10},{14,8},{16,22},{18,... | collective-permute-start | bytes 196616 | tf_op jit(solution)/shard_map/ppermute | solution.py:29
  207.7 9.5 %collective-permute-start.38 = (f32[32,512]{1,0:T(8,128)S(1)}, f32[32,512]{1,0:T(8,128)S(1)}, u32[]{:S(2)}, u32[]{:S(2)}) collective-permute-start(f32[32,512]{1,0:T(8,128)S(1)} %add_add_fusion.1), channel_id=1, source_target_pairs={{0,8},{2,10},{4,12},{6,14},{8,0},{10,2},{12,4},{14,6},{16,24},{18,... | collective-permute-start | bytes 196616 | tf_op jit(solution)/shard_map/ppermute | solution.py:29
  209.2 8.8 %collective-permute-start.39 = (f32[32,512]{1,0:T(8,128)S(1)}, f32[32,512]{1,0:T(8,128)S(1)}, u32[]{:S(2)}, u32[]{:S(2)}) collective-permute-start(f32[32,512]{1,0:T(8,128)S(1)} %add_add_fusion.1), channel_id=1, source_target_pairs={{0,1},{1,0},{2,3},{3,2},{4,5},{5,4},{6,7},{7,6},{8,9},{9,8},{10,11... | collective-permute-start | bytes 196616 | tf_op jit(solution)/shard_map/ppermute | solution.py:578
  217.2 3.7 %collective-permute-start.40 = (f32[32,512]{1,0:T(8,128)S(1)}, f32[32,512]{1,0:T(8,128)S(1)}, u32[]{:S(2)}, u32[]{:S(2)}) collective-permute-start(f32[32,512]{1,0:T(8,128)S(1)} %add_add_fusion.1), channel_id=1, source_target_pairs={{0,9},{1,8},{2,11},{3,10},{4,13},{5,12},{6,15},{7,14},{8,1},{9,0},... | collective-permute-start | bytes 196616 | tf_op jit(solution)/shard_map/ppermute | solution.py:578
  220.9 17.4 %collective-permute-start.44 = (bf16[512,512]{1,0:T(8,128)(2,1)}, bf16[512,512]{1,0:T(8,128)(2,1)}, u32[]{:S(2)}, u32[]{:S(2)}) collective-permute-start(bf16[512,512]{1,0:T(8,128)(2,1)} %get-tuple-element.217.refs_3_), channel_id=1, source_target_pairs={{0,2},{2,0},{4,6},{6,4},{8,10},{10,8},{12,14},{14,12},{16,18},{18,... | collective-permute-start | bytes 1572872 | tf_op jit(solution)/shard_map/ppermute | solution.py:29
  221.1 17.1 %collective-permute-start.45 = (bf16[512,384]{1,0:T(8,128)(2,1)}, bf16[512,384]{1,0:T(8,128)(2,1)S(1)}, u32[]{:S(2)}, u32[]{:S(2)}) collective-permute-start(bf16[512,384]{1,0:T(8,128)(2,1)} %get-tuple-element.218.refs_4_), channel_id=1, source_target_pairs={{0,4},{2,6},{4,0},{6,2},{8,12},{10,14},{12,8},{14,10},{16,20},{18,... | collective-permute-start | bytes 1179656 | tf_op jit(solution)/shard_map/ppermute | solution.py:29
  222.3 16.0 %collective-permute-start.46 = (bf16[512,384]{1,0:T(8,128)(2,1)}, bf16[512,384]{1,0:T(8,128)(2,1)S(1)}, u32[]{:S(2)}, u32[]{:S(2)}) collective-permute-start(bf16[512,384]{1,0:T(8,128)(2,1)} %get-tuple-element.219.refs_5_), channel_id=1, source_target_pairs={{0,8},{2,10},{4,12},{6,14},{8,0},{10,2},{12,4},{14,6},{16,24},{18,... | collective-permute-start | bytes 1179656 | tf_op jit(solution)/shard_map/ppermute | solution.py:29
  230.0 4.9 %collective-permute-start.41 = (f32[8,128]{1,0:T(8,128)S(1)}, f32[8,128]{1,0:T(8,128)S(1)}, u32[]{:S(2)}, u32[]{:S(2)}) collective-permute-start(f32[8,128]{1,0:T(8,128)S(1)} %get-tuple-element.224), channel_id=1, source_target_pairs={{0,2},{2,0},{4,6},{6,4},{8,10},{10,8},{12,14},{14,12},{16,18},{18,... | collective-permute-start | bytes 12296 | tf_op jit(solution)/shard_map/ppermute | solution.py:29
  231.5 4.3 %collective-permute-start.42 = (f32[8,128]{1,0:T(8,128)S(1)}, f32[8,128]{1,0:T(8,128)S(1)}, u32[]{:S(2)}, u32[]{:S(2)}) collective-permute-start(f32[8,128]{1,0:T(8,128)S(1)} %get-tuple-element.224), channel_id=1, source_target_pairs={{0,4},{2,6},{4,0},{6,2},{8,12},{10,14},{12,8},{14,10},{16,20},{18,... | collective-permute-start | bytes 12296 | tf_op jit(solution)/shard_map/ppermute | solution.py:29
  234.9 3.4 %collective-permute-start.43 = (f32[8,128]{1,0:T(8,128)S(1)}, f32[8,128]{1,0:T(8,128)S(1)}, u32[]{:S(2)}, u32[]{:S(2)}) collective-permute-start(f32[8,128]{1,0:T(8,128)S(1)} %get-tuple-element.224), channel_id=1, source_target_pairs={{0,6},{2,4},{4,2},{6,0},{8,14},{10,12},{12,10},{14,8},{16,22},{18,... | collective-permute-start | bytes 12296 | tf_op jit(solution)/shard_map/ppermute | solution.py:29
  238.3 3.6 %collective-permute-start.47 = (f32[8,128]{1,0:T(8,128)S(1)}, f32[8,128]{1,0:T(8,128)S(1)}, u32[]{:S(2)}, u32[]{:S(2)}) collective-permute-start(f32[8,128]{1,0:T(8,128)S(1)} %add_add_fusion.3), channel_id=1, source_target_pairs={{0,8},{2,10},{4,12},{6,14},{8,0},{10,2},{12,4},{14,6},{16,24},{18,... | collective-permute-start | bytes 12296 | tf_op jit(solution)/shard_map/ppermute | solution.py:29
  (31 other events, 664.9 us)

commit v10 on v8

--- a/solution.py
+++ b/solution.py
@@ -535,6 +535,7 @@
         scratch=buffers + [pltpu.VMEM(sums_shape, f32)], whole=range(16), streamed_out=range(3),
     )
     in_own, in_sent, stats = outs[:3], outs[3:6], outs[6]
+    got_in = along_axes(in_sent)
 
     width_pick = lax.dynamic_index_in_dim(width_states, expert, 1, keepdims=False)
 
@@ -569,15 +570,13 @@
 
     stats, got_out = lax.optimization_barrier((stats, got_out))
     group_sums, whole_sums = totals(stats)
-    in_sent, whole_sums = lax.optimization_barrier((in_sent, whole_sums))
-    got_in = along_axes(in_sent)
+    whole_sums, got_in = lax.optimization_barrier((whole_sums, got_in))
     factors, norms = call(
         norm_kernel, 52,
         [shape((STAT_ROWS, lanes), f32), shape((8, 128), f32)],
         prev, group_sums, whole_sums, *in_own, *in_sent, *out_own, *out_sent,
         scratch=fetched(in_own, in_sent, out_own, out_sent), whole=range(3, 15),
     )
-    norms, got_in = lax.optimization_barrier((norms, got_in))
     norms = totals(norms)[1]
     update_in, update_out = call(
         functools.partial(final_kernel, bounds), 52,

time: 250 us -> 248 us (level)
  waiting for transfers between devices: 132 us -> 120 us
  local copies, waits for them, and re-layouts: 14.2 us -> 19.5 us
  starting transfers between devices: 56.9 us -> 61.2 us
    ppermute x46, waiting for transfers between devices: 126 us -> 117 us  [swap(): return lax.ppermute(value, axis, pairs)]
    ppermute x4, waiting for transfers between devices: 6.24 us -> 2.37 us  [other(): return lax.ppermute(values, ('expert', 'ffn'), moves)]
    ppermute x4, starting transfers between devices: 11.8 us -> 14.4 us  [other(): return lax.ppermute(values, ('expert', 'ffn'), moves)]
    unnamed x76 -> x78, local copies, waits for them, and re-layouts: 11.9 us -> 12 us
  transfers between devices with their start and end apart: 51 -> 51, of which waited for: 32 -> 25; matrix products, arithmetic and copies ran while one was open for 0% -> 3% of each run, Pallas kernels for 11% -> 9%
where the time goes in v10:
time: 248 us
  waiting for transfers between devices  120 us (48%)
  starting transfers between devices  61.2 us (25%)
  Pallas kernels  42.6 us (17%)
  local copies, waits for them, and re-layouts  19.5 us (8%)
  other arithmetic  3.12 us (1%)
    ppermute x46, waiting for transfers between devices, swap(): return lax.ppermute(value, axis, pairs)  117 us
    pallas_call x16, Pallas kernels, call(): pl.pallas_call(kernel, out_shape=out_shape, in_specs=[spec(value, n, stre...  42.6 us
    ppermute x46, starting transfers between devices, swap(): return lax.ppermute(value, axis, pairs)  39.3 us
    ppermute x4, starting transfers between devices, other(): return lax.ppermute(values, ('expert', 'ffn'), moves)  14.4 us
    unnamed x78, local copies, waits for them, and re-layouts  12 us
    all_to_all x1, starting transfers between devices, shards(): lax.all_to_all(routed, 'expert', split_axis=0, concat_axis=0, tiled=True)  7.45 us
  transfers between devices with their start and end apart: 51, of which 25 were waited for; matrix products, arithmetic and copies ran while one was open for 3% of the time, Pallas kernels for 9%

profile of v10, /device:TPU:1, one launch (start us, length us, event | category | flops | bytes accessed | tf_op | source)
XLA Modules:
  0.0 247.6 jit_solution(8014388061807389644)
XLA Ops:
  2.7 1.2 copy-done.24
  3.9 2.0 shard_map.86
  5.9 7.5 %all-to-all-start = ((bf16[16,40,1024]{2,1,0:T(8,128)(2,1)}), bf16[16,40,1024]{2,1,0:T(8,128)(2,1)}, u32[]{:S(2)}, u32[]{:S(2)}) async-start(bf16[16,40,1024]{2,1,0:T(8,128)(2,1)} %bitcast), calls=%async_computation | async-start | bytes 2621440 | tf_op jit(solution)/shard_map/all_to_all | solution.py:463
  13.3 1.7 copy-done.16
  15.1 1.3 shard_map.87
  20.2 1.3 collective-permute-start
  23.9 23.5 %collective-permute-done.1.refs_9_.refs_12_ = bf16[3072,128]{1,0:T(8,128)(2,1)S(1)} collective-permute-done((bf16[3072,128]{1,0:T(8,128)(2,1)S(1)}, bf16[3072,128]{1,0:T(8,128)(2,1)S(1)}, u32[]{:S(2)}, u32[]{:S(2)}) %collective-permute-start.1) | collective-permute-done | bytes 786464 | tf_op jit(solution)/shard_map/ppermute | solution.py:29
  47.4 5.5 %collective-permute-done.2.refs_10_.refs_13_ = bf16[3072,128]{1,0:T(8,128)(2,1)S(1)} collective-permute-done((bf16[3072,128]{1,0:T(8,128)(2,1)S(1)}, bf16[3072,128]{1,0:T(8,128)(2,1)S(1)}, u32[]{:S(2)}, u32[]{:S(2)}) %collective-permute-start.2) | collective-permute-done | bytes 786464 | tf_op jit(solution)/shard_map/ppermute | solution.py:29
  52.9 1.7 collective-permute-done.refs_8_.refs_11_
  54.6 1.4 copy.11
  56.1 1.5 collective-permute-start.3
  58.0 1.9 collective-permute-start.5
  59.9 24.8 %collective-permute-done.3 = bf16[8,80,1024]{2,1,0:T(8,128)(2,1)S(1)} collective-permute-done((bf16[8,80,1024]{2,1,0:T(8,128)(2,1)S(1)}, bf16[8,80,1024]{2,1,0:T(8,128)(2,1)S(1)}, u32[]{:S(2)}, u32[]{:S(2)}) %collective-permute-start.3) | collective-permute-done | bytes 1310752 | tf_op jit(solution)/shard_map/ppermute | solution.py:29
  84.7 1.3 collective-permute-done.4
  87.5 2.9 %collective-permute-start.7 = (bf16[3,8,80,1024]{3,2,1,0:T(8,128)(2,1)S(1)}, bf16[3,8,80,1024]{3,2,1,0:T(8,128)(2,1)S(1)}, u32[]{:S(2)}, u32[]{:S(2)}) collective-permute-start(bf16[3,8,80,1024]{3,2,1,0:T(8,128)(2,1)S(1)} %pad_maximum_fusion.refs_1_), channel_id=1, source_target_pairs={{0,1},{1,0},{2,3},{3,2},{4,5},{5,4},{6,7},{7,6},{8,9},{9,8},{10,11... | collective-permute-start | bytes 11796488 | tf_op jit(solution)/shard_map/ppermute | solution.py:29
  90.5 2.2 shard_map.88
  92.7 1.5 collective-permute-start.10
  94.7 4.0 %collective-permute-done.6.refs_0_.refs_2_ = bf16[8,80,1024]{2,1,0:T(8,128)(2,1)S(1)} collective-permute-done((bf16[8,80,1024]{2,1,0:T(8,128)(2,1)S(1)}, bf16[8,80,1024]{2,1,0:T(8,128)(2,1)S(1)}, u32[]{:S(2)}, u32[]{:S(2)}) %collective-permute-start.6) | collective-permute-done | bytes 1310752 | tf_op jit(solution)/shard_map/ppermute | solution.py:29
  98.7 2.2 shard_map.89
  101.0 2.2 shard_map.91
  103.3 2.2 shard_map.90
  111.4 2.4 collective-permute-done.11.refs_6_
  114.4 13.5 %collective-permute-done.12.refs_7_ = bf16[160,896]{1,0:T(8,128)(2,1)S(1)} collective-permute-done((bf16[160,896]{1,0:T(8,128)(2,1)S(1)}, bf16[160,896]{1,0:T(8,128)(2,1)S(1)}, u32[]{:S(2)}, u32[]{:S(2)}) %collective-permute-start.12) | collective-permute-done | bytes 286752 | tf_op jit(solution)/shard_map/ppermute | solution.py:29
  132.3 1.4 collective-permute-done.14.refs_3_
  134.6 1.5 collective-permute-done.16.refs_5_
  137.3 3.1 %collective-permute-done.21.refs_6_ = bf16[160,768]{1,0:T(8,128)(2,1)S(1)} collective-permute-done((bf16[160,768]{1,0:T(8,128)(2,1)S(1)}, bf16[160,768]{1,0:T(8,128)(2,1)S(1)}, u32[]{:S(2)}, u32[]{:S(2)}) %collective-permute-start.21) | collective-permute-done | bytes 245792 | tf_op jit(solution)/shard_map/ppermute | solution.py:29
  141.3 1.4 collective-permute-start.25
  144.7 9.2 %collective-permute-done.24.refs_3_ = bf16[160,768]{1,0:T(8,128)(2,1)S(1)} collective-permute-done((bf16[160,768]{1,0:T(8,128)(2,1)S(1)}, bf16[160,768]{1,0:T(8,128)(2,1)S(1)}, u32[]{:S(2)}, u32[]{:S(2)}) %collective-permute-start.24) | collective-permute-done | bytes 245792 | tf_op jit(solution)/shard_map/ppermute | solution.py:29
  154.6 1.2 collective-permute-start.29
  157.2 7.6 %collective-permute-done.30.refs_13_ = bf16[320,896]{1,0:T(8,128)(2,1)S(1)} collective-permute-done((bf16[320,896]{1,0:T(8,128)(2,1)S(1)}, bf16[320,896]{1,0:T(8,128)(2,1)S(1)}, u32[]{:S(2)}, u32[]{:S(2)}) %collective-permute-start.30) | collective-permute-done | bytes 573472 | tf_op jit(solution)/shard_map/ppermute | solution.py:29
  164.8 5.0 %collective-permute-done.29.refs_11_ = bf16[320,896]{1,0:T(8,128)(2,1)S(1)} collective-permute-done((bf16[320,896]{1,0:T(8,128)(2,1)S(1)}, bf16[320,896]{1,0:T(8,128)(2,1)S(1)}, u32[]{:S(2)}, u32[]{:S(2)}) %collective-permute-start.29) | collective-permute-done | bytes 573472 | tf_op jit(solution)/shard_map/ppermute | solution.py:29
  169.8 7.3 %collective-permute-done.31.refs_15_ = bf16[320,896]{1,0:T(8,128)(2,1)S(1)} collective-permute-done((bf16[320,896]{1,0:T(8,128)(2,1)S(1)}, bf16[320,896]{1,0:T(8,128)(2,1)S(1)}, u32[]{:S(2)}, u32[]{:S(2)}) %collective-permute-start.31) | collective-permute-done | bytes 573472 | tf_op jit(solution)/shard_map/ppermute | solution.py:29
  178.0 7.9 %shard_map.98 = (f32[512,512]{1,0:T(8,128)}, f32[384,512]{1,0:T(8,128)}, f32[384,512]{1,0:T(8,128)}, bf16[512,512]{1,0:T(8,128)(2,1)}, bf16[384,512]{1,0:T(8,128...) custom-call(bf16[8,80,1024]{2,1,0:T(8,128)(2,1)} %bitcast.23, bf16[3,8,80,1024]{3,2,1,0:T(8,128)(2,1)} %copy-done.1, ...), custom_call_target="tpu_custom_call" | custom-call | tf_op jit(solution)/shard_map/pallas_call | solution.py:75
  186.9 10.0 %shard_map.99 = (f32[512,512]{1,0:T(8,128)}, f32[512,384]{1,0:T(8,128)}, f32[512,384]{1,0:T(8,128)}, bf16[512,512]{1,0:T(8,128)(2,1)}, bf16[512,384]{1,0:T(8,128...) custom-call(bf16[8,80,1024]{2,1,0:T(8,128)(2,1)} %bitcast.24, bf16[3,8,80,1024]{3,2,1,0:T(8,128)(2,1)} %copy-done.1, ...), custom_call_target="tpu_custom_call" | custom-call | tf_op jit(solution)/shard_map/pallas_call | solution.py:75
  198.1 1.5 collective-permute-start.36
  200.9 1.5 collective-permute-start.42
  202.3 1.5 collective-permute-start.43
  203.8 1.5 add_add_fusion.1
  205.3 1.5 collective-permute-start.38
  209.2 8.2 %collective-permute-start.39 = (f32[32,512]{1,0:T(8,128)}, f32[32,512]{1,0:T(8,128)}, u32[]{:S(2)}, u32[]{:S(2)}) collective-permute-start(f32[32,512]{1,0:T(8,128)} %add_add_fusion.1), channel_id=1, source_target_pairs={{0,1},{1,0},{2,3},{3,2},{4,5},{5,4},{6,7},{7,6},{8,9},{9,8},{10,11... | collective-permute-start | bytes 196616 | tf_op jit(solution)/shard_map/ppermute | solution.py:566
  217.4 2.7 %collective-permute-start.40 = (f32[32,512]{1,0:T(8,128)}, f32[32,512]{1,0:T(8,128)}, u32[]{:S(2)}, u32[]{:S(2)}) collective-permute-start(f32[32,512]{1,0:T(8,128)} %add_add_fusion.1), channel_id=1, source_target_pairs={{0,9},{1,8},{2,11},{3,10},{4,13},{5,12},{6,15},{7,14},{8,1},{9,0},... | collective-permute-start | bytes 196616 | tf_op jit(solution)/shard_map/ppermute | solution.py:566
  220.9 2.2 concatenate.3.prev
  226.3 4.4 %shard_map.100 = (f32[32,512]{1,0:T(8,128)S(1)}, f32[8,128]{1,0:T(8,128)S(1)}) custom-call(f32[32,512]{1,0:T(8,128)S(1)} %concatenate.3.prev, f32[32,512]{1,0:T(8,128)S(1)} %get-tuple-element.221.group_sums, f32[32,512]{1,0:T(8,128)S(1)} %get-tuple-element.197.whole_sums, f32[512,512]{1,0:T(8,128)} %get-tuple-element.198.refs_0_, ...), custom_call_target="tpu_custom_call" | custom-call | tf_op jit(solution)/shard_map/pallas_call | solution.py:75
  231.9 1.6 collective-permute-start.46
  233.7 1.6 collective-permute-done.46
  235.4 2.9 %collective-permute-start.48 = (f32[8,128]{1,0:T(8,128)S(1)}, f32[8,128]{1,0:T(8,128)S(1)}, u32[]{:S(2)}, u32[]{:S(2)}) collective-permute-start(f32[8,128]{1,0:T(8,128)S(1)} %add_add_fusion.3), channel_id=1, source_target_pairs={{0,1},{1,0},{2,3},{3,2},{4,5},{5,4},{6,7},{7,6},{8,9},{9,8},{10,11... | collective-permute-start | bytes 12296 | tf_op jit(solution)/shard_map/ppermute | solution.py:566
  239.2 2.2 collective-permute-done.49
  241.4 6.0 %shard_map.101 = (bf16[512,2560]{1,0:T(8,128)(2,1)}, bf16[2560,512]{1,0:T(8,128)(2,1)}) custom-call(f32[32,512]{1,0:T(8,128)S(1)} %concatenate.3.prev, f32[32,512]{1,0:T(8,128)S(1)} %get-tuple-element.204.factors, f32[32,512]{1,0:T(8,128)S(1)} %get-tuple-element.197.whole_sums, f32[8,128]{1,0:T(8,128)S(1)} %add_add_fusion.2.norms, ...), custom_call_target="tpu_custom_call" | custom-call | tf_op jit(solution)/shard_map/pallas_call | solution.py:75
  (172 shorter events, 41.9 us)
Async XLA Ops:
  5.9 48.8 %all-to-all-start = ((bf16[16,40,1024]{2,1,0:T(8,128)(2,1)}), bf16[16,40,1024]{2,1,0:T(8,128)(2,1)}, u32[]{:S(2)}, u32[]{:S(2)}) async-start(bf16[16,40,1024]{2,1,0:T(8,128)(2,1)} %bitcast), calls=%async_computation | async-start | bytes 2621440 | tf_op jit(solution)/shard_map/all_to_all | solution.py:463
  20.2 34.4 %collective-permute-start = (bf16[4096,128]{1,0:T(8,128)(2,1)S(1)}, bf16[4096,128]{1,0:T(8,128)(2,1)S(1)}, u32[]{:S(2)}, u32[]{:S(2)}) collective-permute-start(bf16[4096,128]{1,0:T(8,128)(2,1)S(1)} %get-tuple-element.108), channel_id=1, source_target_pairs={{0,2},{2,0},{4,6},{6,4},{8,10},{10,8},{12,14},{14,12},{16,18},{18,... | collective-permute-start | bytes 3145736 | tf_op jit(solution)/shard_map/ppermute | solution.py:29
  21.5 25.9 %collective-permute-start.1 = (bf16[3072,128]{1,0:T(8,128)(2,1)S(1)}, bf16[3072,128]{1,0:T(8,128)(2,1)S(1)}, u32[]{:S(2)}, u32[]{:S(2)}) collective-permute-start(bf16[3072,128]{1,0:T(8,128)(2,1)S(1)} %get-tuple-element.109), channel_id=1, source_target_pairs={{0,4},{2,6},{4,0},{6,2},{8,12},{10,14},{12,8},{14,10},{16,20},{18,... | collective-permute-start | bytes 2359304 | tf_op jit(solution)/shard_map/ppermute | solution.py:29
  22.7 30.2 %collective-permute-start.2 = (bf16[3072,128]{1,0:T(8,128)(2,1)S(1)}, bf16[3072,128]{1,0:T(8,128)(2,1)S(1)}, u32[]{:S(2)}, u32[]{:S(2)}) collective-permute-start(bf16[3072,128]{1,0:T(8,128)(2,1)S(1)} %get-tuple-element.110), channel_id=1, source_target_pairs={{0,8},{2,10},{4,12},{6,14},{8,0},{10,2},{12,4},{14,6},{16,24},{18,... | collective-permute-start | bytes 2359304 | tf_op jit(solution)/shard_map/ppermute | solution.py:29
  56.1 28.7 %collective-permute-start.3 = (bf16[8,80,1024]{2,1,0:T(8,128)(2,1)S(1)}, bf16[8,80,1024]{2,1,0:T(8,128)(2,1)S(1)}, u32[]{:S(2)}, u32[]{:S(2)}) collective-permute-start(bf16[8,80,1024]{2,1,0:T(8,128)(2,1)S(1)} %bitcast.17), channel_id=1, source_target_pairs={{0,2},{2,0},{4,6},{6,4},{8,10},{10,8},{12,14},{14,12},{16,18},{18,... | collective-permute-start | bytes 3932168 | tf_op jit(solution)/shard_map/ppermute | solution.py:29
  57.6 28.4 %collective-permute-start.4 = (bf16[8,80,1024]{2,1,0:T(8,128)(2,1)S(1)}, bf16[8,80,1024]{2,1,0:T(8,128)(2,1)S(1)}, u32[]{:S(2)}, u32[]{:S(2)}) collective-permute-start(bf16[8,80,1024]{2,1,0:T(8,128)(2,1)S(1)} %bitcast.18), channel_id=1, source_target_pairs={{0,4},{2,6},{4,0},{6,2},{8,12},{10,14},{12,8},{14,10},{16,20},{18,... | collective-permute-start | bytes 3932168 | tf_op jit(solution)/shard_map/ppermute | solution.py:29
  58.0 28.8 %collective-permute-start.5 = (bf16[8,80,1024]{2,1,0:T(8,128)(2,1)S(1)}, bf16[8,80,1024]{2,1,0:T(8,128)(2,1)S(1)}, u32[]{:S(2)}, u32[]{:S(2)}) collective-permute-start(bf16[8,80,1024]{2,1,0:T(8,128)(2,1)S(1)} %bitcast.19), channel_id=1, source_target_pairs={{0,8},{2,10},{4,12},{6,14},{8,0},{10,2},{12,4},{14,6},{16,24},{18,... | collective-permute-start | bytes 3932168 | tf_op jit(solution)/shard_map/ppermute | solution.py:29
  87.5 11.2 %collective-permute-start.7 = (bf16[3,8,80,1024]{3,2,1,0:T(8,128)(2,1)S(1)}, bf16[3,8,80,1024]{3,2,1,0:T(8,128)(2,1)S(1)}, u32[]{:S(2)}, u32[]{:S(2)}) collective-permute-start(bf16[3,8,80,1024]{3,2,1,0:T(8,128)(2,1)S(1)} %pad_maximum_fusion.refs_1_), channel_id=1, source_target_pairs={{0,1},{1,0},{2,3},{3,2},{4,5},{5,4},{6,7},{7,6},{8,9},{9,8},{10,11... | collective-permute-start | bytes 11796488 | tf_op jit(solution)/shard_map/ppermute | solution.py:29
  90.4 8.3 %collective-permute-start.6 = (bf16[8,80,1024]{2,1,0:T(8,128)(2,1)S(1)}, bf16[8,80,1024]{2,1,0:T(8,128)(2,1)S(1)}, u32[]{:S(2)}, u32[]{:S(2)}) collective-permute-start(bf16[8,80,1024]{2,1,0:T(8,128)(2,1)S(1)} %bitcast.20), channel_id=1, source_target_pairs={{0,1},{1,0},{2,3},{3,2},{4,5},{5,4},{6,7},{7,6},{8,9},{9,8},{10,11... | collective-permute-start | bytes 3932168 | tf_op jit(solution)/shard_map/ppermute | solution.py:29
  92.7 14.0 %collective-permute-start.10 = (bf16[320,896]{1,0:T(8,128)(2,1)S(1)}, bf16[320,896]{1,0:T(8,128)(2,1)S(1)}, u32[]{:S(2)}, u32[]{:S(2)}) collective-permute-start(bf16[320,896]{1,0:T(8,128)(2,1)S(1)} %get-tuple-element.126), channel_id=1, source_target_pairs={{0,8},{2,10},{4,12},{6,14},{8,0},{10,2},{12,4},{14,6},{16,24},{18,... | collective-permute-start | bytes 1720328 | tf_op jit(solution)/shard_map/ppermute | solution.py:29
  94.2 13.6 %collective-permute-start.9 = (bf16[320,896]{1,0:T(8,128)(2,1)S(1)}, bf16[320,896]{1,0:T(8,128)(2,1)S(1)}, u32[]{:S(2)}, u32[]{:S(2)}) collective-permute-start(bf16[320,896]{1,0:T(8,128)(2,1)S(1)} %get-tuple-element.125), channel_id=1, source_target_pairs={{0,4},{2,6},{4,0},{6,2},{8,12},{10,14},{12,8},{14,10},{16,20},{18,... | collective-permute-start | bytes 1720328 | tf_op jit(solution)/shard_map/ppermute | solution.py:29
  94.3 11.5 %collective-permute-start.8 = (bf16[320,768]{1,0:T(8,128)(2,1)S(1)}, bf16[320,768]{1,0:T(8,128)(2,1)S(1)}, u32[]{:S(2)}, u32[]{:S(2)}) collective-permute-start(bf16[320,768]{1,0:T(8,128)(2,1)S(1)} %get-tuple-element.124), channel_id=1, source_target_pairs={{0,2},{2,0},{4,6},{6,4},{8,10},{10,8},{12,14},{14,12},{16,18},{18,... | collective-permute-start | bytes 1474568 | tf_op jit(solution)/shard_map/ppermute | solution.py:29
  108.1 5.7 %collective-permute-start.11 = (bf16[160,768]{1,0:T(8,128)(2,1)S(1)}, bf16[160,768]{1,0:T(8,128)(2,1)S(1)}, u32[]{:S(2)}, u32[]{:S(2)}) collective-permute-start(bf16[160,768]{1,0:T(8,128)(2,1)S(1)} %get-tuple-element.158), channel_id=1, source_target_pairs={{0,2},{2,0},{4,6},{6,4},{8,10},{10,8},{12,14},{14,12},{16,18},{18,... | collective-permute-start | bytes 737288 | tf_op jit(solution)/shard_map/ppermute | solution.py:29
  108.6 21.7 %collective-permute-start.18 = (bf16[320,768]{1,0:T(8,128)(2,1)S(1)}, bf16[320,768]{1,0:T(8,128)(2,1)S(1)}, u32[]{:S(2)}, u32[]{:S(2)}) collective-permute-start(bf16[320,768]{1,0:T(8,128)(2,1)S(1)} %get-tuple-element.127), channel_id=1, source_target_pairs={{0,2},{2,0},{4,6},{6,4},{8,10},{10,8},{12,14},{14,12},{16,18},{18,... | collective-permute-start | bytes 1474568 | tf_op jit(solution)/shard_map/ppermute | solution.py:29
  109.6 21.2 %collective-permute-start.19 = (bf16[320,896]{1,0:T(8,128)(2,1)S(1)}, bf16[320,896]{1,0:T(8,128)(2,1)S(1)}, u32[]{:S(2)}, u32[]{:S(2)}) collective-permute-start(bf16[320,896]{1,0:T(8,128)(2,1)S(1)} %get-tuple-element.128), channel_id=1, source_target_pairs={{0,4},{2,6},{4,0},{6,2},{8,12},{10,14},{12,8},{14,10},{16,20},{18,... | collective-permute-start | bytes 1720328 | tf_op jit(solution)/shard_map/ppermute | solution.py:29
  109.7 21.2 %collective-permute-start.20 = (bf16[320,896]{1,0:T(8,128)(2,1)S(1)}, bf16[320,896]{1,0:T(8,128)(2,1)S(1)}, u32[]{:S(2)}, u32[]{:S(2)}) collective-permute-start(bf16[320,896]{1,0:T(8,128)(2,1)S(1)} %get-tuple-element.129), channel_id=1, source_target_pairs={{0,8},{2,10},{4,12},{6,14},{8,0},{10,2},{12,4},{14,6},{16,24},{18,... | collective-permute-start | bytes 1720328 | tf_op jit(solution)/shard_map/ppermute | solution.py:29
  110.2 17.6 %collective-permute-start.12 = (bf16[160,896]{1,0:T(8,128)(2,1)S(1)}, bf16[160,896]{1,0:T(8,128)(2,1)S(1)}, u32[]{:S(2)}, u32[]{:S(2)}) collective-permute-start(bf16[160,896]{1,0:T(8,128)(2,1)S(1)} %get-tuple-element.159), channel_id=1, source_target_pairs={{0,4},{2,6},{4,0},{6,2},{8,12},{10,14},{12,8},{14,10},{16,20},{18,... | collective-permute-start | bytes 860168 | tf_op jit(solution)/shard_map/ppermute | solution.py:29
  113.8 14.1 %collective-permute-start.13 = (bf16[160,896]{1,0:T(8,128)(2,1)S(1)}, bf16[160,896]{1,0:T(8,128)(2,1)S(1)}, u32[]{:S(2)}, u32[]{:S(2)}) collective-permute-start(bf16[160,896]{1,0:T(8,128)(2,1)S(1)} %get-tuple-element.160), channel_id=1, source_target_pairs={{0,8},{2,10},{4,12},{6,14},{8,0},{10,2},{12,4},{14,6},{16,24},{18,... | collective-permute-start | bytes 860168 | tf_op jit(solution)/shard_map/ppermute | solution.py:29
  128.6 5.1 %collective-permute-start.14 = (bf16[160,768]{1,0:T(8,128)(2,1)S(1)}, bf16[160,768]{1,0:T(8,128)(2,1)S(1)}, u32[]{:S(2)}, u32[]{:S(2)}) collective-permute-start(bf16[160,768]{1,0:T(8,128)(2,1)S(1)} %get-tuple-element.161.refs_0_), channel_id=1, source_target_pairs={{0,2},{2,0},{4,6},{6,4},{8,10},{10,8},{12,14},{14,12},{16,18},{18,... | collective-permute-start | bytes 737288 | tf_op jit(solution)/shard_map/ppermute | solution.py:29
  129.1 5.5 %collective-permute-start.15 = (bf16[160,896]{1,0:T(8,128)(2,1)S(1)}, bf16[160,896]{1,0:T(8,128)(2,1)S(1)}, u32[]{:S(2)}, u32[]{:S(2)}) collective-permute-start(bf16[160,896]{1,0:T(8,128)(2,1)S(1)} %get-tuple-element.162.refs_1_), channel_id=1, source_target_pairs={{0,4},{2,6},{4,0},{6,2},{8,12},{10,14},{12,8},{14,10},{16,20},{18,... | collective-permute-start | bytes 860168 | tf_op jit(solution)/shard_map/ppermute | solution.py:29
  130.3 5.8 %collective-permute-start.16 = (bf16[160,896]{1,0:T(8,128)(2,1)S(1)}, bf16[160,896]{1,0:T(8,128)(2,1)S(1)}, u32[]{:S(2)}, u32[]{:S(2)}) collective-permute-start(bf16[160,896]{1,0:T(8,128)(2,1)S(1)} %get-tuple-element.163.refs_2_), channel_id=1, source_target_pairs={{0,8},{2,10},{4,12},{6,14},{8,0},{10,2},{12,4},{14,6},{16,24},{18,... | collective-permute-start | bytes 860168 | tf_op jit(solution)/shard_map/ppermute | solution.py:29
  131.1 9.3 %collective-permute-start.22 = (bf16[160,896]{1,0:T(8,128)(2,1)S(1)}, bf16[160,896]{1,0:T(8,128)(2,1)S(1)}, u32[]{:S(2)}, u32[]{:S(2)}) collective-permute-start(bf16[160,896]{1,0:T(8,128)(2,1)S(1)} %get-tuple-element.178), channel_id=1, source_target_pairs={{0,4},{2,6},{4,0},{6,2},{8,12},{10,14},{12,8},{14,10},{16,20},{18,... | collective-permute-start | bytes 860168 | tf_op jit(solution)/shard_map/ppermute | solution.py:29
  131.4 9.1 %collective-permute-start.23 = (bf16[160,896]{1,0:T(8,128)(2,1)S(1)}, bf16[160,896]{1,0:T(8,128)(2,1)S(1)}, u32[]{:S(2)}, u32[]{:S(2)}) collective-permute-start(bf16[160,896]{1,0:T(8,128)(2,1)S(1)} %get-tuple-element.179), channel_id=1, source_target_pairs={{0,8},{2,10},{4,12},{6,14},{8,0},{10,2},{12,4},{14,6},{16,24},{18,... | collective-permute-start | bytes 860168 | tf_op jit(solution)/shard_map/ppermute | solution.py:29
  133.7 6.7 %collective-permute-start.21 = (bf16[160,768]{1,0:T(8,128)(2,1)S(1)}, bf16[160,768]{1,0:T(8,128)(2,1)S(1)}, u32[]{:S(2)}, u32[]{:S(2)}) collective-permute-start(bf16[160,768]{1,0:T(8,128)(2,1)S(1)} %get-tuple-element.177), channel_id=1, source_target_pairs={{0,2},{2,0},{4,6},{6,4},{8,10},{10,8},{12,14},{14,12},{16,18},{18,... | collective-permute-start | bytes 737288 | tf_op jit(solution)/shard_map/ppermute | solution.py:29
  136.2 20.6 %collective-permute-start.17 = (bf16[320,768]{1,0:T(8,128)(2,1)S(1)}, bf16[320,768]{1,0:T(8,128)(2,1)S(1)}, u32[]{:S(2)}, u32[]{:S(2)}) collective-permute-start(bf16[320,768]{1,0:T(8,128)(2,1)S(1)} %get-tuple-element.164.refs_4_), channel_id=1, source_target_pairs={{0,2},{2,0},{4,6},{6,4},{8,10},{10,8},{12,14},{14,12},{16,18},{18,... | collective-permute-start | bytes 1474568 | tf_op jit(solution)/shard_map/ppermute | solution.py:29
  141.3 13.1 %collective-permute-start.25 = (bf16[160,896]{1,0:T(8,128)(2,1)S(1)}, bf16[160,896]{1,0:T(8,128)(2,1)S(1)}, u32[]{:S(2)}, u32[]{:S(2)}) collective-permute-start(bf16[160,896]{1,0:T(8,128)(2,1)S(1)} %get-tuple-element.181.refs_1_), channel_id=1, source_target_pairs={{0,4},{2,6},{4,0},{6,2},{8,12},{10,14},{12,8},{14,10},{16,20},{18,... | collective-permute-start | bytes 860168 | tf_op jit(solution)/shard_map/ppermute | solution.py:29
  142.7 11.8 %collective-permute-start.26 = (bf16[160,896]{1,0:T(8,128)(2,1)S(1)}, bf16[160,896]{1,0:T(8,128)(2,1)S(1)}, u32[]{:S(2)}, u32[]{:S(2)}) collective-permute-start(bf16[160,896]{1,0:T(8,128)(2,1)S(1)} %get-tuple-element.182.refs_2_), channel_id=1, source_target_pairs={{0,8},{2,10},{4,12},{6,14},{8,0},{10,2},{12,4},{14,6},{16,24},{18,... | collective-permute-start | bytes 860168 | tf_op jit(solution)/shard_map/ppermute | solution.py:29
  143.0 10.9 %collective-permute-start.24 = (bf16[160,768]{1,0:T(8,128)(2,1)S(1)}, bf16[160,768]{1,0:T(8,128)(2,1)S(1)}, u32[]{:S(2)}, u32[]{:S(2)}) collective-permute-start(bf16[160,768]{1,0:T(8,128)(2,1)S(1)} %get-tuple-element.180.refs_0_), channel_id=1, source_target_pairs={{0,2},{2,0},{4,6},{6,4},{8,10},{10,8},{12,14},{14,12},{16,18},{18,... | collective-permute-start | bytes 737288 | tf_op jit(solution)/shard_map/ppermute | solution.py:29
  143.6 13.6 %collective-permute-start.28 = (bf16[320,896]{1,0:T(8,128)(2,1)S(1)}, bf16[320,896]{1,0:T(8,128)(2,1)S(1)}, u32[]{:S(2)}, u32[]{:S(2)}) collective-permute-start(bf16[320,896]{1,0:T(8,128)(2,1)S(1)} %get-tuple-element.184.refs_8_), channel_id=1, source_target_pairs={{0,4},{2,6},{4,0},{6,2},{8,12},{10,14},{12,8},{14,10},{16,20},{18,... | collective-permute-start | bytes 1720328 | tf_op jit(solution)/shard_map/ppermute | solution.py:29
  153.9 10.9 %collective-permute-start.30 = (bf16[320,896]{1,0:T(8,128)(2,1)S(1)}, bf16[320,896]{1,0:T(8,128)(2,1)S(1)}, u32[]{:S(2)}, u32[]{:S(2)}) collective-permute-start(bf16[320,896]{1,0:T(8,128)(2,1)S(1)} %get-tuple-element.186.refs_12_), channel_id=1, source_target_pairs={{0,8},{2,10},{4,12},{6,14},{8,0},{10,2},{12,4},{14,6},{16,24},{18,... | collective-permute-start | bytes 1720328 | tf_op jit(solution)/shard_map/ppermute | solution.py:29
  154.6 15.1 %collective-permute-start.29 = (bf16[320,896]{1,0:T(8,128)(2,1)S(1)}, bf16[320,896]{1,0:T(8,128)(2,1)S(1)}, u32[]{:S(2)}, u32[]{:S(2)}) collective-permute-start(bf16[320,896]{1,0:T(8,128)(2,1)S(1)} %get-tuple-element.185.refs_10_), channel_id=1, source_target_pairs={{0,4},{2,6},{4,0},{6,2},{8,12},{10,14},{12,8},{14,10},{16,20},{18,... | collective-permute-start | bytes 1720328 | tf_op jit(solution)/shard_map/ppermute | solution.py:29
  155.9 21.2 %collective-permute-start.31 = (bf16[320,896]{1,0:T(8,128)(2,1)S(1)}, bf16[320,896]{1,0:T(8,128)(2,1)S(1)}, u32[]{:S(2)}, u32[]{:S(2)}) collective-permute-start(bf16[320,896]{1,0:T(8,128)(2,1)S(1)} %get-tuple-element.187.refs_14_), channel_id=1, source_target_pairs={{0,8},{2,10},{4,12},{6,14},{8,0},{10,2},{12,4},{14,6},{16,24},{18,... | collective-permute-start | bytes 1720328 | tf_op jit(solution)/shard_map/ppermute | solution.py:29
  156.8 8.0 %collective-permute-start.27 = (bf16[320,768]{1,0:T(8,128)(2,1)S(1)}, bf16[320,768]{1,0:T(8,128)(2,1)S(1)}, u32[]{:S(2)}, u32[]{:S(2)}) collective-permute-start(bf16[320,768]{1,0:T(8,128)(2,1)S(1)} %get-tuple-element.183.refs_6_), channel_id=1, source_target_pairs={{0,2},{2,0},{4,6},{6,4},{8,10},{10,8},{12,14},{14,12},{16,18},{18,... | collective-permute-start | bytes 1474568 | tf_op jit(solution)/shard_map/ppermute | solution.py:29
  185.9 11.1 %collective-permute-start.32 = (bf16[512,512]{1,0:T(8,128)(2,1)}, bf16[512,512]{1,0:T(8,128)(2,1)S(1)}, u32[]{:S(2)}, u32[]{:S(2)}) collective-permute-start(bf16[512,512]{1,0:T(8,128)(2,1)} %get-tuple-element.190.refs_9_), channel_id=1, source_target_pairs={{0,2},{2,0},{4,6},{6,4},{8,10},{10,8},{12,14},{14,12},{16,18},{18,... | collective-permute-start | bytes 1572872 | tf_op jit(solution)/shard_map/ppermute | solution.py:29
  186.3 10.6 %collective-permute-start.33 = (bf16[384,512]{1,0:T(8,128)(2,1)}, bf16[384,512]{1,0:T(8,128)(2,1)S(1)}, u32[]{:S(2)}, u32[]{:S(2)}) collective-permute-start(bf16[384,512]{1,0:T(8,128)(2,1)} %get-tuple-element.191.refs_10_), channel_id=1, source_target_pairs={{0,4},{2,6},{4,0},{6,2},{8,12},{10,14},{12,8},{14,10},{16,20},{18,... | collective-permute-start | bytes 1179656 | tf_op jit(solution)/shard_map/ppermute | solution.py:29
  186.3 10.6 %collective-permute-start.34 = (bf16[384,512]{1,0:T(8,128)(2,1)}, bf16[384,512]{1,0:T(8,128)(2,1)S(1)}, u32[]{:S(2)}, u32[]{:S(2)}) collective-permute-start(bf16[384,512]{1,0:T(8,128)(2,1)} %get-tuple-element.192.refs_11_), channel_id=1, source_target_pairs={{0,8},{2,10},{4,12},{6,14},{8,0},{10,2},{12,4},{14,6},{16,24},{18,... | collective-permute-start | bytes 1179656 | tf_op jit(solution)/shard_map/ppermute | solution.py:29
  197.0 5.4 %collective-permute-start.35 = (f32[32,512]{1,0:T(8,128)}, f32[32,512]{1,0:T(8,128)S(1)}, u32[]{:S(2)}, u32[]{:S(2)}) collective-permute-start(f32[32,512]{1,0:T(8,128)} %get-tuple-element.193), channel_id=1, source_target_pairs={{0,2},{2,0},{4,6},{6,4},{8,10},{10,8},{12,14},{14,12},{16,18},{18,... | collective-permute-start | bytes 196616 | tf_op jit(solution)/shard_map/ppermute | solution.py:29
  198.1 5.7 %collective-permute-start.36 = (f32[32,512]{1,0:T(8,128)}, f32[32,512]{1,0:T(8,128)S(1)}, u32[]{:S(2)}, u32[]{:S(2)}) collective-permute-start(f32[32,512]{1,0:T(8,128)} %get-tuple-element.193), channel_id=1, source_target_pairs={{0,4},{2,6},{4,0},{6,2},{8,12},{10,14},{12,8},{14,10},{16,20},{18,... | collective-permute-start | bytes 196616 | tf_op jit(solution)/shard_map/ppermute | solution.py:29
  199.5 4.3 %collective-permute-start.37 = (f32[32,512]{1,0:T(8,128)}, f32[32,512]{1,0:T(8,128)S(1)}, u32[]{:S(2)}, u32[]{:S(2)}) collective-permute-start(f32[32,512]{1,0:T(8,128)} %get-tuple-element.193), channel_id=1, source_target_pairs={{0,6},{2,4},{4,2},{6,0},{8,14},{10,12},{12,10},{14,8},{16,22},{18,... | collective-permute-start | bytes 196616 | tf_op jit(solution)/shard_map/ppermute | solution.py:29
  199.7 24.4 %collective-permute-start.41 = (bf16[512,512]{1,0:T(8,128)(2,1)}, bf16[512,512]{1,0:T(8,128)(2,1)S(1)}, u32[]{:S(2)}, u32[]{:S(2)}) collective-permute-start(bf16[512,512]{1,0:T(8,128)(2,1)} %get-tuple-element.194.refs_3_), channel_id=1, source_target_pairs={{0,2},{2,0},{4,6},{6,4},{8,10},{10,8},{12,14},{14,12},{16,18},{18,... | collective-permute-start | bytes 1572872 | tf_op jit(solution)/shard_map/ppermute | solution.py:29
  200.9 23.2 %collective-permute-start.42 = (bf16[512,384]{1,0:T(8,128)(2,1)}, bf16[512,384]{1,0:T(8,128)(2,1)S(1)}, u32[]{:S(2)}, u32[]{:S(2)}) collective-permute-start(bf16[512,384]{1,0:T(8,128)(2,1)} %get-tuple-element.195.refs_4_), channel_id=1, source_target_pairs={{0,4},{2,6},{4,0},{6,2},{8,12},{10,14},{12,8},{14,10},{16,20},{18,... | collective-permute-start | bytes 1179656 | tf_op jit(solution)/shard_map/ppermute | solution.py:29
  202.3 21.8 %collective-permute-start.43 = (bf16[512,384]{1,0:T(8,128)(2,1)}, bf16[512,384]{1,0:T(8,128)(2,1)S(1)}, u32[]{:S(2)}, u32[]{:S(2)}) collective-permute-start(bf16[512,384]{1,0:T(8,128)(2,1)} %get-tuple-element.196.refs_5_), channel_id=1, source_target_pairs={{0,8},{2,10},{4,12},{6,14},{8,0},{10,2},{12,4},{14,6},{16,24},{18,... | collective-permute-start | bytes 1179656 | tf_op jit(solution)/shard_map/ppermute | solution.py:29
  205.3 12.1 %collective-permute-start.38 = (f32[32,512]{1,0:T(8,128)}, f32[32,512]{1,0:T(8,128)}, u32[]{:S(2)}, u32[]{:S(2)}) collective-permute-start(f32[32,512]{1,0:T(8,128)} %add_add_fusion.1), channel_id=1, source_target_pairs={{0,8},{2,10},{4,12},{6,14},{8,0},{10,2},{12,4},{14,6},{16,24},{18,... | collective-permute-start | bytes 196616 | tf_op jit(solution)/shard_map/ppermute | solution.py:29
  209.2 13.9 %collective-permute-start.39 = (f32[32,512]{1,0:T(8,128)}, f32[32,512]{1,0:T(8,128)}, u32[]{:S(2)}, u32[]{:S(2)}) collective-permute-start(f32[32,512]{1,0:T(8,128)} %add_add_fusion.1), channel_id=1, source_target_pairs={{0,1},{1,0},{2,3},{3,2},{4,5},{5,4},{6,7},{7,6},{8,9},{9,8},{10,11... | collective-permute-start | bytes 196616 | tf_op jit(solution)/shard_map/ppermute | solution.py:566
  217.4 5.7 %collective-permute-start.40 = (f32[32,512]{1,0:T(8,128)}, f32[32,512]{1,0:T(8,128)}, u32[]{:S(2)}, u32[]{:S(2)}) collective-permute-start(f32[32,512]{1,0:T(8,128)} %add_add_fusion.1), channel_id=1, source_target_pairs={{0,9},{1,8},{2,11},{3,10},{4,13},{5,12},{6,15},{7,14},{8,1},{9,0},... | collective-permute-start | bytes 196616 | tf_op jit(solution)/shard_map/ppermute | solution.py:566
  231.9 3.4 %collective-permute-start.46 = (f32[8,128]{1,0:T(8,128)S(1)}, f32[8,128]{1,0:T(8,128)S(1)}, u32[]{:S(2)}, u32[]{:S(2)}) collective-permute-start(f32[8,128]{1,0:T(8,128)S(1)} %get-tuple-element.205), channel_id=1, source_target_pairs={{0,6},{2,4},{4,2},{6,0},{8,14},{10,12},{12,10},{14,8},{16,22},{18,... | collective-permute-start | bytes 12296 | tf_op jit(solution)/shard_map/ppermute | solution.py:29
  235.3 3.7 %collective-permute-start.47 = (f32[8,128]{1,0:T(8,128)S(1)}, f32[8,128]{1,0:T(8,128)S(1)}, u32[]{:S(2)}, u32[]{:S(2)}) collective-permute-start(f32[8,128]{1,0:T(8,128)S(1)} %add_add_fusion.3), channel_id=1, source_target_pairs={{0,8},{2,10},{4,12},{6,14},{8,0},{10,2},{12,4},{14,6},{16,24},{18,... | collective-permute-start | bytes 12296 | tf_op jit(solution)/shard_map/ppermute | solution.py:29
  235.4 3.7 %collective-permute-start.48 = (f32[8,128]{1,0:T(8,128)S(1)}, f32[8,128]{1,0:T(8,128)S(1)}, u32[]{:S(2)}, u32[]{:S(2)}) collective-permute-start(f32[8,128]{1,0:T(8,128)S(1)} %add_add_fusion.3), channel_id=1, source_target_pairs={{0,1},{1,0},{2,3},{3,2},{4,5},{5,4},{6,7},{7,6},{8,9},{9,8},{10,11... | collective-permute-start | bytes 12296 | tf_op jit(solution)/shard_map/ppermute | solution.py:566
  (41 other events, 740.7 us)
